TPU v7x, 32 devices: a whole 2x2x4 slice. The times are simulated.
32 devices in a mesh: gx: 8 (over z, y), gy: 4 (over x, core).
Axes of the slice: x: 2, y: 2, z: 4, core: 2. Of those that a mesh axis runs over, the one named last changes fastest.
Arguments:
- mass_per_volume: float32 [1024, 2048], P('gy', 'gx'), may hold values from 0.5 to 2
- motion_speed: float32 [1024, 3, 2048], P('gy', None, 'gx'), may hold values from -3 to 3
- agitation_energy: float32 [1024, 2048], P('gy', 'gx'), may hold values from 0.5 to 2
- shear_deviatoric: float32 [1024, 5, 2048], P('gy', None, 'gx'), may hold values from -2.4 to 2.4
- thermal_current_array: float32 [1024, 3, 2048], P('gy', None, 'gx'), may hold values from -2.4 to 2.4
Outputs:
- rate: float32 [1024, 13, 2048], P('gy', None, 'gx')
All inputs are finite; a program needn't handle non-finite values.
Results may differ from a plain program's by a relative error of at most 0.0043.
The roundings to bfloat16 on the way count: a program that leaves them out, or rounds other values in their place, can miss the bound.
Values may be sent and summed in bfloat16 or wider, within the bound.
No kernel may reach another device: no remote copies, remote signals or barrier semaphores. Data moves between devices by JAX's collectives and lax.ppermute only.
A program may use at most 64 MiB of HBM per device.

v0:
```python
import math

import jax
import jax.numpy as jnp
from jax import lax
from jax.sharding import PartitionSpec as P

CROSS_NODES = 1024


time_step = 0.05
enforcement_weight = 4.0
plate_speed = 0.5
dissipation_speed = 0.25


def extended(shard, sides, width):
    for axis, dim in sides:
        count, length = (lax.axis_size(axis), shard.shape[dim])
        up = [(i, (i + 1) % count) for i in range(count)]
        down = [(j, i) for i, j in up]
        last = lax.slice_in_dim(shard, length - width, length, axis=dim)
        initial = lax.slice_in_dim(shard, 0, width, axis=dim)
        before = lax.ppermute(last, axis, up)
        after = lax.ppermute(initial, axis, down)
        shard = jnp.concatenate([before, shard, after], axis=dim)
    return shard


def derivative_rows(first, count, size):
    last = size - 1
    half = math.pi / (2.0 * last)
    rows = first + jnp.arange(count, dtype=jnp.int32)
    cols = jnp.arange(size, dtype=jnp.int32)
    summed = (rows[:, None] + cols[None, :]).astype(jnp.float32)
    differ = rows[:, None] - cols[None, :]
    same = differ == 0
    denom = -2.0 * jnp.sin(half * summed) * jnp.sin(half * differ.astype(jnp.float32))
    safe = jnp.where(same, jnp.float32(1.0), denom)

    def weights(index):
        edge = jnp.where((index == 0) | (index == last), jnp.float32(2.0), jnp.float32(1.0))
        parity = (1 - 2 * (index % 2)).astype(jnp.float32)
        return edge * parity

    ratio = weights(rows)[:, None] / weights(cols)[None, :]
    scale = math.pi / last * jnp.sin(2.0 * half * rows.astype(jnp.float32))
    offdiag = jnp.where(same, jnp.float32(0.0), scale[:, None] * ratio / safe)
    diagonal = -jnp.sum(offdiag, axis=1)
    return (offdiag + jnp.where(same, diagonal[:, None], jnp.float32(0.0))).astype(jnp.bfloat16)


def fluxes(unknown_collection):
    agitation_energy = unknown_collection[:, 4]
    motion_speed = [unknown_collection[:, 1], unknown_collection[:, 2], unknown_collection[:, 3]]
    traction_matrix = [
        [unknown_collection[:, 5], unknown_collection[:, 6], unknown_collection[:, 8]],
        [unknown_collection[:, 6], unknown_collection[:, 7], unknown_collection[:, 9]],
        [
            unknown_collection[:, 8],
            unknown_collection[:, 9],
            -(unknown_collection[:, 5] + unknown_collection[:, 7]),
        ],
    ]
    thermal_current_entry = [
        unknown_collection[:, 10],
        unknown_collection[:, 11],
        unknown_collection[:, 12],
    ]
    pairs = [(0, 0), (0, 1), (1, 1), (0, 2), (1, 2)]
    result = []
    for spatial_axis_number in (0, 1):
        transported_quantity = motion_speed[spatial_axis_number]
        local_quantity = [unknown_collection[:, 0] * transported_quantity]
        for leading_subscript in range(3):
            local_quantity.append(
                motion_speed[leading_subscript] * transported_quantity
                + traction_matrix[leading_subscript][spatial_axis_number]
                + (agitation_energy if leading_subscript == spatial_axis_number else 0.0)
            )
        local_quantity.append(
            transported_quantity * agitation_energy
            + 2.0 / 3.0 * thermal_current_entry[spatial_axis_number]
        )
        for leading_subscript, trailing_subscript in pairs:
            production_entry = (
                transported_quantity * traction_matrix[leading_subscript][trailing_subscript]
            )
            production_entry = production_entry + 0.4 * (
                (
                    thermal_current_entry[leading_subscript]
                    if trailing_subscript == spatial_axis_number
                    else 0.0
                )
                + (
                    thermal_current_entry[trailing_subscript]
                    if leading_subscript == spatial_axis_number
                    else 0.0
                )
            )
            production_entry = production_entry - (
                4.0 / 15.0 * thermal_current_entry[spatial_axis_number]
                if leading_subscript == trailing_subscript
                else 0.0
            )
            local_quantity.append(production_entry)
        for leading_subscript in range(3):
            local_quantity.append(
                transported_quantity * thermal_current_entry[leading_subscript]
                + agitation_energy * traction_matrix[leading_subscript][spatial_axis_number]
                + (
                    2.5 * agitation_energy * agitation_energy
                    if leading_subscript == spatial_axis_number
                    else 0.0
                )
            )
        result.append(jnp.stack(local_quantity, axis=1))
    return (result[0], result[1])


def source(unknown_collection, rows, size):
    mass_per_volume = unknown_collection[:, 0]
    agitation_energy = unknown_collection[:, 4]
    impact_often_measure = mass_per_volume * jnp.sqrt(agitation_energy * agitation_energy + 0.25)
    plate_condition = jnp.where(
        rows == 0,
        jnp.float32(1.0),
        jnp.where(rows == size - 1, jnp.float32(-1.0), jnp.float32(0.0)),
    )[:, None]
    radial_distribution = jnp.abs(plate_condition)
    blank_quantity = jnp.zeros_like(mass_per_volume)
    production_entries = [
        blank_quantity,
        -enforcement_weight
        * radial_distribution
        * (unknown_collection[:, 1] - plate_speed * plate_condition),
        blank_quantity,
        blank_quantity,
        -dissipation_speed * impact_often_measure * agitation_energy
        - enforcement_weight * radial_distribution * (agitation_energy - 1.0),
    ]
    production_entries = production_entries + [
        -0.8 * impact_often_measure * unknown_collection[:, k] for k in range(5, 10)
    ]
    production_entries = production_entries + [
        -0.55 * impact_often_measure * unknown_collection[:, k] for k in range(10, 13)
    ]
    return jnp.stack(production_entries, axis=1)


def streamwise(flux_x):
    padded = extended(flux_x, (("gx", 2),), 3)
    width = flux_x.shape[2]
    coeffs = (0.75, -0.15, 1.0 / 60.0)
    along = jnp.zeros_like(flux_x)
    for k in range(3):
        upper = padded[:, :, 4 + k : 4 + k + width]
        lower = padded[:, :, 2 - k : 2 - k + width]
        along = along + coeffs[k] * (upper - lower)
    return along


def wall_normal(lowered, grid):
    piece = lax.all_gather(lowered, "gy", axis=0, tiled=True)
    summed = jnp.dot(grid, piece.reshape(piece.shape[0], -1), preferred_element_type=jnp.float32)
    return summed.reshape(lowered.shape)


def section_rate(unknown_collection, grid, rows):
    flux_x, flux_y = fluxes(unknown_collection)
    along = streamwise(flux_x)
    across = wall_normal(flux_y.astype(jnp.bfloat16), grid)
    return -(along + across) + source(unknown_collection, rows, CROSS_NODES)


def on_device(
    mass_per_volume, motion_speed, agitation_energy, shear_deviatoric, thermal_current_array
):
    unknown_collection = jnp.concatenate(
        [
            mass_per_volume[:, None],
            motion_speed,
            agitation_energy[:, None],
            shear_deviatoric,
            thermal_current_array,
        ],
        axis=1,
    )
    height = unknown_collection.shape[0]
    first = lax.axis_index("gy") * height
    rows = first + jnp.arange(height, dtype=jnp.int32)
    grid = derivative_rows(first, height, CROSS_NODES)
    first_rate = section_rate(unknown_collection, grid, rows)
    middle = unknown_collection + time_step * first_rate
    second_rate = section_rate(middle, grid, rows)
    return 0.5 * (first_rate + second_rate)


def solution(mesh):
    return jax.shard_map(
        on_device,
        mesh=mesh,
        in_specs=(
            P("gy", "gx"),
            P("gy", None, "gx"),
            P("gy", "gx"),
            P("gy", None, "gx"),
            P("gy", None, "gx"),
        ),
        out_specs=P("gy", None, "gx"),
        check_vma=False,
    )
```

profile of v0, /device:TPU:0, one launch (start us, length us, event | category | flops | bytes accessed | tf_op | source)
XLA Modules:
  0.0 188.6 jit_solution(17868473325460940261)
XLA Ops:
  6.5 1.1 copy.7
  7.6 1.4 copy.6
  9.0 1.1 copy.9
  10.1 1.7 copy.8
  11.8 1.4 copy.15
  13.9 0.7 constant_dynamic-update-slice_fusion.12
  14.6 0.7 constant_dynamic-update-slice_fusion.11
  17.4 0.7 constant_dynamic-update-slice_fusion.7
  18.1 0.7 constant_dynamic-update-slice_fusion.6
  19.5 0.7 constant_dynamic-update-slice_fusion.4
  20.2 0.7 constant_dynamic-update-slice_fusion.3
  20.9 0.7 constant_dynamic-update-slice_fusion.2
  21.7 0.7 constant_dynamic-update-slice_fusion.1
  23.7 3.0 %collective-permute-start.1 = (f32[256,13,3]{0,2,1:T(4,128)S(1)}, f32[256,13,3]{0,2,1:T(4,128)S(1)}, u32[]{:S(2)}, u32[]{:S(2)}) collective-permute-start(f32[256,13,3]{0,2,1:T(4,128)S(1)} %get-tuple-element.19), channel_id=1, source_target_pairs={{0,4},{4,8},{8,12},{12,16},{16,20},{20,24},{24,28},{28,0},{1,5},{5... | collective-permute-start | bytes 119816 | tf_op jit(solution)/shard_map/ppermute | solution.py:24
  26.7 3.3 %collective-permute-start = (f32[256,13,3]{0,2,1:T(4,128)S(1)}, f32[256,13,3]{0,2,1:T(4,128)S(1)}, u32[]{:S(2)}, u32[]{:S(2)}) collective-permute-start(f32[256,13,3]{0,2,1:T(4,128)S(1)} %get-tuple-element.18), channel_id=1, source_target_pairs={{4,0},{8,4},{12,8},{16,12},{20,16},{24,20},{28,24},{0,28},{5,1},{9... | collective-permute-start | bytes 119816 | tf_op jit(solution)/shard_map/ppermute | solution.py:25
  30.5 7.6 %fusion.40 = f32[256]{0:T(256)S(1)} fusion(f32[1024]{0:T(1024)S(1)} %fusion.82, f32[256]{0:T(256)S(1)} %get-tuple-element.28, f32[256]{0:T(256)S(1)} %get-tuple-element.29, s32[256]{0:T(256)S(1)} %iota_add_fusion), kind=kLoop, calls=%fused_computation.56 | loop fusion | flops 3931904 | bytes 8192 | tf_op jit(solution)/shard_map/reduce_sum | solution.py:49
  38.2 1.7 copy-done.4
  39.9 35.9 %all-gather.3.cloned.1.call-done = bf16[1024,13,256]{0,2,1:T(8,128)(2,1)} async-done(((bf16[256,13,256]{0,2,1:T(8,128)(2,1)}), bf16[1024,13,256]{0,2,1:T(8,128)(2,1)}) %all-gather.3.cloned.1.call-update) | async-done | bytes 6815760 | tf_op jit(solution)/shard_map/all_gather | solution.py:164
  75.8 22.4 %multiply_add_fusion = (f32[256,13,256]{0,2,1:T(8,128)S(1)}, f32[256,13,256]{0,2,1:T(8,128)}) fusion(f32[256,13,256]{0,2,1:T(8,128)} %copy-done.4, f32[256,13,256]{0,2,1:T(8,128)} %copy-done.2, bf16[1024,13,256]{0,2,1:T(8,128)(2,1)} %all-gather.3.cloned.1.call-done, f32[256]{0:T(256)S(1)} %neg.13, s32[256]{0:T(256)S(1)} %iota_add_fusion, ...), kind=kOutput, calls=%fused_computation.48 | convolution fusion | flops 1765474304 | bytes 23943168 | tf_op jit(solution)/shard_map/dot_general | solution.py:165
  98.9 0.7 constant_dynamic-update-slice_fusion.30
  102.4 0.7 constant_dynamic-update-slice_fusion.25
  103.1 0.7 constant_dynamic-update-slice_fusion.24
  104.5 0.7 constant_dynamic-update-slice_fusion.22
  105.2 0.7 constant_dynamic-update-slice_fusion.21
  105.9 0.7 constant_dynamic-update-slice_fusion.20
  106.6 0.7 constant_dynamic-update-slice_fusion.19
  108.7 1.5 collective-permute-start.3
  110.1 3.3 %collective-permute-start.2 = (f32[256,13,3]{0,2,1:T(4,128)S(1)}, f32[256,13,3]{0,2,1:T(4,128)S(1)}, u32[]{:S(2)}, u32[]{:S(2)}) collective-permute-start(f32[256,13,3]{0,2,1:T(4,128)S(1)} %get-tuple-element.9), channel_id=1, source_target_pairs={{4,0},{8,4},{12,8},{16,12},{20,16},{24,20},{28,24},{0,28},{5,1},{9... | collective-permute-start | bytes 119816 | tf_op jit(solution)/shard_map/ppermute | solution.py:25
  113.5 2.1 %collective-permute-done.3 = f32[256,13,3]{0,2,1:T(4,128)S(1)} collective-permute-done((f32[256,13,3]{0,2,1:T(4,128)S(1)}, f32[256,13,3]{0,2,1:T(4,128)S(1)}, u32[]{:S(2)}, u32[]{:S(2)}) %collective-permute-start.3) | collective-permute-done | bytes 39968 | tf_op jit(solution)/shard_map/ppermute | solution.py:24
  115.6 42.1 %all-gather.5.cloned.1.call-done = bf16[1024,13,256]{0,2,1:T(8,128)(2,1)} async-done(((bf16[256,13,256]{0,2,1:T(8,128)(2,1)}), bf16[1024,13,256]{0,2,1:T(8,128)(2,1)}) %all-gather.5.cloned.1.call-update) | async-done | bytes 6815760 | tf_op jit(solution)/shard_map/all_gather | solution.py:164
  157.6 21.2 %fusion.13 = f32[256,13,256]{0,2,1:T(8,128)S(1)} fusion(f32[256,13,256]{0,2,1:T(8,128)} %get-tuple-element.27, f32[256,13,256]{0,2,1:T(8,128)} %copy-done.3, f32[256,13,3]{0,2,1:T(4,128)S(1)} %collective-permute-done.3, f32[256,13,3]{0,2,1:T(4,128)S(1)} %collective-permute-done.2, f32[256,13,256]{0,2,1:T(8,128)} %copy-done.1, ...), kind=kOutput, calls=%fused_computation.21 | convolution fusion | flops 1765474304 | bytes 20535296 | tf_op jit(solution)/shard_map/dot_general | solution.py:165
  178.8 3.0 %copy.41 = f32[256,13,256]{2,0,1:T(8,128)} copy(f32[256,13,256]{0,2,1:T(8,128)S(1)} %fusion.13) | data formatting | bytes 6815744 | tf_op jit(solution)/shard_map/mul | solution.py:196
  (82 shorter events, 10.5 us)
Async XLA Ops:
  6.5 69.3 %all-gather.3.cloned.1.call-start = ((), (), s32[]{:S(2)}) async-start(), calls=%async_computation | async-start | bytes 8519680 | tf_op jit(solution)/shard_map/all_gather | solution.py:164
  22.4 135.2 %all-gather.5.cloned.1.call-start = ((), (), s32[]{:S(2)}) async-start(), calls=%async_computation.1 | async-start | bytes 8519680 | tf_op jit(solution)/shard_map/all_gather | solution.py:164
  23.6 6.8 %copy-start = (f32[256,13,256]{0,2,1:T(8,128)}, f32[256,13,256]{0,2,1:T(8,128)S(1)}, u32[]{:S(2)}) copy-start(f32[256,13,256]{0,2,1:T(8,128)S(1)} %get-tuple-element.20) | copy-start | bytes 10223620
  23.7 14.5 %collective-permute-start.1 = (f32[256,13,3]{0,2,1:T(4,128)S(1)}, f32[256,13,3]{0,2,1:T(4,128)S(1)}, u32[]{:S(2)}, u32[]{:S(2)}) collective-permute-start(f32[256,13,3]{0,2,1:T(4,128)S(1)} %get-tuple-element.19), channel_id=1, source_target_pairs={{0,4},{4,8},{8,12},{12,16},{16,20},{20,24},{24,28},{28,0},{1,5},{5... | collective-permute-start | bytes 119816 | tf_op jit(solution)/shard_map/ppermute | solution.py:24
  26.7 13.2 %collective-permute-start = (f32[256,13,3]{0,2,1:T(4,128)S(1)}, f32[256,13,3]{0,2,1:T(4,128)S(1)}, u32[]{:S(2)}, u32[]{:S(2)}) collective-permute-start(f32[256,13,3]{0,2,1:T(4,128)S(1)} %get-tuple-element.18), channel_id=1, source_target_pairs={{4,0},{8,4},{12,8},{16,12},{20,16},{24,20},{28,24},{0,28},{5,1},{9... | collective-permute-start | bytes 119816 | tf_op jit(solution)/shard_map/ppermute | solution.py:25
  30.5 7.7 %copy-start.2 = (f32[256,13,256]{0,2,1:T(8,128)}, f32[256,13,256]{0,2,1:T(8,128)S(1)}, u32[]{:S(2)}) copy-start(f32[256,13,256]{0,2,1:T(8,128)S(1)} %bitcast_dynamic-update-slice_fusion.2) | copy-start | bytes 10223620
  38.1 1.8 copy-start.4
  108.6 6.9 %copy-start.1 = (f32[256,13,256]{0,2,1:T(8,128)}, f32[256,13,256]{0,2,1:T(8,128)S(1)}, u32[]{:S(2)}) copy-start(f32[256,13,256]{0,2,1:T(8,128)S(1)} %get-tuple-element.11) | copy-start | bytes 10223620
  108.7 6.9 %collective-permute-start.3 = (f32[256,13,3]{0,2,1:T(4,128)S(1)}, f32[256,13,3]{0,2,1:T(4,128)S(1)}, u32[]{:S(2)}, u32[]{:S(2)}) collective-permute-start(f32[256,13,3]{0,2,1:T(4,128)S(1)} %get-tuple-element.10), channel_id=1, source_target_pairs={{0,4},{4,8},{8,12},{12,16},{16,20},{20,24},{24,28},{28,0},{1,5},{5... | collective-permute-start | bytes 119816 | tf_op jit(solution)/shard_map/ppermute | solution.py:24
  110.1 5.4 %collective-permute-start.2 = (f32[256,13,3]{0,2,1:T(4,128)S(1)}, f32[256,13,3]{0,2,1:T(4,128)S(1)}, u32[]{:S(2)}, u32[]{:S(2)}) collective-permute-start(f32[256,13,3]{0,2,1:T(4,128)S(1)} %get-tuple-element.9), channel_id=1, source_target_pairs={{4,0},{8,4},{12,8},{16,12},{20,16},{24,20},{28,24},{0,28},{5,1},{9... | collective-permute-start | bytes 119816 | tf_op jit(solution)/shard_map/ppermute | solution.py:25
  113.5 2.1 %copy-start.3 = (f32[256,13,256]{0,2,1:T(8,128)}, f32[256,13,256]{0,2,1:T(8,128)S(1)}, u32[]{:S(2)}) copy-start(f32[256,13,256]{0,2,1:T(8,128)S(1)} %multiply_dynamic-update-slice_fusion) | copy-start | bytes 10223620
Sparse Core Ops, SparseCore 0:
  22.5 53.2 all-gather.2
  107.5 50.1 all-gather.4
where the time goes:
time: 189 us
  waiting for transfers between devices  80.1 us (42%)
  matrix products  43.5 us (23%)
  other arithmetic  28.2 us (15%)
  between operations  13.9 us (7%)
  local copies, waits for them, and re-layouts  11.8 us (6%)
  starting transfers between devices  11.1 us (6%)
    all_gather x2, waiting for transfers between devices, wall_normal(): piece = lax.all_gather(lowered, 'gy', axis=0, tiled=True)  78 us
    dot_general x2, matrix products, wall_normal(): jnp.dot(grid, piece.reshape(piece.shape[0], -1), preferred_element_type=j...  43.5 us
    unnamed x60, other arithmetic  18.8 us
    unnamed x21, local copies, waits for them, and re-layouts  8.69 us
    reduce_sum x1, other arithmetic, derivative_rows(): diagonal = -jnp.sum(offdiag, axis=1)  7.57 us
    ppermute x2, starting transfers between devices, extended(): after = lax.ppermute(initial, axis, down)  6.6 us
    ppermute x2, starting transfers between devices, extended(): before = lax.ppermute(last, axis, up)  4.48 us
  transfers between devices with their start and end apart: 6, of which 3 were waited for; matrix products, arithmetic and copies ran while one was open for 5% of the time, Pallas kernels for 0%

commit v1 on v0

v1 whole, which is shorter than its diff:
```python
import functools
import math

import jax
import jax.numpy as jnp
from jax import lax
from jax.experimental import pallas as pl
from jax.experimental.pallas import tpu as pltpu
from jax.sharding import PartitionSpec as P

time_step = 0.05
enforcement_weight = 4.0
plate_speed = 0.5
dissipation_speed = 0.25
coeffs = (0.75, -0.15, 1.0 / 60.0)

MOMENTS = 13
HALO = 8
RHO, TEMP = 0, 4
VMEM = pl.BlockSpec(memory_space=pltpu.VMEM)
SMEM = pl.BlockSpec(memory_space=pltpu.SMEM)


def params(mib=48):
    return pltpu.CompilerParams(vmem_limit_bytes=mib * 2**20)


def code(f, x):
    if f == RHO:
        return x - 1.25
    if f == TEMP:
        return jnp.exp2(160.0 * (x - 1.25))
    return x


def decode(f, y):
    if f == RHO:
        return y + 1.25
    if f == TEMP:
        return jnp.log2(y) * (1.0 / 160.0) + 1.25
    return y


def flux(u, d, f):
    v = u[1 + d]
    temperature = u[4]
    heat = u[10:13]
    s = [[u[5], u[6], u[8]], [u[6], u[7], u[9]], [u[8], u[9], None]]
    if f == 0:
        return u[0] * v
    if f < 4:
        i = f - 1
        out = u[1 + i] * v + s[i][d]
        return out + temperature if i == d else out
    if f == 4:
        return v * temperature + 2.0 / 3.0 * heat[d]
    if f < 10:
        i, j = ((0, 0), (0, 1), (1, 1), (0, 2), (1, 2))[f - 5]
        out = v * s[i][j]
        weight = {}
        if j == d:
            weight[i] = weight.get(i, 0.0) + 0.4
        if i == d:
            weight[j] = weight.get(j, 0.0) + 0.4
        if i == j:
            weight[d] = weight.get(d, 0.0) - 4.0 / 15.0
        for k, w in weight.items():
            out = out + w * heat[k]
        return out
    i = f - 10
    out = v * heat[i] + temperature * s[i][d]
    return out + 2.5 * temperature * temperature if i == d else out


def sources(u, wall):
    near = jnp.abs(wall)
    nu = u[0] * jnp.sqrt(u[4] * u[4] + 0.25)
    heavy, light = -0.8 * nu, -0.55 * nu
    out = [None] * MOMENTS
    out[1] = -enforcement_weight * near * (u[1] - plate_speed * wall)
    out[4] = -dissipation_speed * nu * u[4] - enforcement_weight * near * (u[4] - 1.0)
    for f in range(5, 10):
        out[f] = heavy * u[f]
    for f in range(10, 13):
        out[f] = light * u[f]
    return out


def along_of(fx):
    count = fx.shape[0]
    total = None
    for k in range(3):
        upper = pltpu.roll(fx, count - (k + 1), 0)
        lower = pltpu.roll(fx, k + 1, 0)
        term = coeffs[k] * (upper - lower)
        total = term if total is None else total + term
    return total


def pack_kernel(n, two, me_ref, rho, vel, temp, stress, heat, *refs):
    if two:
        firsts, (rest, left, right, tall) = refs[:n], refs[n:]
    else:
        firsts, (rest, left, right, tall) = (), refs
    rows, cols = rho.shape
    slab = cols // n
    wide = slab // 2 + 2 * HALO if two else slab + 2 * HALO
    me = me_ref[0]
    tall[0:HALO, :] = jnp.zeros((HALO, rows), jnp.float32)
    tall[HALO + cols :, :] = jnp.zeros((HALO, rows), jnp.float32)
    for f in range(MOMENTS):
        if f == 0:
            x = rho[...]
        elif f < 4:
            x = vel[f - 1]
        elif f == 4:
            x = temp[...]
        elif f < 10:
            x = stress[f - 5]
        else:
            x = heat[f - 10]
        tall[HALO : HALO + cols, :] = code(f, x).T
        left[f] = tall[0 : 2 * HALO, :].astype(jnp.bfloat16)
        right[f] = tall[cols : cols + 2 * HALO, :].astype(jnp.bfloat16)
        for d in range(n):
            start = d * slab
            if two:
                start += 0 if d < n // 2 else wide
                rest[d, f] = tall[start : start + slab // 2, :].astype(jnp.bfloat16)
            else:
                rest[d, f] = tall[start : start + wide, :].astype(jnp.bfloat16)
        for s in range(len(firsts)):
            to = jnp.bitwise_xor(me, s)
            start = to * slab + jnp.where(to < n // 2, slab // 2, 0)
            start = pl.multiple_of(start, 16)
            firsts[s][f] = tall[pl.ds(start, wide), :].astype(jnp.bfloat16)


def patch_kernel(n, me_ref, rest, before, after, *outs):
    me = me_ref[0]
    for s in range(n):
        to = jnp.bitwise_xor(me, s)
        outs[s][...] = rest[to]

        def merge(tile, halo, at_start):
            line = lax.broadcasted_iota(jnp.int32, halo.shape[1:], 0)
            keep = (line < HALO) == at_start
            for f in range(MOMENTS):
                new, old = halo[f].astype(jnp.float32), outs[s][f, tile, :].astype(jnp.float32)
                outs[s][f, tile, :] = jnp.where(keep, new, old).astype(jnp.bfloat16)

        @pl.when(to == 0)
        def _():
            merge(slice(0, 2 * HALO), before, True)

        @pl.when(to == n - 1)
        def _():
            count = outs[s].shape[1]
            merge(slice(count - 2 * HALO, count), after, False)


def grid_kernel(n, rows, me_ref, out, diag):
    size = n * rows
    last = size - 1
    half = math.pi / (2.0 * last)
    me = me_ref[0]
    step = 64 if rows % 64 == 0 else rows

    def weight(index):
        edge = jnp.where((index == 0) | (index == last), 2.0, 1.0)
        return edge * (1 - 2 * (index & 1)).astype(jnp.float32)

    for si in range(n):
        first_i = jnp.bitwise_xor(me, si) * rows
        lanes = pl.ds(si * rows, rows)
        row_i = first_i + lax.broadcasted_iota(jnp.int32, (8, rows), 1)
        angle = half * row_i.astype(jnp.float32)
        sin_i, cos_i = jnp.sin(angle)[0:1], jnp.cos(angle)[0:1]
        front = (-math.pi / last) * sin_i * cos_i * weight(row_i)[0:1]
        diag[...] = jnp.zeros_like(diag)
        for sj in range(n):
            first_j = jnp.bitwise_xor(me, sj) * rows

            def block(t, carry):
                at = t * step
                line = first_j + at
                row_j = line + lax.broadcasted_iota(jnp.int32, (step, 128), 0)
                angle_j = half * row_j.astype(jnp.float32)
                sin_j, cos_j = jnp.sin(angle_j)[:, 0:1], jnp.cos(angle_j)[:, 0:1]
                back = weight(row_j)[:, 0:1]
                back = jnp.where(jnp.abs(back) > 1.5, 0.25 * back, back)
                full_j = line + lax.broadcasted_iota(jnp.int32, (step, rows), 0)
                full_i = first_i + lax.broadcasted_iota(jnp.int32, (step, rows), 1)
                gap = full_i - full_j
                same = gap == 0
                x = half * gap.astype(jnp.float32)
                x2 = x * x
                poly = -1.0 / 39916800.0
                for c in (1 / 362880.0, -1 / 5040.0, 1 / 120.0, -1 / 6.0, 1.0):
                    poly = poly * x2 + c
                minus = x * poly
                plus = sin_i * cos_j + cos_i * sin_j
                denom = jnp.where(same, 1.0, plus * minus)
                off = jnp.where(same, 0.0, front * back / denom)
                diag[...] += jnp.sum(off.reshape(step // 8, 8, rows), axis=0)
                here = pl.ds(pl.multiple_of(sj * rows + at, 16), step)
                out[here, lanes] = off.astype(jnp.bfloat16)
                return carry

            lax.fori_loop(0, rows // step, block, 0)
        total = -jnp.sum(diag[...], axis=0, keepdims=True)
        own = pl.ds(si * rows, rows)
        ij = lax.broadcasted_iota(jnp.int32, (rows, rows), 0)
        ji = lax.broadcasted_iota(jnp.int32, (rows, rows), 1)
        tile = out[own, lanes].astype(jnp.float32)
        out[own, lanes] = jnp.where(ij == ji, total, tile).astype(jnp.bfloat16)


def section_kernel(n, two, second, me_ref, grid, *refs):
    firsts, refs = refs[:n], refs[n:]
    if second:
        rests, refs = refs[:n], refs[n:]
    outs, (u0, u1, r0, fy0, fy1, product) = refs[:n], refs[n:]
    wide, size = u0.shape[1:]
    rows = size // n
    core = wide - 2 * HALO
    me = me_ref[0]
    right_first = me < n // 2
    lane = rows if rows < 128 else 128
    parts = rows // lane

    for s in range(n):
        here = pl.ds(s * rows, rows)
        for f in range(MOMENTS):
            if not second:
                u0[f, :, here] = decode(f, firsts[s][f].astype(jnp.float32))
            else:
                new = rests[s][f].astype(jnp.float32)
                fresh = pl.ds(pl.multiple_of(jnp.where(right_first, 0, 2 * HALO), 16), core)
                u0[f, fresh, here] = decode(f, new)
                src = pl.ds(pl.multiple_of(jnp.where(right_first, 0, core), 16), 2 * HALO)
                dst = pl.ds(pl.multiple_of(jnp.where(right_first, core, 0), 16), 2 * HALO)
                old = firsts[s][f, src, :].astype(jnp.float32)
                u0[f, dst, here] = decode(f, old)

    def walls(s, p, count):
        line = jnp.bitwise_xor(me, s) * rows + p * lane
        line = line + lax.broadcasted_iota(jnp.int32, (count, lane), 1)
        return jnp.where(line == 0, 1.0, jnp.where(line == size - 1, -1.0, 0.0))

    for s in range(n):
        for p in range(parts):
            here = pl.ds(s * rows + p * lane, lane)
            u = [u0[f, :, here] for f in range(MOMENTS)]
            for f in range(MOMENTS):
                fy0[f * wide : (f + 1) * wide, here] = flux(u, 1, f).astype(jnp.bfloat16)

    middle = slice(HALO, HALO + core)
    for s in range(n):
        block = pl.ds(s * rows, rows)
        product[...] = jnp.dot(fy0[...], grid[:, block], preferred_element_type=jnp.float32)
        for p in range(parts):
            here = pl.ds(s * rows + p * lane, lane)
            there = pl.ds(p * lane, lane)
            u = [u0[f, :, here] for f in range(MOMENTS)]
            src = sources(u, walls(s, p, wide))
            new = []
            for f in range(MOMENTS):
                across = product[f * wide : (f + 1) * wide, there]
                rate = -(along_of(flux(u, 0, f)) + across)
                if src[f] is not None:
                    rate = rate + src[f]
                r0[f, :, here] = rate[middle]
                new.append(u[f] + time_step * rate)
                u1[f, :, here] = new[f]
            inner = [x[middle] for x in new]
            for f in range(MOMENTS):
                fy1[f * core : (f + 1) * core, here] = flux(inner, 1, f).astype(jnp.bfloat16)

    for s in range(n):
        block = pl.ds(s * rows, rows)
        product[0 : MOMENTS * core, :] = jnp.dot(
            fy1[...], grid[:, block], preferred_element_type=jnp.float32
        )
        for p in range(parts):
            here = pl.ds(s * rows + p * lane, lane)
            there = pl.ds(p * lane, lane)
            u = [u1[f, :, here] for f in range(MOMENTS)]
            inner = [x[middle] for x in u]
            src = sources(inner, walls(s, p, core))
            for f in range(MOMENTS):
                across = product[f * core : (f + 1) * core, there]
                rate = -(along_of(flux(u, 0, f))[middle] + across)
                if src[f] is not None:
                    rate = rate + src[f]
                rate = 0.5 * (r0[f, :, here] + rate)
                outs[s][f, :, there] = rate.astype(outs[s].dtype)


def unpack_kernel(n, two, me_ref, *refs):
    chunks = [refs[:n], refs[n : 2 * n]] if two else [refs[:n]]
    out, tall = refs[-2:]
    cols = tall.shape[0]
    slab = cols // n
    width = slab // len(chunks)
    me = me_ref[0]
    for f in range(MOMENTS):
        for s in range(n):
            of = jnp.bitwise_xor(me, s)
            for c, arrays in enumerate(chunks):
                start = of * slab
                if two:
                    start += jnp.where(of < n // 2, width * (1 - c), width * c)
                here = pl.ds(pl.multiple_of(start, 16), width)
                tall[here, :] = arrays[s][f].astype(jnp.float32)
        out[f] = tall[...].T


def exchange(arrays, n):
    got = [arrays[0]]
    for s in range(1, n):
        got.append(lax.ppermute(arrays[s], "gy", [(i, i ^ s) for i in range(n)]))
    return got


def on_device(rho, vel, temp, stress, heat):
    rows, cols = rho.shape
    n = lax.axis_size("gy")
    ring = lax.axis_size("gx")
    size, slab = n * rows, cols // n
    two = slab % 32 == 0
    core = slab // 2 if two else slab
    wide = core + 2 * HALO
    half = jnp.bfloat16
    me = lax.axis_index("gy").astype(jnp.int32).reshape(1)
    vel, stress, heat = (jnp.swapaxes(a, 0, 1) for a in (vel, stress, heat))

    def message(width, kind=half):
        return jax.ShapeDtypeStruct((MOMENTS, width, rows), kind)

    spare = core if two else wide
    shapes = [message(wide)] * (n if two else 0)
    shapes += [jax.ShapeDtypeStruct((n, MOMENTS, spare, rows), half)] + [message(2 * HALO)] * 2
    packed = pl.pallas_call(
        functools.partial(pack_kernel, n, two),
        out_shape=shapes,
        in_specs=[SMEM] + [VMEM] * 5,
        out_specs=[VMEM] * len(shapes),
        scratch_shapes=[pltpu.VMEM((cols + 2 * HALO, rows), jnp.float32)],
        compiler_params=params(),
        name="pack",
    )(me, rho, vel, temp, stress, heat)
    rest, left, right = packed[-3:]
    up = [(i, (i + 1) % ring) for i in range(ring)]
    before = lax.ppermute(right, "gx", up)
    after = lax.ppermute(left, "gx", [(j, i) for i, j in up])
    firsts = exchange(packed[:n], n) if two else None

    grid = pl.pallas_call(
        functools.partial(grid_kernel, n, rows),
        out_shape=jax.ShapeDtypeStruct((size, size), half),
        in_specs=[SMEM],
        out_specs=VMEM,
        scratch_shapes=[pltpu.VMEM((8, rows), jnp.float32)],
        compiler_params=params(),
        name="grid",
    )(me)
    rests = pl.pallas_call(
        functools.partial(patch_kernel, n),
        out_shape=[message(spare)] * n,
        in_specs=[SMEM] + [VMEM] * 3,
        out_specs=[VMEM] * n,
        compiler_params=params(),
        name="patch",
    )(me, rest, before, after)
    rests = exchange(rests, n)

    def sections(second, *arrays):
        return pl.pallas_call(
            functools.partial(section_kernel, n, two, second),
            out_shape=[message(core, jnp.float32)] + [message(core)] * (n - 1),
            in_specs=[SMEM] + [VMEM] * (1 + len(arrays)),
            out_specs=[VMEM] * n,
            scratch_shapes=[
                pltpu.VMEM((MOMENTS, wide, size), jnp.float32),
                pltpu.VMEM((MOMENTS, wide, size), jnp.float32),
                pltpu.VMEM((MOMENTS, core, size), jnp.float32),
                pltpu.VMEM((MOMENTS * wide, size), half),
                pltpu.VMEM((MOMENTS * core, size), half),
                pltpu.VMEM((MOMENTS * wide, rows), jnp.float32),
            ],
            compiler_params=params(),
            name="sections",
        )(me, grid, *arrays)

    if two:
        back = exchange(sections(False, *firsts), n)
        back += exchange(sections(True, *firsts, *rests), n)
    else:
        back = exchange(sections(False, *rests), n)
    out = pl.pallas_call(
        functools.partial(unpack_kernel, n, two),
        out_shape=jax.ShapeDtypeStruct((MOMENTS, rows, cols), jnp.float32),
        in_specs=[SMEM] + [VMEM] * len(back),
        out_specs=VMEM,
        scratch_shapes=[pltpu.VMEM((cols, rows), jnp.float32)],
        compiler_params=params(),
        name="unpack",
    )(me, *back)
    return jnp.swapaxes(out, 0, 1)


def solution(mesh):
    return jax.shard_map(
        on_device,
        mesh=mesh,
        in_specs=(
            P("gy", "gx"),
            P("gy", None, "gx"),
            P("gy", "gx"),
            P("gy", None, "gx"),
            P("gy", None, "gx"),
        ),
        out_specs=P("gy", None, "gx"),
        check_vma=False,
    )
```

time: 189 us -> 73.4 us (0.39)
  waiting for transfers between devices: 80.1 us -> 20.9 us
  matrix products: 43.5 us -> 0 us
  Pallas kernels: 0 us -> 31.7 us
  other arithmetic: 28.2 us -> 0 us
  between operations: 13.9 us -> 0.06 us
  local copies, waits for them, and re-layouts: 11.8 us -> 5.48 us
  starting transfers between devices: 11.1 us -> 14.7 us
    all_gather x2 -> x0, waiting for transfers between devices: 78 us -> none  [wall_normal(): piece = lax.all_gather(lowered, 'gy', axis=0, tiled=True)]
    dot_general x2 -> x0, matrix products: 43.5 us -> none  [wall_normal(): jnp.dot(grid, piece.reshape(piece.shape[0], -1), preferred_element_type=j...]
    pallas_call x0 -> x6, Pallas kernels: none -> 31.7 us  [the longest x2 14.4 us: sections(): pl.pallas_call(functools.partial(section_kernel, n, two, second), out_sha...]
    ppermute x4 -> x14, waiting for transfers between devices: 2.07 us -> 20.9 us  [the longest x12 17 us: exchange(): got.append(lax.ppermute(arrays[s], 'gy', [(i, i ^ s) for i in range(n)]))]
    unnamed x60 -> x0, other arithmetic: 18.8 us -> none
    reduce_sum x1 -> x0, other arithmetic: 7.57 us -> none  [derivative_rows(): diagonal = -jnp.sum(offdiag, axis=1)]
    ppermute x4 -> x14, starting transfers between devices: 11.1 us -> 14.7 us  [the longest x12 8.58 us: exchange(): got.append(lax.ppermute(arrays[s], 'gy', [(i, i ^ s) for i in range(n)]))]
    unnamed x21 -> x10, local copies, waits for them, and re-layouts: 8.69 us -> 5.48 us
  transfers between devices with their start and end apart: 6 -> 14, of which waited for: 3 -> 7; matrix products, arithmetic and copies ran while one was open for 5% -> 0% of each run, Pallas kernels for 0% -> 28%
where the time goes in v1:
time: 73.4 us; the launch traced here: 72.8 us
  Pallas kernels  31.7 us (43%)
  waiting for transfers between devices  20.9 us (28%)
  starting transfers between devices  14.7 us (20%)
  local copies, waits for them, and re-layouts  5.48 us (7%)
    ppermute x12, waiting for transfers between devices, exchange(): got.append(lax.ppermute(arrays[s], 'gy', [(i, i ^ s) for i in range(n)]))  17 us
    pallas_call x2, Pallas kernels, sections(): pl.pallas_call(functools.partial(section_kernel, n, two, second), out_sha...  14.4 us
    pallas_call x1, Pallas kernels, on_device(): pl.pallas_call(functools.partial(grid_kernel, n, rows), out_shape=jax.Sha...  13.5 us
    ppermute x12, starting transfers between devices, exchange(): got.append(lax.ppermute(arrays[s], 'gy', [(i, i ^ s) for i in range(n)]))  8.58 us
    unnamed x10, local copies, waits for them, and re-layouts  5.48 us
    ppermute x1, starting transfers between devices, on_device(): after = lax.ppermute(left, 'gx', [(j, i) for i, j in up])  3.1 us
    ppermute x1, starting transfers between devices, on_device(): before = lax.ppermute(right, 'gx', up)  3.02 us
    ppermute x1, waiting for transfers between devices, on_device(): before = lax.ppermute(right, 'gx', up)  3.02 us
  transfers between devices with their start and end apart: 14, of which 7 were waited for; matrix products, arithmetic and copies ran while one was open for 0% of the time, Pallas kernels for 28%

profile of v1, /device:TPU:0, one launch (start us, length us, event | category | flops | bytes accessed | tf_op | source)
XLA Modules:
  0.0 72.8 jit_solution(10106817521414967915)
XLA Ops:
  0.0 1.3 %copy-done = f32[256,5,256]{2,0,1:T(8,128)S(1)} copy-done((f32[256,5,256]{2,0,1:T(8,128)S(1)}, f32[256,5,256]{2,0,1:T(8,128)}, u32[]{:S(2)}) %copy-start) | copy-done | bytes 1310744
  1.3 1.1 %copy-done.1 = f32[256,3,256]{2,0,1:T(8,128)S(1)} copy-done((f32[256,3,256]{2,0,1:T(8,128)S(1)}, f32[256,3,256]{2,0,1:T(8,128)}, u32[]{:S(2)}) %copy-start.1) | copy-done | bytes 786456
  2.5 1.1 %copy-done.2 = f32[256,3,256]{2,0,1:T(8,128)S(1)} copy-done((f32[256,3,256]{2,0,1:T(8,128)S(1)}, f32[256,3,256]{2,0,1:T(8,128)}, u32[]{:S(2)}) %copy-start.2) | copy-done | bytes 786456
  3.6 0.9 %copy-done.3 = f32[256,256]{1,0:T(8,128)S(1)} copy-done((f32[256,256]{1,0:T(8,128)S(1)}, f32[256,256]{1,0:T(8,128)}, u32[]{:S(2)}) %copy-start.3) | copy-done | bytes 262168
  4.5 0.9 %copy-done.4 = f32[256,256]{1,0:T(8,128)S(1)} copy-done((f32[256,256]{1,0:T(8,128)S(1)}, f32[256,256]{1,0:T(8,128)}, u32[]{:S(2)}) %copy-start.4) | copy-done | bytes 262168
  5.5 1.0 %pack.1 = (bf16[13,48,256]{2,1,0:T(8,128)(2,1)S(1)}, bf16[13,48,256]{2,1,0:T(8,128)(2,1)S(1)}, bf16[13,48,256]{2,1,0:T(8,128)(2,1)S(1)}, bf16[13,48,256]{2,1,0:T...) custom-call(s32[1]{0:T(128)} %bitcast.me_ref, ...), custom_call_target="tpu_custom_call" | custom-call | tf_op jit(solution)/shard_map/pack/pallas_call | solution.py:344
  6.5 3.0 %collective-permute-start.6 = (bf16[13,16,256]{2,1,0:T(8,128)(2,1)S(1)}, bf16[13,16,256]{2,1,0:T(8,128)(2,1)S(1)}, u32[]{:S(2)}, u32[]{:S(2)}) collective-permute-start(bf16[13,16,256]{2,1,0:T(8,128)(2,1)S(1)} %get-tuple-element.33), channel_id=1, source_target_pairs={{0,4},{4,8},{8,12},{12,16},{16,20},{20,24},{24,28},{28,0},{1,5},{5... | collective-permute-start | bytes 319496 | tf_op jit(solution)/shard_map/ppermute | solution.py:355
  9.5 3.1 %collective-permute-start.7 = (bf16[13,16,256]{2,1,0:T(8,128)(2,1)S(1)}, bf16[13,16,256]{2,1,0:T(8,128)(2,1)S(1)}, u32[]{:S(2)}, u32[]{:S(2)}) collective-permute-start(bf16[13,16,256]{2,1,0:T(8,128)(2,1)S(1)} %get-tuple-element.34), channel_id=1, source_target_pairs={{4,0},{8,4},{12,8},{16,12},{20,16},{24,20},{28,24},{0,28},{5,1},{9... | collective-permute-start | bytes 319496 | tf_op jit(solution)/shard_map/ppermute | solution.py:356
  12.6 3.0 %collective-permute-done.6.before = bf16[13,16,256]{2,1,0:T(8,128)(2,1)S(1)} collective-permute-done((bf16[13,16,256]{2,1,0:T(8,128)(2,1)S(1)}, bf16[13,16,256]{2,1,0:T(8,128)(2,1)S(1)}, u32[]{:S(2)}, u32[]{:S(2)}) %collective-permute-start.6) | collective-permute-done | bytes 106528 | tf_op jit(solution)/shard_map/ppermute | solution.py:355
  15.6 0.9 %collective-permute-done.7.after = bf16[13,16,256]{2,1,0:T(8,128)(2,1)S(1)} collective-permute-done((bf16[13,16,256]{2,1,0:T(8,128)(2,1)S(1)}, bf16[13,16,256]{2,1,0:T(8,128)(2,1)S(1)}, u32[]{:S(2)}, u32[]{:S(2)}) %collective-permute-start.7) | collective-permute-done | bytes 106528 | tf_op jit(solution)/shard_map/ppermute | solution.py:356
  16.5 0.1 patch.1
  16.6 0.1 collective-permute-start.8
  16.6 0.5 collective-permute-start
  17.1 1.5 %collective-permute-start.1 = (bf16[13,48,256]{2,1,0:T(8,128)(2,1)S(1)}, bf16[13,48,256]{2,1,0:T(8,128)(2,1)S(1)}, u32[]{:S(2)}, u32[]{:S(2)}) collective-permute-start(bf16[13,48,256]{2,1,0:T(8,128)(2,1)S(1)} %get-tuple-element.26), channel_id=1, source_target_pairs={{0,2},{1,3},{2,0},{3,1},{4,6},{5,7},{6,4},{7,5},{8,10},{9,11},{10,... | collective-permute-start | bytes 958472 | tf_op jit(solution)/shard_map/ppermute | solution.py:322
  18.7 0.0 collective-permute-start.2
  18.7 1.4 %collective-permute-start.9 = (bf16[13,32,256]{2,1,0:T(8,128)(2,1)S(1)}, bf16[13,32,256]{2,1,0:T(8,128)(2,1)S(1)}, u32[]{:S(2)}, u32[]{:S(2)}) collective-permute-start(bf16[13,32,256]{2,1,0:T(8,128)(2,1)S(1)} %get-tuple-element.37), channel_id=1, source_target_pairs={{0,2},{1,3},{2,0},{3,1},{4,6},{5,7},{6,4},{7,5},{8,10},{9,11},{10,... | collective-permute-start | bytes 638984 | tf_op jit(solution)/shard_map/ppermute | solution.py:322
  20.1 0.0 collective-permute-done.8.refs_5_
  20.1 0.6 collective-permute-start.10
  20.6 13.5 %grid.1 = bf16[1024,1024]{1,0:T(8,128)(2,1)S(1)} custom-call(s32[1]{0:T(128)} %bitcast.me_ref), custom_call_target="tpu_custom_call" | custom-call | tf_op jit(solution)/shard_map/grid/pallas_call | solution.py:359
  34.1 4.8 %collective-permute-done.9.refs_6_ = bf16[13,32,256]{2,1,0:T(8,128)(2,1)S(1)} collective-permute-done((bf16[13,32,256]{2,1,0:T(8,128)(2,1)S(1)}, bf16[13,32,256]{2,1,0:T(8,128)(2,1)S(1)}, u32[]{:S(2)}, u32[]{:S(2)}) %collective-permute-start.9) | collective-permute-done | bytes 213024 | tf_op jit(solution)/shard_map/ppermute | solution.py:322
  38.9 2.8 %collective-permute-done.10.refs_7_ = bf16[13,32,256]{2,1,0:T(8,128)(2,1)S(1)} collective-permute-done((bf16[13,32,256]{2,1,0:T(8,128)(2,1)S(1)}, bf16[13,32,256]{2,1,0:T(8,128)(2,1)S(1)}, u32[]{:S(2)}, u32[]{:S(2)}) %collective-permute-start.10) | collective-permute-done | bytes 213024 | tf_op jit(solution)/shard_map/ppermute | solution.py:322
  41.8 0.0 collective-permute-done.1.refs_2_
  41.8 7.3 %sections.3 = (f32[13,32,256]{2,1,0:T(8,128)S(1)}, bf16[13,32,256]{2,1,0:T(8,128)(2,1)S(1)}, bf16[13,32,256]{2,1,0:T(8,128)(2,1)S(1)}, bf16[13,32,256]{2,1,0:T(8,128)(2,1)S(1)}) custom-call(s32[1]{0:T(128)} %bitcast.me_ref, bf16[1024,1024]{1,0:T(8,128)(2,1)S(1)} %grid.1, bf16[13,48,256]{2,1,0:T(8,128)(2,1)S(1)} %get-tuple-element.24.refs_0_, ...), custom_call_target="tpu_custom_call" | custom-call | tf_op jit(solution)/shard_map/sections/pallas_call | solution.py:379
  49.1 0.8 %collective-permute-start.11 = (bf16[13,32,256]{2,1,0:T(8,128)(2,1)S(1)}, bf16[13,32,256]{2,1,0:T(8,128)(2,1)S(1)}, u32[]{:S(2)}, u32[]{:S(2)}) collective-permute-start(bf16[13,32,256]{2,1,0:T(8,128)(2,1)S(1)} %get-tuple-element.40), channel_id=1, source_target_pairs={{0,1},{1,0},{2,3},{3,2},{4,5},{5,4},{6,7},{7,6},{8,9},{9,8},{10,11... | collective-permute-start | bytes 638984 | tf_op jit(solution)/shard_map/ppermute | solution.py:322
  49.9 1.5 %collective-permute-start.12 = (bf16[13,32,256]{2,1,0:T(8,128)(2,1)S(1)}, bf16[13,32,256]{2,1,0:T(8,128)(2,1)S(1)}, u32[]{:S(2)}, u32[]{:S(2)}) collective-permute-start(bf16[13,32,256]{2,1,0:T(8,128)(2,1)S(1)} %get-tuple-element.41), channel_id=1, source_target_pairs={{0,2},{1,3},{2,0},{3,1},{4,6},{5,7},{6,4},{7,5},{8,10},{9,11},{10,... | collective-permute-start | bytes 638984 | tf_op jit(solution)/shard_map/ppermute | solution.py:322
  51.4 7.0 %sections.2 = (f32[13,32,256]{2,1,0:T(8,128)S(1)}, bf16[13,32,256]{2,1,0:T(8,128)(2,1)S(1)}, bf16[13,32,256]{2,1,0:T(8,128)(2,1)S(1)}, bf16[13,32,256]{2,1,0:T(8,128)(2,1)S(1)}) custom-call(s32[1]{0:T(128)} %bitcast.me_ref, bf16[1024,1024]{1,0:T(8,128)(2,1)S(1)} %grid.1, bf16[13,48,256]{2,1,0:T(8,128)(2,1)S(1)} %get-tuple-element.24.refs_0_, ...), custom_call_target="tpu_custom_call" | custom-call | tf_op jit(solution)/shard_map/sections/pallas_call | solution.py:379
  58.4 0.7 collective-permute-start.3
  59.1 1.5 %collective-permute-start.4 = (bf16[13,32,256]{2,1,0:T(8,128)(2,1)S(1)}, bf16[13,32,256]{2,1,0:T(8,128)(2,1)S(1)}, u32[]{:S(2)}, u32[]{:S(2)}) collective-permute-start(bf16[13,32,256]{2,1,0:T(8,128)(2,1)S(1)} %get-tuple-element.30), channel_id=1, source_target_pairs={{0,2},{1,3},{2,0},{3,1},{4,6},{5,7},{6,4},{7,5},{8,10},{9,11},{10,... | collective-permute-start | bytes 638984 | tf_op jit(solution)/shard_map/ppermute | solution.py:322
  60.7 0.1 collective-permute-done.13.refs_7_
  60.8 6.4 %collective-permute-done.4.refs_2_ = bf16[13,32,256]{2,1,0:T(8,128)(2,1)S(1)} collective-permute-done((bf16[13,32,256]{2,1,0:T(8,128)(2,1)S(1)}, bf16[13,32,256]{2,1,0:T(8,128)(2,1)S(1)}, u32[]{:S(2)}, u32[]{:S(2)}) %collective-permute-start.4) | collective-permute-done | bytes 213024 | tf_op jit(solution)/shard_map/ppermute | solution.py:322
  67.2 2.8 %collective-permute-done.5.refs_3_ = bf16[13,32,256]{2,1,0:T(8,128)(2,1)S(1)} collective-permute-done((bf16[13,32,256]{2,1,0:T(8,128)(2,1)S(1)}, bf16[13,32,256]{2,1,0:T(8,128)(2,1)S(1)}, u32[]{:S(2)}, u32[]{:S(2)}) %collective-permute-start.5) | collective-permute-done | bytes 213024 | tf_op jit(solution)/shard_map/ppermute | solution.py:322
  70.1 2.8 %unpack.1 = f32[13,256,256]{2,1,0:T(8,128)} custom-call(s32[1]{0:T(128)} %bitcast.me_ref, f32[13,32,256]{2,1,0:T(8,128)S(1)} %get-tuple-element.28.refs_0_, bf16[13,32,256]{2,1,0:T(8,128)(2,1)S(1)} %collective-permute-done.3.refs_1_, bf16[13,32,256]{2,1,0:T(8,128)(2,1)S(1)} %collective-permute-done.4.refs_2_, ...), custom_call_target="tpu_custom_call" | custom-call | tf_op jit(solution)/shard_map/unpack/pallas_call | solution.py:401
  (12 shorter events, 0.0 us)
Async XLA Ops:
  0.0 1.3 %copy-start = (f32[256,5,256]{2,0,1:T(8,128)S(1)}, f32[256,5,256]{2,0,1:T(8,128)}, u32[]{:S(2)}) copy-start(f32[256,5,256]{2,0,1:T(8,128)} %param.8) | copy-start | bytes 3932164
  1.3 1.1 %copy-start.1 = (f32[256,3,256]{2,0,1:T(8,128)S(1)}, f32[256,3,256]{2,0,1:T(8,128)}, u32[]{:S(2)}) copy-start(f32[256,3,256]{2,0,1:T(8,128)} %param.6) | copy-start | bytes 2359300
  2.5 1.1 %copy-start.2 = (f32[256,3,256]{2,0,1:T(8,128)S(1)}, f32[256,3,256]{2,0,1:T(8,128)}, u32[]{:S(2)}) copy-start(f32[256,3,256]{2,0,1:T(8,128)} %param.9) | copy-start | bytes 2359300
  3.6 0.9 %copy-start.3 = (f32[256,256]{1,0:T(8,128)S(1)}, f32[256,256]{1,0:T(8,128)}, u32[]{:S(2)}) copy-start(f32[256,256]{1,0:T(8,128)} %rho.1) | copy-start | bytes 786436
  4.5 0.9 %copy-start.4 = (f32[256,256]{1,0:T(8,128)S(1)}, f32[256,256]{1,0:T(8,128)}, u32[]{:S(2)}) copy-start(f32[256,256]{1,0:T(8,128)} %temp.1) | copy-start | bytes 786436
  6.5 9.1 %collective-permute-start.6 = (bf16[13,16,256]{2,1,0:T(8,128)(2,1)S(1)}, bf16[13,16,256]{2,1,0:T(8,128)(2,1)S(1)}, u32[]{:S(2)}, u32[]{:S(2)}) collective-permute-start(bf16[13,16,256]{2,1,0:T(8,128)(2,1)S(1)} %get-tuple-element.33), channel_id=1, source_target_pairs={{0,4},{4,8},{8,12},{12,16},{16,20},{20,24},{24,28},{28,0},{1,5},{5... | collective-permute-start | bytes 319496 | tf_op jit(solution)/shard_map/ppermute | solution.py:355
  9.5 7.0 %collective-permute-start.7 = (bf16[13,16,256]{2,1,0:T(8,128)(2,1)S(1)}, bf16[13,16,256]{2,1,0:T(8,128)(2,1)S(1)}, u32[]{:S(2)}, u32[]{:S(2)}) collective-permute-start(bf16[13,16,256]{2,1,0:T(8,128)(2,1)S(1)} %get-tuple-element.34), channel_id=1, source_target_pairs={{4,0},{8,4},{12,8},{16,12},{20,16},{24,20},{28,24},{0,28},{5,1},{9... | collective-permute-start | bytes 319496 | tf_op jit(solution)/shard_map/ppermute | solution.py:356
  16.6 3.5 %collective-permute-start.8 = (bf16[13,32,256]{2,1,0:T(8,128)(2,1)S(1)}, bf16[13,32,256]{2,1,0:T(8,128)(2,1)S(1)}, u32[]{:S(2)}, u32[]{:S(2)}) collective-permute-start(bf16[13,32,256]{2,1,0:T(8,128)(2,1)S(1)} %get-tuple-element.36), channel_id=1, source_target_pairs={{0,1},{1,0},{2,3},{3,2},{4,5},{5,4},{6,7},{7,6},{8,9},{9,8},{10,11... | collective-permute-start | bytes 638984 | tf_op jit(solution)/shard_map/ppermute | solution.py:322
  16.6 25.1 %collective-permute-start = (bf16[13,48,256]{2,1,0:T(8,128)(2,1)S(1)}, bf16[13,48,256]{2,1,0:T(8,128)(2,1)S(1)}, u32[]{:S(2)}, u32[]{:S(2)}) collective-permute-start(bf16[13,48,256]{2,1,0:T(8,128)(2,1)S(1)} %get-tuple-element.25), channel_id=1, source_target_pairs={{0,1},{1,0},{2,3},{3,2},{4,5},{5,4},{6,7},{7,6},{8,9},{9,8},{10,11... | collective-permute-start | bytes 958472 | tf_op jit(solution)/shard_map/ppermute | solution.py:322
  17.1 24.6 %collective-permute-start.1 = (bf16[13,48,256]{2,1,0:T(8,128)(2,1)S(1)}, bf16[13,48,256]{2,1,0:T(8,128)(2,1)S(1)}, u32[]{:S(2)}, u32[]{:S(2)}) collective-permute-start(bf16[13,48,256]{2,1,0:T(8,128)(2,1)S(1)} %get-tuple-element.26), channel_id=1, source_target_pairs={{0,2},{1,3},{2,0},{3,1},{4,6},{5,7},{6,4},{7,5},{8,10},{9,11},{10,... | collective-permute-start | bytes 958472 | tf_op jit(solution)/shard_map/ppermute | solution.py:322
  18.7 23.1 %collective-permute-start.2 = (bf16[13,48,256]{2,1,0:T(8,128)(2,1)S(1)}, bf16[13,48,256]{2,1,0:T(8,128)(2,1)S(1)}, u32[]{:S(2)}, u32[]{:S(2)}) collective-permute-start(bf16[13,48,256]{2,1,0:T(8,128)(2,1)S(1)} %get-tuple-element.27), channel_id=1, source_target_pairs={{0,3},{1,2},{2,1},{3,0},{4,7},{5,6},{6,5},{7,4},{8,11},{9,10},{10,... | collective-permute-start | bytes 958472 | tf_op jit(solution)/shard_map/ppermute | solution.py:322
  18.7 20.3 %collective-permute-start.9 = (bf16[13,32,256]{2,1,0:T(8,128)(2,1)S(1)}, bf16[13,32,256]{2,1,0:T(8,128)(2,1)S(1)}, u32[]{:S(2)}, u32[]{:S(2)}) collective-permute-start(bf16[13,32,256]{2,1,0:T(8,128)(2,1)S(1)} %get-tuple-element.37), channel_id=1, source_target_pairs={{0,2},{1,3},{2,0},{3,1},{4,6},{5,7},{6,4},{7,5},{8,10},{9,11},{10,... | collective-permute-start | bytes 638984 | tf_op jit(solution)/shard_map/ppermute | solution.py:322
  20.1 21.7 %collective-permute-start.10 = (bf16[13,32,256]{2,1,0:T(8,128)(2,1)S(1)}, bf16[13,32,256]{2,1,0:T(8,128)(2,1)S(1)}, u32[]{:S(2)}, u32[]{:S(2)}) collective-permute-start(bf16[13,32,256]{2,1,0:T(8,128)(2,1)S(1)} %get-tuple-element.38), channel_id=1, source_target_pairs={{0,3},{1,2},{2,1},{3,0},{4,7},{5,6},{6,5},{7,4},{8,11},{9,10},{10,... | collective-permute-start | bytes 638984 | tf_op jit(solution)/shard_map/ppermute | solution.py:322
  49.1 11.5 %collective-permute-start.11 = (bf16[13,32,256]{2,1,0:T(8,128)(2,1)S(1)}, bf16[13,32,256]{2,1,0:T(8,128)(2,1)S(1)}, u32[]{:S(2)}, u32[]{:S(2)}) collective-permute-start(bf16[13,32,256]{2,1,0:T(8,128)(2,1)S(1)} %get-tuple-element.40), channel_id=1, source_target_pairs={{0,1},{1,0},{2,3},{3,2},{4,5},{5,4},{6,7},{7,6},{8,9},{9,8},{10,11... | collective-permute-start | bytes 638984 | tf_op jit(solution)/shard_map/ppermute | solution.py:322
  49.9 10.8 %collective-permute-start.12 = (bf16[13,32,256]{2,1,0:T(8,128)(2,1)S(1)}, bf16[13,32,256]{2,1,0:T(8,128)(2,1)S(1)}, u32[]{:S(2)}, u32[]{:S(2)}) collective-permute-start(bf16[13,32,256]{2,1,0:T(8,128)(2,1)S(1)} %get-tuple-element.41), channel_id=1, source_target_pairs={{0,2},{1,3},{2,0},{3,1},{4,6},{5,7},{6,4},{7,5},{8,10},{9,11},{10,... | collective-permute-start | bytes 638984 | tf_op jit(solution)/shard_map/ppermute | solution.py:322
  51.4 9.4 %collective-permute-start.13 = (bf16[13,32,256]{2,1,0:T(8,128)(2,1)S(1)}, bf16[13,32,256]{2,1,0:T(8,128)(2,1)S(1)}, u32[]{:S(2)}, u32[]{:S(2)}) collective-permute-start(bf16[13,32,256]{2,1,0:T(8,128)(2,1)S(1)} %get-tuple-element.42), channel_id=1, source_target_pairs={{0,3},{1,2},{2,1},{3,0},{4,7},{5,6},{6,5},{7,4},{8,11},{9,10},{10,... | collective-permute-start | bytes 638984 | tf_op jit(solution)/shard_map/ppermute | solution.py:322
  58.4 2.4 %collective-permute-start.3 = (bf16[13,32,256]{2,1,0:T(8,128)(2,1)S(1)}, bf16[13,32,256]{2,1,0:T(8,128)(2,1)S(1)}, u32[]{:S(2)}, u32[]{:S(2)}) collective-permute-start(bf16[13,32,256]{2,1,0:T(8,128)(2,1)S(1)} %get-tuple-element.29), channel_id=1, source_target_pairs={{0,1},{1,0},{2,3},{3,2},{4,5},{5,4},{6,7},{7,6},{8,9},{9,8},{10,11... | collective-permute-start | bytes 638984 | tf_op jit(solution)/shard_map/ppermute | solution.py:322
  59.1 8.1 %collective-permute-start.4 = (bf16[13,32,256]{2,1,0:T(8,128)(2,1)S(1)}, bf16[13,32,256]{2,1,0:T(8,128)(2,1)S(1)}, u32[]{:S(2)}, u32[]{:S(2)}) collective-permute-start(bf16[13,32,256]{2,1,0:T(8,128)(2,1)S(1)} %get-tuple-element.30), channel_id=1, source_target_pairs={{0,2},{1,3},{2,0},{3,1},{4,6},{5,7},{6,4},{7,5},{8,10},{9,11},{10,... | collective-permute-start | bytes 638984 | tf_op jit(solution)/shard_map/ppermute | solution.py:322
  60.7 9.4 %collective-permute-start.5 = (bf16[13,32,256]{2,1,0:T(8,128)(2,1)S(1)}, bf16[13,32,256]{2,1,0:T(8,128)(2,1)S(1)}, u32[]{:S(2)}, u32[]{:S(2)}) collective-permute-start(bf16[13,32,256]{2,1,0:T(8,128)(2,1)S(1)} %get-tuple-element.31), channel_id=1, source_target_pairs={{0,3},{1,2},{2,1},{3,0},{4,7},{5,6},{6,5},{7,4},{8,11},{9,10},{10,... | collective-permute-start | bytes 638984 | tf_op jit(solution)/shard_map/ppermute | solution.py:322

commit v2 on v1

--- a/solution.py
+++ b/solution.py
@@ -18,7 +18,14 @@
 HALO = 8
 RHO, TEMP = 0, 4
 VMEM = pl.BlockSpec(memory_space=pltpu.VMEM)
+HBM = pl.BlockSpec(memory_space=pltpu.HBM)
 SMEM = pl.BlockSpec(memory_space=pltpu.SMEM)
+
+
+def cost(micros):
+    return pl.CostEstimate(
+        flops=int(micros * 1e9), bytes_accessed=int(micros * 3e6), transcendentals=0
+    )
 
 
 def params(mib=48):
@@ -99,48 +106,58 @@
 
 def pack_kernel(n, two, me_ref, rho, vel, temp, stress, heat, *refs):
     if two:
-        firsts, (rest, left, right, tall) = refs[:n], refs[n:]
-    else:
-        firsts, (rest, left, right, tall) = (), refs
+        firsts, refs = refs[:n], refs[n:]
+    tall, given, strip, arrived = refs
     rows, cols = rho.shape
     slab = cols // n
-    wide = slab // 2 + 2 * HALO if two else slab + 2 * HALO
+    wide = slab // 2 + 2 * HALO
     me = me_ref[0]
-    tall[0:HALO, :] = jnp.zeros((HALO, rows), jnp.float32)
-    tall[HALO + cols :, :] = jnp.zeros((HALO, rows), jnp.float32)
+    copies = []
     for f in range(MOMENTS):
         if f == 0:
-            x = rho[...]
+            src = rho
         elif f < 4:
-            x = vel[f - 1]
+            src = vel.at[f - 1]
         elif f == 4:
-            x = temp[...]
+            src = temp
         elif f < 10:
-            x = stress[f - 5]
+            src = stress.at[f - 5]
         else:
-            x = heat[f - 10]
-        tall[HALO : HALO + cols, :] = code(f, x).T
-        left[f] = tall[0 : 2 * HALO, :].astype(jnp.bfloat16)
-        right[f] = tall[cols : cols + 2 * HALO, :].astype(jnp.bfloat16)
-        for d in range(n):
-            start = d * slab
-            if two:
-                start += 0 if d < n // 2 else wide
-                rest[d, f] = tall[start : start + slab // 2, :].astype(jnp.bfloat16)
-            else:
-                rest[d, f] = tall[start : start + wide, :].astype(jnp.bfloat16)
-        for s in range(len(firsts)):
-            to = jnp.bitwise_xor(me, s)
-            start = to * slab + jnp.where(to < n // 2, slab // 2, 0)
-            start = pl.multiple_of(start, 16)
-            firsts[s][f] = tall[pl.ds(start, wide), :].astype(jnp.bfloat16)
-
-
-def patch_kernel(n, me_ref, rest, before, after, *outs):
+            src = heat.at[f - 10]
+        copies.append(pltpu.make_async_copy(src, given.at[f], arrived.at[f]))
+        copies[f].start()
+    strip[0:HALO, :] = jnp.zeros((HALO, rows), jnp.float32)
+    strip[HALO + cols :, :] = jnp.zeros((HALO, rows), jnp.float32)
+    for f in range(MOMENTS):
+        copies[f].wait()
+        strip[HALO : HALO + cols, :] = code(f, given[f]).T
+        tall[f] = strip[...].astype(jnp.bfloat16)
+        if two:
+            for s in range(n):
+                to = jnp.bitwise_xor(me, s)
+                start = to * slab + jnp.where(to < n // 2, slab // 2, 0)
+                start = pl.multiple_of(start, 16)
+                firsts[s][f] = strip[pl.ds(start, wide), :].astype(jnp.bfloat16)
+
+
+def edge_kernel(tall, left, right):
+    cols = tall.shape[1] - 2 * HALO
+    left[...] = tall[:, 0 : 2 * HALO, :]
+    right[...] = tall[:, cols : cols + 2 * HALO, :]
+
+
+def rest_kernel(n, two, me_ref, tall, before, after, *outs):
     me = me_ref[0]
+    slab = (tall.shape[1] - 2 * HALO) // n
+    count = outs[0].shape[1]
     for s in range(n):
         to = jnp.bitwise_xor(me, s)
-        outs[s][...] = rest[to]
+        start = to * slab
+        if two:
+            start += jnp.where(to < n // 2, 0, slab // 2 + 2 * HALO)
+        start = pl.multiple_of(start, 16)
+        for f in range(MOMENTS):
+            outs[s][f] = tall[f, pl.ds(start, count), :]
 
         def merge(tile, halo, at_start):
             line = lax.broadcasted_iota(jnp.int32, halo.shape[1:], 0)
@@ -155,71 +172,74 @@
 
         @pl.when(to == n - 1)
         def _():
-            count = outs[s].shape[1]
             merge(slice(count - 2 * HALO, count), after, False)
 
 
-def grid_kernel(n, rows, me_ref, out, diag):
+def grid_kernel(n, rows, me_ref, out, sin_col, cos_col, back_col, line_col, total):
     size = n * rows
     last = size - 1
     half = math.pi / (2.0 * last)
     me = me_ref[0]
-    step = 64 if rows % 64 == 0 else rows
-
-    def weight(index):
-        edge = jnp.where((index == 0) | (index == last), 2.0, 1.0)
-        return edge * (1 - 2 * (index & 1)).astype(jnp.float32)
-
-    for si in range(n):
-        first_i = jnp.bitwise_xor(me, si) * rows
-        lanes = pl.ds(si * rows, rows)
-        row_i = first_i + lax.broadcasted_iota(jnp.int32, (8, rows), 1)
-        angle = half * row_i.astype(jnp.float32)
-        sin_i, cos_i = jnp.sin(angle)[0:1], jnp.cos(angle)[0:1]
-        front = (-math.pi / last) * sin_i * cos_i * weight(row_i)[0:1]
-        diag[...] = jnp.zeros_like(diag)
-        for sj in range(n):
-            first_j = jnp.bitwise_xor(me, sj) * rows
+    step = 64
+    lane = min(rows, 128)
+
+    def table(s):
+        line = jnp.bitwise_xor(me, s) * rows + lax.broadcasted_iota(jnp.int32, (8, rows), 1)
+        angle = half * line.astype(jnp.float32)
+        edge = (line == 0) | (line == last)
+        sign = (1 - 2 * (line & 1)).astype(jnp.float32)
+        return line.astype(jnp.float32), jnp.sin(angle), jnp.cos(angle), edge, sign
+
+    def column(x):
+        return jnp.broadcast_to(x[0:1], (lane, rows)).T
+
+    for s in range(n):
+        line, sine, cosine, edge, sign = table(s)
+        here = pl.ds(s * rows, rows)
+        line_col[here, :] = column(line)
+        sin_col[here, :] = column(sine)
+        cos_col[here, :] = column(cosine)
+        back_col[here, :] = column(jnp.where(edge, 0.5 * sign, sign))
+
+    for s in range(n):
+        line, sine, cosine, edge, sign = table(s)
+        front = (-math.pi / last) * sine * cosine * jnp.where(edge, 2.0 * sign, sign)
+        for p in range(rows // lane):
+            here = pl.ds(s * rows + p * lane, lane)
+            line_i, sin_i, cos_i, front_i = (
+                x[0:1, p * lane : (p + 1) * lane] for x in (line, sine, cosine, front)
+            )
+            total[...] = jnp.zeros_like(total)
 
             def block(t, carry):
-                at = t * step
-                line = first_j + at
-                row_j = line + lax.broadcasted_iota(jnp.int32, (step, 128), 0)
-                angle_j = half * row_j.astype(jnp.float32)
-                sin_j, cos_j = jnp.sin(angle_j)[:, 0:1], jnp.cos(angle_j)[:, 0:1]
-                back = weight(row_j)[:, 0:1]
-                back = jnp.where(jnp.abs(back) > 1.5, 0.25 * back, back)
-                full_j = line + lax.broadcasted_iota(jnp.int32, (step, rows), 0)
-                full_i = first_i + lax.broadcasted_iota(jnp.int32, (step, rows), 1)
-                gap = full_i - full_j
-                same = gap == 0
-                x = half * gap.astype(jnp.float32)
+                down = pl.ds(pl.multiple_of(t * step, step), step)
+                gap = line_i - line_col[down, :]
+                same = gap == 0.0
+                x = half * gap
                 x2 = x * x
                 poly = -1.0 / 39916800.0
                 for c in (1 / 362880.0, -1 / 5040.0, 1 / 120.0, -1 / 6.0, 1.0):
                     poly = poly * x2 + c
-                minus = x * poly
-                plus = sin_i * cos_j + cos_i * sin_j
-                denom = jnp.where(same, 1.0, plus * minus)
-                off = jnp.where(same, 0.0, front * back / denom)
-                diag[...] += jnp.sum(off.reshape(step // 8, 8, rows), axis=0)
-                here = pl.ds(pl.multiple_of(sj * rows + at, 16), step)
-                out[here, lanes] = off.astype(jnp.bfloat16)
+                plus = sin_i * cos_col[down, :] + cos_i * sin_col[down, :]
+                denom = jnp.where(same, 1.0, plus * (x * poly))
+                off = jnp.where(same, 0.0, front_i * back_col[down, :] / denom)
+                total[...] += jnp.sum(off.reshape(step // 8, 8, lane), axis=0)
+                out[down, here] = off.astype(jnp.bfloat16)
                 return carry
 
-            lax.fori_loop(0, rows // step, block, 0)
-        total = -jnp.sum(diag[...], axis=0, keepdims=True)
-        own = pl.ds(si * rows, rows)
-        ij = lax.broadcasted_iota(jnp.int32, (rows, rows), 0)
-        ji = lax.broadcasted_iota(jnp.int32, (rows, rows), 1)
-        tile = out[own, lanes].astype(jnp.float32)
-        out[own, lanes] = jnp.where(ij == ji, total, tile).astype(jnp.bfloat16)
+            lax.fori_loop(0, size // step, block, 0)
+            diagonal = -jnp.sum(total[...], axis=0, keepdims=True)
+            same = lax.broadcasted_iota(jnp.int32, (lane, lane), 0) == (
+                lax.broadcasted_iota(jnp.int32, (lane, lane), 1)
+            )
+            tile = out[here, here].astype(jnp.float32)
+            out[here, here] = jnp.where(same, diagonal, tile).astype(jnp.bfloat16)
 
 
 def section_kernel(n, two, second, me_ref, grid, *refs):
     firsts, refs = refs[:n], refs[n:]
     if second:
-        rests, refs = refs[:n], refs[n:]
+        rests, refs = refs[:n], refs[n + 1 :]
     outs, (u0, u1, r0, fy0, fy1, product) = refs[:n], refs[n:]
     wide, size = u0.shape[1:]
     rows = size // n
@@ -338,48 +358,64 @@
     def message(width, kind=half):
         return jax.ShapeDtypeStruct((MOMENTS, width, rows), kind)
 
-    spare = core if two else wide
-    shapes = [message(wide)] * (n if two else 0)
-    shapes += [jax.ShapeDtypeStruct((n, MOMENTS, spare, rows), half)] + [message(2 * HALO)] * 2
-    packed = pl.pallas_call(
+    count = n if two else 0
+    *firsts, tall = pl.pallas_call(
         functools.partial(pack_kernel, n, two),
-        out_shape=shapes,
-        in_specs=[SMEM] + [VMEM] * 5,
-        out_specs=[VMEM] * len(shapes),
-        scratch_shapes=[pltpu.VMEM((cols + 2 * HALO, rows), jnp.float32)],
-        compiler_params=params(),
+        out_shape=[message(wide)] * count + [message(cols + 2 * HALO)],
+        in_specs=[SMEM] + [HBM] * 5,
+        out_specs=[VMEM] * (count + 1),
+        scratch_shapes=[
+            pltpu.VMEM((MOMENTS, rows, cols), jnp.float32),
+            pltpu.VMEM((cols + 2 * HALO, rows), jnp.float32),
+            pltpu.SemaphoreType.DMA((MOMENTS,)),
+        ],
+        compiler_params=params(56),
+        cost_estimate=cost(2),
         name="pack",
     )(me, rho, vel, temp, stress, heat)
-    rest, left, right = packed[-3:]
+    if two:
+        firsts = exchange(firsts, n)
+    left, right = pl.pallas_call(
+        edge_kernel,
+        out_shape=[message(2 * HALO)] * 2,
+        in_specs=[VMEM],
+        out_specs=[VMEM] * 2,
+        compiler_params=params(),
+        cost_estimate=cost(0.2),
+        name="edges",
+    )(tall)
     up = [(i, (i + 1) % ring) for i in range(ring)]
     before = lax.ppermute(right, "gx", up)
     after = lax.ppermute(left, "gx", [(j, i) for i, j in up])
-    firsts = exchange(packed[:n], n) if two else None
-
+
+    lane = min(rows, 128)
     grid = pl.pallas_call(
         functools.partial(grid_kernel, n, rows),
         out_shape=jax.ShapeDtypeStruct((size, size), half),
         in_specs=[SMEM],
         out_specs=VMEM,
-        scratch_shapes=[pltpu.VMEM((8, rows), jnp.float32)],
+        scratch_shapes=[pltpu.VMEM((size, lane), jnp.float32)] * 4
+        + [pltpu.VMEM((8, lane), jnp.float32)],
         compiler_params=params(),
+        cost_estimate=cost(5),
         name="grid",
     )(me)
     rests = pl.pallas_call(
-        functools.partial(patch_kernel, n),
-        out_shape=[message(spare)] * n,
+        functools.partial(rest_kernel, n, two),
+        out_shape=[message(core if two else wide)] * n,
         in_specs=[SMEM] + [VMEM] * 3,
         out_specs=[VMEM] * n,
         compiler_params=params(),
-        name="patch",
-    )(me, rest, before, after)
+        cost_estimate=cost(0.2),
+        name="rest",
+    )(me, tall, before, after)
     rests = exchange(rests, n)
 
     def sections(second, *arrays):
         return pl.pallas_call(
             functools.partial(section_kernel, n, two, second),
             out_shape=[message(core, jnp.float32)] + [message(core)] * (n - 1),
-            in_specs=[SMEM] + [VMEM] * (1 + len(arrays)),
+            in_specs=[SMEM] + [VMEM] * (2 * n + 1 if second else n + 1) + [HBM] * second,
             out_specs=[VMEM] * n,
             scratch_shapes=[
                 pltpu.VMEM((MOMENTS, wide, size), jnp.float32),
@@ -390,12 +426,14 @@
                 pltpu.VMEM((MOMENTS * wide, rows), jnp.float32),
             ],
             compiler_params=params(),
+            cost_estimate=cost(7),
             name="sections",
         )(me, grid, *arrays)
 
     if two:
-        back = exchange(sections(False, *firsts), n)
-        back += exchange(sections(True, *firsts, *rests), n)
+        first = sections(False, *firsts)
+        back = exchange(first, n)
+        back += exchange(sections(True, *firsts, *rests, first[1]), n)
     else:
         back = exchange(sections(False, *rests), n)
     out = pl.pallas_call(
@@ -405,6 +443,7 @@
         out_specs=VMEM,
         scratch_shapes=[pltpu.VMEM((cols, rows), jnp.float32)],
         compiler_params=params(),
+        cost_estimate=cost(3),
         name="unpack",
     )(me, *back)
     return jnp.swapaxes(out, 0, 1)

time: 73.4 us -> 60.2 us (0.82)
  waiting for transfers between devices: 20.9 us -> 16.2 us
  local copies, waits for them, and re-layouts: 5.48 us -> 1.49 us
  Pallas kernels: 31.7 us -> 28 us
    pallas_call x1, Pallas kernels: 13.5 us -> 5.85 us  [on_device(): pl.pallas_call(functools.partial(grid_kernel, n, rows), out_shape=jax.Sha...]
    unnamed x10 -> x6, local copies, waits for them, and re-layouts: 5.48 us -> 1.49 us
    pallas_call x2 -> x3, Pallas kernels: 1.05 us -> 4.96 us  [the longest x1 4.66 us: on_device(): pl.pallas_call(functools.partial(pack_kernel, n, two), out_shape=[message...]
    ppermute x1, waiting for transfers between devices: 3.02 us -> 0.01 us  [on_device(): before = lax.ppermute(right, 'gx', up)]
    ppermute x12, waiting for transfers between devices: 17 us -> 16.2 us  [exchange(): got.append(lax.ppermute(arrays[s], 'gy', [(i, i ^ s) for i in range(n)]))]
    ppermute x1, waiting for transfers between devices: 0.87 us -> 0.01 us  [on_device(): after = lax.ppermute(left, 'gx', [(j, i) for i, j in up])]
  transfers between devices with their start and end apart: 14 -> 14, of which waited for: 7 -> 5; matrix products, arithmetic and copies ran while one was open for 0% -> 0% of each run, Pallas kernels for 28% -> 34%
where the time goes in v2:
time: 60.2 us; the launch traced here: 60.1 us
  Pallas kernels  28 us (47%)
  waiting for transfers between devices  16.2 us (27%)
  starting transfers between devices  14.4 us (24%)
  local copies, waits for them, and re-layouts  1.49 us (2%)
    ppermute x12, waiting for transfers between devices, exchange(): got.append(lax.ppermute(arrays[s], 'gy', [(i, i ^ s) for i in range(n)]))  16.2 us
    pallas_call x2, Pallas kernels, sections(): pl.pallas_call(functools.partial(section_kernel, n, two, second), out_sha...  14.4 us
    ppermute x12, starting transfers between devices, exchange(): got.append(lax.ppermute(arrays[s], 'gy', [(i, i ^ s) for i in range(n)]))  8.23 us
    pallas_call x1, Pallas kernels, on_device(): pl.pallas_call(functools.partial(grid_kernel, n, rows), out_shape=jax.Sha...  5.85 us
    pallas_call x1, Pallas kernels, on_device(): pl.pallas_call(functools.partial(pack_kernel, n, two), out_shape=[message...  4.66 us
    ppermute x1, starting transfers between devices, on_device(): after = lax.ppermute(left, 'gx', [(j, i) for i, j in up])  3.1 us
    ppermute x1, starting transfers between devices, on_device(): before = lax.ppermute(right, 'gx', up)  3.02 us
    pallas_call x1, Pallas kernels, on_device(): pl.pallas_call(functools.partial(unpack_kernel, n, two), out_shape=jax.Sh...  2.8 us
  transfers between devices with their start and end apart: 14, of which 5 were waited for; matrix products, arithmetic and copies ran while one was open for 0% of the time, Pallas kernels for 34%

profile of v2, /device:TPU:0, one launch (start us, length us, event | category | flops | bytes accessed | tf_op | source)
XLA Modules:
  0.0 60.1 jit_solution(15825529300671788362)
XLA Ops:
  0.0 4.7 %pack.1 = (bf16[13,48,256]{2,1,0:T(8,128)(2,1)}, bf16[13,48,256]{2,1,0:T(8,128)(2,1)}, bf16[13,48,256]{2,1,0:T(8,128)(2,1)}, bf16[13,48,256]{2,1,0:T(8,128)(2,1)}, bf16[13,272,256]{2,1,0:T(8,128)(2,1)}) custom-call(s32[1]{0:T(128)} %bitcast.me_ref, f32[256,256]{1,0:T(8,128)} %rho.1, f32[3,256,256]{2,1,0:T(8,128)} %bitcast.6, f32[256,256]{1,0:T(8,128)} %temp.1, ...), custom_call_target="tpu_custom_call" | custom-call | flops 2000000000 | bytes 6000000 | tf_op jit(solution)/shard_map/pack/pallas_call | solution.py:362
  4.7 0.0 copy-start
  4.7 1.5 %copy-done = bf16[13,272,256]{2,1,0:T(8,128)(2,1)S(1)} copy-done((bf16[13,272,256]{2,1,0:T(8,128)(2,1)S(1)}, bf16[13,272,256]{2,1,0:T(8,128)(2,1)}, u32[]{:S(2)}) %copy-start) | copy-done | bytes 1810456
  6.2 3.0 %collective-permute-start.6 = (bf16[13,16,256]{2,1,0:T(8,128)(2,1)S(1)}, bf16[13,16,256]{2,1,0:T(8,128)(2,1)S(1)}, u32[]{:S(2)}, u32[]{:S(2)}) collective-permute-start(bf16[13,16,256]{2,1,0:T(8,128)(2,1)S(1)} %get-tuple-element.33), channel_id=1, source_target_pairs={{0,4},{4,8},{8,12},{12,16},{16,20},{20,24},{24,28},{28,0},{1,5},{5... | collective-permute-start | bytes 319496 | tf_op jit(solution)/shard_map/ppermute | solution.py:388
  9.2 3.1 %collective-permute-start.7 = (bf16[13,16,256]{2,1,0:T(8,128)(2,1)S(1)}, bf16[13,16,256]{2,1,0:T(8,128)(2,1)S(1)}, u32[]{:S(2)}, u32[]{:S(2)}) collective-permute-start(bf16[13,16,256]{2,1,0:T(8,128)(2,1)S(1)} %get-tuple-element.34), channel_id=1, source_target_pairs={{4,0},{8,4},{12,8},{16,12},{20,16},{24,20},{28,24},{0,28},{5,1},{9... | collective-permute-start | bytes 319496 | tf_op jit(solution)/shard_map/ppermute | solution.py:389
  12.3 0.0 collective-permute-start
  12.3 1.6 %collective-permute-start.1 = (bf16[13,48,256]{2,1,0:T(8,128)(2,1)}, bf16[13,48,256]{2,1,0:T(8,128)(2,1)S(1)}, u32[]{:S(2)}, u32[]{:S(2)}) collective-permute-start(bf16[13,48,256]{2,1,0:T(8,128)(2,1)} %get-tuple-element.26), channel_id=1, source_target_pairs={{0,2},{1,3},{2,0},{3,1},{4,6},{5,7},{6,4},{7,5},{8,10},{9,11},{10,... | collective-permute-start | bytes 958472 | tf_op jit(solution)/shard_map/ppermute | solution.py:342
  13.9 0.2 collective-permute-start.2
  14.2 5.8 %grid.1 = bf16[1024,1024]{1,0:T(8,128)(2,1)S(1)} custom-call(s32[1]{0:T(128)} %bitcast.me_ref), custom_call_target="tpu_custom_call" | custom-call | flops 5000000000 | bytes 15000000 | tf_op jit(solution)/shard_map/grid/pallas_call | solution.py:392
  20.0 0.0 collective-permute-done.6.before
  20.0 0.0 collective-permute-done.7.after
  20.1 0.3 rest.1
  20.4 0.3 collective-permute-start.8
  20.7 1.6 %collective-permute-start.9 = (bf16[13,32,256]{2,1,0:T(8,128)(2,1)S(1)}, bf16[13,32,256]{2,1,0:T(8,128)(2,1)S(1)}, u32[]{:S(2)}, u32[]{:S(2)}) collective-permute-start(bf16[13,32,256]{2,1,0:T(8,128)(2,1)S(1)} %get-tuple-element.37), channel_id=1, source_target_pairs={{0,2},{1,3},{2,0},{3,1},{4,6},{5,7},{6,4},{7,5},{8,10},{9,11},{10,... | collective-permute-start | bytes 638984 | tf_op jit(solution)/shard_map/ppermute | solution.py:342
  22.3 0.0 collective-permute-done.refs_1_
  22.3 0.0 collective-permute-start.10
  22.3 0.5 collective-permute-done.1.refs_2_
  22.9 6.1 %collective-permute-done.2.refs_3_ = bf16[13,48,256]{2,1,0:T(8,128)(2,1)S(1)} collective-permute-done((bf16[13,48,256]{2,1,0:T(8,128)(2,1)}, bf16[13,48,256]{2,1,0:T(8,128)(2,1)S(1)}, u32[]{:S(2)}, u32[]{:S(2)}) %collective-permute-start.2) | collective-permute-done | bytes 319520 | tf_op jit(solution)/shard_map/ppermute | solution.py:342
  28.9 6.8 %sections.2 = (f32[13,32,256]{2,1,0:T(8,128)S(1)}, bf16[13,32,256]{2,1,0:T(8,128)(2,1)S(1)}, bf16[13,32,256]{2,1,0:T(8,128)(2,1)S(1)}, bf16[13,32,256]{2,1,0:T(8,128)(2,1)S(1)}) custom-call(s32[1]{0:T(128)} %bitcast.me_ref, bf16[1024,1024]{1,0:T(8,128)(2,1)S(1)} %grid.1, bf16[13,48,256]{2,1,0:T(8,128)(2,1)S(1)} %copy-done.2, ...), custom_call_target="tpu_custom_call" | custom-call | flops 7000000000 | bytes 21000000 | tf_op jit(solution)/shard_map/sections/pallas_call | solution.py:415
  35.8 1.6 %collective-permute-start.4 = (bf16[13,32,256]{2,1,0:T(8,128)(2,1)S(1)}, bf16[13,32,256]{2,1,0:T(8,128)(2,1)S(1)}, u32[]{:S(2)}, u32[]{:S(2)}) collective-permute-start(bf16[13,32,256]{2,1,0:T(8,128)(2,1)S(1)} %get-tuple-element.30), channel_id=1, source_target_pairs={{0,2},{1,3},{2,0},{3,1},{4,6},{5,7},{6,4},{7,5},{8,10},{9,11},{10,... | collective-permute-start | bytes 638984 | tf_op jit(solution)/shard_map/ppermute | solution.py:342
  37.4 0.3 collective-permute-start.5
  37.8 0.3 collective-permute-done.10.refs_7_
  38.1 7.6 %sections.3 = (f32[13,32,256]{2,1,0:T(8,128)S(1)}, bf16[13,32,256]{2,1,0:T(8,128)(2,1)S(1)}, bf16[13,32,256]{2,1,0:T(8,128)(2,1)S(1)}, bf16[13,32,256]{2,1,0:T(8,128)(2,1)S(1)}) custom-call(s32[1]{0:T(128)} %bitcast.me_ref, bf16[1024,1024]{1,0:T(8,128)(2,1)S(1)} %grid.1, bf16[13,48,256]{2,1,0:T(8,128)(2,1)S(1)} %copy-done.2, ...), custom_call_target="tpu_custom_call" | custom-call | flops 7000000000 | bytes 21000000 | tf_op jit(solution)/shard_map/sections/pallas_call | solution.py:415
  45.6 0.3 collective-permute-start.11
  45.9 1.6 %collective-permute-start.12 = (bf16[13,32,256]{2,1,0:T(8,128)(2,1)S(1)}, bf16[13,32,256]{2,1,0:T(8,128)(2,1)S(1)}, u32[]{:S(2)}, u32[]{:S(2)}) collective-permute-start(bf16[13,32,256]{2,1,0:T(8,128)(2,1)S(1)} %get-tuple-element.41), channel_id=1, source_target_pairs={{0,2},{1,3},{2,0},{3,1},{4,6},{5,7},{6,4},{7,5},{8,10},{9,11},{10,... | collective-permute-start | bytes 638984 | tf_op jit(solution)/shard_map/ppermute | solution.py:342
  47.5 0.0 collective-permute-start.13
  47.6 0.0 collective-permute-done.4.refs_2_
  47.6 0.5 collective-permute-start.3
  48.0 0.0 collective-permute-done.5.refs_3_
  48.0 5.9 %collective-permute-done.12.refs_6_ = bf16[13,32,256]{2,1,0:T(8,128)(2,1)S(1)} collective-permute-done((bf16[13,32,256]{2,1,0:T(8,128)(2,1)S(1)}, bf16[13,32,256]{2,1,0:T(8,128)(2,1)S(1)}, u32[]{:S(2)}, u32[]{:S(2)}) %collective-permute-start.12) | collective-permute-done | bytes 213024 | tf_op jit(solution)/shard_map/ppermute | solution.py:342
  54.0 3.3 %collective-permute-done.13.refs_7_ = bf16[13,32,256]{2,1,0:T(8,128)(2,1)S(1)} collective-permute-done((bf16[13,32,256]{2,1,0:T(8,128)(2,1)S(1)}, bf16[13,32,256]{2,1,0:T(8,128)(2,1)S(1)}, u32[]{:S(2)}, u32[]{:S(2)}) %collective-permute-start.13) | collective-permute-done | bytes 213024 | tf_op jit(solution)/shard_map/ppermute | solution.py:342
  57.3 2.8 %unpack.1 = f32[13,256,256]{2,1,0:T(8,128)} custom-call(s32[1]{0:T(128)} %bitcast.me_ref, f32[13,32,256]{2,1,0:T(8,128)S(1)} %get-tuple-element.28.refs_0_, bf16[13,32,256]{2,1,0:T(8,128)(2,1)S(1)} %collective-permute-done.3.refs_1_, bf16[13,32,256]{2,1,0:T(8,128)(2,1)S(1)} %collective-permute-done.4.refs_2_, ...), custom_call_target="tpu_custom_call" | custom-call | flops 3000000000 | bytes 9000000 | tf_op jit(solution)/shard_map/unpack/pallas_call | solution.py:439
  (9 shorter events, 0.0 us)
Async XLA Ops:
  4.7 1.5 %copy-start = (bf16[13,272,256]{2,1,0:T(8,128)(2,1)S(1)}, bf16[13,272,256]{2,1,0:T(8,128)(2,1)}, u32[]{:S(2)}) copy-start(bf16[13,272,256]{2,1,0:T(8,128)(2,1)} %get-tuple-element.32.tall) | copy-start | bytes 5431300
  6.2 13.8 %collective-permute-start.6 = (bf16[13,16,256]{2,1,0:T(8,128)(2,1)S(1)}, bf16[13,16,256]{2,1,0:T(8,128)(2,1)S(1)}, u32[]{:S(2)}, u32[]{:S(2)}) collective-permute-start(bf16[13,16,256]{2,1,0:T(8,128)(2,1)S(1)} %get-tuple-element.33), channel_id=1, source_target_pairs={{0,4},{4,8},{8,12},{12,16},{16,20},{20,24},{24,28},{28,0},{1,5},{5... | collective-permute-start | bytes 319496 | tf_op jit(solution)/shard_map/ppermute | solution.py:388
  9.2 10.8 %collective-permute-start.7 = (bf16[13,16,256]{2,1,0:T(8,128)(2,1)S(1)}, bf16[13,16,256]{2,1,0:T(8,128)(2,1)S(1)}, u32[]{:S(2)}, u32[]{:S(2)}) collective-permute-start(bf16[13,16,256]{2,1,0:T(8,128)(2,1)S(1)} %get-tuple-element.34), channel_id=1, source_target_pairs={{4,0},{8,4},{12,8},{16,12},{20,16},{24,20},{28,24},{0,28},{5,1},{9... | collective-permute-start | bytes 319496 | tf_op jit(solution)/shard_map/ppermute | solution.py:389
  12.3 10.0 %collective-permute-start = (bf16[13,48,256]{2,1,0:T(8,128)(2,1)}, bf16[13,48,256]{2,1,0:T(8,128)(2,1)S(1)}, u32[]{:S(2)}, u32[]{:S(2)}) collective-permute-start(bf16[13,48,256]{2,1,0:T(8,128)(2,1)} %get-tuple-element.25), channel_id=1, source_target_pairs={{0,1},{1,0},{2,3},{3,2},{4,5},{5,4},{6,7},{7,6},{8,9},{9,8},{10,11... | collective-permute-start | bytes 958472 | tf_op jit(solution)/shard_map/ppermute | solution.py:342
  12.3 10.5 %collective-permute-start.1 = (bf16[13,48,256]{2,1,0:T(8,128)(2,1)}, bf16[13,48,256]{2,1,0:T(8,128)(2,1)S(1)}, u32[]{:S(2)}, u32[]{:S(2)}) collective-permute-start(bf16[13,48,256]{2,1,0:T(8,128)(2,1)} %get-tuple-element.26), channel_id=1, source_target_pairs={{0,2},{1,3},{2,0},{3,1},{4,6},{5,7},{6,4},{7,5},{8,10},{9,11},{10,... | collective-permute-start | bytes 958472 | tf_op jit(solution)/shard_map/ppermute | solution.py:342
  13.9 6.1 %copy-start.1 = (bf16[13,272,256]{2,1,0:T(8,128)(2,1)S(1)}, bf16[13,272,256]{2,1,0:T(8,128)(2,1)}, u32[]{:S(2)}) copy-start(bf16[13,272,256]{2,1,0:T(8,128)(2,1)} %get-tuple-element.32.tall) | copy-start | bytes 5431300
  13.9 15.0 %copy-start.2 = (bf16[13,48,256]{2,1,0:T(8,128)(2,1)S(1)}, bf16[13,48,256]{2,1,0:T(8,128)(2,1)}, u32[]{:S(2)}) copy-start(bf16[13,48,256]{2,1,0:T(8,128)(2,1)} %get-tuple-element.24.refs_0_) | copy-start | bytes 958468
  13.9 15.0 %collective-permute-start.2 = (bf16[13,48,256]{2,1,0:T(8,128)(2,1)}, bf16[13,48,256]{2,1,0:T(8,128)(2,1)S(1)}, u32[]{:S(2)}, u32[]{:S(2)}) collective-permute-start(bf16[13,48,256]{2,1,0:T(8,128)(2,1)} %get-tuple-element.27), channel_id=1, source_target_pairs={{0,3},{1,2},{2,1},{3,0},{4,7},{5,6},{6,5},{7,4},{8,11},{9,10},{10,... | collective-permute-start | bytes 958472 | tf_op jit(solution)/shard_map/ppermute | solution.py:342
  20.4 17.4 %collective-permute-start.8 = (bf16[13,32,256]{2,1,0:T(8,128)(2,1)S(1)}, bf16[13,32,256]{2,1,0:T(8,128)(2,1)S(1)}, u32[]{:S(2)}, u32[]{:S(2)}) collective-permute-start(bf16[13,32,256]{2,1,0:T(8,128)(2,1)S(1)} %get-tuple-element.36), channel_id=1, source_target_pairs={{0,1},{1,0},{2,3},{3,2},{4,5},{5,4},{6,7},{7,6},{8,9},{9,8},{10,11... | collective-permute-start | bytes 638984 | tf_op jit(solution)/shard_map/ppermute | solution.py:342
  20.7 17.1 %collective-permute-start.9 = (bf16[13,32,256]{2,1,0:T(8,128)(2,1)S(1)}, bf16[13,32,256]{2,1,0:T(8,128)(2,1)S(1)}, u32[]{:S(2)}, u32[]{:S(2)}) collective-permute-start(bf16[13,32,256]{2,1,0:T(8,128)(2,1)S(1)} %get-tuple-element.37), channel_id=1, source_target_pairs={{0,2},{1,3},{2,0},{3,1},{4,6},{5,7},{6,4},{7,5},{8,10},{9,11},{10,... | collective-permute-start | bytes 638984 | tf_op jit(solution)/shard_map/ppermute | solution.py:342
  22.3 15.7 %collective-permute-start.10 = (bf16[13,32,256]{2,1,0:T(8,128)(2,1)S(1)}, bf16[13,32,256]{2,1,0:T(8,128)(2,1)S(1)}, u32[]{:S(2)}, u32[]{:S(2)}) collective-permute-start(bf16[13,32,256]{2,1,0:T(8,128)(2,1)S(1)} %get-tuple-element.38), channel_id=1, source_target_pairs={{0,3},{1,2},{2,1},{3,0},{4,7},{5,6},{6,5},{7,4},{8,11},{9,10},{10,... | collective-permute-start | bytes 638984 | tf_op jit(solution)/shard_map/ppermute | solution.py:342
  35.8 11.8 %collective-permute-start.4 = (bf16[13,32,256]{2,1,0:T(8,128)(2,1)S(1)}, bf16[13,32,256]{2,1,0:T(8,128)(2,1)S(1)}, u32[]{:S(2)}, u32[]{:S(2)}) collective-permute-start(bf16[13,32,256]{2,1,0:T(8,128)(2,1)S(1)} %get-tuple-element.30), channel_id=1, source_target_pairs={{0,2},{1,3},{2,0},{3,1},{4,6},{5,7},{6,4},{7,5},{8,10},{9,11},{10,... | collective-permute-start | bytes 638984 | tf_op jit(solution)/shard_map/ppermute | solution.py:342
  37.4 10.6 %collective-permute-start.5 = (bf16[13,32,256]{2,1,0:T(8,128)(2,1)S(1)}, bf16[13,32,256]{2,1,0:T(8,128)(2,1)S(1)}, u32[]{:S(2)}, u32[]{:S(2)}) collective-permute-start(bf16[13,32,256]{2,1,0:T(8,128)(2,1)S(1)} %get-tuple-element.31), channel_id=1, source_target_pairs={{0,3},{1,2},{2,1},{3,0},{4,7},{5,6},{6,5},{7,4},{8,11},{9,10},{10,... | collective-permute-start | bytes 638984 | tf_op jit(solution)/shard_map/ppermute | solution.py:342
  45.6 2.4 %collective-permute-start.11 = (bf16[13,32,256]{2,1,0:T(8,128)(2,1)S(1)}, bf16[13,32,256]{2,1,0:T(8,128)(2,1)S(1)}, u32[]{:S(2)}, u32[]{:S(2)}) collective-permute-start(bf16[13,32,256]{2,1,0:T(8,128)(2,1)S(1)} %get-tuple-element.40), channel_id=1, source_target_pairs={{0,1},{1,0},{2,3},{3,2},{4,5},{5,4},{6,7},{7,6},{8,9},{9,8},{10,11... | collective-permute-start | bytes 638984 | tf_op jit(solution)/shard_map/ppermute | solution.py:342
  45.9 8.1 %collective-permute-start.12 = (bf16[13,32,256]{2,1,0:T(8,128)(2,1)S(1)}, bf16[13,32,256]{2,1,0:T(8,128)(2,1)S(1)}, u32[]{:S(2)}, u32[]{:S(2)}) collective-permute-start(bf16[13,32,256]{2,1,0:T(8,128)(2,1)S(1)} %get-tuple-element.41), channel_id=1, source_target_pairs={{0,2},{1,3},{2,0},{3,1},{4,6},{5,7},{6,4},{7,5},{8,10},{9,11},{10,... | collective-permute-start | bytes 638984 | tf_op jit(solution)/shard_map/ppermute | solution.py:342
  47.5 9.8 %collective-permute-start.13 = (bf16[13,32,256]{2,1,0:T(8,128)(2,1)S(1)}, bf16[13,32,256]{2,1,0:T(8,128)(2,1)S(1)}, u32[]{:S(2)}, u32[]{:S(2)}) collective-permute-start(bf16[13,32,256]{2,1,0:T(8,128)(2,1)S(1)} %get-tuple-element.42), channel_id=1, source_target_pairs={{0,3},{1,2},{2,1},{3,0},{4,7},{5,6},{6,5},{7,4},{8,11},{9,10},{10,... | collective-permute-start | bytes 638984 | tf_op jit(solution)/shard_map/ppermute | solution.py:342
  47.6 9.7 %collective-permute-start.3 = (bf16[13,32,256]{2,1,0:T(8,128)(2,1)S(1)}, bf16[13,32,256]{2,1,0:T(8,128)(2,1)S(1)}, u32[]{:S(2)}, u32[]{:S(2)}) collective-permute-start(bf16[13,32,256]{2,1,0:T(8,128)(2,1)S(1)} %get-tuple-element.29.refs_8_), channel_id=1, source_target_pairs={{0,1},{1,0},{2,3},{3,2},{4,5},{5,4},{6,7},{7,6},{8,9},{9,8},{10,11... | collective-permute-start | bytes 638984 | tf_op jit(solution)/shard_map/ppermute | solution.py:342

commit v3 on v2

--- a/solution.py
+++ b/solution.py
@@ -18,6 +18,7 @@
 HALO = 8
 RHO, TEMP = 0, 4
 VMEM = pl.BlockSpec(memory_space=pltpu.VMEM)
+ANY = pl.BlockSpec(memory_space=pl.ANY)
 HBM = pl.BlockSpec(memory_space=pltpu.HBM)
 SMEM = pl.BlockSpec(memory_space=pltpu.SMEM)
 
@@ -105,9 +106,10 @@
 
 
 def pack_kernel(n, two, me_ref, rho, vel, temp, stress, heat, *refs):
-    if two:
-        firsts, refs = refs[:n], refs[n:]
-    tall, given, strip, arrived = refs
+    count = n if two else 0
+    outs, (strip, given, arrived), refs = refs[: count + 3], refs[count + 3 : count + 6], refs[count + 6 :]
+    held, left_at = refs[: count + 3], refs[-1]
+    firsts, (tall, left, right) = held[:count], held[count:]
     rows, cols = rho.shape
     slab = cols // n
     wide = slab // 2 + 2 * HALO
@@ -128,22 +130,29 @@
         copies[f].start()
     strip[0:HALO, :] = jnp.zeros((HALO, rows), jnp.float32)
     strip[HALO + cols :, :] = jnp.zeros((HALO, rows), jnp.float32)
+    leaving = []
     for f in range(MOMENTS):
         copies[f].wait()
         strip[HALO : HALO + cols, :] = code(f, given[f]).T
+        for s in range(count):
+            to = jnp.bitwise_xor(me, s)
+            start = to * slab + jnp.where(to < n // 2, slab // 2, 0)
+            start = pl.multiple_of(start, 16)
+            firsts[s][f] = strip[pl.ds(start, wide), :].astype(jnp.bfloat16)
         tall[f] = strip[...].astype(jnp.bfloat16)
-        if two:
-            for s in range(n):
-                to = jnp.bitwise_xor(me, s)
-                start = to * slab + jnp.where(to < n // 2, slab // 2, 0)
-                start = pl.multiple_of(start, 16)
-                firsts[s][f] = strip[pl.ds(start, wide), :].astype(jnp.bfloat16)
-
-
-def edge_kernel(tall, left, right):
-    cols = tall.shape[1] - 2 * HALO
-    left[...] = tall[:, 0 : 2 * HALO, :]
-    right[...] = tall[:, cols : cols + 2 * HALO, :]
+        left[f] = tall[f, 0 : 2 * HALO, :]
+        right[f] = tall[f, cols : cols + 2 * HALO, :]
+        for k, (mine, out) in enumerate(zip(held, outs)):
+            copy = pltpu.make_async_copy(mine.at[f], out.at[f], left_at.at[k, f])
+            copy.start()
+            leaving.append(copy)
+    for copy in leaving:
+        copy.wait()
+
+
+def edge_kernel(left, right, after, left_out, right_out):
+    left_out[...] = left[...]
+    right_out[...] = right[...]
 
 
 def rest_kernel(n, two, me_ref, tall, before, after, *outs):
@@ -175,7 +184,7 @@
             merge(slice(count - 2 * HALO, count), after, False)
 
 
-def grid_kernel(n, rows, me_ref, out, sin_col, cos_col, back_col, line_col, total):
+def grid_kernel(n, rows, slots, me_ref, out, sin_col, cos_col, back_col, line_col, total):
     size = n * rows
     last = size - 1
     half = math.pi / (2.0 * last)
@@ -201,11 +210,12 @@
         cos_col[here, :] = column(cosine)
         back_col[here, :] = column(jnp.where(edge, 0.5 * sign, sign))
 
-    for s in range(n):
+    for index, s in enumerate(slots):
         line, sine, cosine, edge, sign = table(s)
         front = (-math.pi / last) * sine * cosine * jnp.where(edge, 2.0 * sign, sign)
         for p in range(rows // lane):
-            here = pl.ds(s * rows + p * lane, lane)
+            here = pl.ds(index * rows + p * lane, lane)
+            own = pl.ds(s * rows + p * lane, lane)
             line_i, sin_i, cos_i, front_i = (
                 x[0:1, p * lane : (p + 1) * lane] for x in (line, sine, cosine, front)
             )
@@ -232,21 +242,22 @@
             same = lax.broadcasted_iota(jnp.int32, (lane, lane), 0) == (
                 lax.broadcasted_iota(jnp.int32, (lane, lane), 1)
             )
-            tile = out[here, here].astype(jnp.float32)
-            out[here, here] = jnp.where(same, diagonal, tile).astype(jnp.bfloat16)
-
-
-def section_kernel(n, two, second, me_ref, grid, *refs):
+            tile = out[own, here].astype(jnp.float32)
+            out[own, here] = jnp.where(same, diagonal, tile).astype(jnp.bfloat16)
+
+
+def section_kernel(n, two, second, far, near, me_ref, grid_far, grid_near, *refs):
     firsts, refs = refs[:n], refs[n:]
     if second:
         rests, refs = refs[:n], refs[n + 1 :]
-    outs, (u0, u1, r0, fy0, fy1, product) = refs[:n], refs[n:]
+    outs, refs = refs[: len(far)], refs[len(far) :]
+    u1, r0, fy1, u0, fy0, product = refs
     wide, size = u0.shape[1:]
     rows = size // n
     core = wide - 2 * HALO
     me = me_ref[0]
     right_first = me < n // 2
-    lane = rows if rows < 128 else 128
+    lane = min(rows, 128)
     parts = rows // lane
 
     for s in range(n):
@@ -263,11 +274,6 @@
                 old = firsts[s][f, src, :].astype(jnp.float32)
                 u0[f, dst, here] = decode(f, old)
 
-    def walls(s, p, count):
-        line = jnp.bitwise_xor(me, s) * rows + p * lane
-        line = line + lax.broadcasted_iota(jnp.int32, (count, lane), 1)
-        return jnp.where(line == 0, 1.0, jnp.where(line == size - 1, -1.0, 0.0))
-
     for s in range(n):
         for p in range(parts):
             here = pl.ds(s * rows + p * lane, lane)
@@ -277,13 +283,14 @@
 
     middle = slice(HALO, HALO + core)
     for s in range(n):
-        block = pl.ds(s * rows, rows)
-        product[...] = jnp.dot(fy0[...], grid[:, block], preferred_element_type=jnp.float32)
+        weights = (grid_far, far) if s in far else (grid_near, near)
+        block = pl.ds(weights[1].index(s) * rows, rows)
+        product[...] = jnp.dot(fy0[...], weights[0][:, block], preferred_element_type=jnp.float32)
         for p in range(parts):
             here = pl.ds(s * rows + p * lane, lane)
             there = pl.ds(p * lane, lane)
             u = [u0[f, :, here] for f in range(MOMENTS)]
-            src = sources(u, walls(s, p, wide))
+            src = sources(u, walls(me, s, p, n, rows, wide))
             new = []
             for f in range(MOMENTS):
                 across = product[f * wide : (f + 1) * wide, there]
@@ -297,50 +304,89 @@
             for f in range(MOMENTS):
                 fy1[f * core : (f + 1) * core, here] = flux(inner, 1, f).astype(jnp.bfloat16)
 
-    for s in range(n):
-        block = pl.ds(s * rows, rows)
+    finish(n, far, me_ref, grid_far, u1, r0, fy1, outs, product)
+
+
+def finish_kernel(n, near, chunks, me_ref, grid_near, *refs):
+    states, outs, product = refs[: 3 * chunks], refs[-1 - len(near) : -1], refs[-1]
+    core = outs[0].shape[1] // chunks
+    for c in range(chunks):
+        part = [out.at[:, c * core : (c + 1) * core, :] for out in outs]
+        finish(n, near, me_ref, grid_near, *states[3 * c : 3 * c + 3], part, product)
+
+
+def walls(me, s, p, n, rows, count):
+    lane = min(rows, 128)
+    line = jnp.bitwise_xor(me, s) * rows + p * lane
+    line = line + lax.broadcasted_iota(jnp.int32, (count, lane), 1)
+    return jnp.where(line == 0, 1.0, jnp.where(line == n * rows - 1, -1.0, 0.0))
+
+
+def finish(n, slots, me_ref, grid, u1, r0, fy1, outs, product):
+    wide, size = u1.shape[1:]
+    rows = size // n
+    core = wide - 2 * HALO
+    lane = min(rows, 128)
+    me = me_ref[0]
+    middle = slice(HALO, HALO + core)
+    for k, s in enumerate(slots):
+        block = pl.ds(k * rows, rows)
         product[0 : MOMENTS * core, :] = jnp.dot(
             fy1[...], grid[:, block], preferred_element_type=jnp.float32
         )
-        for p in range(parts):
+        for p in range(rows // lane):
             here = pl.ds(s * rows + p * lane, lane)
             there = pl.ds(p * lane, lane)
             u = [u1[f, :, here] for f in range(MOMENTS)]
             inner = [x[middle] for x in u]
-            src = sources(inner, walls(s, p, core))
+            src = sources(inner, walls(me, s, p, n, rows, core))
             for f in range(MOMENTS):
                 across = product[f * core : (f + 1) * core, there]
                 rate = -(along_of(flux(u, 0, f))[middle] + across)
                 if src[f] is not None:
                     rate = rate + src[f]
                 rate = 0.5 * (r0[f, :, here] + rate)
-                outs[s][f, :, there] = rate.astype(outs[s].dtype)
-
-
-def unpack_kernel(n, two, me_ref, *refs):
-    chunks = [refs[:n], refs[n : 2 * n]] if two else [refs[:n]]
-    out, tall = refs[-2:]
+                outs[k][f, :, there] = rate.astype(outs[k].dtype)
+
+
+def arrived_kernel(*refs):
+    refs[-1][...] = jnp.zeros_like(refs[-1])
+
+
+def unpack_kernel(n, far, near, chunks, me_ref, *refs):
+    staying, refs = refs[: len(near)], refs[len(near) :]
+    out, tall, held, leaving = refs[-4:]
     cols = tall.shape[0]
     slab = cols // n
-    width = slab // len(chunks)
+    width = slab // chunks
     me = me_ref[0]
+    copies = []
     for f in range(MOMENTS):
-        for s in range(n):
+        for s in near + far:
             of = jnp.bitwise_xor(me, s)
-            for c, arrays in enumerate(chunks):
+            for c in range(chunks):
                 start = of * slab
-                if two:
+                if chunks == 2:
                     start += jnp.where(of < n // 2, width * (1 - c), width * c)
                 here = pl.ds(pl.multiple_of(start, 16), width)
-                tall[here, :] = arrays[s][f].astype(jnp.float32)
-        out[f] = tall[...].T
-
-
-def exchange(arrays, n):
-    got = [arrays[0]]
-    for s in range(1, n):
-        got.append(lax.ppermute(arrays[s], "gy", [(i, i ^ s) for i in range(n)]))
-    return got
+                if s in near:
+                    piece = staying[near.index(s)][f, c * width : (c + 1) * width, :]
+                else:
+                    piece = refs[c * len(far) + far.index(s)][f]
+                tall[here, :] = piece.astype(jnp.float32)
+        held[f] = tall[...].T
+        copies.append(pltpu.make_async_copy(held.at[f], out.at[f], leaving.at[f]))
+        copies[f].start()
+    for copy in copies:
+        copy.wait()
+
+
+def to_partner(array, n, s):
+    return array if s == 0 else lax.ppermute(array, "gy", [(i, i ^ s) for i in range(n)])
+
+
+def exchange(arrays, n, slots):
+    return [to_partner(array, n, s) for array, s in zip(arrays, slots)]
 
 
 def on_device(rho, vel, temp, stress, heat):
@@ -359,47 +405,56 @@
         return jax.ShapeDtypeStruct((MOMENTS, width, rows), kind)
 
     count = n if two else 0
-    *firsts, tall = pl.pallas_call(
+    shapes = [message(wide)] * count + [message(cols + 2 * HALO)] + [message(2 * HALO)] * 2
+    *firsts, tall, left, right = pl.pallas_call(
         functools.partial(pack_kernel, n, two),
-        out_shape=[message(wide)] * count + [message(cols + 2 * HALO)],
+        out_shape=shapes,
         in_specs=[SMEM] + [HBM] * 5,
-        out_specs=[VMEM] * (count + 1),
+        out_specs=[ANY] * len(shapes),
         scratch_shapes=[
+            pltpu.VMEM((cols + 2 * HALO, rows), jnp.float32),
             pltpu.VMEM((MOMENTS, rows, cols), jnp.float32),
-            pltpu.VMEM((cols + 2 * HALO, rows), jnp.float32),
             pltpu.SemaphoreType.DMA((MOMENTS,)),
-        ],
+        ]
+        + [pltpu.VMEM(x.shape, x.dtype) for x in shapes]
+        + [pltpu.SemaphoreType.DMA((len(shapes), MOMENTS))],
         compiler_params=params(56),
         cost_estimate=cost(2),
         name="pack",
     )(me, rho, vel, temp, stress, heat)
     if two:
-        firsts = exchange(firsts, n)
+        firsts = exchange(firsts, n, range(n))
+
+    lane = min(rows, 128)
+
+    def grid_of(slots):
+        return pl.pallas_call(
+            functools.partial(grid_kernel, n, rows, slots),
+            out_shape=jax.ShapeDtypeStruct((size, len(slots) * rows), half),
+            in_specs=[SMEM],
+            out_specs=VMEM,
+            scratch_shapes=[pltpu.VMEM((size, lane), jnp.float32)] * 4
+            + [pltpu.VMEM((8, lane), jnp.float32)],
+            compiler_params=params(24),
+            cost_estimate=cost(3),
+            name="grid",
+        )(me)
+
+    far, near = (tuple(range(n // 2, n)), tuple(range(n // 2)))
+    grid = {far: grid_of(far)}
     left, right = pl.pallas_call(
         edge_kernel,
         out_shape=[message(2 * HALO)] * 2,
-        in_specs=[VMEM],
+        in_specs=[VMEM] * 2 + [ANY],
         out_specs=[VMEM] * 2,
-        compiler_params=params(),
+        compiler_params=params(24),
         cost_estimate=cost(0.2),
         name="edges",
-    )(tall)
+    )(left, right, grid[far])
     up = [(i, (i + 1) % ring) for i in range(ring)]
     before = lax.ppermute(right, "gx", up)
     after = lax.ppermute(left, "gx", [(j, i) for i, j in up])
-
-    lane = min(rows, 128)
-    grid = pl.pallas_call(
-        functools.partial(grid_kernel, n, rows),
-        out_shape=jax.ShapeDtypeStruct((size, size), half),
-        in_specs=[SMEM],
-        out_specs=VMEM,
-        scratch_shapes=[pltpu.VMEM((size, lane), jnp.float32)] * 4
-        + [pltpu.VMEM((8, lane), jnp.float32)],
-        compiler_params=params(),
-        cost_estimate=cost(5),
-        name="grid",
-    )(me)
+    grid[near] = grid_of(near)
     rests = pl.pallas_call(
         functools.partial(rest_kernel, n, two),
         out_shape=[message(core if two else wide)] * n,
@@ -409,43 +464,75 @@
         cost_estimate=cost(0.2),
         name="rest",
     )(me, tall, before, after)
-    rests = exchange(rests, n)
+    rests = exchange(rests, n, range(n))
 
     def sections(second, *arrays):
-        return pl.pallas_call(
-            functools.partial(section_kernel, n, two, second),
-            out_shape=[message(core, jnp.float32)] + [message(core)] * (n - 1),
-            in_specs=[SMEM] + [VMEM] * (2 * n + 1 if second else n + 1) + [HBM] * second,
-            out_specs=[VMEM] * n,
+        state = [
+            jax.ShapeDtypeStruct((MOMENTS, wide, size), jnp.float32),
+            jax.ShapeDtypeStruct((MOMENTS, core, size), jnp.float32),
+            jax.ShapeDtypeStruct((MOMENTS * core, size), half),
+        ]
+        *crossing, u1, r0, fy1 = pl.pallas_call(
+            functools.partial(section_kernel, n, two, second, far, near),
+            out_shape=[message(core)] * len(far) + state,
+            in_specs=[SMEM] + [VMEM] * (2 * n + 2 if second else n + 2) + [ANY] * second,
+            out_specs=[VMEM] * (len(far) + 3),
             scratch_shapes=[
                 pltpu.VMEM((MOMENTS, wide, size), jnp.float32),
-                pltpu.VMEM((MOMENTS, wide, size), jnp.float32),
-                pltpu.VMEM((MOMENTS, core, size), jnp.float32),
                 pltpu.VMEM((MOMENTS * wide, size), half),
-                pltpu.VMEM((MOMENTS * core, size), half),
                 pltpu.VMEM((MOMENTS * wide, rows), jnp.float32),
             ],
-            compiler_params=params(),
-            cost_estimate=cost(7),
+            compiler_params=params(24),
+            cost_estimate=cost(6),
             name="sections",
-        )(me, grid, *arrays)
+        )(me, grid[far], grid[near], *arrays)
+        return crossing, [u1, r0, fy1]
+
+    def finished(states, *ties):
+        return pl.pallas_call(
+            functools.partial(finish_kernel, n, near, len(states) // 3),
+            out_shape=[message(slab, jnp.float32)] + [message(slab)] * (len(near) - 1),
+            in_specs=[SMEM] + [VMEM] * (len(states) + 1) + [ANY] * len(ties),
+            out_specs=[VMEM] * len(near),
+            scratch_shapes=[pltpu.VMEM((MOMENTS * core, rows), jnp.float32)],
+            compiler_params=params(24),
+            cost_estimate=cost(4),
+            name="finish",
+        )(me, grid[near], *states, *ties)
 
     if two:
-        first = sections(False, *firsts)
-        back = exchange(first, n)
-        back += exchange(sections(True, *firsts, *rests, first[1]), n)
+        crossing, states = sections(False, *firsts)
+        back = exchange(crossing, n, far)
+        crossing, more = sections(True, *firsts, *rests, crossing[0])
+        staying = finished(states + more, *back)
+        back += exchange(crossing, n, far)
     else:
-        back = exchange(sections(False, *rests), n)
+        crossing, states = sections(False, *rests)
+        staying = finished(states)
+        back = exchange(crossing, n, far)
+    staying = exchange(staying, n, near)
+    arrived = pl.pallas_call(
+        arrived_kernel,
+        out_shape=jax.ShapeDtypeStruct((8, 128), jnp.float32),
+        in_specs=[ANY] * len(back),
+        out_specs=VMEM,
+        cost_estimate=cost(6),
+        name="arrived",
+    )(*back)
     out = pl.pallas_call(
-        functools.partial(unpack_kernel, n, two),
+        functools.partial(unpack_kernel, n, far, near, 2 if two else 1),
         out_shape=jax.ShapeDtypeStruct((MOMENTS, rows, cols), jnp.float32),
-        in_specs=[SMEM] + [VMEM] * len(back),
-        out_specs=VMEM,
-        scratch_shapes=[pltpu.VMEM((cols, rows), jnp.float32)],
-        compiler_params=params(),
+        in_specs=[SMEM] + [VMEM] * (len(staying) + len(back)) + [ANY],
+        out_specs=ANY,
+        scratch_shapes=[
+            pltpu.VMEM((cols, rows), jnp.float32),
+            pltpu.VMEM((MOMENTS, rows, cols), jnp.float32),
+            pltpu.SemaphoreType.DMA((MOMENTS,)),
+        ],
+        compiler_params=params(24),
         cost_estimate=cost(3),
         name="unpack",
-    )(me, *back)
+    )(me, *staying, *back, arrived)
     return jnp.swapaxes(out, 0, 1)
 
 

time: 60.2 us -> 57 us (0.947)
  waiting for transfers between devices: 16.2 us -> 9.15 us
  local copies, waits for them, and re-layouts: 1.49 us -> 4.15 us
  Pallas kernels: 28 us -> 29.1 us
    ppermute x12 -> x11, waiting for transfers between devices: 16.2 us -> 8.26 us  [to_partner(): lax.ppermute(array, 'gy', [(i, i ^ s) for i in range(n)])]
    unnamed x6 -> x30, local copies, waits for them, and re-layouts: 1.49 us -> 4.15 us
    ppermute x1, starting transfers between devices: 3.02 us -> 1.77 us  [on_device(): before = lax.ppermute(right, 'gx', up)]
    pallas_call x5 -> x8, Pallas kernels: 27.7 us -> 28.8 us  [the longest x2 12.1 us: sections(): pl.pallas_call(functools.partial(section_kernel, n, two, second, far, nea...]
    ppermute x12 -> x11, starting transfers between devices: 8.23 us -> 9.2 us  [to_partner(): lax.ppermute(array, 'gy', [(i, i ^ s) for i in range(n)])]
  transfers between devices with their start and end apart: 14 -> 13, of which waited for: 5 -> 7; matrix products, arithmetic and copies ran while one was open for 0% -> 0% of each run, Pallas kernels for 34% -> 40%
where the time goes in v3:
time: 57 us; the launch traced here: 56.8 us
  Pallas kernels  29.1 us (51%)
  starting transfers between devices  14.1 us (25%)
  waiting for transfers between devices  9.15 us (16%)
  local copies, waits for them, and re-layouts  4.15 us (7%)
    pallas_call x2, Pallas kernels, sections(): pl.pallas_call(functools.partial(section_kernel, n, two, second, far, nea...  12.1 us
    ppermute x11, starting transfers between devices, to_partner(): lax.ppermute(array, 'gy', [(i, i ^ s) for i in range(n)])  9.2 us
    ppermute x11, waiting for transfers between devices, to_partner(): lax.ppermute(array, 'gy', [(i, i ^ s) for i in range(n)])  8.26 us
    pallas_call x2, Pallas kernels, grid_of(): pl.pallas_call(functools.partial(grid_kernel, n, rows, slots), out_shape=...  6.42 us
    pallas_call x1, Pallas kernels, on_device(): pl.pallas_call(functools.partial(pack_kernel, n, two), out_shape=shapes,...  4.54 us
    unnamed x30, local copies, waits for them, and re-layouts  4.15 us
    ppermute x1, starting transfers between devices, on_device(): after = lax.ppermute(left, 'gx', [(j, i) for i, j in up])  3.11 us
    pallas_call x1, Pallas kernels, finished(): pl.pallas_call(functools.partial(finish_kernel, n, near, len(states) // 3...  3.11 us
  transfers between devices with their start and end apart: 13, of which 7 were waited for; matrix products, arithmetic and copies ran while one was open for 0% of the time, Pallas kernels for 40%

profile of v3, /device:TPU:0, one launch (start us, length us, event | category | flops | bytes accessed | tf_op | source)
XLA Modules:
  0.0 56.8 jit_solution(1273700434033218446)
XLA Ops:
  0.0 4.5 %pack.1 = (bf16[13,48,256]{2,1,0:T(8,128)(2,1)}, bf16[13,48,256]{2,1,0:T(8,128)(2,1)}, bf16[13,48,256]{2,1,0:T(8,128)(2,1)}, bf16[13,48,256]{2,1,0:T(8,128)(2,1)...) custom-call(s32[1]{0:T(128)} %bitcast.me_ref, f32[256,256]{1,0:T(8,128)} %rho.1, ...), custom_call_target="tpu_custom_call" | custom-call | flops 2000000000 | bytes 6000000 | tf_op jit(solution)/shard_map/pack/pallas_call | solution.py:409
  4.5 0.5 collective-permute-start
  5.1 2.6 %collective-permute-start.1 = (bf16[13,48,256]{2,1,0:T(8,128)(2,1)}, bf16[13,48,256]{2,1,0:T(8,128)(2,1)S(1)}, u32[]{:S(2)}, u32[]{:S(2)}) collective-permute-start(bf16[13,48,256]{2,1,0:T(8,128)(2,1)} %get-tuple-element.32), channel_id=1, source_target_pairs={{0,2},{1,3},{2,0},{3,1},{4,6},{5,7},{6,4},{7,5},{8,10},{9,11},{10,... | collective-permute-start | bytes 958472 | tf_op jit(solution)/shard_map/ppermute | solution.py:385
  7.7 3.2 %grid.3.grid_far.after = bf16[1024,512]{1,0:T(8,128)(2,1)S(1)} custom-call(s32[1]{0:T(128)} %bitcast.me_ref), custom_call_target="tpu_custom_call" | custom-call | flops 3000000000 | bytes 9000000 | tf_op jit(solution)/shard_map/grid/pallas_call | solution.py:431
  11.0 1.8 %collective-permute-start.3 = (bf16[13,16,256]{2,1,0:T(8,128)(2,1)S(1)}, bf16[13,16,256]{2,1,0:T(8,128)(2,1)S(1)}, u32[]{:S(2)}, u32[]{:S(2)}) collective-permute-start(bf16[13,16,256]{2,1,0:T(8,128)(2,1)S(1)} %get-tuple-element.40), channel_id=1, source_target_pairs={{0,4},{4,8},{8,12},{12,16},{16,20},{20,24},{24,28},{28,0},{1,5},{5... | collective-permute-start | bytes 319496 | tf_op jit(solution)/shard_map/ppermute | solution.py:455
  12.8 3.1 %collective-permute-start.4 = (bf16[13,16,256]{2,1,0:T(8,128)(2,1)S(1)}, bf16[13,16,256]{2,1,0:T(8,128)(2,1)S(1)}, u32[]{:S(2)}, u32[]{:S(2)}) collective-permute-start(bf16[13,16,256]{2,1,0:T(8,128)(2,1)S(1)} %get-tuple-element.41), channel_id=1, source_target_pairs={{4,0},{8,4},{12,8},{16,12},{20,16},{24,20},{28,24},{0,28},{5,1},{9... | collective-permute-start | bytes 319496 | tf_op jit(solution)/shard_map/ppermute | solution.py:456
  15.9 3.2 %grid.2.grid_near = bf16[1024,512]{1,0:T(8,128)(2,1)S(1)} custom-call(s32[1]{0:T(128)} %bitcast.me_ref), custom_call_target="tpu_custom_call" | custom-call | flops 3000000000 | bytes 9000000 | tf_op jit(solution)/shard_map/grid/pallas_call | solution.py:431
  19.1 0.3 collective-permute-done.3.before
  19.4 0.6 %collective-permute-done.4.after = bf16[13,16,256]{2,1,0:T(8,128)(2,1)S(1)} collective-permute-done((bf16[13,16,256]{2,1,0:T(8,128)(2,1)S(1)}, bf16[13,16,256]{2,1,0:T(8,128)(2,1)S(1)}, u32[]{:S(2)}, u32[]{:S(2)}) %collective-permute-start.4) | collective-permute-done | bytes 106528 | tf_op jit(solution)/shard_map/ppermute | solution.py:456
  20.0 0.3 rest.1
  20.3 0.1 collective-permute-start.5
  20.4 1.6 %collective-permute-start.6 = (bf16[13,32,256]{2,1,0:T(8,128)(2,1)S(1)}, bf16[13,32,256]{2,1,0:T(8,128)(2,1)S(1)}, u32[]{:S(2)}, u32[]{:S(2)}) collective-permute-start(bf16[13,32,256]{2,1,0:T(8,128)(2,1)S(1)} %get-tuple-element.44), channel_id=1, source_target_pairs={{0,2},{1,3},{2,0},{3,1},{4,6},{5,7},{6,4},{7,5},{8,10},{9,11},{10,... | collective-permute-start | bytes 638984 | tf_op jit(solution)/shard_map/ppermute | solution.py:385
  22.0 0.3 collective-permute-start.7
  22.2 0.4 collective-permute-done.2.refs_3_
  22.6 5.8 %sections.2 = (bf16[13,32,256]{2,1,0:T(8,128)(2,1)S(1)}, bf16[13,32,256]{2,1,0:T(8,128)(2,1)S(1)}, f32[13,48,1024]{2,1,0:T(8,128)S(1)}, f32[13,32,1024]{2,1,0:T(8,128)S(1)}, bf16[416,1024]{1,0:T(8,128)(2,1)S(1)}) custom-call(s32[1]{0:T(128)} %bitcast.me_ref, bf16[1024,512]{1,0:T(8,128)(2,1)S(1)} %grid.3.grid_far.after, bf16[1024,512]{1,0:T(8,128)(2,1)S(1)} %grid.2.grid_near, ...), custom_call_target="tpu_custom_call" | custom-call | flops 6000000000 | bytes 18000000 | tf_op jit(solution)/shard_map/sections/pallas_call | solution.py:475
  28.4 1.6 %collective-permute-start.8 = (bf16[13,32,256]{2,1,0:T(8,128)(2,1)S(1)}, bf16[13,32,256]{2,1,0:T(8,128)(2,1)S(1)}, u32[]{:S(2)}, u32[]{:S(2)}) collective-permute-start(bf16[13,32,256]{2,1,0:T(8,128)(2,1)S(1)} %get-tuple-element.46.refs_8_), channel_id=1, source_target_pairs={{0,2},{1,3},{2,0},{3,1},{4,6},{5,7},{6,4},{7,5},{8,10},{9,11},{10,... | collective-permute-start | bytes 638984 | tf_op jit(solution)/shard_map/ppermute | solution.py:385
  30.0 2.1 %collective-permute-done.7.refs_7_ = bf16[13,32,256]{2,1,0:T(8,128)(2,1)S(1)} collective-permute-done((bf16[13,32,256]{2,1,0:T(8,128)(2,1)S(1)}, bf16[13,32,256]{2,1,0:T(8,128)(2,1)S(1)}, u32[]{:S(2)}, u32[]{:S(2)}) %collective-permute-start.7) | collective-permute-done | bytes 213024 | tf_op jit(solution)/shard_map/ppermute | solution.py:385
  32.1 6.3 %sections.3 = (bf16[13,32,256]{2,1,0:T(8,128)(2,1)S(1)}, bf16[13,32,256]{2,1,0:T(8,128)(2,1)S(1)}, f32[13,48,1024]{2,1,0:T(8,128)S(1)}, f32[13,32,1024]{2,1,0:T(8,128)S(1)}, bf16[416,1024]{1,0:T(8,128)(2,1)S(1)}) custom-call(s32[1]{0:T(128)} %bitcast.me_ref, bf16[1024,512]{1,0:T(8,128)(2,1)S(1)} %grid.3.grid_far.after, bf16[1024,512]{1,0:T(8,128)(2,1)S(1)} %grid.2.grid_near, ...), custom_call_target="tpu_custom_call" | custom-call | flops 6000000000 | bytes 18000000 | tf_op jit(solution)/shard_map/sections/pallas_call | solution.py:475
  38.5 1.6 %collective-permute-start.11 = (bf16[13,32,256]{2,1,0:T(8,128)(2,1)S(1)}, bf16[13,32,256]{2,1,0:T(8,128)(2,1)S(1)}, u32[]{:S(2)}, u32[]{:S(2)}) collective-permute-start(bf16[13,32,256]{2,1,0:T(8,128)(2,1)S(1)} %get-tuple-element.53), channel_id=1, source_target_pairs={{0,2},{1,3},{2,0},{3,1},{4,6},{5,7},{6,4},{7,5},{8,10},{9,11},{10,... | collective-permute-start | bytes 638984 | tf_op jit(solution)/shard_map/ppermute | solution.py:385
  40.1 0.5 collective-permute-start.12
  40.6 0.6 %collective-permute-done.9.refs_7_.refs_1_.refs_3_ = bf16[13,32,256]{2,1,0:T(8,128)(2,1)S(1)} collective-permute-done((bf16[13,32,256]{2,1,0:T(8,128)(2,1)S(1)}, bf16[13,32,256]{2,1,0:T(8,128)(2,1)S(1)}, u32[]{:S(2)}, u32[]{:S(2)}) %collective-permute-start.9) | collective-permute-done | bytes 213024 | tf_op jit(solution)/shard_map/ppermute | solution.py:385
  41.3 3.1 %finish.1 = (f32[13,64,256]{2,1,0:T(8,128)S(1)}, bf16[13,64,256]{2,1,0:T(8,128)(2,1)S(1)}) custom-call(s32[1]{0:T(128)} %bitcast.me_ref, bf16[1024,512]{1,0:T(8,128)(2,1)S(1)} %grid.2.grid_near, f32[13,48,1024]{2,1,0:T(8,128)S(1)} %get-tuple-element.34.refs_0_, f32[13,32,1024]{2,1,0:T(8,128)S(1)} %get-tuple-element.35.refs_1_, ...), custom_call_target="tpu_custom_call" | custom-call | flops 4000000000 | bytes 12000000 | tf_op jit(solution)/shard_map/finish/pallas_call | solution.py:492
  44.4 0.9 %copy-done.11 = f32[13,64,256]{2,1,0:T(8,128)} copy-done((f32[13,64,256]{2,1,0:T(8,128)}, f32[13,64,256]{2,1,0:T(8,128)S(1)}, u32[]{:S(2)}) %copy-start.11) | copy-done | bytes 851992
  45.3 0.3 collective-permute-start.10
  45.6 1.1 %collective-permute-done.11.refs_2_.refs_4_ = bf16[13,32,256]{2,1,0:T(8,128)(2,1)S(1)} collective-permute-done((bf16[13,32,256]{2,1,0:T(8,128)(2,1)S(1)}, bf16[13,32,256]{2,1,0:T(8,128)(2,1)S(1)}, u32[]{:S(2)}, u32[]{:S(2)}) %collective-permute-start.11) | collective-permute-done | bytes 213024 | tf_op jit(solution)/shard_map/ppermute | solution.py:385
  46.7 4.1 %collective-permute-done.12.refs_3_.refs_5_ = bf16[13,32,256]{2,1,0:T(8,128)(2,1)S(1)} collective-permute-done((bf16[13,32,256]{2,1,0:T(8,128)(2,1)S(1)}, bf16[13,32,256]{2,1,0:T(8,128)(2,1)S(1)}, u32[]{:S(2)}, u32[]{:S(2)}) %collective-permute-start.12) | collective-permute-done | bytes 213024 | tf_op jit(solution)/shard_map/ppermute | solution.py:385
  50.8 0.7 %copy-done.9 = bf16[13,32,256]{2,1,0:T(8,128)(2,1)} copy-done((bf16[13,32,256]{2,1,0:T(8,128)(2,1)}, bf16[13,32,256]{2,1,0:T(8,128)(2,1)S(1)}, u32[]{:S(2)}) %copy-start.9) | copy-done | bytes 213016
  51.4 0.6 %arrived.1.refs_6_ = f32[8,128]{1,0:T(8,128)} custom-call(bf16[13,32,256]{2,1,0:T(8,128)(2,1)} %copy-done.3, bf16[13,32,256]{2,1,0:T(8,128)(2,1)} %copy-done.5, bf16[13,32,256]{2,1,0:T(8,128)(2,1)} %copy-done.7, bf16[13,32,256]{2,1,0:T(8,128)(2,1)} %copy-done.9), custom_call_target="tpu_custom_call" | custom-call | flops 6000000000 | bytes 18000000 | tf_op jit(solution)/shard_map/arrived/pallas_call | solution.py:514
  52.1 0.9 %copy-done.8 = bf16[13,32,256]{2,1,0:T(8,128)(2,1)S(1)} copy-done((bf16[13,32,256]{2,1,0:T(8,128)(2,1)S(1)}, bf16[13,32,256]{2,1,0:T(8,128)(2,1)}, u32[]{:S(2)}) %copy-start.8) | copy-done | bytes 213016
  53.0 0.9 %copy-done.10 = bf16[13,32,256]{2,1,0:T(8,128)(2,1)S(1)} copy-done((bf16[13,32,256]{2,1,0:T(8,128)(2,1)S(1)}, bf16[13,32,256]{2,1,0:T(8,128)(2,1)}, u32[]{:S(2)}) %copy-start.10) | copy-done | bytes 213016
  53.9 0.7 %copy-done.14 = f32[8,128]{1,0:T(8,128)S(1)} copy-done((f32[8,128]{1,0:T(8,128)S(1)}, f32[8,128]{1,0:T(8,128)}, u32[]{:S(2)}) %copy-start.14) | copy-done | bytes 4120
  54.6 2.0 %unpack.1 = f32[13,256,256]{2,1,0:T(8,128)} custom-call(s32[1]{0:T(128)} %bitcast.me_ref, f32[13,64,256]{2,1,0:T(8,128)S(1)} %copy-done.12, bf16[13,64,256]{2,1,0:T(8,128)(2,1)S(1)} %collective-permute-done.10.refs_1_, bf16[13,32,256]{2,1,0:T(8,128)(2,1)S(1)} %copy-done.4, bf16[13,32,256]{2,1,0:T(8,128)(2,1)S(1)} %copy-done.6, ...), custom_call_target="tpu_custom_call" | custom-call | flops 3000000000 | bytes 9000000 | tf_op jit(solution)/shard_map/unpack/pallas_call | solution.py:522
  (34 shorter events, 0.1 us)
Async XLA Ops:
  4.5 17.4 %collective-permute-start = (bf16[13,48,256]{2,1,0:T(8,128)(2,1)}, bf16[13,48,256]{2,1,0:T(8,128)(2,1)S(1)}, u32[]{:S(2)}, u32[]{:S(2)}) collective-permute-start(bf16[13,48,256]{2,1,0:T(8,128)(2,1)} %get-tuple-element.31), channel_id=1, source_target_pairs={{0,1},{1,0},{2,3},{3,2},{4,5},{5,4},{6,7},{7,6},{8,9},{9,8},{10,11... | collective-permute-start | bytes 958472 | tf_op jit(solution)/shard_map/ppermute | solution.py:385
  5.1 17.1 %collective-permute-start.1 = (bf16[13,48,256]{2,1,0:T(8,128)(2,1)}, bf16[13,48,256]{2,1,0:T(8,128)(2,1)S(1)}, u32[]{:S(2)}, u32[]{:S(2)}) collective-permute-start(bf16[13,48,256]{2,1,0:T(8,128)(2,1)} %get-tuple-element.32), channel_id=1, source_target_pairs={{0,2},{1,3},{2,0},{3,1},{4,6},{5,7},{6,4},{7,5},{8,10},{9,11},{10,... | collective-permute-start | bytes 958472 | tf_op jit(solution)/shard_map/ppermute | solution.py:385
  7.7 3.3 %copy-start.1 = (bf16[13,16,256]{2,1,0:T(8,128)(2,1)S(1)}, bf16[13,16,256]{2,1,0:T(8,128)(2,1)}, u32[]{:S(2)}) copy-start(bf16[13,16,256]{2,1,0:T(8,128)(2,1)} %get-tuple-element.38.left) | copy-start | bytes 319492
  7.7 3.3 %copy-start.2 = (bf16[13,16,256]{2,1,0:T(8,128)(2,1)S(1)}, bf16[13,16,256]{2,1,0:T(8,128)(2,1)}, u32[]{:S(2)}) copy-start(bf16[13,16,256]{2,1,0:T(8,128)(2,1)} %get-tuple-element.39.right) | copy-start | bytes 319492
  7.7 14.9 %collective-permute-start.2 = (bf16[13,48,256]{2,1,0:T(8,128)(2,1)}, bf16[13,48,256]{2,1,0:T(8,128)(2,1)S(1)}, u32[]{:S(2)}, u32[]{:S(2)}) collective-permute-start(bf16[13,48,256]{2,1,0:T(8,128)(2,1)} %get-tuple-element.33), channel_id=1, source_target_pairs={{0,3},{1,2},{2,1},{3,0},{4,7},{5,6},{6,5},{7,4},{8,11},{9,10},{10,... | collective-permute-start | bytes 958472 | tf_op jit(solution)/shard_map/ppermute | solution.py:385
  11.0 8.4 %collective-permute-start.3 = (bf16[13,16,256]{2,1,0:T(8,128)(2,1)S(1)}, bf16[13,16,256]{2,1,0:T(8,128)(2,1)S(1)}, u32[]{:S(2)}, u32[]{:S(2)}) collective-permute-start(bf16[13,16,256]{2,1,0:T(8,128)(2,1)S(1)} %get-tuple-element.40), channel_id=1, source_target_pairs={{0,4},{4,8},{8,12},{12,16},{16,20},{20,24},{24,28},{28,0},{1,5},{5... | collective-permute-start | bytes 319496 | tf_op jit(solution)/shard_map/ppermute | solution.py:455
  12.8 7.2 %copy-start = (bf16[13,272,256]{2,1,0:T(8,128)(2,1)S(1)}, bf16[13,272,256]{2,1,0:T(8,128)(2,1)}, u32[]{:S(2)}) copy-start(bf16[13,272,256]{2,1,0:T(8,128)(2,1)} %get-tuple-element.37.tall) | copy-start | bytes 5431300
  12.8 7.2 %collective-permute-start.4 = (bf16[13,16,256]{2,1,0:T(8,128)(2,1)S(1)}, bf16[13,16,256]{2,1,0:T(8,128)(2,1)S(1)}, u32[]{:S(2)}, u32[]{:S(2)}) collective-permute-start(bf16[13,16,256]{2,1,0:T(8,128)(2,1)S(1)} %get-tuple-element.41), channel_id=1, source_target_pairs={{4,0},{8,4},{12,8},{16,12},{20,16},{24,20},{28,24},{0,28},{5,1},{9... | collective-permute-start | bytes 319496 | tf_op jit(solution)/shard_map/ppermute | solution.py:456
  19.1 3.5 %copy-start.13 = (bf16[13,48,256]{2,1,0:T(8,128)(2,1)S(1)}, bf16[13,48,256]{2,1,0:T(8,128)(2,1)}, u32[]{:S(2)}) copy-start(bf16[13,48,256]{2,1,0:T(8,128)(2,1)} %get-tuple-element.30.refs_0_) | copy-start | bytes 958468
  20.3 9.8 %collective-permute-start.5 = (bf16[13,32,256]{2,1,0:T(8,128)(2,1)S(1)}, bf16[13,32,256]{2,1,0:T(8,128)(2,1)S(1)}, u32[]{:S(2)}, u32[]{:S(2)}) collective-permute-start(bf16[13,32,256]{2,1,0:T(8,128)(2,1)S(1)} %get-tuple-element.43), channel_id=1, source_target_pairs={{0,1},{1,0},{2,3},{3,2},{4,5},{5,4},{6,7},{7,6},{8,9},{9,8},{10,11... | collective-permute-start | bytes 638984 | tf_op jit(solution)/shard_map/ppermute | solution.py:385
  20.4 9.7 %collective-permute-start.6 = (bf16[13,32,256]{2,1,0:T(8,128)(2,1)S(1)}, bf16[13,32,256]{2,1,0:T(8,128)(2,1)S(1)}, u32[]{:S(2)}, u32[]{:S(2)}) collective-permute-start(bf16[13,32,256]{2,1,0:T(8,128)(2,1)S(1)} %get-tuple-element.44), channel_id=1, source_target_pairs={{0,2},{1,3},{2,0},{3,1},{4,6},{5,7},{6,4},{7,5},{8,10},{9,11},{10,... | collective-permute-start | bytes 638984 | tf_op jit(solution)/shard_map/ppermute | solution.py:385
  22.0 10.2 %collective-permute-start.7 = (bf16[13,32,256]{2,1,0:T(8,128)(2,1)S(1)}, bf16[13,32,256]{2,1,0:T(8,128)(2,1)S(1)}, u32[]{:S(2)}, u32[]{:S(2)}) collective-permute-start(bf16[13,32,256]{2,1,0:T(8,128)(2,1)S(1)} %get-tuple-element.45), channel_id=1, source_target_pairs={{0,3},{1,2},{2,1},{3,0},{4,7},{5,6},{6,5},{7,4},{8,11},{9,10},{10,... | collective-permute-start | bytes 638984 | tf_op jit(solution)/shard_map/ppermute | solution.py:385
  28.4 12.2 %collective-permute-start.8 = (bf16[13,32,256]{2,1,0:T(8,128)(2,1)S(1)}, bf16[13,32,256]{2,1,0:T(8,128)(2,1)S(1)}, u32[]{:S(2)}, u32[]{:S(2)}) collective-permute-start(bf16[13,32,256]{2,1,0:T(8,128)(2,1)S(1)} %get-tuple-element.46.refs_8_), channel_id=1, source_target_pairs={{0,2},{1,3},{2,0},{3,1},{4,6},{5,7},{6,4},{7,5},{8,10},{9,11},{10,... | collective-permute-start | bytes 638984 | tf_op jit(solution)/shard_map/ppermute | solution.py:385
  30.0 11.2 %collective-permute-start.9 = (bf16[13,32,256]{2,1,0:T(8,128)(2,1)S(1)}, bf16[13,32,256]{2,1,0:T(8,128)(2,1)S(1)}, u32[]{:S(2)}, u32[]{:S(2)}) collective-permute-start(bf16[13,32,256]{2,1,0:T(8,128)(2,1)S(1)} %get-tuple-element.50), channel_id=1, source_target_pairs={{0,3},{1,2},{2,1},{3,0},{4,7},{5,6},{6,5},{7,4},{8,11},{9,10},{10,... | collective-permute-start | bytes 638984 | tf_op jit(solution)/shard_map/ppermute | solution.py:385
  38.5 8.2 %collective-permute-start.11 = (bf16[13,32,256]{2,1,0:T(8,128)(2,1)S(1)}, bf16[13,32,256]{2,1,0:T(8,128)(2,1)S(1)}, u32[]{:S(2)}, u32[]{:S(2)}) collective-permute-start(bf16[13,32,256]{2,1,0:T(8,128)(2,1)S(1)} %get-tuple-element.53), channel_id=1, source_target_pairs={{0,2},{1,3},{2,0},{3,1},{4,6},{5,7},{6,4},{7,5},{8,10},{9,11},{10,... | collective-permute-start | bytes 638984 | tf_op jit(solution)/shard_map/ppermute | solution.py:385
  40.1 10.7 %collective-permute-start.12 = (bf16[13,32,256]{2,1,0:T(8,128)(2,1)S(1)}, bf16[13,32,256]{2,1,0:T(8,128)(2,1)S(1)}, u32[]{:S(2)}, u32[]{:S(2)}) collective-permute-start(bf16[13,32,256]{2,1,0:T(8,128)(2,1)S(1)} %get-tuple-element.54), channel_id=1, source_target_pairs={{0,3},{1,2},{2,1},{3,0},{4,7},{5,6},{6,5},{7,4},{8,11},{9,10},{10,... | collective-permute-start | bytes 638984 | tf_op jit(solution)/shard_map/ppermute | solution.py:385
  40.6 3.8 %copy-start.3 = (bf16[13,32,256]{2,1,0:T(8,128)(2,1)}, bf16[13,32,256]{2,1,0:T(8,128)(2,1)S(1)}, u32[]{:S(2)}) copy-start(bf16[13,32,256]{2,1,0:T(8,128)(2,1)S(1)} %collective-permute-done.8.refs_6_.refs_0_.refs_2_) | copy-start | bytes 638980
  41.3 3.1 %copy-start.5 = (bf16[13,32,256]{2,1,0:T(8,128)(2,1)}, bf16[13,32,256]{2,1,0:T(8,128)(2,1)S(1)}, u32[]{:S(2)}) copy-start(bf16[13,32,256]{2,1,0:T(8,128)(2,1)S(1)} %collective-permute-done.9.refs_7_.refs_1_.refs_3_) | copy-start | bytes 638980
  44.4 0.9 %copy-start.11 = (f32[13,64,256]{2,1,0:T(8,128)}, f32[13,64,256]{2,1,0:T(8,128)S(1)}, u32[]{:S(2)}) copy-start(f32[13,64,256]{2,1,0:T(8,128)S(1)} %get-tuple-element.51.refs_0_) | copy-start | bytes 2555908
  45.3 6.7 %copy-start.4 = (bf16[13,32,256]{2,1,0:T(8,128)(2,1)S(1)}, bf16[13,32,256]{2,1,0:T(8,128)(2,1)}, u32[]{:S(2)}) copy-start(bf16[13,32,256]{2,1,0:T(8,128)(2,1)} %copy-done.3) | copy-start | bytes 638980
  45.3 6.7 %copy-start.6 = (bf16[13,32,256]{2,1,0:T(8,128)(2,1)S(1)}, bf16[13,32,256]{2,1,0:T(8,128)(2,1)}, u32[]{:S(2)}) copy-start(bf16[13,32,256]{2,1,0:T(8,128)(2,1)} %copy-done.5) | copy-start | bytes 638980
  45.3 6.7 %copy-start.12 = (f32[13,64,256]{2,1,0:T(8,128)S(1)}, f32[13,64,256]{2,1,0:T(8,128)}, u32[]{:S(2)}) copy-start(f32[13,64,256]{2,1,0:T(8,128)} %copy-done.11) | copy-start | bytes 2555908
  45.3 6.7 %collective-permute-start.10 = (bf16[13,64,256]{2,1,0:T(8,128)(2,1)S(1)}, bf16[13,64,256]{2,1,0:T(8,128)(2,1)S(1)}, u32[]{:S(2)}, u32[]{:S(2)}) collective-permute-start(bf16[13,64,256]{2,1,0:T(8,128)(2,1)S(1)} %get-tuple-element.52), channel_id=1, source_target_pairs={{0,1},{1,0},{2,3},{3,2},{4,5},{5,4},{6,7},{7,6},{8,9},{9,8},{10,11... | collective-permute-start | bytes 1277960 | tf_op jit(solution)/shard_map/ppermute | solution.py:385
  46.7 4.1 %copy-start.7 = (bf16[13,32,256]{2,1,0:T(8,128)(2,1)}, bf16[13,32,256]{2,1,0:T(8,128)(2,1)S(1)}, u32[]{:S(2)}) copy-start(bf16[13,32,256]{2,1,0:T(8,128)(2,1)S(1)} %collective-permute-done.11.refs_2_.refs_4_) | copy-start | bytes 638980
  50.8 0.7 %copy-start.9 = (bf16[13,32,256]{2,1,0:T(8,128)(2,1)}, bf16[13,32,256]{2,1,0:T(8,128)(2,1)S(1)}, u32[]{:S(2)}) copy-start(bf16[13,32,256]{2,1,0:T(8,128)(2,1)S(1)} %collective-permute-done.12.refs_3_.refs_5_) | copy-start | bytes 638980
  52.1 0.9 %copy-start.8 = (bf16[13,32,256]{2,1,0:T(8,128)(2,1)S(1)}, bf16[13,32,256]{2,1,0:T(8,128)(2,1)}, u32[]{:S(2)}) copy-start(bf16[13,32,256]{2,1,0:T(8,128)(2,1)} %copy-done.7) | copy-start | bytes 638980
  53.0 0.9 %copy-start.10 = (bf16[13,32,256]{2,1,0:T(8,128)(2,1)S(1)}, bf16[13,32,256]{2,1,0:T(8,128)(2,1)}, u32[]{:S(2)}) copy-start(bf16[13,32,256]{2,1,0:T(8,128)(2,1)} %copy-done.9) | copy-start | bytes 638980
  53.9 0.7 %copy-start.14 = (f32[8,128]{1,0:T(8,128)S(1)}, f32[8,128]{1,0:T(8,128)}, u32[]{:S(2)}) copy-start(f32[8,128]{1,0:T(8,128)} %arrived.1.refs_6_) | copy-start | bytes 12292

commit v4 on v3

--- a/solution.py
+++ b/solution.py
@@ -105,47 +105,53 @@
     return total
 
 
+GROUPS = ((0, 1), (1, 4), (4, 5), (5, 8), (8, 10), (10, 13))
+
+
 def pack_kernel(n, two, me_ref, rho, vel, temp, stress, heat, *refs):
     count = n if two else 0
-    outs, (strip, given, arrived), refs = refs[: count + 3], refs[count + 3 : count + 6], refs[count + 6 :]
-    held, left_at = refs[: count + 3], refs[-1]
-    firsts, (tall, left, right) = held[:count], held[count:]
+    total = count + 3
+    outs, (strip, given, arrived), refs = refs[:total], refs[total : total + 3], refs[total + 3 :]
+    held, left_at = refs[:total], refs[-1]
+    tall, left, right = held[count:]
     rows, cols = rho.shape
     slab = cols // n
     wide = slab // 2 + 2 * HALO
     me = me_ref[0]
+    parts = (rho, vel, temp, stress.at[0:3], stress.at[3:5], heat)
     copies = []
-    for f in range(MOMENTS):
-        if f == 0:
-            src = rho
-        elif f < 4:
-            src = vel.at[f - 1]
-        elif f == 4:
-            src = temp
-        elif f < 10:
-            src = stress.at[f - 5]
-        else:
-            src = heat.at[f - 10]
-        copies.append(pltpu.make_async_copy(src, given.at[f], arrived.at[f]))
-        copies[f].start()
+    for k, (first, end) in enumerate(GROUPS):
+        dst = given.at[first] if k in (0, 2) else given.at[first:end]
+        copies.append(pltpu.make_async_copy(parts[k], dst, arrived.at[k]))
+        copies[k].start()
     strip[0:HALO, :] = jnp.zeros((HALO, rows), jnp.float32)
     strip[HALO + cols :, :] = jnp.zeros((HALO, rows), jnp.float32)
     leaving = []
-    for f in range(MOMENTS):
-        copies[f].wait()
-        strip[HALO : HALO + cols, :] = code(f, given[f]).T
-        for s in range(count):
-            to = jnp.bitwise_xor(me, s)
-            start = to * slab + jnp.where(to < n // 2, slab // 2, 0)
-            start = pl.multiple_of(start, 16)
-            firsts[s][f] = strip[pl.ds(start, wide), :].astype(jnp.bfloat16)
-        tall[f] = strip[...].astype(jnp.bfloat16)
-        left[f] = tall[f, 0 : 2 * HALO, :]
-        right[f] = tall[f, cols : cols + 2 * HALO, :]
-        for k, (mine, out) in enumerate(zip(held, outs)):
-            copy = pltpu.make_async_copy(mine.at[f], out.at[f], left_at.at[k, f])
-            copy.start()
-            leaving.append(copy)
+
+    def leave(k, span, at):
+        copy = pltpu.make_async_copy(held[k].at[span], outs[k].at[span], left_at.at[k, at])
+        copy.start()
+        leaving.append(copy)
+
+    done = 0
+    for k, (first, end) in enumerate(GROUPS):
+        copies[k].wait()
+        for f in range(first, end):
+            strip[HALO : HALO + cols, :] = code(f, given[f]).T
+            for s in range(count):
+                to = jnp.bitwise_xor(me, s)
+                start = to * slab + jnp.where(to < n // 2, slab // 2, 0)
+                start = pl.multiple_of(start, 16)
+                held[s][f] = strip[pl.ds(start, wide), :].astype(jnp.bfloat16)
+            tall[f] = strip[...].astype(jnp.bfloat16)
+            left[f] = tall[f, 0 : 2 * HALO, :]
+            right[f] = tall[f, cols : cols + 2 * HALO, :]
+        if k in (1, 3, 5):
+            for s in range(count + 1):
+                leave(s, slice(done, end), k // 2)
+            done = end
+    for s in (count + 1, count + 2):
+        leave(s, slice(0, MOMENTS), 0)
     for copy in leaving:
         copy.wait()
 
@@ -404,8 +410,8 @@
     def message(width, kind=half):
         return jax.ShapeDtypeStruct((MOMENTS, width, rows), kind)
 
-    count = n if two else 0
-    shapes = [message(wide)] * count + [message(cols + 2 * HALO)] + [message(2 * HALO)] * 2
+    shapes = [message(wide)] * n if two else []
+    shapes += [message(cols + 2 * HALO)] + [message(2 * HALO)] * 2
     *firsts, tall, left, right = pl.pallas_call(
         functools.partial(pack_kernel, n, two),
         out_shape=shapes,
@@ -414,10 +420,10 @@
         scratch_shapes=[
             pltpu.VMEM((cols + 2 * HALO, rows), jnp.float32),
             pltpu.VMEM((MOMENTS, rows, cols), jnp.float32),
-            pltpu.SemaphoreType.DMA((MOMENTS,)),
+            pltpu.SemaphoreType.DMA((len(GROUPS),)),
         ]
         + [pltpu.VMEM(x.shape, x.dtype) for x in shapes]
-        + [pltpu.SemaphoreType.DMA((len(shapes), MOMENTS))],
+        + [pltpu.SemaphoreType.DMA((len(shapes), 3))],
         compiler_params=params(56),
         cost_estimate=cost(2),
         name="pack",
@@ -516,6 +522,7 @@
         out_shape=jax.ShapeDtypeStruct((8, 128), jnp.float32),
         in_specs=[ANY] * len(back),
         out_specs=VMEM,
+        compiler_params=params(1),
         cost_estimate=cost(6),
         name="arrived",
     )(*back)

time: 57 us -> 52.3 us (0.918)
  local copies, waits for them, and re-layouts: 4.15 us -> 0.02 us
  Pallas kernels: 29.1 us -> 27.7 us
  waiting for transfers between devices: 9.15 us -> 10.1 us
    unnamed x30 -> x8, local copies, waits for them, and re-layouts: 4.15 us -> 0.02 us
    ppermute x11, waiting for transfers between devices: 8.26 us -> 9.18 us  [to_partner(): lax.ppermute(array, 'gy', [(i, i ^ s) for i in range(n)])]
    pallas_call x1, Pallas kernels: 4.54 us -> 3.75 us  [on_device(): pl.pallas_call(functools.partial(pack_kernel, n, two), out_shape=shapes,...]
    pallas_call x1, Pallas kernels: 0.59 us -> 0.01 us  [on_device(): pl.pallas_call(arrived_kernel, out_shape=jax.ShapeDtypeStruct((8, 128), j...]
  transfers between devices with their start and end apart: 13 -> 13, of which waited for: 7 -> 7; matrix products, arithmetic and copies ran while one was open for 0% -> 0% of each run, Pallas kernels for 40% -> 42%
where the time goes in v4:
time: 52.3 us; the launch traced here: 52.2 us
  Pallas kernels  27.7 us (53%)
  starting transfers between devices  14.1 us (27%)
  waiting for transfers between devices  10.1 us (19%)
    pallas_call x2, Pallas kernels, sections(): pl.pallas_call(functools.partial(section_kernel, n, two, second, far, nea...  12.2 us
    ppermute x11, starting transfers between devices, to_partner(): lax.ppermute(array, 'gy', [(i, i ^ s) for i in range(n)])  9.22 us
    ppermute x11, waiting for transfers between devices, to_partner(): lax.ppermute(array, 'gy', [(i, i ^ s) for i in range(n)])  9.18 us
    pallas_call x2, Pallas kernels, grid_of(): pl.pallas_call(functools.partial(grid_kernel, n, rows, slots), out_shape=...  6.42 us
    pallas_call x1, Pallas kernels, on_device(): pl.pallas_call(functools.partial(pack_kernel, n, two), out_shape=shapes,...  3.75 us
    ppermute x1, starting transfers between devices, on_device(): after = lax.ppermute(left, 'gx', [(j, i) for i, j in up])  3.11 us
    pallas_call x1, Pallas kernels, finished(): pl.pallas_call(functools.partial(finish_kernel, n, near, len(states) // 3...  3.06 us
    pallas_call x1, Pallas kernels, on_device(): pl.pallas_call(functools.partial(unpack_kernel, n, far, near, 2 if two el...  2.02 us
  transfers between devices with their start and end apart: 13, of which 7 were waited for; matrix products, arithmetic and copies ran while one was open for 0% of the time, Pallas kernels for 42%

profile of v4, /device:TPU:0, one launch (start us, length us, event | category | flops | bytes accessed | tf_op | source)
XLA Modules:
  0.0 52.2 jit_solution(16756594604217400786)
XLA Ops:
  0.0 3.8 %pack.1 = (bf16[13,48,256]{2,1,0:T(8,128)(2,1)}, bf16[13,48,256]{2,1,0:T(8,128)(2,1)}, bf16[13,48,256]{2,1,0:T(8,128)(2,1)}, bf16[13,48,256]{2,1,0:T(8,128)(2,1)...) custom-call(s32[1]{0:T(128)} %bitcast.me_ref, f32[256,256]{1,0:T(8,128)} %rho.1, ...), custom_call_target="tpu_custom_call" | custom-call | flops 2000000000 | bytes 6000000 | tf_op jit(solution)/shard_map/pack/pallas_call | solution.py:415
  3.8 0.5 %collective-permute-start = (bf16[13,48,256]{2,1,0:T(8,128)(2,1)}, bf16[13,48,256]{2,1,0:T(8,128)(2,1)S(1)}, u32[]{:S(2)}, u32[]{:S(2)}) collective-permute-start(bf16[13,48,256]{2,1,0:T(8,128)(2,1)} %get-tuple-element.31), channel_id=1, source_target_pairs={{0,1},{1,0},{2,3},{3,2},{4,5},{5,4},{6,7},{7,6},{8,9},{9,8},{10,11... | collective-permute-start | bytes 958472 | tf_op jit(solution)/shard_map/ppermute | solution.py:391
  4.3 2.6 %collective-permute-start.1 = (bf16[13,48,256]{2,1,0:T(8,128)(2,1)}, bf16[13,48,256]{2,1,0:T(8,128)(2,1)S(1)}, u32[]{:S(2)}, u32[]{:S(2)}) collective-permute-start(bf16[13,48,256]{2,1,0:T(8,128)(2,1)} %get-tuple-element.32), channel_id=1, source_target_pairs={{0,2},{1,3},{2,0},{3,1},{4,6},{5,7},{6,4},{7,5},{8,10},{9,11},{10,... | collective-permute-start | bytes 958472 | tf_op jit(solution)/shard_map/ppermute | solution.py:391
  6.9 0.1 collective-permute-start.2
  6.9 3.2 %grid.3.grid_far.after = bf16[1024,512]{1,0:T(8,128)(2,1)S(1)} custom-call(s32[1]{0:T(128)} %bitcast.me_ref), custom_call_target="tpu_custom_call" | custom-call | flops 3000000000 | bytes 9000000 | tf_op jit(solution)/shard_map/grid/pallas_call | solution.py:437
  10.2 1.8 %collective-permute-start.3 = (bf16[13,16,256]{2,1,0:T(8,128)(2,1)S(1)}, bf16[13,16,256]{2,1,0:T(8,128)(2,1)S(1)}, u32[]{:S(2)}, u32[]{:S(2)}) collective-permute-start(bf16[13,16,256]{2,1,0:T(8,128)(2,1)S(1)} %get-tuple-element.40), channel_id=1, source_target_pairs={{0,4},{4,8},{8,12},{12,16},{16,20},{20,24},{24,28},{28,0},{1,5},{5... | collective-permute-start | bytes 319496 | tf_op jit(solution)/shard_map/ppermute | solution.py:461
  12.0 3.1 %collective-permute-start.4 = (bf16[13,16,256]{2,1,0:T(8,128)(2,1)S(1)}, bf16[13,16,256]{2,1,0:T(8,128)(2,1)S(1)}, u32[]{:S(2)}, u32[]{:S(2)}) collective-permute-start(bf16[13,16,256]{2,1,0:T(8,128)(2,1)S(1)} %get-tuple-element.41), channel_id=1, source_target_pairs={{4,0},{8,4},{12,8},{16,12},{20,16},{24,20},{28,24},{0,28},{5,1},{9... | collective-permute-start | bytes 319496 | tf_op jit(solution)/shard_map/ppermute | solution.py:462
  15.1 3.2 %grid.2.grid_near = bf16[1024,512]{1,0:T(8,128)(2,1)S(1)} custom-call(s32[1]{0:T(128)} %bitcast.me_ref), custom_call_target="tpu_custom_call" | custom-call | flops 3000000000 | bytes 9000000 | tf_op jit(solution)/shard_map/grid/pallas_call | solution.py:437
  18.3 0.3 collective-permute-done.3.before
  18.6 0.6 %collective-permute-done.4.after = bf16[13,16,256]{2,1,0:T(8,128)(2,1)S(1)} collective-permute-done((bf16[13,16,256]{2,1,0:T(8,128)(2,1)S(1)}, bf16[13,16,256]{2,1,0:T(8,128)(2,1)S(1)}, u32[]{:S(2)}, u32[]{:S(2)}) %collective-permute-start.4) | collective-permute-done | bytes 106528 | tf_op jit(solution)/shard_map/ppermute | solution.py:462
  19.2 0.3 rest.1
  19.5 0.1 collective-permute-start.5
  19.6 1.6 %collective-permute-start.6 = (bf16[13,32,256]{2,1,0:T(8,128)(2,1)S(1)}, bf16[13,32,256]{2,1,0:T(8,128)(2,1)S(1)}, u32[]{:S(2)}, u32[]{:S(2)}) collective-permute-start(bf16[13,32,256]{2,1,0:T(8,128)(2,1)S(1)} %get-tuple-element.44), channel_id=1, source_target_pairs={{0,2},{1,3},{2,0},{3,1},{4,6},{5,7},{6,4},{7,5},{8,10},{9,11},{10,... | collective-permute-start | bytes 638984 | tf_op jit(solution)/shard_map/ppermute | solution.py:391
  21.2 0.0 collective-permute-done.refs_1_
  21.2 0.3 collective-permute-start.7
  21.4 0.0 collective-permute-done.1.refs_2_
  21.4 0.3 collective-permute-done.2.refs_3_
  21.8 5.8 %sections.2 = (bf16[13,32,256]{2,1,0:T(8,128)(2,1)S(1)}, bf16[13,32,256]{2,1,0:T(8,128)(2,1)S(1)}, f32[13,48,1024]{2,1,0:T(8,128)S(1)}, f32[13,32,1024]{2,1,0:T(8,128)S(1)}, bf16[416,1024]{1,0:T(8,128)(2,1)S(1)}) custom-call(s32[1]{0:T(128)} %bitcast.me_ref, bf16[1024,512]{1,0:T(8,128)(2,1)S(1)} %grid.3.grid_far.after, bf16[1024,512]{1,0:T(8,128)(2,1)S(1)} %grid.2.grid_near, ...), custom_call_target="tpu_custom_call" | custom-call | flops 6000000000 | bytes 18000000 | tf_op jit(solution)/shard_map/sections/pallas_call | solution.py:481
  27.6 1.6 %collective-permute-start.8 = (bf16[13,32,256]{2,1,0:T(8,128)(2,1)S(1)}, bf16[13,32,256]{2,1,0:T(8,128)(2,1)S(1)}, u32[]{:S(2)}, u32[]{:S(2)}) collective-permute-start(bf16[13,32,256]{2,1,0:T(8,128)(2,1)S(1)} %get-tuple-element.46.refs_8_), channel_id=1, source_target_pairs={{0,2},{1,3},{2,0},{3,1},{4,6},{5,7},{6,4},{7,5},{8,10},{9,11},{10,... | collective-permute-start | bytes 638984 | tf_op jit(solution)/shard_map/ppermute | solution.py:391
  29.2 0.0 collective-permute-start.9
  29.3 2.1 %collective-permute-done.7.refs_7_ = bf16[13,32,256]{2,1,0:T(8,128)(2,1)S(1)} collective-permute-done((bf16[13,32,256]{2,1,0:T(8,128)(2,1)S(1)}, bf16[13,32,256]{2,1,0:T(8,128)(2,1)S(1)}, u32[]{:S(2)}, u32[]{:S(2)}) %collective-permute-start.7) | collective-permute-done | bytes 213024 | tf_op jit(solution)/shard_map/ppermute | solution.py:391
  31.4 6.4 %sections.3 = (bf16[13,32,256]{2,1,0:T(8,128)(2,1)S(1)}, bf16[13,32,256]{2,1,0:T(8,128)(2,1)S(1)}, f32[13,48,1024]{2,1,0:T(8,128)S(1)}, f32[13,32,1024]{2,1,0:T(8,128)S(1)}, bf16[416,1024]{1,0:T(8,128)(2,1)S(1)}) custom-call(s32[1]{0:T(128)} %bitcast.me_ref, bf16[1024,512]{1,0:T(8,128)(2,1)S(1)} %grid.3.grid_far.after, bf16[1024,512]{1,0:T(8,128)(2,1)S(1)} %grid.2.grid_near, ...), custom_call_target="tpu_custom_call" | custom-call | flops 6000000000 | bytes 18000000 | tf_op jit(solution)/shard_map/sections/pallas_call | solution.py:481
  37.7 1.6 %collective-permute-start.11 = (bf16[13,32,256]{2,1,0:T(8,128)(2,1)S(1)}, bf16[13,32,256]{2,1,0:T(8,128)(2,1)S(1)}, u32[]{:S(2)}, u32[]{:S(2)}) collective-permute-start(bf16[13,32,256]{2,1,0:T(8,128)(2,1)S(1)} %get-tuple-element.53), channel_id=1, source_target_pairs={{0,2},{1,3},{2,0},{3,1},{4,6},{5,7},{6,4},{7,5},{8,10},{9,11},{10,... | collective-permute-start | bytes 638984 | tf_op jit(solution)/shard_map/ppermute | solution.py:391
  39.3 0.5 %collective-permute-start.12 = (bf16[13,32,256]{2,1,0:T(8,128)(2,1)S(1)}, bf16[13,32,256]{2,1,0:T(8,128)(2,1)S(1)}, u32[]{:S(2)}, u32[]{:S(2)}) collective-permute-start(bf16[13,32,256]{2,1,0:T(8,128)(2,1)S(1)} %get-tuple-element.54), channel_id=1, source_target_pairs={{0,3},{1,2},{2,1},{3,0},{4,7},{5,6},{6,5},{7,4},{8,11},{9,10},{10,... | collective-permute-start | bytes 638984 | tf_op jit(solution)/shard_map/ppermute | solution.py:391
  39.9 0.0 collective-permute-done.8.refs_6_.refs_0_.refs_2_
  39.9 0.6 %collective-permute-done.9.refs_7_.refs_1_.refs_3_ = bf16[13,32,256]{2,1,0:T(8,128)(2,1)S(1)} collective-permute-done((bf16[13,32,256]{2,1,0:T(8,128)(2,1)S(1)}, bf16[13,32,256]{2,1,0:T(8,128)(2,1)S(1)}, u32[]{:S(2)}, u32[]{:S(2)}) %collective-permute-start.9) | collective-permute-done | bytes 213024 | tf_op jit(solution)/shard_map/ppermute | solution.py:391
  40.5 3.1 %finish.1 = (f32[13,64,256]{2,1,0:T(8,128)S(1)}, bf16[13,64,256]{2,1,0:T(8,128)(2,1)S(1)}) custom-call(s32[1]{0:T(128)} %bitcast.me_ref, bf16[1024,512]{1,0:T(8,128)(2,1)S(1)} %grid.2.grid_near, f32[13,48,1024]{2,1,0:T(8,128)S(1)} %get-tuple-element.34.refs_0_, f32[13,32,1024]{2,1,0:T(8,128)S(1)} %get-tuple-element.35.refs_1_, ...), custom_call_target="tpu_custom_call" | custom-call | flops 4000000000 | bytes 12000000 | tf_op jit(solution)/shard_map/finish/pallas_call | solution.py:498
  43.5 0.3 collective-permute-start.10
  43.9 2.0 %collective-permute-done.11.refs_2_.refs_4_ = bf16[13,32,256]{2,1,0:T(8,128)(2,1)S(1)} collective-permute-done((bf16[13,32,256]{2,1,0:T(8,128)(2,1)S(1)}, bf16[13,32,256]{2,1,0:T(8,128)(2,1)S(1)}, u32[]{:S(2)}, u32[]{:S(2)}) %collective-permute-start.11) | collective-permute-done | bytes 213024 | tf_op jit(solution)/shard_map/ppermute | solution.py:391
  45.9 4.1 %collective-permute-done.12.refs_3_.refs_5_ = bf16[13,32,256]{2,1,0:T(8,128)(2,1)S(1)} collective-permute-done((bf16[13,32,256]{2,1,0:T(8,128)(2,1)S(1)}, bf16[13,32,256]{2,1,0:T(8,128)(2,1)S(1)}, u32[]{:S(2)}, u32[]{:S(2)}) %collective-permute-start.12) | collective-permute-done | bytes 213024 | tf_op jit(solution)/shard_map/ppermute | solution.py:391
  50.0 0.0 collective-permute-done.10.refs_1_
  50.0 2.0 %unpack.1 = f32[13,256,256]{2,1,0:T(8,128)} custom-call(s32[1]{0:T(128)} %bitcast.me_ref, f32[13,64,256]{2,1,0:T(8,128)S(1)} %get-tuple-element.51.refs_0_, bf16[13,64,256]{2,1,0:T(8,128)(2,1)S(1)} %collective-permute-done.10.refs_1_, bf16[13,32,256]{2,1,0:T(8,128)(2,1)S(1)} %collective-permute-done.8.refs_6_.refs_0_.refs_2_, ...), custom_call_target="tpu_custom_call" | custom-call | flops 3000000000 | bytes 9000000 | tf_op jit(solution)/shard_map/unpack/pallas_call | solution.py:529
  (12 shorter events, 0.0 us)
Async XLA Ops:
  3.8 17.4 %collective-permute-start = (bf16[13,48,256]{2,1,0:T(8,128)(2,1)}, bf16[13,48,256]{2,1,0:T(8,128)(2,1)S(1)}, u32[]{:S(2)}, u32[]{:S(2)}) collective-permute-start(bf16[13,48,256]{2,1,0:T(8,128)(2,1)} %get-tuple-element.31), channel_id=1, source_target_pairs={{0,1},{1,0},{2,3},{3,2},{4,5},{5,4},{6,7},{7,6},{8,9},{9,8},{10,11... | collective-permute-start | bytes 958472 | tf_op jit(solution)/shard_map/ppermute | solution.py:391
  4.3 17.2 %collective-permute-start.1 = (bf16[13,48,256]{2,1,0:T(8,128)(2,1)}, bf16[13,48,256]{2,1,0:T(8,128)(2,1)S(1)}, u32[]{:S(2)}, u32[]{:S(2)}) collective-permute-start(bf16[13,48,256]{2,1,0:T(8,128)(2,1)} %get-tuple-element.32), channel_id=1, source_target_pairs={{0,2},{1,3},{2,0},{3,1},{4,6},{5,7},{6,4},{7,5},{8,10},{9,11},{10,... | collective-permute-start | bytes 958472 | tf_op jit(solution)/shard_map/ppermute | solution.py:391
  6.9 3.3 %copy-start.1 = (bf16[13,16,256]{2,1,0:T(8,128)(2,1)S(1)}, bf16[13,16,256]{2,1,0:T(8,128)(2,1)}, u32[]{:S(2)}) copy-start(bf16[13,16,256]{2,1,0:T(8,128)(2,1)} %get-tuple-element.38.left) | copy-start | bytes 319492
  6.9 3.3 %copy-start.2 = (bf16[13,16,256]{2,1,0:T(8,128)(2,1)S(1)}, bf16[13,16,256]{2,1,0:T(8,128)(2,1)}, u32[]{:S(2)}) copy-start(bf16[13,16,256]{2,1,0:T(8,128)(2,1)} %get-tuple-element.39.right) | copy-start | bytes 319492
  6.9 14.9 %collective-permute-start.2 = (bf16[13,48,256]{2,1,0:T(8,128)(2,1)}, bf16[13,48,256]{2,1,0:T(8,128)(2,1)S(1)}, u32[]{:S(2)}, u32[]{:S(2)}) collective-permute-start(bf16[13,48,256]{2,1,0:T(8,128)(2,1)} %get-tuple-element.33), channel_id=1, source_target_pairs={{0,3},{1,2},{2,1},{3,0},{4,7},{5,6},{6,5},{7,4},{8,11},{9,10},{10,... | collective-permute-start | bytes 958472 | tf_op jit(solution)/shard_map/ppermute | solution.py:391
  10.2 8.4 %collective-permute-start.3 = (bf16[13,16,256]{2,1,0:T(8,128)(2,1)S(1)}, bf16[13,16,256]{2,1,0:T(8,128)(2,1)S(1)}, u32[]{:S(2)}, u32[]{:S(2)}) collective-permute-start(bf16[13,16,256]{2,1,0:T(8,128)(2,1)S(1)} %get-tuple-element.40), channel_id=1, source_target_pairs={{0,4},{4,8},{8,12},{12,16},{16,20},{20,24},{24,28},{28,0},{1,5},{5... | collective-permute-start | bytes 319496 | tf_op jit(solution)/shard_map/ppermute | solution.py:461
  12.0 7.2 %copy-start = (bf16[13,272,256]{2,1,0:T(8,128)(2,1)S(1)}, bf16[13,272,256]{2,1,0:T(8,128)(2,1)}, u32[]{:S(2)}) copy-start(bf16[13,272,256]{2,1,0:T(8,128)(2,1)} %get-tuple-element.37.tall) | copy-start | bytes 5431300
  12.0 7.2 %collective-permute-start.4 = (bf16[13,16,256]{2,1,0:T(8,128)(2,1)S(1)}, bf16[13,16,256]{2,1,0:T(8,128)(2,1)S(1)}, u32[]{:S(2)}, u32[]{:S(2)}) collective-permute-start(bf16[13,16,256]{2,1,0:T(8,128)(2,1)S(1)} %get-tuple-element.41), channel_id=1, source_target_pairs={{4,0},{8,4},{12,8},{16,12},{20,16},{24,20},{28,24},{0,28},{5,1},{9... | collective-permute-start | bytes 319496 | tf_op jit(solution)/shard_map/ppermute | solution.py:462
  18.3 3.5 %copy-start.3 = (bf16[13,48,256]{2,1,0:T(8,128)(2,1)S(1)}, bf16[13,48,256]{2,1,0:T(8,128)(2,1)}, u32[]{:S(2)}) copy-start(bf16[13,48,256]{2,1,0:T(8,128)(2,1)} %get-tuple-element.30.refs_0_) | copy-start | bytes 958468
  19.5 9.8 %collective-permute-start.5 = (bf16[13,32,256]{2,1,0:T(8,128)(2,1)S(1)}, bf16[13,32,256]{2,1,0:T(8,128)(2,1)S(1)}, u32[]{:S(2)}, u32[]{:S(2)}) collective-permute-start(bf16[13,32,256]{2,1,0:T(8,128)(2,1)S(1)} %get-tuple-element.43), channel_id=1, source_target_pairs={{0,1},{1,0},{2,3},{3,2},{4,5},{5,4},{6,7},{7,6},{8,9},{9,8},{10,11... | collective-permute-start | bytes 638984 | tf_op jit(solution)/shard_map/ppermute | solution.py:391
  19.6 9.7 %collective-permute-start.6 = (bf16[13,32,256]{2,1,0:T(8,128)(2,1)S(1)}, bf16[13,32,256]{2,1,0:T(8,128)(2,1)S(1)}, u32[]{:S(2)}, u32[]{:S(2)}) collective-permute-start(bf16[13,32,256]{2,1,0:T(8,128)(2,1)S(1)} %get-tuple-element.44), channel_id=1, source_target_pairs={{0,2},{1,3},{2,0},{3,1},{4,6},{5,7},{6,4},{7,5},{8,10},{9,11},{10,... | collective-permute-start | bytes 638984 | tf_op jit(solution)/shard_map/ppermute | solution.py:391
  21.2 10.2 %collective-permute-start.7 = (bf16[13,32,256]{2,1,0:T(8,128)(2,1)S(1)}, bf16[13,32,256]{2,1,0:T(8,128)(2,1)S(1)}, u32[]{:S(2)}, u32[]{:S(2)}) collective-permute-start(bf16[13,32,256]{2,1,0:T(8,128)(2,1)S(1)} %get-tuple-element.45), channel_id=1, source_target_pairs={{0,3},{1,2},{2,1},{3,0},{4,7},{5,6},{6,5},{7,4},{8,11},{9,10},{10,... | collective-permute-start | bytes 638984 | tf_op jit(solution)/shard_map/ppermute | solution.py:391
  27.6 12.2 %collective-permute-start.8 = (bf16[13,32,256]{2,1,0:T(8,128)(2,1)S(1)}, bf16[13,32,256]{2,1,0:T(8,128)(2,1)S(1)}, u32[]{:S(2)}, u32[]{:S(2)}) collective-permute-start(bf16[13,32,256]{2,1,0:T(8,128)(2,1)S(1)} %get-tuple-element.46.refs_8_), channel_id=1, source_target_pairs={{0,2},{1,3},{2,0},{3,1},{4,6},{5,7},{6,4},{7,5},{8,10},{9,11},{10,... | collective-permute-start | bytes 638984 | tf_op jit(solution)/shard_map/ppermute | solution.py:391
  29.2 11.2 %collective-permute-start.9 = (bf16[13,32,256]{2,1,0:T(8,128)(2,1)S(1)}, bf16[13,32,256]{2,1,0:T(8,128)(2,1)S(1)}, u32[]{:S(2)}, u32[]{:S(2)}) collective-permute-start(bf16[13,32,256]{2,1,0:T(8,128)(2,1)S(1)} %get-tuple-element.50), channel_id=1, source_target_pairs={{0,3},{1,2},{2,1},{3,0},{4,7},{5,6},{6,5},{7,4},{8,11},{9,10},{10,... | collective-permute-start | bytes 638984 | tf_op jit(solution)/shard_map/ppermute | solution.py:391
  37.7 8.2 %collective-permute-start.11 = (bf16[13,32,256]{2,1,0:T(8,128)(2,1)S(1)}, bf16[13,32,256]{2,1,0:T(8,128)(2,1)S(1)}, u32[]{:S(2)}, u32[]{:S(2)}) collective-permute-start(bf16[13,32,256]{2,1,0:T(8,128)(2,1)S(1)} %get-tuple-element.53), channel_id=1, source_target_pairs={{0,2},{1,3},{2,0},{3,1},{4,6},{5,7},{6,4},{7,5},{8,10},{9,11},{10,... | collective-permute-start | bytes 638984 | tf_op jit(solution)/shard_map/ppermute | solution.py:391
  39.3 10.7 %collective-permute-start.12 = (bf16[13,32,256]{2,1,0:T(8,128)(2,1)S(1)}, bf16[13,32,256]{2,1,0:T(8,128)(2,1)S(1)}, u32[]{:S(2)}, u32[]{:S(2)}) collective-permute-start(bf16[13,32,256]{2,1,0:T(8,128)(2,1)S(1)} %get-tuple-element.54), channel_id=1, source_target_pairs={{0,3},{1,2},{2,1},{3,0},{4,7},{5,6},{6,5},{7,4},{8,11},{9,10},{10,... | collective-permute-start | bytes 638984 | tf_op jit(solution)/shard_map/ppermute | solution.py:391
  43.5 6.4 %collective-permute-start.10 = (bf16[13,64,256]{2,1,0:T(8,128)(2,1)S(1)}, bf16[13,64,256]{2,1,0:T(8,128)(2,1)S(1)}, u32[]{:S(2)}, u32[]{:S(2)}) collective-permute-start(bf16[13,64,256]{2,1,0:T(8,128)(2,1)S(1)} %get-tuple-element.52), channel_id=1, source_target_pairs={{0,1},{1,0},{2,3},{3,2},{4,5},{5,4},{6,7},{7,6},{8,9},{9,8},{10,11... | collective-permute-start | bytes 1277960 | tf_op jit(solution)/shard_map/ppermute | solution.py:391

commit v5 on v4

--- a/solution.py
+++ b/solution.py
@@ -105,58 +105,62 @@
     return total
 
 
-GROUPS = ((0, 1), (1, 4), (4, 5), (5, 8), (8, 10), (10, 13))
-
-
-def pack_kernel(n, two, me_ref, rho, vel, temp, stress, heat, *refs):
-    count = n if two else 0
-    total = count + 3
-    outs, (strip, given, arrived), refs = refs[:total], refs[total : total + 3], refs[total + 3 :]
-    held, left_at = refs[:total], refs[-1]
-    tall, left, right = held[count:]
-    rows, cols = rho.shape
+def message_start(me, s, slab):
+    to = jnp.bitwise_xor(me, s)
+    return pl.multiple_of(to * slab + jnp.where(to % 2 == 0, slab // 2, 0), 16)
+
+
+def pack_kernel(n, moments, ranges, extra, me_ref, *refs):
+    inputs, refs = refs[:moments], refs[moments:]
+    total = len(ranges) + (3 if extra else 0)
+    outs, refs = refs[-2 * total - 4 : -total - 4], refs[-total - 4 :]
+    (strip, given, arrived), held, left_at = refs[:3], refs[3 : 3 + total], refs[-1]
+    rows, cols = given.shape[1:]
     slab = cols // n
-    wide = slab // 2 + 2 * HALO
     me = me_ref[0]
-    parts = (rho, vel, temp, stress.at[0:3], stress.at[3:5], heat)
-    copies = []
-    for k, (first, end) in enumerate(GROUPS):
-        dst = given.at[first] if k in (0, 2) else given.at[first:end]
-        copies.append(pltpu.make_async_copy(parts[k], dst, arrived.at[k]))
-        copies[k].start()
+    copies, end = [], 0
+    for k, src in enumerate(inputs):
+        first, end = end, end + (1 if len(src.shape) == 2 else src.shape[0])
+        dst = given.at[first] if len(src.shape) == 2 else given.at[first:end]
+        copies.append((first, end, pltpu.make_async_copy(src, dst, arrived.at[k])))
+        copies[k][2].start()
     strip[0:HALO, :] = jnp.zeros((HALO, rows), jnp.float32)
     strip[HALO + cols :, :] = jnp.zeros((HALO, rows), jnp.float32)
     leaving = []
 
-    def leave(k, span, at):
+    def leave(k, first, last, at):
+        span = pl.ds(first, last - first)
         copy = pltpu.make_async_copy(held[k].at[span], outs[k].at[span], left_at.at[k, at])
         copy.start()
         leaving.append(copy)
 
-    done = 0
-    for k, (first, end) in enumerate(GROUPS):
-        copies[k].wait()
+    for at, (first, end, copy) in enumerate(copies):
+        copy.wait()
         for f in range(first, end):
             strip[HALO : HALO + cols, :] = code(f, given[f]).T
-            for s in range(count):
-                to = jnp.bitwise_xor(me, s)
-                start = to * slab + jnp.where(to < n // 2, slab // 2, 0)
-                start = pl.multiple_of(start, 16)
-                held[s][f] = strip[pl.ds(start, wide), :].astype(jnp.bfloat16)
-            tall[f] = strip[...].astype(jnp.bfloat16)
-            left[f] = tall[f, 0 : 2 * HALO, :]
-            right[f] = tall[f, cols : cols + 2 * HALO, :]
-        if k in (1, 3, 5):
-            for s in range(count + 1):
-                leave(s, slice(done, end), k // 2)
-            done = end
-    for s in (count + 1, count + 2):
-        leave(s, slice(0, MOMENTS), 0)
+            for k, (s, low, high) in enumerate(ranges):
+                if low <= f < high:
+                    wide = held[k].shape[1]
+                    here = pl.ds(message_start(me, s, slab), wide)
+                    held[k][f - low] = strip[here, :].astype(jnp.bfloat16)
+            if extra:
+                tall, left, right = held[-3:]
+                tall[f] = strip[...].astype(jnp.bfloat16)
+                left[f] = tall[f, 0 : 2 * HALO, :]
+                right[f] = tall[f, cols : cols + 2 * HALO, :]
+        for k, (s, low, high) in enumerate(ranges):
+            if max(first, low) < min(end, high):
+                leave(k, max(first, low) - low, min(end, high) - low, at)
+        if extra and at % 2 == 0:
+            leave(total - 3, 0 if at == 0 else copies[at - 1][0], end, at)
+    if extra:
+        leave(total - 2, 0, MOMENTS, 0)
+        leave(total - 1, 0, MOMENTS, 0)
     for copy in leaving:
         copy.wait()
 
 
-def edge_kernel(left, right, after, left_out, right_out):
+def edge_kernel(left, right, tie, left_out, right_out):
     left_out[...] = left[...]
     right_out[...] = right[...]
 
@@ -169,7 +173,7 @@
         to = jnp.bitwise_xor(me, s)
         start = to * slab
         if two:
-            start += jnp.where(to < n // 2, 0, slab // 2 + 2 * HALO)
+            start += jnp.where(to % 2 == 0, 0, slab // 2 + 2 * HALO)
         start = pl.multiple_of(start, 16)
         for f in range(MOMENTS):
             outs[s][f] = tall[f, pl.ds(start, count), :]
@@ -252,7 +256,31 @@
             out[own, here] = jnp.where(same, diagonal, tile).astype(jnp.bfloat16)
 
 
-def section_kernel(n, two, second, far, near, me_ref, grid_far, grid_near, *refs):
+def weights_of(parts, grids, s, down=slice(None)):
+    for part, grid in zip(parts, grids):
+        if s in part:
+            rows = grid.shape[1] // len(part)
+            at = part.index(s) * rows
+            return grid[down, at : at + rows]
+
+
+def flip_kernel(n, parts, far, *refs):
+    grids, out = refs[: len(parts)], refs[-1]
+    rows = out.shape[0] // n
+    line = lax.broadcasted_iota(jnp.int32, (rows, rows), 0)
+    turn = line + lax.broadcasted_iota(jnp.int32, (rows, rows), 1) == rows - 1
+    turn = jnp.where(turn, 1.0, 0.0).astype(jnp.bfloat16)
+    for k, s in enumerate(far):
+        for a in range(n):
+            down = (a ^ (n - 1)) * rows
+            tile = weights_of(parts, grids, s ^ (n - 1), slice(down, down + rows))
+            tile = jnp.dot(turn, tile, preferred_element_type=jnp.float32).astype(jnp.bfloat16)
+            tile = -jnp.dot(tile, turn, preferred_element_type=jnp.float32)
+            out[a * rows : (a + 1) * rows, k * rows : (k + 1) * rows] = tile.astype(jnp.bfloat16)
+
+
+def section_kernel(n, two, second, far, parts, me_ref, *refs):
+    grids, refs = refs[: len(parts)], refs[len(parts) :]
     firsts, refs = refs[:n], refs[n:]
     if second:
         rests, refs = refs[:n], refs[n + 1 :]
@@ -262,9 +290,9 @@
     rows = size // n
     core = wide - 2 * HALO
     me = me_ref[0]
-    right_first = me < n // 2
+    right_first = me % 2 == 0
     lane = min(rows, 128)
-    parts = rows // lane
+    strips = rows // lane
 
     for s in range(n):
         here = pl.ds(s * rows, rows)
@@ -281,7 +309,7 @@
                 u0[f, dst, here] = decode(f, old)
 
     for s in range(n):
-        for p in range(parts):
+        for p in range(strips):
             here = pl.ds(s * rows + p * lane, lane)
             u = [u0[f, :, here] for f in range(MOMENTS)]
             for f in range(MOMENTS):
@@ -289,10 +317,9 @@
 
     middle = slice(HALO, HALO + core)
     for s in range(n):
-        weights = (grid_far, far) if s in far else (grid_near, near)
-        block = pl.ds(weights[1].index(s) * rows, rows)
-        product[...] = jnp.dot(fy0[...], weights[0][:, block], preferred_element_type=jnp.float32)
-        for p in range(parts):
+        weights = weights_of(parts, grids, s)
+        product[...] = jnp.dot(fy0[...], weights, preferred_element_type=jnp.float32)
+        for p in range(strips):
             here = pl.ds(s * rows + p * lane, lane)
             there = pl.ds(p * lane, lane)
             u = [u0[f, :, here] for f in range(MOMENTS)]
@@ -310,15 +337,16 @@
             for f in range(MOMENTS):
                 fy1[f * core : (f + 1) * core, here] = flux(inner, 1, f).astype(jnp.bfloat16)
 
-    finish(n, far, me_ref, grid_far, u1, r0, fy1, outs, product)
-
-
-def finish_kernel(n, near, chunks, me_ref, grid_near, *refs):
+    finish(n, far, me_ref, parts, grids, u1, r0, fy1, outs, product)
+
+
+def finish_kernel(n, near, parts, chunks, me_ref, *refs):
+    grids, refs = refs[: len(parts)], refs[len(parts) :]
     states, outs, product = refs[: 3 * chunks], refs[-1 - len(near) : -1], refs[-1]
     core = outs[0].shape[1] // chunks
     for c in range(chunks):
         part = [out.at[:, c * core : (c + 1) * core, :] for out in outs]
-        finish(n, near, me_ref, grid_near, *states[3 * c : 3 * c + 3], part, product)
+        finish(n, near, me_ref, parts, grids, *states[3 * c : 3 * c + 3], part, product)
 
 
 def walls(me, s, p, n, rows, count):
@@ -328,7 +356,7 @@
     return jnp.where(line == 0, 1.0, jnp.where(line == n * rows - 1, -1.0, 0.0))
 
 
-def finish(n, slots, me_ref, grid, u1, r0, fy1, outs, product):
+def finish(n, slots, me_ref, parts, grids, u1, r0, fy1, outs, product):
     wide, size = u1.shape[1:]
     rows = size // n
     core = wide - 2 * HALO
@@ -336,9 +364,9 @@
     me = me_ref[0]
     middle = slice(HALO, HALO + core)
     for k, s in enumerate(slots):
-        block = pl.ds(k * rows, rows)
+        weights = weights_of(parts, grids, s)
         product[0 : MOMENTS * core, :] = jnp.dot(
-            fy1[...], grid[:, block], preferred_element_type=jnp.float32
+            fy1[...], weights, preferred_element_type=jnp.float32
         )
         for p in range(rows // lane):
             here = pl.ds(s * rows + p * lane, lane)
@@ -373,7 +401,7 @@
             for c in range(chunks):
                 start = of * slab
                 if chunks == 2:
-                    start += jnp.where(of < n // 2, width * (1 - c), width * c)
+                    start += jnp.where(of % 2 == 0, width * (1 - c), width * c)
                 here = pl.ds(pl.multiple_of(start, 16), width)
                 if s in near:
                     piece = staying[near.index(s)][f, c * width : (c + 1) * width, :]
@@ -392,7 +420,8 @@
 
 
 def exchange(arrays, n, slots):
-    return [to_partner(array, n, s) for array, s in zip(arrays, slots)]
+    pairs = list(zip(arrays, slots))[::-1]
+    return [to_partner(array, n, s) for array, s in pairs][::-1]
 
 
 def on_device(rho, vel, temp, stress, heat):
@@ -410,26 +439,38 @@
     def message(width, kind=half):
         return jax.ShapeDtypeStruct((MOMENTS, width, rows), kind)
 
-    shapes = [message(wide)] * n if two else []
-    shapes += [message(cols + 2 * HALO)] + [message(2 * HALO)] * 2
-    *firsts, tall, left, right = pl.pallas_call(
-        functools.partial(pack_kernel, n, two),
-        out_shape=shapes,
-        in_specs=[SMEM] + [HBM] * 5,
-        out_specs=[ANY] * len(shapes),
-        scratch_shapes=[
-            pltpu.VMEM((cols + 2 * HALO, rows), jnp.float32),
-            pltpu.VMEM((MOMENTS, rows, cols), jnp.float32),
-            pltpu.SemaphoreType.DMA((len(GROUPS),)),
-        ]
-        + [pltpu.VMEM(x.shape, x.dtype) for x in shapes]
-        + [pltpu.SemaphoreType.DMA((len(shapes), 3))],
-        compiler_params=params(56),
-        cost_estimate=cost(2),
-        name="pack",
-    )(me, rho, vel, temp, stress, heat)
+    far, near = (tuple(range(n // 2, n)), tuple(range(n // 2)))
+    inputs = (rho, vel, temp, stress, heat)
+
+    def pack(arrays, ranges, extra, *ties):
+        shapes = [jax.ShapeDtypeStruct((high - low, wide, rows), half) for s, low, high in ranges]
+        if extra:
+            shapes += [message(cols + 2 * HALO)] + [message(2 * HALO)] * 2
+        count = sum(1 if len(a.shape) == 2 else a.shape[0] for a in arrays)
+        return pl.pallas_call(
+            functools.partial(pack_kernel, n, len(arrays), ranges, extra),
+            out_shape=shapes,
+            in_specs=[SMEM] + [HBM] * len(arrays) + [ANY] * len(ties),
+            out_specs=[ANY] * len(shapes),
+            scratch_shapes=[
+                pltpu.VMEM((cols + 2 * HALO, rows), jnp.float32),
+                pltpu.VMEM((count, rows, cols), jnp.float32),
+                pltpu.SemaphoreType.DMA((len(arrays),)),
+            ]
+            + [pltpu.VMEM(x.shape, x.dtype) for x in shapes]
+            + [pltpu.SemaphoreType.DMA((len(shapes), len(arrays)))],
+            compiler_params=params(56),
+            cost_estimate=cost(0.05),
+            name="pack",
+        )(me, *arrays, *ties)
+
+    firsts = []
     if two:
+        firsts = pack(inputs, tuple((s, 0, MOMENTS) for s in range(n)), False)
+        tall, left, right = pack(inputs, (), True, firsts[0])
         firsts = exchange(firsts, n, range(n))
+    else:
+        tall, left, right = pack(inputs, (), True)
 
     lane = min(rows, 128)
 
@@ -442,32 +483,41 @@
             scratch_shapes=[pltpu.VMEM((size, lane), jnp.float32)] * 4
             + [pltpu.VMEM((8, lane), jnp.float32)],
             compiler_params=params(24),
-            cost_estimate=cost(3),
+            cost_estimate=cost(0.05),
             name="grid",
         )(me)
 
-    far, near = (tuple(range(n // 2, n)), tuple(range(n // 2)))
-    grid = {far: grid_of(far)}
+    parts = (near[: n // 4], near[n // 4 :])
+    grids = [grid_of(part) for part in parts]
     left, right = pl.pallas_call(
         edge_kernel,
         out_shape=[message(2 * HALO)] * 2,
         in_specs=[VMEM] * 2 + [ANY],
         out_specs=[VMEM] * 2,
         compiler_params=params(24),
-        cost_estimate=cost(0.2),
+        cost_estimate=cost(0.01),
         name="edges",
-    )(left, right, grid[far])
+    )(left, right, grids[0])
     up = [(i, (i + 1) % ring) for i in range(ring)]
     before = lax.ppermute(right, "gx", up)
     after = lax.ppermute(left, "gx", [(j, i) for i, j in up])
-    grid[near] = grid_of(near)
+    turned = pl.pallas_call(
+        functools.partial(flip_kernel, n, parts, far),
+        out_shape=jax.ShapeDtypeStruct((size, len(far) * rows), half),
+        in_specs=[VMEM] * 2,
+        out_specs=VMEM,
+        compiler_params=params(24),
+        cost_estimate=cost(0.02),
+        name="flip",
+    )(*grids)
+    all_parts, all_grids = (*parts, far), (*grids, turned)
     rests = pl.pallas_call(
         functools.partial(rest_kernel, n, two),
         out_shape=[message(core if two else wide)] * n,
         in_specs=[SMEM] + [VMEM] * 3,
         out_specs=[VMEM] * n,
         compiler_params=params(),
-        cost_estimate=cost(0.2),
+        cost_estimate=cost(0.01),
         name="rest",
     )(me, tall, before, after)
     rests = exchange(rests, n, range(n))
@@ -479,9 +529,9 @@
             jax.ShapeDtypeStruct((MOMENTS * core, size), half),
         ]
         *crossing, u1, r0, fy1 = pl.pallas_call(
-            functools.partial(section_kernel, n, two, second, far, near),
+            functools.partial(section_kernel, n, two, second, far, all_parts),
             out_shape=[message(core)] * len(far) + state,
-            in_specs=[SMEM] + [VMEM] * (2 * n + 2 if second else n + 2) + [ANY] * second,
+            in_specs=[SMEM] + [VMEM] * (len(arrays) + 3 - second) + [ANY] * second,
             out_specs=[VMEM] * (len(far) + 3),
             scratch_shapes=[
                 pltpu.VMEM((MOMENTS, wide, size), jnp.float32),
@@ -491,20 +541,20 @@
             compiler_params=params(24),
             cost_estimate=cost(6),
             name="sections",
-        )(me, grid[far], grid[near], *arrays)
+        )(me, *all_grids, *arrays)
         return crossing, [u1, r0, fy1]
 
     def finished(states, *ties):
         return pl.pallas_call(
-            functools.partial(finish_kernel, n, near, len(states) // 3),
+            functools.partial(finish_kernel, n, near, parts, len(states) // 3),
             out_shape=[message(slab, jnp.float32)] + [message(slab)] * (len(near) - 1),
-            in_specs=[SMEM] + [VMEM] * (len(states) + 1) + [ANY] * len(ties),
+            in_specs=[SMEM] + [VMEM] * (len(states) + 2) + [ANY] * len(ties),
             out_specs=[VMEM] * len(near),
             scratch_shapes=[pltpu.VMEM((MOMENTS * core, rows), jnp.float32)],
             compiler_params=params(24),
             cost_estimate=cost(4),
             name="finish",
-        )(me, grid[near], *states, *ties)
+        )(me, *grids, *states, *ties)
 
     if two:
         crossing, states = sections(False, *firsts)

time: 52.3 us -> 56 us (1.071)
  local copies, waits for them, and re-layouts: 0.02 us -> 1.93 us
  Pallas kernels: 27.7 us -> 28.9 us
    pallas_call x4 -> x6, Pallas kernels: 19 us -> 22.7 us  [the longest x2 12.1 us: sections(): pl.pallas_call(functools.partial(section_kernel, n, two, second, far, all...]
    pallas_call x2, Pallas kernels: 6.42 us -> 3.85 us  [grid_of(): pl.pallas_call(functools.partial(grid_kernel, n, rows, slots), out_shape=...]
    unnamed x8, local copies, waits for them, and re-layouts: 0.02 us -> 1.93 us
  transfers between devices with their start and end apart: 13 -> 13, of which waited for: 7 -> 6; matrix products, arithmetic and copies ran while one was open for 0% -> 0% of each run, Pallas kernels for 42% -> 42%
where the time goes in v5:
time: 56 us; the launch traced here: 55.9 us
  Pallas kernels  28.9 us (52%)
  starting transfers between devices  14.3 us (26%)
  waiting for transfers between devices  10.4 us (19%)
  local copies, waits for them, and re-layouts  1.93 us (3%)
    pallas_call x2, Pallas kernels, sections(): pl.pallas_call(functools.partial(section_kernel, n, two, second, far, all...  12.1 us
    ppermute x11, starting transfers between devices, to_partner(): lax.ppermute(array, 'gy', [(i, i ^ s) for i in range(n)])  9.39 us
    ppermute x11, waiting for transfers between devices, to_partner(): lax.ppermute(array, 'gy', [(i, i ^ s) for i in range(n)])  9.07 us
    pallas_call x2, Pallas kernels, pack(): pl.pallas_call(functools.partial(pack_kernel, n, len(arrays), ranges, ext...  6.71 us
    pallas_call x2, Pallas kernels, grid_of(): pl.pallas_call(functools.partial(grid_kernel, n, rows, slots), out_shape=...  3.85 us
    ppermute x1, starting transfers between devices, on_device(): after = lax.ppermute(left, 'gx', [(j, i) for i, j in up])  3.1 us
    pallas_call x1, Pallas kernels, finished(): pl.pallas_call(functools.partial(finish_kernel, n, near, parts, len(state...  3.09 us
    pallas_call x1, Pallas kernels, on_device(): pl.pallas_call(functools.partial(unpack_kernel, n, far, near, 2 if two el...  2.02 us
  transfers between devices with their start and end apart: 13, of which 6 were waited for; matrix products, arithmetic and copies ran while one was open for 0% of the time, Pallas kernels for 42%

profile of v5, /device:TPU:0, one launch (start us, length us, event | category | flops | bytes accessed | tf_op | source)
XLA Modules:
  0.0 55.9 jit_solution(9599727987135065806)
XLA Ops:
  0.0 3.4 %pack.2 = (bf16[13,48,256]{2,1,0:T(8,128)(2,1)}, bf16[13,48,256]{2,1,0:T(8,128)(2,1)}, bf16[13,48,256]{2,1,0:T(8,128)(2,1)}, bf16[13,48,256]{2,1,0:T(8,128)(2,1)}) custom-call(s32[1]{0:T(128)} %bitcast.me_ref, f32[256,256]{1,0:T(8,128)} %refs_0_.3, f32[3,256,256]{2,1,0:T(8,128)} %bitcast.7, f32[256,256]{1,0:T(8,128)} %refs_2_.3, f32[5,256,256]{2,1,0:T(8,128)} %bitcast.5, ...), custom_call_target="tpu_custom_call" | custom-call | flops 50000000 | bytes 150000 | tf_op jit(solution)/shard_map/pack/pallas_call | solution.py:450
  3.4 0.5 collective-permute-start
  3.9 2.6 %collective-permute-start.1 = (bf16[13,48,256]{2,1,0:T(8,128)(2,1)}, bf16[13,48,256]{2,1,0:T(8,128)(2,1)S(1)}, u32[]{:S(2)}, u32[]{:S(2)}) collective-permute-start(bf16[13,48,256]{2,1,0:T(8,128)(2,1)} %get-tuple-element.32), channel_id=1, source_target_pairs={{0,2},{1,3},{2,0},{3,1},{4,6},{5,7},{6,4},{7,5},{8,10},{9,11},{10,... | collective-permute-start | bytes 958472 | tf_op jit(solution)/shard_map/ppermute | solution.py:419
  6.4 0.1 collective-permute-start.2
  6.5 1.9 %grid.2.refs_0_.tie = bf16[1024,256]{1,0:T(8,128)(2,1)S(1)} custom-call(s32[1]{0:T(128)} %bitcast.me_ref), custom_call_target="tpu_custom_call" | custom-call | flops 50000000 | bytes 150000 | tf_op jit(solution)/shard_map/grid/pallas_call | solution.py:478
  8.4 3.4 %pack.3 = (bf16[13,272,256]{2,1,0:T(8,128)(2,1)}, bf16[13,16,256]{2,1,0:T(8,128)(2,1)}, bf16[13,16,256]{2,1,0:T(8,128)(2,1)}) custom-call(s32[1]{0:T(128)} %bitcast.me_ref, f32[256,256]{1,0:T(8,128)} %refs_0_.3, f32[3,256,256]{2,1,0:T(8,128)} %bitcast.8, f32[256,256]{1,0:T(8,128)} %refs_2_.3, f32[5,256,256]{2,1,0:T(8,128)} %bitcast.6, ...), custom_call_target="tpu_custom_call" | custom-call | flops 50000000 | bytes 150000 | tf_op jit(solution)/shard_map/pack/pallas_call | solution.py:450
  11.8 0.0 copy-start
  11.8 1.0 %copy-done.2 = bf16[13,16,256]{2,1,0:T(8,128)(2,1)S(1)} copy-done((bf16[13,16,256]{2,1,0:T(8,128)(2,1)S(1)}, bf16[13,16,256]{2,1,0:T(8,128)(2,1)}, u32[]{:S(2)}) %copy-start.2) | copy-done | bytes 106520
  12.9 0.9 %copy-done.3 = bf16[13,16,256]{2,1,0:T(8,128)(2,1)S(1)} copy-done((bf16[13,16,256]{2,1,0:T(8,128)(2,1)S(1)}, bf16[13,16,256]{2,1,0:T(8,128)(2,1)}, u32[]{:S(2)}) %copy-start.3) | copy-done | bytes 106520
  13.8 1.8 %collective-permute-start.3 = (bf16[13,16,256]{2,1,0:T(8,128)(2,1)S(1)}, bf16[13,16,256]{2,1,0:T(8,128)(2,1)S(1)}, u32[]{:S(2)}, u32[]{:S(2)}) collective-permute-start(bf16[13,16,256]{2,1,0:T(8,128)(2,1)S(1)} %get-tuple-element.40), channel_id=1, source_target_pairs={{0,4},{4,8},{8,12},{12,16},{16,20},{20,24},{24,28},{28,0},{1,5},{5... | collective-permute-start | bytes 319496 | tf_op jit(solution)/shard_map/ppermute | solution.py:502
  15.6 3.1 %collective-permute-start.4 = (bf16[13,16,256]{2,1,0:T(8,128)(2,1)S(1)}, bf16[13,16,256]{2,1,0:T(8,128)(2,1)S(1)}, u32[]{:S(2)}, u32[]{:S(2)}) collective-permute-start(bf16[13,16,256]{2,1,0:T(8,128)(2,1)S(1)} %get-tuple-element.41), channel_id=1, source_target_pairs={{4,0},{8,4},{12,8},{16,12},{20,16},{24,20},{28,24},{0,28},{5,1},{9... | collective-permute-start | bytes 319496 | tf_op jit(solution)/shard_map/ppermute | solution.py:503
  18.7 1.9 %grid.3.refs_1_ = bf16[1024,256]{1,0:T(8,128)(2,1)S(1)} custom-call(s32[1]{0:T(128)} %bitcast.me_ref), custom_call_target="tpu_custom_call" | custom-call | flops 50000000 | bytes 150000 | tf_op jit(solution)/shard_map/grid/pallas_call | solution.py:478
  20.6 0.8 %flip.1.refs_2_ = bf16[1024,512]{1,0:T(8,128)(2,1)S(1)} custom-call(bf16[1024,256]{1,0:T(8,128)(2,1)S(1)} %grid.2.refs_0_.tie, bf16[1024,256]{1,0:T(8,128)(2,1)S(1)} %grid.3.refs_1_), custom_call_target="tpu_custom_call" | custom-call | flops 20000000 | bytes 60000 | tf_op jit(solution)/shard_map/flip/pallas_call | solution.py:504
  21.4 0.8 %collective-permute-done.3.before = bf16[13,16,256]{2,1,0:T(8,128)(2,1)S(1)} collective-permute-done((bf16[13,16,256]{2,1,0:T(8,128)(2,1)S(1)}, bf16[13,16,256]{2,1,0:T(8,128)(2,1)S(1)}, u32[]{:S(2)}, u32[]{:S(2)}) %collective-permute-start.3) | collective-permute-done | bytes 106528 | tf_op jit(solution)/shard_map/ppermute | solution.py:502
  22.2 0.6 %collective-permute-done.4.after = bf16[13,16,256]{2,1,0:T(8,128)(2,1)S(1)} collective-permute-done((bf16[13,16,256]{2,1,0:T(8,128)(2,1)S(1)}, bf16[13,16,256]{2,1,0:T(8,128)(2,1)S(1)}, u32[]{:S(2)}, u32[]{:S(2)}) %collective-permute-start.4) | collective-permute-done | bytes 106528 | tf_op jit(solution)/shard_map/ppermute | solution.py:503
  22.8 0.3 rest.1
  23.1 0.1 collective-permute-start.5
  23.2 1.6 %collective-permute-start.6 = (bf16[13,32,256]{2,1,0:T(8,128)(2,1)S(1)}, bf16[13,32,256]{2,1,0:T(8,128)(2,1)S(1)}, u32[]{:S(2)}, u32[]{:S(2)}) collective-permute-start(bf16[13,32,256]{2,1,0:T(8,128)(2,1)S(1)} %get-tuple-element.44), channel_id=1, source_target_pairs={{0,2},{1,3},{2,0},{3,1},{4,6},{5,7},{6,4},{7,5},{8,10},{9,11},{10,... | collective-permute-start | bytes 638984 | tf_op jit(solution)/shard_map/ppermute | solution.py:419
  24.7 0.3 collective-permute-start.7
  25.0 5.8 %sections.2 = (bf16[13,32,256]{2,1,0:T(8,128)(2,1)S(1)}, bf16[13,32,256]{2,1,0:T(8,128)(2,1)S(1)}, f32[13,48,1024]{2,1,0:T(8,128)S(1)}, f32[13,32,1024]{2,1,0:T(8,128)S(1)}, bf16[416,1024]{1,0:T(8,128)(2,1)S(1)}) custom-call(s32[1]{0:T(128)} %bitcast.me_ref, bf16[1024,256]{1,0:T(8,128)(2,1)S(1)} %grid.2.refs_0_.tie, bf16[1024,256]{1,0:T(8,128)(2,1)S(1)} %grid.3.refs_1_, ...), custom_call_target="tpu_custom_call" | custom-call | flops 6000000000 | bytes 18000000 | tf_op jit(solution)/shard_map/sections/pallas_call | solution.py:531
  30.8 1.6 %collective-permute-start.8 = (bf16[13,32,256]{2,1,0:T(8,128)(2,1)S(1)}, bf16[13,32,256]{2,1,0:T(8,128)(2,1)S(1)}, u32[]{:S(2)}, u32[]{:S(2)}) collective-permute-start(bf16[13,32,256]{2,1,0:T(8,128)(2,1)S(1)} %get-tuple-element.46.refs_11_), channel_id=1, source_target_pairs={{0,2},{1,3},{2,0},{3,1},{4,6},{5,7},{6,4},{7,5},{8,10},{9,11},{10,... | collective-permute-start | bytes 638984 | tf_op jit(solution)/shard_map/ppermute | solution.py:419
  32.4 0.2 collective-permute-start.9
  32.6 2.3 %collective-permute-done.7.refs_10_ = bf16[13,32,256]{2,1,0:T(8,128)(2,1)S(1)} collective-permute-done((bf16[13,32,256]{2,1,0:T(8,128)(2,1)S(1)}, bf16[13,32,256]{2,1,0:T(8,128)(2,1)S(1)}, u32[]{:S(2)}, u32[]{:S(2)}) %collective-permute-start.7) | collective-permute-done | bytes 213024 | tf_op jit(solution)/shard_map/ppermute | solution.py:419
  34.9 6.3 %sections.3 = (bf16[13,32,256]{2,1,0:T(8,128)(2,1)S(1)}, bf16[13,32,256]{2,1,0:T(8,128)(2,1)S(1)}, f32[13,48,1024]{2,1,0:T(8,128)S(1)}, f32[13,32,1024]{2,1,0:T(8,128)S(1)}, bf16[416,1024]{1,0:T(8,128)(2,1)S(1)}) custom-call(s32[1]{0:T(128)} %bitcast.me_ref, bf16[1024,256]{1,0:T(8,128)(2,1)S(1)} %grid.2.refs_0_.tie, bf16[1024,256]{1,0:T(8,128)(2,1)S(1)} %grid.3.refs_1_, ...), custom_call_target="tpu_custom_call" | custom-call | flops 6000000000 | bytes 18000000 | tf_op jit(solution)/shard_map/sections/pallas_call | solution.py:531
  41.3 1.5 %collective-permute-start.11 = (bf16[13,32,256]{2,1,0:T(8,128)(2,1)S(1)}, bf16[13,32,256]{2,1,0:T(8,128)(2,1)S(1)}, u32[]{:S(2)}, u32[]{:S(2)}) collective-permute-start(bf16[13,32,256]{2,1,0:T(8,128)(2,1)S(1)} %get-tuple-element.53), channel_id=1, source_target_pairs={{0,2},{1,3},{2,0},{3,1},{4,6},{5,7},{6,4},{7,5},{8,10},{9,11},{10,... | collective-permute-start | bytes 638984 | tf_op jit(solution)/shard_map/ppermute | solution.py:419
  42.8 0.6 %collective-permute-start.12 = (bf16[13,32,256]{2,1,0:T(8,128)(2,1)S(1)}, bf16[13,32,256]{2,1,0:T(8,128)(2,1)S(1)}, u32[]{:S(2)}, u32[]{:S(2)}) collective-permute-start(bf16[13,32,256]{2,1,0:T(8,128)(2,1)S(1)} %get-tuple-element.54), channel_id=1, source_target_pairs={{0,3},{1,2},{2,1},{3,0},{4,7},{5,6},{6,5},{7,4},{8,11},{9,10},{10,... | collective-permute-start | bytes 638984 | tf_op jit(solution)/shard_map/ppermute | solution.py:419
  43.5 0.6 %collective-permute-done.9.refs_9_.refs_1_.refs_3_ = bf16[13,32,256]{2,1,0:T(8,128)(2,1)S(1)} collective-permute-done((bf16[13,32,256]{2,1,0:T(8,128)(2,1)S(1)}, bf16[13,32,256]{2,1,0:T(8,128)(2,1)S(1)}, u32[]{:S(2)}, u32[]{:S(2)}) %collective-permute-start.9) | collective-permute-done | bytes 213024 | tf_op jit(solution)/shard_map/ppermute | solution.py:419
  44.1 3.1 %finish.1 = (f32[13,64,256]{2,1,0:T(8,128)S(1)}, bf16[13,64,256]{2,1,0:T(8,128)(2,1)S(1)}) custom-call(s32[1]{0:T(128)} %bitcast.me_ref, bf16[1024,256]{1,0:T(8,128)(2,1)S(1)} %grid.2.refs_0_.tie, bf16[1024,256]{1,0:T(8,128)(2,1)S(1)} %grid.3.refs_1_, f32[13,48,1024]{2,1,0:T(8,128)S(1)} %get-tuple-element.34.refs_2_, ...), custom_call_target="tpu_custom_call" | custom-call | flops 4000000000 | bytes 12000000 | tf_op jit(solution)/shard_map/finish/pallas_call | solution.py:548
  47.2 0.3 collective-permute-start.10
  47.5 2.0 %collective-permute-done.11.refs_2_.refs_4_ = bf16[13,32,256]{2,1,0:T(8,128)(2,1)S(1)} collective-permute-done((bf16[13,32,256]{2,1,0:T(8,128)(2,1)S(1)}, bf16[13,32,256]{2,1,0:T(8,128)(2,1)S(1)}, u32[]{:S(2)}, u32[]{:S(2)}) %collective-permute-start.11) | collective-permute-done | bytes 213024 | tf_op jit(solution)/shard_map/ppermute | solution.py:419
  49.5 4.2 %collective-permute-done.12.refs_3_.refs_5_ = bf16[13,32,256]{2,1,0:T(8,128)(2,1)S(1)} collective-permute-done((bf16[13,32,256]{2,1,0:T(8,128)(2,1)S(1)}, bf16[13,32,256]{2,1,0:T(8,128)(2,1)S(1)}, u32[]{:S(2)}, u32[]{:S(2)}) %collective-permute-start.12) | collective-permute-done | bytes 213024 | tf_op jit(solution)/shard_map/ppermute | solution.py:419
  53.7 2.0 %unpack.1 = f32[13,256,256]{2,1,0:T(8,128)} custom-call(s32[1]{0:T(128)} %bitcast.me_ref, f32[13,64,256]{2,1,0:T(8,128)S(1)} %get-tuple-element.51.refs_0_, bf16[13,64,256]{2,1,0:T(8,128)(2,1)S(1)} %collective-permute-done.10.refs_1_, bf16[13,32,256]{2,1,0:T(8,128)(2,1)S(1)} %collective-permute-done.8.refs_8_.refs_0_.refs_2_, ...), custom_call_target="tpu_custom_call" | custom-call | flops 3000000000 | bytes 9000000 | tf_op jit(solution)/shard_map/unpack/pallas_call | solution.py:579
  (14 shorter events, 0.0 us)
Async XLA Ops:
  3.4 21.4 %collective-permute-start = (bf16[13,48,256]{2,1,0:T(8,128)(2,1)}, bf16[13,48,256]{2,1,0:T(8,128)(2,1)S(1)}, u32[]{:S(2)}, u32[]{:S(2)}) collective-permute-start(bf16[13,48,256]{2,1,0:T(8,128)(2,1)} %get-tuple-element.31), channel_id=1, source_target_pairs={{0,1},{1,0},{2,3},{3,2},{4,5},{5,4},{6,7},{7,6},{8,9},{9,8},{10,11... | collective-permute-start | bytes 958472 | tf_op jit(solution)/shard_map/ppermute | solution.py:419
  3.9 21.2 %collective-permute-start.1 = (bf16[13,48,256]{2,1,0:T(8,128)(2,1)}, bf16[13,48,256]{2,1,0:T(8,128)(2,1)S(1)}, u32[]{:S(2)}, u32[]{:S(2)}) collective-permute-start(bf16[13,48,256]{2,1,0:T(8,128)(2,1)} %get-tuple-element.32), channel_id=1, source_target_pairs={{0,2},{1,3},{2,0},{3,1},{4,6},{5,7},{6,4},{7,5},{8,10},{9,11},{10,... | collective-permute-start | bytes 958472 | tf_op jit(solution)/shard_map/ppermute | solution.py:419
  6.4 18.6 %collective-permute-start.2 = (bf16[13,48,256]{2,1,0:T(8,128)(2,1)}, bf16[13,48,256]{2,1,0:T(8,128)(2,1)S(1)}, u32[]{:S(2)}, u32[]{:S(2)}) collective-permute-start(bf16[13,48,256]{2,1,0:T(8,128)(2,1)} %get-tuple-element.33), channel_id=1, source_target_pairs={{0,3},{1,2},{2,1},{3,0},{4,7},{5,6},{6,5},{7,4},{8,11},{9,10},{10,... | collective-permute-start | bytes 958472 | tf_op jit(solution)/shard_map/ppermute | solution.py:419
  11.8 11.0 %copy-start = (bf16[13,272,256]{2,1,0:T(8,128)(2,1)S(1)}, bf16[13,272,256]{2,1,0:T(8,128)(2,1)}, u32[]{:S(2)}) copy-start(bf16[13,272,256]{2,1,0:T(8,128)(2,1)} %get-tuple-element.37.tall) | copy-start | bytes 5431300
  11.8 1.0 %copy-start.2 = (bf16[13,16,256]{2,1,0:T(8,128)(2,1)S(1)}, bf16[13,16,256]{2,1,0:T(8,128)(2,1)}, u32[]{:S(2)}) copy-start(bf16[13,16,256]{2,1,0:T(8,128)(2,1)} %get-tuple-element.38.left) | copy-start | bytes 319492
  12.9 0.9 %copy-start.3 = (bf16[13,16,256]{2,1,0:T(8,128)(2,1)S(1)}, bf16[13,16,256]{2,1,0:T(8,128)(2,1)}, u32[]{:S(2)}) copy-start(bf16[13,16,256]{2,1,0:T(8,128)(2,1)} %get-tuple-element.39.right) | copy-start | bytes 319492
  13.8 8.4 %collective-permute-start.3 = (bf16[13,16,256]{2,1,0:T(8,128)(2,1)S(1)}, bf16[13,16,256]{2,1,0:T(8,128)(2,1)S(1)}, u32[]{:S(2)}, u32[]{:S(2)}) collective-permute-start(bf16[13,16,256]{2,1,0:T(8,128)(2,1)S(1)} %get-tuple-element.40), channel_id=1, source_target_pairs={{0,4},{4,8},{8,12},{12,16},{16,20},{20,24},{24,28},{28,0},{1,5},{5... | collective-permute-start | bytes 319496 | tf_op jit(solution)/shard_map/ppermute | solution.py:502
  15.6 7.2 %collective-permute-start.4 = (bf16[13,16,256]{2,1,0:T(8,128)(2,1)S(1)}, bf16[13,16,256]{2,1,0:T(8,128)(2,1)S(1)}, u32[]{:S(2)}, u32[]{:S(2)}) collective-permute-start(bf16[13,16,256]{2,1,0:T(8,128)(2,1)S(1)} %get-tuple-element.41), channel_id=1, source_target_pairs={{4,0},{8,4},{12,8},{16,12},{20,16},{24,20},{28,24},{0,28},{5,1},{9... | collective-permute-start | bytes 319496 | tf_op jit(solution)/shard_map/ppermute | solution.py:503
  20.6 4.4 %copy-start.1 = (bf16[13,48,256]{2,1,0:T(8,128)(2,1)S(1)}, bf16[13,48,256]{2,1,0:T(8,128)(2,1)}, u32[]{:S(2)}) copy-start(bf16[13,48,256]{2,1,0:T(8,128)(2,1)} %get-tuple-element.30.refs_3_.refs_5_) | copy-start | bytes 958468
  23.1 9.5 %collective-permute-start.5 = (bf16[13,32,256]{2,1,0:T(8,128)(2,1)S(1)}, bf16[13,32,256]{2,1,0:T(8,128)(2,1)S(1)}, u32[]{:S(2)}, u32[]{:S(2)}) collective-permute-start(bf16[13,32,256]{2,1,0:T(8,128)(2,1)S(1)} %get-tuple-element.43), channel_id=1, source_target_pairs={{0,1},{1,0},{2,3},{3,2},{4,5},{5,4},{6,7},{7,6},{8,9},{9,8},{10,11... | collective-permute-start | bytes 638984 | tf_op jit(solution)/shard_map/ppermute | solution.py:419
  23.2 9.5 %collective-permute-start.6 = (bf16[13,32,256]{2,1,0:T(8,128)(2,1)S(1)}, bf16[13,32,256]{2,1,0:T(8,128)(2,1)S(1)}, u32[]{:S(2)}, u32[]{:S(2)}) collective-permute-start(bf16[13,32,256]{2,1,0:T(8,128)(2,1)S(1)} %get-tuple-element.44), channel_id=1, source_target_pairs={{0,2},{1,3},{2,0},{3,1},{4,6},{5,7},{6,4},{7,5},{8,10},{9,11},{10,... | collective-permute-start | bytes 638984 | tf_op jit(solution)/shard_map/ppermute | solution.py:419
  24.7 10.2 %collective-permute-start.7 = (bf16[13,32,256]{2,1,0:T(8,128)(2,1)S(1)}, bf16[13,32,256]{2,1,0:T(8,128)(2,1)S(1)}, u32[]{:S(2)}, u32[]{:S(2)}) collective-permute-start(bf16[13,32,256]{2,1,0:T(8,128)(2,1)S(1)} %get-tuple-element.45), channel_id=1, source_target_pairs={{0,3},{1,2},{2,1},{3,0},{4,7},{5,6},{6,5},{7,4},{8,11},{9,10},{10,... | collective-permute-start | bytes 638984 | tf_op jit(solution)/shard_map/ppermute | solution.py:419
  30.8 12.6 %collective-permute-start.8 = (bf16[13,32,256]{2,1,0:T(8,128)(2,1)S(1)}, bf16[13,32,256]{2,1,0:T(8,128)(2,1)S(1)}, u32[]{:S(2)}, u32[]{:S(2)}) collective-permute-start(bf16[13,32,256]{2,1,0:T(8,128)(2,1)S(1)} %get-tuple-element.46.refs_11_), channel_id=1, source_target_pairs={{0,2},{1,3},{2,0},{3,1},{4,6},{5,7},{6,4},{7,5},{8,10},{9,11},{10,... | collective-permute-start | bytes 638984 | tf_op jit(solution)/shard_map/ppermute | solution.py:419
  32.4 11.7 %collective-permute-start.9 = (bf16[13,32,256]{2,1,0:T(8,128)(2,1)S(1)}, bf16[13,32,256]{2,1,0:T(8,128)(2,1)S(1)}, u32[]{:S(2)}, u32[]{:S(2)}) collective-permute-start(bf16[13,32,256]{2,1,0:T(8,128)(2,1)S(1)} %get-tuple-element.50), channel_id=1, source_target_pairs={{0,3},{1,2},{2,1},{3,0},{4,7},{5,6},{6,5},{7,4},{8,11},{9,10},{10,... | collective-permute-start | bytes 638984 | tf_op jit(solution)/shard_map/ppermute | solution.py:419
  41.3 8.2 %collective-permute-start.11 = (bf16[13,32,256]{2,1,0:T(8,128)(2,1)S(1)}, bf16[13,32,256]{2,1,0:T(8,128)(2,1)S(1)}, u32[]{:S(2)}, u32[]{:S(2)}) collective-permute-start(bf16[13,32,256]{2,1,0:T(8,128)(2,1)S(1)} %get-tuple-element.53), channel_id=1, source_target_pairs={{0,2},{1,3},{2,0},{3,1},{4,6},{5,7},{6,4},{7,5},{8,10},{9,11},{10,... | collective-permute-start | bytes 638984 | tf_op jit(solution)/shard_map/ppermute | solution.py:419
  42.8 10.8 %collective-permute-start.12 = (bf16[13,32,256]{2,1,0:T(8,128)(2,1)S(1)}, bf16[13,32,256]{2,1,0:T(8,128)(2,1)S(1)}, u32[]{:S(2)}, u32[]{:S(2)}) collective-permute-start(bf16[13,32,256]{2,1,0:T(8,128)(2,1)S(1)} %get-tuple-element.54), channel_id=1, source_target_pairs={{0,3},{1,2},{2,1},{3,0},{4,7},{5,6},{6,5},{7,4},{8,11},{9,10},{10,... | collective-permute-start | bytes 638984 | tf_op jit(solution)/shard_map/ppermute | solution.py:419
  47.2 6.5 %collective-permute-start.10 = (bf16[13,64,256]{2,1,0:T(8,128)(2,1)S(1)}, bf16[13,64,256]{2,1,0:T(8,128)(2,1)S(1)}, u32[]{:S(2)}, u32[]{:S(2)}) collective-permute-start(bf16[13,64,256]{2,1,0:T(8,128)(2,1)S(1)} %get-tuple-element.52), channel_id=1, source_target_pairs={{0,1},{1,0},{2,3},{3,2},{4,5},{5,4},{6,7},{7,6},{8,9},{9,8},{10,11... | collective-permute-start | bytes 1277960 | tf_op jit(solution)/shard_map/ppermute | solution.py:419

commit v6 on v5

--- a/solution.py
+++ b/solution.py
@@ -110,11 +110,11 @@
     return pl.multiple_of(to * slab + jnp.where(to % 2 == 0, slab // 2, 0), 16)
 
 
-def pack_kernel(n, moments, ranges, extra, me_ref, *refs):
-    inputs, refs = refs[:moments], refs[moments:]
-    total = len(ranges) + (3 if extra else 0)
-    outs, refs = refs[-2 * total - 4 : -total - 4], refs[-total - 4 :]
-    (strip, given, arrived), held, left_at = refs[:3], refs[3 : 3 + total], refs[-1]
+def pack_kernel(n, two, me_ref, *refs):
+    inputs, refs = refs[:5], refs[5:]
+    count = n if two else 0
+    outs, (strip, given, arrived), refs = refs[: count + 1], refs[count + 1 : count + 4], refs[count + 4 :]
+    held, left_at = refs[:-1], refs[-1]
     rows, cols = given.shape[1:]
     slab = cols // n
     me = me_ref[0]
@@ -127,42 +127,30 @@
     strip[0:HALO, :] = jnp.zeros((HALO, rows), jnp.float32)
     strip[HALO + cols :, :] = jnp.zeros((HALO, rows), jnp.float32)
     leaving = []
-
-    def leave(k, first, last, at):
-        span = pl.ds(first, last - first)
-        copy = pltpu.make_async_copy(held[k].at[span], outs[k].at[span], left_at.at[k, at])
-        copy.start()
-        leaving.append(copy)
-
+    done = 0
     for at, (first, end, copy) in enumerate(copies):
         copy.wait()
         for f in range(first, end):
             strip[HALO : HALO + cols, :] = code(f, given[f]).T
-            for k, (s, low, high) in enumerate(ranges):
-                if low <= f < high:
-                    wide = held[k].shape[1]
-                    here = pl.ds(message_start(me, s, slab), wide)
-                    held[k][f - low] = strip[here, :].astype(jnp.bfloat16)
-            if extra:
-                tall, left, right = held[-3:]
-                tall[f] = strip[...].astype(jnp.bfloat16)
-                left[f] = tall[f, 0 : 2 * HALO, :]
-                right[f] = tall[f, cols : cols + 2 * HALO, :]
-        for k, (s, low, high) in enumerate(ranges):
-            if max(first, low) < min(end, high):
-                leave(k, max(first, low) - low, min(end, high) - low, at)
-        if extra and at % 2 == 0:
-            leave(total - 3, 0 if at == 0 else copies[at - 1][0], end, at)
-    if extra:
-        leave(total - 2, 0, MOMENTS, 0)
-        leave(total - 1, 0, MOMENTS, 0)
+            for s in range(count):
+                here = pl.ds(message_start(me, s, slab), held[s].shape[1])
+                held[s][f] = strip[here, :].astype(jnp.bfloat16)
+            held[count][f] = strip[...].astype(jnp.bfloat16)
+        if at % 2 == 0:
+            span = pl.ds(done, end - done)
+            for k, out in enumerate(outs):
+                copy = pltpu.make_async_copy(held[k].at[span], out.at[span], left_at.at[k, at // 2])
+                copy.start()
+                leaving.append(copy)
+            done = end
     for copy in leaving:
         copy.wait()
 
 
-def edge_kernel(left, right, tie, left_out, right_out):
-    left_out[...] = left[...]
-    right_out[...] = right[...]
+def edge_kernel(tall, tie, left, right):
+    cols = tall.shape[1] - 2 * HALO
+    left[...] = tall[:, 0 : 2 * HALO, :]
+    right[...] = tall[:, cols : cols + 2 * HALO, :]
 
 
 def rest_kernel(n, two, me_ref, tall, before, after, *outs):
@@ -194,7 +182,8 @@
             merge(slice(count - 2 * HALO, count), after, False)
 
 
-def grid_kernel(n, rows, slots, me_ref, out, sin_col, cos_col, back_col, line_col, total):
+def grid_kernel(n, rows, slots, me_ref, *refs):
+    out, sin_col, cos_col, back_col, line_col, total = refs[-6:]
     size = n * rows
     last = size - 1
     half = math.pi / (2.0 * last)
@@ -279,11 +268,21 @@
             out[a * rows : (a + 1) * rows, k * rows : (k + 1) * rows] = tile.astype(jnp.bfloat16)
 
 
+def far_first(arrays):
+    half = len(arrays) // 2
+    return [arrays[0], *arrays[half:], *arrays[1:half]]
+
+
+def in_slots(arrays):
+    half = len(arrays) // 2
+    return [arrays[0], *arrays[half + 1 :], *arrays[1 : half + 1]]
+
+
 def section_kernel(n, two, second, far, parts, me_ref, *refs):
     grids, refs = refs[: len(parts)], refs[len(parts) :]
-    firsts, refs = refs[:n], refs[n:]
+    firsts, refs = in_slots(refs[:n]), refs[n:]
     if second:
-        rests, refs = refs[:n], refs[n + 1 :]
+        rests, refs = in_slots(refs[:n]), refs[n + 1 :]
     outs, refs = refs[: len(far)], refs[len(far) :]
     u1, r0, fy1, u0, fy0, product = refs
     wide, size = u0.shape[1:]
@@ -442,62 +441,59 @@
     far, near = (tuple(range(n // 2, n)), tuple(range(n // 2)))
     inputs = (rho, vel, temp, stress, heat)
 
-    def pack(arrays, ranges, extra, *ties):
-        shapes = [jax.ShapeDtypeStruct((high - low, wide, rows), half) for s, low, high in ranges]
-        if extra:
-            shapes += [message(cols + 2 * HALO)] + [message(2 * HALO)] * 2
-        count = sum(1 if len(a.shape) == 2 else a.shape[0] for a in arrays)
+    def pack(arrays):
+        shapes = [message(wide)] * n if two else []
+        shapes += [message(cols + 2 * HALO)]
         return pl.pallas_call(
-            functools.partial(pack_kernel, n, len(arrays), ranges, extra),
+            functools.partial(pack_kernel, n, two),
             out_shape=shapes,
-            in_specs=[SMEM] + [HBM] * len(arrays) + [ANY] * len(ties),
+            in_specs=[SMEM] + [HBM] * len(arrays),
             out_specs=[ANY] * len(shapes),
             scratch_shapes=[
                 pltpu.VMEM((cols + 2 * HALO, rows), jnp.float32),
-                pltpu.VMEM((count, rows, cols), jnp.float32),
+                pltpu.VMEM((MOMENTS, rows, cols), jnp.float32),
                 pltpu.SemaphoreType.DMA((len(arrays),)),
             ]
             + [pltpu.VMEM(x.shape, x.dtype) for x in shapes]
-            + [pltpu.SemaphoreType.DMA((len(shapes), len(arrays)))],
+            + [pltpu.SemaphoreType.DMA((len(shapes), 3))],
             compiler_params=params(56),
-            cost_estimate=cost(0.05),
+            cost_estimate=cost(2),
             name="pack",
-        )(me, *arrays, *ties)
+        )(me, *arrays)
 
     firsts = []
     if two:
-        firsts = pack(inputs, tuple((s, 0, MOMENTS) for s in range(n)), False)
-        tall, left, right = pack(inputs, (), True, firsts[0])
+        *firsts, tall = pack(inputs)
         firsts = exchange(firsts, n, range(n))
     else:
-        tall, left, right = pack(inputs, (), True)
+        (tall,) = pack(inputs)
 
     lane = min(rows, 128)
 
-    def grid_of(slots):
+    def grid_of(slots, *ties):
         return pl.pallas_call(
             functools.partial(grid_kernel, n, rows, slots),
             out_shape=jax.ShapeDtypeStruct((size, len(slots) * rows), half),
-            in_specs=[SMEM],
+            in_specs=[SMEM] + [ANY] * len(ties),
             out_specs=VMEM,
             scratch_shapes=[pltpu.VMEM((size, lane), jnp.float32)] * 4
             + [pltpu.VMEM((8, lane), jnp.float32)],
             compiler_params=params(24),
-            cost_estimate=cost(0.05),
+            cost_estimate=cost(1),
             name="grid",
-        )(me)
+        )(me, *ties)
 
     parts = (near[: n // 4], near[n // 4 :])
     grids = [grid_of(part) for part in parts]
     left, right = pl.pallas_call(
         edge_kernel,
         out_shape=[message(2 * HALO)] * 2,
-        in_specs=[VMEM] * 2 + [ANY],
+        in_specs=[VMEM, ANY],
         out_specs=[VMEM] * 2,
         compiler_params=params(24),
-        cost_estimate=cost(0.01),
+        cost_estimate=cost(0.2),
         name="edges",
-    )(left, right, grids[0])
+    )(tall, grids[0])
     up = [(i, (i + 1) % ring) for i in range(ring)]
     before = lax.ppermute(right, "gx", up)
     after = lax.ppermute(left, "gx", [(j, i) for i, j in up])
@@ -507,7 +503,7 @@
         in_specs=[VMEM] * 2,
         out_specs=VMEM,
         compiler_params=params(24),
-        cost_estimate=cost(0.02),
+        cost_estimate=cost(0.3),
         name="flip",
     )(*grids)
     all_parts, all_grids = (*parts, far), (*grids, turned)
@@ -517,7 +513,7 @@
         in_specs=[SMEM] + [VMEM] * 3,
         out_specs=[VMEM] * n,
         compiler_params=params(),
-        cost_estimate=cost(0.01),
+        cost_estimate=cost(0.2),
         name="rest",
     )(me, tall, before, after)
     rests = exchange(rests, n, range(n))
@@ -557,13 +553,14 @@
         )(me, *grids, *states, *ties)
 
     if two:
+        firsts, rests = far_first(firsts), far_first(rests)
         crossing, states = sections(False, *firsts)
         back = exchange(crossing, n, far)
         crossing, more = sections(True, *firsts, *rests, crossing[0])
         staying = finished(states + more, *back)
         back += exchange(crossing, n, far)
     else:
-        crossing, states = sections(False, *rests)
+        crossing, states = sections(False, *far_first(rests))
         staying = finished(states)
         back = exchange(crossing, n, far)
     staying = exchange(staying, n, near)

time: 56 us -> 51 us (0.911)
  Pallas kernels: 28.9 us -> 26.1 us
  local copies, waits for them, and re-layouts: 1.93 us -> 0.01 us
  waiting for transfers between devices: 10.4 us -> 9.21 us
  starting transfers between devices: 14.3 us -> 15.3 us
    pallas_call x2 -> x1, Pallas kernels: 6.71 us -> 3.84 us  [pack(): pl.pallas_call(functools.partial(pack_kernel, n, two), out_shape=shapes,...]
    unnamed x8 -> x4, local copies, waits for them, and re-layouts: 1.93 us -> 0.01 us
    ppermute x11, waiting for transfers between devices: 9.07 us -> 8.09 us  [to_partner(): lax.ppermute(array, 'gy', [(i, i ^ s) for i in range(n)])]
    ppermute x11, starting transfers between devices: 9.39 us -> 10.2 us  [to_partner(): lax.ppermute(array, 'gy', [(i, i ^ s) for i in range(n)])]
  transfers between devices with their start and end apart: 13 -> 13, of which waited for: 6 -> 7; matrix products, arithmetic and copies ran while one was open for 0% -> 0% of each run, Pallas kernels for 42% -> 40%
where the time goes in v6:
time: 51 us; the launch traced here: 50.9 us
  Pallas kernels  26.1 us (51%)
  starting transfers between devices  15.3 us (30%)
  waiting for transfers between devices  9.21 us (18%)
    pallas_call x2, Pallas kernels, sections(): pl.pallas_call(functools.partial(section_kernel, n, two, second, far, all...  12.2 us
    ppermute x11, starting transfers between devices, to_partner(): lax.ppermute(array, 'gy', [(i, i ^ s) for i in range(n)])  10.2 us
    ppermute x11, waiting for transfers between devices, to_partner(): lax.ppermute(array, 'gy', [(i, i ^ s) for i in range(n)])  8.09 us
    pallas_call x2, Pallas kernels, grid_of(): pl.pallas_call(functools.partial(grid_kernel, n, rows, slots), out_shape=...  3.85 us
    pallas_call x1, Pallas kernels, pack(): pl.pallas_call(functools.partial(pack_kernel, n, two), out_shape=shapes,...  3.84 us
    ppermute x1, starting transfers between devices, on_device(): after = lax.ppermute(left, 'gx', [(j, i) for i, j in up])  3.1 us
    pallas_call x1, Pallas kernels, finished(): pl.pallas_call(functools.partial(finish_kernel, n, near, parts, len(state...  3.07 us
    ppermute x1, starting transfers between devices, on_device(): before = lax.ppermute(right, 'gx', up)  2.03 us
  transfers between devices with their start and end apart: 13, of which 7 were waited for; matrix products, arithmetic and copies ran while one was open for 0% of the time, Pallas kernels for 40%

profile of v6, /device:TPU:0, one launch (start us, length us, event | category | flops | bytes accessed | tf_op | source)
XLA Modules:
  0.0 50.9 jit_solution(5631794963019912104)
XLA Ops:
  0.0 3.8 %pack.1 = (bf16[13,48,256]{2,1,0:T(8,128)(2,1)}, bf16[13,48,256]{2,1,0:T(8,128)(2,1)}, bf16[13,48,256]{2,1,0:T(8,128)(2,1)}, bf16[13,48,256]{2,1,0:T(8,128)(2,1)}, bf16[13,272,256]{2,1,0:T(8,128)(2,1)}) custom-call(s32[1]{0:T(128)} %bitcast.me_ref, f32[256,256]{1,0:T(8,128)} %refs_0_.1, f32[3,256,256]{2,1,0:T(8,128)} %bitcast.6, f32[256,256]{1,0:T(8,128)} %refs_2_.1, ...), custom_call_target="tpu_custom_call" | custom-call | flops 2000000000 | bytes 6000000 | tf_op jit(solution)/shard_map/pack/pallas_call | solution.py:447
  3.8 3.0 %collective-permute-start = (bf16[13,48,256]{2,1,0:T(8,128)(2,1)}, bf16[13,48,256]{2,1,0:T(8,128)(2,1)S(1)}, u32[]{:S(2)}, u32[]{:S(2)}) collective-permute-start(bf16[13,48,256]{2,1,0:T(8,128)(2,1)} %get-tuple-element.29), channel_id=1, source_target_pairs={{0,2},{1,3},{2,0},{3,1},{4,6},{5,7},{6,4},{7,5},{8,10},{9,11},{10,... | collective-permute-start | bytes 958472 | tf_op jit(solution)/shard_map/ppermute | solution.py:418
  6.9 0.0 collective-permute-start.1
  6.9 0.2 collective-permute-start.2
  7.0 1.9 %grid.2.refs_0_.tie = bf16[1024,256]{1,0:T(8,128)(2,1)S(1)} custom-call(s32[1]{0:T(128)} %bitcast.me_ref), custom_call_target="tpu_custom_call" | custom-call | flops 1000000000 | bytes 3000000 | tf_op jit(solution)/shard_map/grid/pallas_call | solution.py:474
  9.0 2.0 %collective-permute-start.3 = (bf16[13,16,256]{2,1,0:T(8,128)(2,1)S(1)}, bf16[13,16,256]{2,1,0:T(8,128)(2,1)S(1)}, u32[]{:S(2)}, u32[]{:S(2)}) collective-permute-start(bf16[13,16,256]{2,1,0:T(8,128)(2,1)S(1)} %get-tuple-element.36), channel_id=1, source_target_pairs={{0,4},{4,8},{8,12},{12,16},{16,20},{20,24},{24,28},{28,0},{1,5},{5... | collective-permute-start | bytes 319496 | tf_op jit(solution)/shard_map/ppermute | solution.py:498
  11.0 3.1 %collective-permute-start.4 = (bf16[13,16,256]{2,1,0:T(8,128)(2,1)S(1)}, bf16[13,16,256]{2,1,0:T(8,128)(2,1)S(1)}, u32[]{:S(2)}, u32[]{:S(2)}) collective-permute-start(bf16[13,16,256]{2,1,0:T(8,128)(2,1)S(1)} %get-tuple-element.37), channel_id=1, source_target_pairs={{4,0},{8,4},{12,8},{16,12},{20,16},{24,20},{28,24},{0,28},{5,1},{9... | collective-permute-start | bytes 319496 | tf_op jit(solution)/shard_map/ppermute | solution.py:499
  14.1 1.9 %grid.3.refs_1_ = bf16[1024,256]{1,0:T(8,128)(2,1)S(1)} custom-call(s32[1]{0:T(128)} %bitcast.me_ref), custom_call_target="tpu_custom_call" | custom-call | flops 1000000000 | bytes 3000000 | tf_op jit(solution)/shard_map/grid/pallas_call | solution.py:474
  16.1 0.8 %flip.1.refs_2_ = bf16[1024,512]{1,0:T(8,128)(2,1)S(1)} custom-call(bf16[1024,256]{1,0:T(8,128)(2,1)S(1)} %grid.2.refs_0_.tie, bf16[1024,256]{1,0:T(8,128)(2,1)S(1)} %grid.3.refs_1_), custom_call_target="tpu_custom_call" | custom-call | flops 300000000 | bytes 900000 | tf_op jit(solution)/shard_map/flip/pallas_call | solution.py:500
  16.9 0.4 collective-permute-done.3.before
  17.3 0.7 %collective-permute-done.4.after = bf16[13,16,256]{2,1,0:T(8,128)(2,1)S(1)} collective-permute-done((bf16[13,16,256]{2,1,0:T(8,128)(2,1)S(1)}, bf16[13,16,256]{2,1,0:T(8,128)(2,1)S(1)}, u32[]{:S(2)}, u32[]{:S(2)}) %collective-permute-start.4) | collective-permute-done | bytes 106528 | tf_op jit(solution)/shard_map/ppermute | solution.py:499
  18.0 0.3 rest.1
  18.3 1.6 %collective-permute-start.5 = (bf16[13,32,256]{2,1,0:T(8,128)(2,1)S(1)}, bf16[13,32,256]{2,1,0:T(8,128)(2,1)S(1)}, u32[]{:S(2)}, u32[]{:S(2)}) collective-permute-start(bf16[13,32,256]{2,1,0:T(8,128)(2,1)S(1)} %get-tuple-element.39), channel_id=1, source_target_pairs={{0,2},{1,3},{2,0},{3,1},{4,6},{5,7},{6,4},{7,5},{8,10},{9,11},{10,... | collective-permute-start | bytes 638984 | tf_op jit(solution)/shard_map/ppermute | solution.py:418
  19.9 0.0 collective-permute-start.6
  19.9 0.0 collective-permute-done.refs_4_
  19.9 0.7 %collective-permute-start.7 = (bf16[13,32,256]{2,1,0:T(8,128)(2,1)S(1)}, bf16[13,32,256]{2,1,0:T(8,128)(2,1)S(1)}, u32[]{:S(2)}, u32[]{:S(2)}) collective-permute-start(bf16[13,32,256]{2,1,0:T(8,128)(2,1)S(1)} %get-tuple-element.41), channel_id=1, source_target_pairs={{0,1},{1,0},{2,3},{3,2},{4,5},{5,4},{6,7},{7,6},{8,9},{9,8},{10,11... | collective-permute-start | bytes 638984 | tf_op jit(solution)/shard_map/ppermute | solution.py:418
  20.5 1.4 %collective-permute-done.1.refs_5_ = bf16[13,48,256]{2,1,0:T(8,128)(2,1)S(1)} collective-permute-done((bf16[13,48,256]{2,1,0:T(8,128)(2,1)}, bf16[13,48,256]{2,1,0:T(8,128)(2,1)S(1)}, u32[]{:S(2)}, u32[]{:S(2)}) %collective-permute-start.1) | collective-permute-done | bytes 319520 | tf_op jit(solution)/shard_map/ppermute | solution.py:418
  22.0 5.8 %sections.2 = (bf16[13,32,256]{2,1,0:T(8,128)(2,1)S(1)}, bf16[13,32,256]{2,1,0:T(8,128)(2,1)S(1)}, f32[13,48,1024]{2,1,0:T(8,128)S(1)}, f32[13,32,1024]{2,1,0:T(8,128)S(1)}, bf16[416,1024]{1,0:T(8,128)(2,1)S(1)}) custom-call(s32[1]{0:T(128)} %bitcast.me_ref, bf16[1024,256]{1,0:T(8,128)(2,1)S(1)} %grid.2.refs_0_.tie, bf16[1024,256]{1,0:T(8,128)(2,1)S(1)} %grid.3.refs_1_, ...), custom_call_target="tpu_custom_call" | custom-call | flops 6000000000 | bytes 18000000 | tf_op jit(solution)/shard_map/sections/pallas_call | solution.py:527
  27.8 0.1 collective-permute-start.8
  27.9 1.8 %collective-permute-start.9 = (bf16[13,32,256]{2,1,0:T(8,128)(2,1)S(1)}, bf16[13,32,256]{2,1,0:T(8,128)(2,1)S(1)}, u32[]{:S(2)}, u32[]{:S(2)}) collective-permute-start(bf16[13,32,256]{2,1,0:T(8,128)(2,1)S(1)} %get-tuple-element.46), channel_id=1, source_target_pairs={{0,3},{1,2},{2,1},{3,0},{4,7},{5,6},{6,5},{7,4},{8,11},{9,10},{10,... | collective-permute-start | bytes 638984 | tf_op jit(solution)/shard_map/ppermute | solution.py:418
  29.7 0.1 collective-permute-done.6.refs_9_
  29.8 6.4 %sections.3 = (bf16[13,32,256]{2,1,0:T(8,128)(2,1)S(1)}, bf16[13,32,256]{2,1,0:T(8,128)(2,1)S(1)}, f32[13,48,1024]{2,1,0:T(8,128)S(1)}, f32[13,32,1024]{2,1,0:T(8,128)S(1)}, bf16[416,1024]{1,0:T(8,128)(2,1)S(1)}) custom-call(s32[1]{0:T(128)} %bitcast.me_ref, bf16[1024,256]{1,0:T(8,128)(2,1)S(1)} %grid.2.refs_0_.tie, bf16[1024,256]{1,0:T(8,128)(2,1)S(1)} %grid.3.refs_1_, ...), custom_call_target="tpu_custom_call" | custom-call | flops 6000000000 | bytes 18000000 | tf_op jit(solution)/shard_map/sections/pallas_call | solution.py:527
  36.2 1.6 %collective-permute-start.11 = (bf16[13,32,256]{2,1,0:T(8,128)(2,1)S(1)}, bf16[13,32,256]{2,1,0:T(8,128)(2,1)S(1)}, u32[]{:S(2)}, u32[]{:S(2)}) collective-permute-start(bf16[13,32,256]{2,1,0:T(8,128)(2,1)S(1)} %get-tuple-element.49), channel_id=1, source_target_pairs={{0,2},{1,3},{2,0},{3,1},{4,6},{5,7},{6,4},{7,5},{8,10},{9,11},{10,... | collective-permute-start | bytes 638984 | tf_op jit(solution)/shard_map/ppermute | solution.py:418
  37.8 0.5 collective-permute-start.12
  38.3 0.0 collective-permute-done.8.refs_8_.refs_0_.refs_2_
  38.3 1.3 %collective-permute-done.9.refs_9_.refs_1_.refs_3_ = bf16[13,32,256]{2,1,0:T(8,128)(2,1)S(1)} collective-permute-done((bf16[13,32,256]{2,1,0:T(8,128)(2,1)S(1)}, bf16[13,32,256]{2,1,0:T(8,128)(2,1)S(1)}, u32[]{:S(2)}, u32[]{:S(2)}) %collective-permute-start.9) | collective-permute-done | bytes 213024 | tf_op jit(solution)/shard_map/ppermute | solution.py:418
  39.5 3.1 %finish.1 = (f32[13,64,256]{2,1,0:T(8,128)S(1)}, bf16[13,64,256]{2,1,0:T(8,128)(2,1)S(1)}) custom-call(s32[1]{0:T(128)} %bitcast.me_ref, bf16[1024,256]{1,0:T(8,128)(2,1)S(1)} %grid.2.refs_0_.tie, bf16[1024,256]{1,0:T(8,128)(2,1)S(1)} %grid.3.refs_1_, f32[13,48,1024]{2,1,0:T(8,128)S(1)} %get-tuple-element.32.refs_2_, ...), custom_call_target="tpu_custom_call" | custom-call | flops 4000000000 | bytes 12000000 | tf_op jit(solution)/shard_map/finish/pallas_call | solution.py:544
  42.6 0.8 %collective-permute-start.10 = (bf16[13,64,256]{2,1,0:T(8,128)(2,1)S(1)}, bf16[13,64,256]{2,1,0:T(8,128)(2,1)S(1)}, u32[]{:S(2)}, u32[]{:S(2)}) collective-permute-start(bf16[13,64,256]{2,1,0:T(8,128)(2,1)S(1)} %get-tuple-element.48), channel_id=1, source_target_pairs={{0,1},{1,0},{2,3},{3,2},{4,5},{5,4},{6,7},{7,6},{8,9},{9,8},{10,11... | collective-permute-start | bytes 1277960 | tf_op jit(solution)/shard_map/ppermute | solution.py:418
  43.4 1.6 %collective-permute-done.11.refs_2_.refs_4_ = bf16[13,32,256]{2,1,0:T(8,128)(2,1)S(1)} collective-permute-done((bf16[13,32,256]{2,1,0:T(8,128)(2,1)S(1)}, bf16[13,32,256]{2,1,0:T(8,128)(2,1)S(1)}, u32[]{:S(2)}, u32[]{:S(2)}) %collective-permute-start.11) | collective-permute-done | bytes 213024 | tf_op jit(solution)/shard_map/ppermute | solution.py:418
  45.0 3.7 %collective-permute-done.12.refs_3_.refs_5_ = bf16[13,32,256]{2,1,0:T(8,128)(2,1)S(1)} collective-permute-done((bf16[13,32,256]{2,1,0:T(8,128)(2,1)S(1)}, bf16[13,32,256]{2,1,0:T(8,128)(2,1)S(1)}, u32[]{:S(2)}, u32[]{:S(2)}) %collective-permute-start.12) | collective-permute-done | bytes 213024 | tf_op jit(solution)/shard_map/ppermute | solution.py:418
  48.7 0.0 collective-permute-done.10.refs_1_
  48.7 2.0 %unpack.1 = f32[13,256,256]{2,1,0:T(8,128)} custom-call(s32[1]{0:T(128)} %bitcast.me_ref, f32[13,64,256]{2,1,0:T(8,128)S(1)} %get-tuple-element.47.refs_0_, bf16[13,64,256]{2,1,0:T(8,128)(2,1)S(1)} %collective-permute-done.10.refs_1_, bf16[13,32,256]{2,1,0:T(8,128)(2,1)S(1)} %collective-permute-done.8.refs_8_.refs_0_.refs_2_, ...), custom_call_target="tpu_custom_call" | custom-call | flops 3000000000 | bytes 9000000 | tf_op jit(solution)/shard_map/unpack/pallas_call | solution.py:576
  (9 shorter events, 0.0 us)
Async XLA Ops:
  3.8 16.0 %collective-permute-start = (bf16[13,48,256]{2,1,0:T(8,128)(2,1)}, bf16[13,48,256]{2,1,0:T(8,128)(2,1)S(1)}, u32[]{:S(2)}, u32[]{:S(2)}) collective-permute-start(bf16[13,48,256]{2,1,0:T(8,128)(2,1)} %get-tuple-element.29), channel_id=1, source_target_pairs={{0,2},{1,3},{2,0},{3,1},{4,6},{5,7},{6,4},{7,5},{8,10},{9,11},{10,... | collective-permute-start | bytes 958472 | tf_op jit(solution)/shard_map/ppermute | solution.py:418
  6.9 15.1 %collective-permute-start.1 = (bf16[13,48,256]{2,1,0:T(8,128)(2,1)}, bf16[13,48,256]{2,1,0:T(8,128)(2,1)S(1)}, u32[]{:S(2)}, u32[]{:S(2)}) collective-permute-start(bf16[13,48,256]{2,1,0:T(8,128)(2,1)} %get-tuple-element.30), channel_id=1, source_target_pairs={{0,3},{1,2},{2,1},{3,0},{4,7},{5,6},{6,5},{7,4},{8,11},{9,10},{10,... | collective-permute-start | bytes 958472 | tf_op jit(solution)/shard_map/ppermute | solution.py:418
  6.9 2.1 %copy-start = (bf16[13,272,256]{2,1,0:T(8,128)(2,1)S(1)}, bf16[13,272,256]{2,1,0:T(8,128)(2,1)}, u32[]{:S(2)}) copy-start(bf16[13,272,256]{2,1,0:T(8,128)(2,1)} %get-tuple-element.35.tall) | copy-start | bytes 5431300
  6.9 15.1 %collective-permute-start.2 = (bf16[13,48,256]{2,1,0:T(8,128)(2,1)}, bf16[13,48,256]{2,1,0:T(8,128)(2,1)S(1)}, u32[]{:S(2)}, u32[]{:S(2)}) collective-permute-start(bf16[13,48,256]{2,1,0:T(8,128)(2,1)} %get-tuple-element.31), channel_id=1, source_target_pairs={{0,1},{1,0},{2,3},{3,2},{4,5},{5,4},{6,7},{7,6},{8,9},{9,8},{10,11... | collective-permute-start | bytes 958472 | tf_op jit(solution)/shard_map/ppermute | solution.py:418
  9.0 8.3 %collective-permute-start.3 = (bf16[13,16,256]{2,1,0:T(8,128)(2,1)S(1)}, bf16[13,16,256]{2,1,0:T(8,128)(2,1)S(1)}, u32[]{:S(2)}, u32[]{:S(2)}) collective-permute-start(bf16[13,16,256]{2,1,0:T(8,128)(2,1)S(1)} %get-tuple-element.36), channel_id=1, source_target_pairs={{0,4},{4,8},{8,12},{12,16},{16,20},{20,24},{24,28},{28,0},{1,5},{5... | collective-permute-start | bytes 319496 | tf_op jit(solution)/shard_map/ppermute | solution.py:498
  11.0 7.0 %collective-permute-start.4 = (bf16[13,16,256]{2,1,0:T(8,128)(2,1)S(1)}, bf16[13,16,256]{2,1,0:T(8,128)(2,1)S(1)}, u32[]{:S(2)}, u32[]{:S(2)}) collective-permute-start(bf16[13,16,256]{2,1,0:T(8,128)(2,1)S(1)} %get-tuple-element.37), channel_id=1, source_target_pairs={{4,0},{8,4},{12,8},{16,12},{20,16},{24,20},{28,24},{0,28},{5,1},{9... | collective-permute-start | bytes 319496 | tf_op jit(solution)/shard_map/ppermute | solution.py:499
  16.1 5.9 %copy-start.1 = (bf16[13,48,256]{2,1,0:T(8,128)(2,1)S(1)}, bf16[13,48,256]{2,1,0:T(8,128)(2,1)}, u32[]{:S(2)}) copy-start(bf16[13,48,256]{2,1,0:T(8,128)(2,1)} %get-tuple-element.28.refs_3_) | copy-start | bytes 958468
  18.3 11.4 %collective-permute-start.5 = (bf16[13,32,256]{2,1,0:T(8,128)(2,1)S(1)}, bf16[13,32,256]{2,1,0:T(8,128)(2,1)S(1)}, u32[]{:S(2)}, u32[]{:S(2)}) collective-permute-start(bf16[13,32,256]{2,1,0:T(8,128)(2,1)S(1)} %get-tuple-element.39), channel_id=1, source_target_pairs={{0,2},{1,3},{2,0},{3,1},{4,6},{5,7},{6,4},{7,5},{8,10},{9,11},{10,... | collective-permute-start | bytes 638984 | tf_op jit(solution)/shard_map/ppermute | solution.py:418
  19.9 10.0 %collective-permute-start.6 = (bf16[13,32,256]{2,1,0:T(8,128)(2,1)S(1)}, bf16[13,32,256]{2,1,0:T(8,128)(2,1)S(1)}, u32[]{:S(2)}, u32[]{:S(2)}) collective-permute-start(bf16[13,32,256]{2,1,0:T(8,128)(2,1)S(1)} %get-tuple-element.40), channel_id=1, source_target_pairs={{0,3},{1,2},{2,1},{3,0},{4,7},{5,6},{6,5},{7,4},{8,11},{9,10},{10,... | collective-permute-start | bytes 638984 | tf_op jit(solution)/shard_map/ppermute | solution.py:418
  19.9 10.0 %collective-permute-start.7 = (bf16[13,32,256]{2,1,0:T(8,128)(2,1)S(1)}, bf16[13,32,256]{2,1,0:T(8,128)(2,1)S(1)}, u32[]{:S(2)}, u32[]{:S(2)}) collective-permute-start(bf16[13,32,256]{2,1,0:T(8,128)(2,1)S(1)} %get-tuple-element.41), channel_id=1, source_target_pairs={{0,1},{1,0},{2,3},{3,2},{4,5},{5,4},{6,7},{7,6},{8,9},{9,8},{10,11... | collective-permute-start | bytes 638984 | tf_op jit(solution)/shard_map/ppermute | solution.py:418
  27.8 10.5 %collective-permute-start.8 = (bf16[13,32,256]{2,1,0:T(8,128)(2,1)S(1)}, bf16[13,32,256]{2,1,0:T(8,128)(2,1)S(1)}, u32[]{:S(2)}, u32[]{:S(2)}) collective-permute-start(bf16[13,32,256]{2,1,0:T(8,128)(2,1)S(1)} %get-tuple-element.42.refs_11_), channel_id=1, source_target_pairs={{0,2},{1,3},{2,0},{3,1},{4,6},{5,7},{6,4},{7,5},{8,10},{9,11},{10,... | collective-permute-start | bytes 638984 | tf_op jit(solution)/shard_map/ppermute | solution.py:418
  27.9 11.6 %collective-permute-start.9 = (bf16[13,32,256]{2,1,0:T(8,128)(2,1)S(1)}, bf16[13,32,256]{2,1,0:T(8,128)(2,1)S(1)}, u32[]{:S(2)}, u32[]{:S(2)}) collective-permute-start(bf16[13,32,256]{2,1,0:T(8,128)(2,1)S(1)} %get-tuple-element.46), channel_id=1, source_target_pairs={{0,3},{1,2},{2,1},{3,0},{4,7},{5,6},{6,5},{7,4},{8,11},{9,10},{10,... | collective-permute-start | bytes 638984 | tf_op jit(solution)/shard_map/ppermute | solution.py:418
  36.2 8.8 %collective-permute-start.11 = (bf16[13,32,256]{2,1,0:T(8,128)(2,1)S(1)}, bf16[13,32,256]{2,1,0:T(8,128)(2,1)S(1)}, u32[]{:S(2)}, u32[]{:S(2)}) collective-permute-start(bf16[13,32,256]{2,1,0:T(8,128)(2,1)S(1)} %get-tuple-element.49), channel_id=1, source_target_pairs={{0,2},{1,3},{2,0},{3,1},{4,6},{5,7},{6,4},{7,5},{8,10},{9,11},{10,... | collective-permute-start | bytes 638984 | tf_op jit(solution)/shard_map/ppermute | solution.py:418
  37.8 10.9 %collective-permute-start.12 = (bf16[13,32,256]{2,1,0:T(8,128)(2,1)S(1)}, bf16[13,32,256]{2,1,0:T(8,128)(2,1)S(1)}, u32[]{:S(2)}, u32[]{:S(2)}) collective-permute-start(bf16[13,32,256]{2,1,0:T(8,128)(2,1)S(1)} %get-tuple-element.50), channel_id=1, source_target_pairs={{0,3},{1,2},{2,1},{3,0},{4,7},{5,6},{6,5},{7,4},{8,11},{9,10},{10,... | collective-permute-start | bytes 638984 | tf_op jit(solution)/shard_map/ppermute | solution.py:418
  42.6 6.1 %collective-permute-start.10 = (bf16[13,64,256]{2,1,0:T(8,128)(2,1)S(1)}, bf16[13,64,256]{2,1,0:T(8,128)(2,1)S(1)}, u32[]{:S(2)}, u32[]{:S(2)}) collective-permute-start(bf16[13,64,256]{2,1,0:T(8,128)(2,1)S(1)} %get-tuple-element.48), channel_id=1, source_target_pairs={{0,1},{1,0},{2,3},{3,2},{4,5},{5,4},{6,7},{7,6},{8,9},{9,8},{10,11... | collective-permute-start | bytes 1277960 | tf_op jit(solution)/shard_map/ppermute | solution.py:418

commit v7 on v6

--- a/solution.py
+++ b/solution.py
@@ -94,15 +94,18 @@
     return out
 
 
-def along_of(fx):
-    count = fx.shape[0]
-    total = None
-    for k in range(3):
-        upper = pltpu.roll(fx, count - (k + 1), 0)
-        lower = pltpu.roll(fx, k + 1, 0)
-        term = coeffs[k] * (upper - lower)
-        total = term if total is None else total + term
-    return total
+def along_of(fx, turned, f):
+    count = fx.shape[0] // 8
+    turned[f] = fx
+    x = [turned[f, pl.ds(v, 8, stride=count), :] for v in range(count)]
+    x = [pltpu.roll(y, 1, 0) for y in x[-3:]] + x + [pltpu.roll(y, 7, 0) for y in x[:3]]
+    for v in range(count):
+        total = None
+        for k in range(3):
+            term = coeffs[k] * (x[3 + v + k + 1] - x[3 + v - k - 1])
+            total = term if total is None else total + term
+        turned[MOMENTS + f, pl.ds(v, 8, stride=count), :] = total
+    return turned.at[MOMENTS + f]
 
 
 def message_start(me, s, slab):
@@ -110,36 +113,39 @@
     return pl.multiple_of(to * slab + jnp.where(to % 2 == 0, slab // 2, 0), 16)
 
 
+GROUPS = ((0, 1), (1, 4), (4, 5), (5, 8), (8, 10), (10, 13))
+
+
 def pack_kernel(n, two, me_ref, *refs):
-    inputs, refs = refs[:5], refs[5:]
+    (rho, vel, temp, stress, heat), refs = refs[:5], refs[5:]
+    inputs = (rho, vel, temp, stress.at[0:3], stress.at[3:5], heat)
     count = n if two else 0
     outs, (strip, given, arrived), refs = refs[: count + 1], refs[count + 1 : count + 4], refs[count + 4 :]
     held, left_at = refs[:-1], refs[-1]
     rows, cols = given.shape[1:]
     slab = cols // n
     me = me_ref[0]
-    copies, end = [], 0
-    for k, src in enumerate(inputs):
-        first, end = end, end + (1 if len(src.shape) == 2 else src.shape[0])
-        dst = given.at[first] if len(src.shape) == 2 else given.at[first:end]
-        copies.append((first, end, pltpu.make_async_copy(src, dst, arrived.at[k])))
-        copies[k][2].start()
+    copies = []
+    for k, (first, end) in enumerate(GROUPS):
+        dst = given.at[first] if len(inputs[k].shape) == 2 else given.at[first:end]
+        copies.append(pltpu.make_async_copy(inputs[k], dst, arrived.at[k]))
+        copies[k].start()
     strip[0:HALO, :] = jnp.zeros((HALO, rows), jnp.float32)
     strip[HALO + cols :, :] = jnp.zeros((HALO, rows), jnp.float32)
     leaving = []
     done = 0
-    for at, (first, end, copy) in enumerate(copies):
-        copy.wait()
+    for at, (first, end) in enumerate(GROUPS):
+        copies[at].wait()
         for f in range(first, end):
             strip[HALO : HALO + cols, :] = code(f, given[f]).T
             for s in range(count):
                 here = pl.ds(message_start(me, s, slab), held[s].shape[1])
                 held[s][f] = strip[here, :].astype(jnp.bfloat16)
             held[count][f] = strip[...].astype(jnp.bfloat16)
-        if at % 2 == 0:
+        if at in (1, 3, 4, 5):
             span = pl.ds(done, end - done)
             for k, out in enumerate(outs):
-                copy = pltpu.make_async_copy(held[k].at[span], out.at[span], left_at.at[k, at // 2])
+                copy = pltpu.make_async_copy(held[k].at[span], out.at[span], left_at.at[k, at - 1])
                 copy.start()
                 leaving.append(copy)
             done = end
@@ -284,7 +290,7 @@
     if second:
         rests, refs = in_slots(refs[:n]), refs[n + 1 :]
     outs, refs = refs[: len(far)], refs[len(far) :]
-    u1, r0, fy1, u0, fy0, product = refs
+    u1, r0, fy1, u0, fy0, product, turned = refs
     wide, size = u0.shape[1:]
     rows = size // n
     core = wide - 2 * HALO
@@ -326,7 +332,7 @@
             new = []
             for f in range(MOMENTS):
                 across = product[f * wide : (f + 1) * wide, there]
-                rate = -(along_of(flux(u, 0, f)) + across)
+                rate = -(along_of(flux(u, 0, f), turned, f)[...] + across)
                 if src[f] is not None:
                     rate = rate + src[f]
                 r0[f, :, here] = rate[middle]
@@ -336,16 +342,16 @@
             for f in range(MOMENTS):
                 fy1[f * core : (f + 1) * core, here] = flux(inner, 1, f).astype(jnp.bfloat16)
 
-    finish(n, far, me_ref, parts, grids, u1, r0, fy1, outs, product)
+    finish(n, far, me_ref, parts, grids, u1, r0, fy1, outs, product, turned)
 
 
 def finish_kernel(n, near, parts, chunks, me_ref, *refs):
     grids, refs = refs[: len(parts)], refs[len(parts) :]
-    states, outs, product = refs[: 3 * chunks], refs[-1 - len(near) : -1], refs[-1]
+    states, outs, product, turned = refs[: 3 * chunks], refs[-2 - len(near) : -2], *refs[-2:]
     core = outs[0].shape[1] // chunks
     for c in range(chunks):
         part = [out.at[:, c * core : (c + 1) * core, :] for out in outs]
-        finish(n, near, me_ref, parts, grids, *states[3 * c : 3 * c + 3], part, product)
+        finish(n, near, me_ref, parts, grids, *states[3 * c : 3 * c + 3], part, product, turned)
 
 
 def walls(me, s, p, n, rows, count):
@@ -355,7 +361,7 @@
     return jnp.where(line == 0, 1.0, jnp.where(line == n * rows - 1, -1.0, 0.0))
 
 
-def finish(n, slots, me_ref, parts, grids, u1, r0, fy1, outs, product):
+def finish(n, slots, me_ref, parts, grids, u1, r0, fy1, outs, product, turned):
     wide, size = u1.shape[1:]
     rows = size // n
     core = wide - 2 * HALO
@@ -375,7 +381,7 @@
             src = sources(inner, walls(me, s, p, n, rows, core))
             for f in range(MOMENTS):
                 across = product[f * core : (f + 1) * core, there]
-                rate = -(along_of(flux(u, 0, f))[middle] + across)
+                rate = -(along_of(flux(u, 0, f), turned, f)[middle, :] + across)
                 if src[f] is not None:
                     rate = rate + src[f]
                 rate = 0.5 * (r0[f, :, here] + rate)
@@ -452,10 +458,10 @@
             scratch_shapes=[
                 pltpu.VMEM((cols + 2 * HALO, rows), jnp.float32),
                 pltpu.VMEM((MOMENTS, rows, cols), jnp.float32),
-                pltpu.SemaphoreType.DMA((len(arrays),)),
+                pltpu.SemaphoreType.DMA((len(GROUPS),)),
             ]
             + [pltpu.VMEM(x.shape, x.dtype) for x in shapes]
-            + [pltpu.SemaphoreType.DMA((len(shapes), 3))],
+            + [pltpu.SemaphoreType.DMA((len(shapes), len(GROUPS)))],
             compiler_params=params(56),
             cost_estimate=cost(2),
             name="pack",
@@ -533,6 +539,7 @@
                 pltpu.VMEM((MOMENTS, wide, size), jnp.float32),
                 pltpu.VMEM((MOMENTS * wide, size), half),
                 pltpu.VMEM((MOMENTS * wide, rows), jnp.float32),
+                pltpu.VMEM((2 * MOMENTS, wide, lane), jnp.float32),
             ],
             compiler_params=params(24),
             cost_estimate=cost(6),
@@ -546,7 +553,10 @@
             out_shape=[message(slab, jnp.float32)] + [message(slab)] * (len(near) - 1),
             in_specs=[SMEM] + [VMEM] * (len(states) + 2) + [ANY] * len(ties),
             out_specs=[VMEM] * len(near),
-            scratch_shapes=[pltpu.VMEM((MOMENTS * core, rows), jnp.float32)],
+            scratch_shapes=[
+                pltpu.VMEM((MOMENTS * core, rows), jnp.float32),
+                pltpu.VMEM((2 * MOMENTS, wide, lane), jnp.float32),
+            ],
             compiler_params=params(24),
             cost_estimate=cost(4),
             name="finish",

time: 51 us -> 50.4 us (0.988)
  Pallas kernels: 26.1 us -> 23.5 us
  waiting for transfers between devices: 9.21 us -> 11.3 us
    ppermute x11, waiting for transfers between devices: 8.09 us -> 10.2 us  [to_partner(): lax.ppermute(array, 'gy', [(i, i ^ s) for i in range(n)])]
    pallas_call x2, Pallas kernels: 12.2 us -> 10.2 us  [sections(): pl.pallas_call(functools.partial(section_kernel, n, two, second, far, all...]
  transfers between devices with their start and end apart: 13 -> 13, of which waited for: 7 -> 7; matrix products, arithmetic and copies ran while one was open for 0% -> 0% of each run, Pallas kernels for 40% -> 36%
where the time goes in v7:
time: 50.4 us; the launch traced here: 50.3 us
  Pallas kernels  23.5 us (47%)
  starting transfers between devices  15.2 us (30%)
  waiting for transfers between devices  11.3 us (22%)
    ppermute x11, waiting for transfers between devices, to_partner(): lax.ppermute(array, 'gy', [(i, i ^ s) for i in range(n)])  10.2 us
    pallas_call x2, Pallas kernels, sections(): pl.pallas_call(functools.partial(section_kernel, n, two, second, far, all...  10.2 us
    ppermute x11, starting transfers between devices, to_partner(): lax.ppermute(array, 'gy', [(i, i ^ s) for i in range(n)])  10.1 us
    pallas_call x2, Pallas kernels, grid_of(): pl.pallas_call(functools.partial(grid_kernel, n, rows, slots), out_shape=...  3.85 us
    pallas_call x1, Pallas kernels, pack(): pl.pallas_call(functools.partial(pack_kernel, n, two), out_shape=shapes,...  3.61 us
    ppermute x1, starting transfers between devices, on_device(): after = lax.ppermute(left, 'gx', [(j, i) for i, j in up])  3.1 us
    pallas_call x1, Pallas kernels, finished(): pl.pallas_call(functools.partial(finish_kernel, n, near, parts, len(state...  2.7 us
    ppermute x1, starting transfers between devices, on_device(): before = lax.ppermute(right, 'gx', up)  2.03 us
  transfers between devices with their start and end apart: 13, of which 7 were waited for; matrix products, arithmetic and copies ran while one was open for 0% of the time, Pallas kernels for 36%

profile of v7, /device:TPU:0, one launch (start us, length us, event | category | flops | bytes accessed | tf_op | source)
XLA Modules:
  0.0 50.3 jit_solution(6854346479286355965)
XLA Ops:
  0.0 3.6 %pack.1 = (bf16[13,48,256]{2,1,0:T(8,128)(2,1)}, bf16[13,48,256]{2,1,0:T(8,128)(2,1)}, bf16[13,48,256]{2,1,0:T(8,128)(2,1)}, bf16[13,48,256]{2,1,0:T(8,128)(2,1)}, bf16[13,272,256]{2,1,0:T(8,128)(2,1)}) custom-call(s32[1]{0:T(128)} %bitcast.me_ref, f32[256,256]{1,0:T(8,128)} %refs_0_.1, f32[3,256,256]{2,1,0:T(8,128)} %bitcast.6, f32[256,256]{1,0:T(8,128)} %refs_2_.1, ...), custom_call_target="tpu_custom_call" | custom-call | flops 2000000000 | bytes 6000000 | tf_op jit(solution)/shard_map/pack/pallas_call | solution.py:453
  3.6 3.0 %collective-permute-start = (bf16[13,48,256]{2,1,0:T(8,128)(2,1)}, bf16[13,48,256]{2,1,0:T(8,128)(2,1)S(1)}, u32[]{:S(2)}, u32[]{:S(2)}) collective-permute-start(bf16[13,48,256]{2,1,0:T(8,128)(2,1)} %get-tuple-element.29), channel_id=1, source_target_pairs={{0,2},{1,3},{2,0},{3,1},{4,6},{5,7},{6,4},{7,5},{8,10},{9,11},{10,... | collective-permute-start | bytes 958472 | tf_op jit(solution)/shard_map/ppermute | solution.py:424
  6.6 0.2 collective-permute-start.2
  6.8 1.9 %grid.2.refs_0_.tie = bf16[1024,256]{1,0:T(8,128)(2,1)S(1)} custom-call(s32[1]{0:T(128)} %bitcast.me_ref), custom_call_target="tpu_custom_call" | custom-call | flops 1000000000 | bytes 3000000 | tf_op jit(solution)/shard_map/grid/pallas_call | solution.py:480
  8.8 2.0 %collective-permute-start.3 = (bf16[13,16,256]{2,1,0:T(8,128)(2,1)S(1)}, bf16[13,16,256]{2,1,0:T(8,128)(2,1)S(1)}, u32[]{:S(2)}, u32[]{:S(2)}) collective-permute-start(bf16[13,16,256]{2,1,0:T(8,128)(2,1)S(1)} %get-tuple-element.36), channel_id=1, source_target_pairs={{0,4},{4,8},{8,12},{12,16},{16,20},{20,24},{24,28},{28,0},{1,5},{5... | collective-permute-start | bytes 319496 | tf_op jit(solution)/shard_map/ppermute | solution.py:504
  10.8 3.1 %collective-permute-start.4 = (bf16[13,16,256]{2,1,0:T(8,128)(2,1)S(1)}, bf16[13,16,256]{2,1,0:T(8,128)(2,1)S(1)}, u32[]{:S(2)}, u32[]{:S(2)}) collective-permute-start(bf16[13,16,256]{2,1,0:T(8,128)(2,1)S(1)} %get-tuple-element.37), channel_id=1, source_target_pairs={{4,0},{8,4},{12,8},{16,12},{20,16},{24,20},{28,24},{0,28},{5,1},{9... | collective-permute-start | bytes 319496 | tf_op jit(solution)/shard_map/ppermute | solution.py:505
  13.9 1.9 %grid.3.refs_1_ = bf16[1024,256]{1,0:T(8,128)(2,1)S(1)} custom-call(s32[1]{0:T(128)} %bitcast.me_ref), custom_call_target="tpu_custom_call" | custom-call | flops 1000000000 | bytes 3000000 | tf_op jit(solution)/shard_map/grid/pallas_call | solution.py:480
  15.9 0.8 %flip.1.refs_2_ = bf16[1024,512]{1,0:T(8,128)(2,1)S(1)} custom-call(bf16[1024,256]{1,0:T(8,128)(2,1)S(1)} %grid.2.refs_0_.tie, bf16[1024,256]{1,0:T(8,128)(2,1)S(1)} %grid.3.refs_1_), custom_call_target="tpu_custom_call" | custom-call | flops 300000000 | bytes 900000 | tf_op jit(solution)/shard_map/flip/pallas_call | solution.py:506
  16.7 0.4 collective-permute-done.3.before
  17.1 0.7 %collective-permute-done.4.after = bf16[13,16,256]{2,1,0:T(8,128)(2,1)S(1)} collective-permute-done((bf16[13,16,256]{2,1,0:T(8,128)(2,1)S(1)}, bf16[13,16,256]{2,1,0:T(8,128)(2,1)S(1)}, u32[]{:S(2)}, u32[]{:S(2)}) %collective-permute-start.4) | collective-permute-done | bytes 106528 | tf_op jit(solution)/shard_map/ppermute | solution.py:505
  17.8 0.3 rest.1
  18.1 1.6 %collective-permute-start.5 = (bf16[13,32,256]{2,1,0:T(8,128)(2,1)S(1)}, bf16[13,32,256]{2,1,0:T(8,128)(2,1)S(1)}, u32[]{:S(2)}, u32[]{:S(2)}) collective-permute-start(bf16[13,32,256]{2,1,0:T(8,128)(2,1)S(1)} %get-tuple-element.39), channel_id=1, source_target_pairs={{0,2},{1,3},{2,0},{3,1},{4,6},{5,7},{6,4},{7,5},{8,10},{9,11},{10,... | collective-permute-start | bytes 638984 | tf_op jit(solution)/shard_map/ppermute | solution.py:424
  19.6 0.0 collective-permute-start.6
  19.6 0.0 collective-permute-done.refs_4_
  19.6 0.7 %collective-permute-start.7 = (bf16[13,32,256]{2,1,0:T(8,128)(2,1)S(1)}, bf16[13,32,256]{2,1,0:T(8,128)(2,1)S(1)}, u32[]{:S(2)}, u32[]{:S(2)}) collective-permute-start(bf16[13,32,256]{2,1,0:T(8,128)(2,1)S(1)} %get-tuple-element.41), channel_id=1, source_target_pairs={{0,1},{1,0},{2,3},{3,2},{4,5},{5,4},{6,7},{7,6},{8,9},{9,8},{10,11... | collective-permute-start | bytes 638984 | tf_op jit(solution)/shard_map/ppermute | solution.py:424
  20.3 1.4 %collective-permute-done.1.refs_5_ = bf16[13,48,256]{2,1,0:T(8,128)(2,1)S(1)} collective-permute-done((bf16[13,48,256]{2,1,0:T(8,128)(2,1)}, bf16[13,48,256]{2,1,0:T(8,128)(2,1)S(1)}, u32[]{:S(2)}, u32[]{:S(2)}) %collective-permute-start.1) | collective-permute-done | bytes 319520 | tf_op jit(solution)/shard_map/ppermute | solution.py:424
  21.7 0.0 collective-permute-done.2.refs_6_
  21.7 4.8 %sections.2 = (bf16[13,32,256]{2,1,0:T(8,128)(2,1)S(1)}, bf16[13,32,256]{2,1,0:T(8,128)(2,1)S(1)}, f32[13,48,1024]{2,1,0:T(8,128)S(1)}, f32[13,32,1024]{2,1,0:T(8,128)S(1)}, bf16[416,1024]{1,0:T(8,128)(2,1)S(1)}) custom-call(s32[1]{0:T(128)} %bitcast.me_ref, bf16[1024,256]{1,0:T(8,128)(2,1)S(1)} %grid.2.refs_0_.tie, bf16[1024,256]{1,0:T(8,128)(2,1)S(1)} %grid.3.refs_1_, ...), custom_call_target="tpu_custom_call" | custom-call | flops 6000000000 | bytes 18000000 | tf_op jit(solution)/shard_map/sections/pallas_call | solution.py:533
  26.5 0.1 collective-permute-start.8
  26.7 1.8 %collective-permute-start.9 = (bf16[13,32,256]{2,1,0:T(8,128)(2,1)S(1)}, bf16[13,32,256]{2,1,0:T(8,128)(2,1)S(1)}, u32[]{:S(2)}, u32[]{:S(2)}) collective-permute-start(bf16[13,32,256]{2,1,0:T(8,128)(2,1)S(1)} %get-tuple-element.46), channel_id=1, source_target_pairs={{0,3},{1,2},{2,1},{3,0},{4,7},{5,6},{6,5},{7,4},{8,11},{9,10},{10,... | collective-permute-start | bytes 638984 | tf_op jit(solution)/shard_map/ppermute | solution.py:424
  28.5 0.0 collective-permute-done.5.refs_8_
  28.5 1.7 %collective-permute-done.6.refs_9_ = bf16[13,32,256]{2,1,0:T(8,128)(2,1)S(1)} collective-permute-done((bf16[13,32,256]{2,1,0:T(8,128)(2,1)S(1)}, bf16[13,32,256]{2,1,0:T(8,128)(2,1)S(1)}, u32[]{:S(2)}, u32[]{:S(2)}) %collective-permute-start.6) | collective-permute-done | bytes 213024 | tf_op jit(solution)/shard_map/ppermute | solution.py:424
  30.2 5.4 %sections.3 = (bf16[13,32,256]{2,1,0:T(8,128)(2,1)S(1)}, bf16[13,32,256]{2,1,0:T(8,128)(2,1)S(1)}, f32[13,48,1024]{2,1,0:T(8,128)S(1)}, f32[13,32,1024]{2,1,0:T(8,128)S(1)}, bf16[416,1024]{1,0:T(8,128)(2,1)S(1)}) custom-call(s32[1]{0:T(128)} %bitcast.me_ref, bf16[1024,256]{1,0:T(8,128)(2,1)S(1)} %grid.2.refs_0_.tie, bf16[1024,256]{1,0:T(8,128)(2,1)S(1)} %grid.3.refs_1_, ...), custom_call_target="tpu_custom_call" | custom-call | flops 6000000000 | bytes 18000000 | tf_op jit(solution)/shard_map/sections/pallas_call | solution.py:533
  35.6 0.8 %collective-permute-start.11 = (bf16[13,32,256]{2,1,0:T(8,128)(2,1)S(1)}, bf16[13,32,256]{2,1,0:T(8,128)(2,1)S(1)}, u32[]{:S(2)}, u32[]{:S(2)}) collective-permute-start(bf16[13,32,256]{2,1,0:T(8,128)(2,1)S(1)} %get-tuple-element.49), channel_id=1, source_target_pairs={{0,2},{1,3},{2,0},{3,1},{4,6},{5,7},{6,4},{7,5},{8,10},{9,11},{10,... | collective-permute-start | bytes 638984 | tf_op jit(solution)/shard_map/ppermute | solution.py:424
  36.4 1.3 %collective-permute-start.12 = (bf16[13,32,256]{2,1,0:T(8,128)(2,1)S(1)}, bf16[13,32,256]{2,1,0:T(8,128)(2,1)S(1)}, u32[]{:S(2)}, u32[]{:S(2)}) collective-permute-start(bf16[13,32,256]{2,1,0:T(8,128)(2,1)S(1)} %get-tuple-element.50), channel_id=1, source_target_pairs={{0,3},{1,2},{2,1},{3,0},{4,7},{5,6},{6,5},{7,4},{8,11},{9,10},{10,... | collective-permute-start | bytes 638984 | tf_op jit(solution)/shard_map/ppermute | solution.py:424
  37.7 1.5 %collective-permute-done.9.refs_9_.refs_1_.refs_3_ = bf16[13,32,256]{2,1,0:T(8,128)(2,1)S(1)} collective-permute-done((bf16[13,32,256]{2,1,0:T(8,128)(2,1)S(1)}, bf16[13,32,256]{2,1,0:T(8,128)(2,1)S(1)}, u32[]{:S(2)}, u32[]{:S(2)}) %collective-permute-start.9) | collective-permute-done | bytes 213024 | tf_op jit(solution)/shard_map/ppermute | solution.py:424
  39.2 2.7 %finish.1 = (f32[13,64,256]{2,1,0:T(8,128)S(1)}, bf16[13,64,256]{2,1,0:T(8,128)(2,1)S(1)}) custom-call(s32[1]{0:T(128)} %bitcast.me_ref, bf16[1024,256]{1,0:T(8,128)(2,1)S(1)} %grid.2.refs_0_.tie, bf16[1024,256]{1,0:T(8,128)(2,1)S(1)} %grid.3.refs_1_, f32[13,48,1024]{2,1,0:T(8,128)S(1)} %get-tuple-element.32.refs_2_, ...), custom_call_target="tpu_custom_call" | custom-call | flops 4000000000 | bytes 12000000 | tf_op jit(solution)/shard_map/finish/pallas_call | solution.py:551
  41.9 0.6 %collective-permute-start.10 = (bf16[13,64,256]{2,1,0:T(8,128)(2,1)S(1)}, bf16[13,64,256]{2,1,0:T(8,128)(2,1)S(1)}, u32[]{:S(2)}, u32[]{:S(2)}) collective-permute-start(bf16[13,64,256]{2,1,0:T(8,128)(2,1)S(1)} %get-tuple-element.48), channel_id=1, source_target_pairs={{0,1},{1,0},{2,3},{3,2},{4,5},{5,4},{6,7},{7,6},{8,9},{9,8},{10,11... | collective-permute-start | bytes 1277960 | tf_op jit(solution)/shard_map/ppermute | solution.py:424
  42.6 2.0 %collective-permute-done.11.refs_2_.refs_4_ = bf16[13,32,256]{2,1,0:T(8,128)(2,1)S(1)} collective-permute-done((bf16[13,32,256]{2,1,0:T(8,128)(2,1)S(1)}, bf16[13,32,256]{2,1,0:T(8,128)(2,1)S(1)}, u32[]{:S(2)}, u32[]{:S(2)}) %collective-permute-start.11) | collective-permute-done | bytes 213024 | tf_op jit(solution)/shard_map/ppermute | solution.py:424
  44.5 3.5 %collective-permute-done.12.refs_3_.refs_5_ = bf16[13,32,256]{2,1,0:T(8,128)(2,1)S(1)} collective-permute-done((bf16[13,32,256]{2,1,0:T(8,128)(2,1)S(1)}, bf16[13,32,256]{2,1,0:T(8,128)(2,1)S(1)}, u32[]{:S(2)}, u32[]{:S(2)}) %collective-permute-start.12) | collective-permute-done | bytes 213024 | tf_op jit(solution)/shard_map/ppermute | solution.py:424
  48.1 0.0 collective-permute-done.10.refs_1_
  48.1 2.0 %unpack.1 = f32[13,256,256]{2,1,0:T(8,128)} custom-call(s32[1]{0:T(128)} %bitcast.me_ref, f32[13,64,256]{2,1,0:T(8,128)S(1)} %get-tuple-element.47.refs_0_, bf16[13,64,256]{2,1,0:T(8,128)(2,1)S(1)} %collective-permute-done.10.refs_1_, bf16[13,32,256]{2,1,0:T(8,128)(2,1)S(1)} %collective-permute-done.8.refs_8_.refs_0_.refs_2_, ...), custom_call_target="tpu_custom_call" | custom-call | flops 3000000000 | bytes 9000000 | tf_op jit(solution)/shard_map/unpack/pallas_call | solution.py:586
  (9 shorter events, 0.0 us)
Async XLA Ops:
  3.6 16.0 %collective-permute-start = (bf16[13,48,256]{2,1,0:T(8,128)(2,1)}, bf16[13,48,256]{2,1,0:T(8,128)(2,1)S(1)}, u32[]{:S(2)}, u32[]{:S(2)}) collective-permute-start(bf16[13,48,256]{2,1,0:T(8,128)(2,1)} %get-tuple-element.29), channel_id=1, source_target_pairs={{0,2},{1,3},{2,0},{3,1},{4,6},{5,7},{6,4},{7,5},{8,10},{9,11},{10,... | collective-permute-start | bytes 958472 | tf_op jit(solution)/shard_map/ppermute | solution.py:424
  6.6 15.1 %collective-permute-start.1 = (bf16[13,48,256]{2,1,0:T(8,128)(2,1)}, bf16[13,48,256]{2,1,0:T(8,128)(2,1)S(1)}, u32[]{:S(2)}, u32[]{:S(2)}) collective-permute-start(bf16[13,48,256]{2,1,0:T(8,128)(2,1)} %get-tuple-element.30), channel_id=1, source_target_pairs={{0,3},{1,2},{2,1},{3,0},{4,7},{5,6},{6,5},{7,4},{8,11},{9,10},{10,... | collective-permute-start | bytes 958472 | tf_op jit(solution)/shard_map/ppermute | solution.py:424
  6.6 2.1 %copy-start = (bf16[13,272,256]{2,1,0:T(8,128)(2,1)S(1)}, bf16[13,272,256]{2,1,0:T(8,128)(2,1)}, u32[]{:S(2)}) copy-start(bf16[13,272,256]{2,1,0:T(8,128)(2,1)} %get-tuple-element.35.tall) | copy-start | bytes 5431300
  6.6 15.1 %collective-permute-start.2 = (bf16[13,48,256]{2,1,0:T(8,128)(2,1)}, bf16[13,48,256]{2,1,0:T(8,128)(2,1)S(1)}, u32[]{:S(2)}, u32[]{:S(2)}) collective-permute-start(bf16[13,48,256]{2,1,0:T(8,128)(2,1)} %get-tuple-element.31), channel_id=1, source_target_pairs={{0,1},{1,0},{2,3},{3,2},{4,5},{5,4},{6,7},{7,6},{8,9},{9,8},{10,11... | collective-permute-start | bytes 958472 | tf_op jit(solution)/shard_map/ppermute | solution.py:424
  8.8 8.3 %collective-permute-start.3 = (bf16[13,16,256]{2,1,0:T(8,128)(2,1)S(1)}, bf16[13,16,256]{2,1,0:T(8,128)(2,1)S(1)}, u32[]{:S(2)}, u32[]{:S(2)}) collective-permute-start(bf16[13,16,256]{2,1,0:T(8,128)(2,1)S(1)} %get-tuple-element.36), channel_id=1, source_target_pairs={{0,4},{4,8},{8,12},{12,16},{16,20},{20,24},{24,28},{28,0},{1,5},{5... | collective-permute-start | bytes 319496 | tf_op jit(solution)/shard_map/ppermute | solution.py:504
  10.8 7.0 %collective-permute-start.4 = (bf16[13,16,256]{2,1,0:T(8,128)(2,1)S(1)}, bf16[13,16,256]{2,1,0:T(8,128)(2,1)S(1)}, u32[]{:S(2)}, u32[]{:S(2)}) collective-permute-start(bf16[13,16,256]{2,1,0:T(8,128)(2,1)S(1)} %get-tuple-element.37), channel_id=1, source_target_pairs={{4,0},{8,4},{12,8},{16,12},{20,16},{24,20},{28,24},{0,28},{5,1},{9... | collective-permute-start | bytes 319496 | tf_op jit(solution)/shard_map/ppermute | solution.py:505
  15.8 5.9 %copy-start.1 = (bf16[13,48,256]{2,1,0:T(8,128)(2,1)S(1)}, bf16[13,48,256]{2,1,0:T(8,128)(2,1)}, u32[]{:S(2)}) copy-start(bf16[13,48,256]{2,1,0:T(8,128)(2,1)} %get-tuple-element.28.refs_3_) | copy-start | bytes 958468
  18.1 10.4 %collective-permute-start.5 = (bf16[13,32,256]{2,1,0:T(8,128)(2,1)S(1)}, bf16[13,32,256]{2,1,0:T(8,128)(2,1)S(1)}, u32[]{:S(2)}, u32[]{:S(2)}) collective-permute-start(bf16[13,32,256]{2,1,0:T(8,128)(2,1)S(1)} %get-tuple-element.39), channel_id=1, source_target_pairs={{0,2},{1,3},{2,0},{3,1},{4,6},{5,7},{6,4},{7,5},{8,10},{9,11},{10,... | collective-permute-start | bytes 638984 | tf_op jit(solution)/shard_map/ppermute | solution.py:424
  19.6 10.6 %collective-permute-start.6 = (bf16[13,32,256]{2,1,0:T(8,128)(2,1)S(1)}, bf16[13,32,256]{2,1,0:T(8,128)(2,1)S(1)}, u32[]{:S(2)}, u32[]{:S(2)}) collective-permute-start(bf16[13,32,256]{2,1,0:T(8,128)(2,1)S(1)} %get-tuple-element.40), channel_id=1, source_target_pairs={{0,3},{1,2},{2,1},{3,0},{4,7},{5,6},{6,5},{7,4},{8,11},{9,10},{10,... | collective-permute-start | bytes 638984 | tf_op jit(solution)/shard_map/ppermute | solution.py:424
  19.6 10.6 %collective-permute-start.7 = (bf16[13,32,256]{2,1,0:T(8,128)(2,1)S(1)}, bf16[13,32,256]{2,1,0:T(8,128)(2,1)S(1)}, u32[]{:S(2)}, u32[]{:S(2)}) collective-permute-start(bf16[13,32,256]{2,1,0:T(8,128)(2,1)S(1)} %get-tuple-element.41), channel_id=1, source_target_pairs={{0,1},{1,0},{2,3},{3,2},{4,5},{5,4},{6,7},{7,6},{8,9},{9,8},{10,11... | collective-permute-start | bytes 638984 | tf_op jit(solution)/shard_map/ppermute | solution.py:424
  26.5 11.2 %collective-permute-start.8 = (bf16[13,32,256]{2,1,0:T(8,128)(2,1)S(1)}, bf16[13,32,256]{2,1,0:T(8,128)(2,1)S(1)}, u32[]{:S(2)}, u32[]{:S(2)}) collective-permute-start(bf16[13,32,256]{2,1,0:T(8,128)(2,1)S(1)} %get-tuple-element.42.refs_11_), channel_id=1, source_target_pairs={{0,2},{1,3},{2,0},{3,1},{4,6},{5,7},{6,4},{7,5},{8,10},{9,11},{10,... | collective-permute-start | bytes 638984 | tf_op jit(solution)/shard_map/ppermute | solution.py:424
  26.7 12.6 %collective-permute-start.9 = (bf16[13,32,256]{2,1,0:T(8,128)(2,1)S(1)}, bf16[13,32,256]{2,1,0:T(8,128)(2,1)S(1)}, u32[]{:S(2)}, u32[]{:S(2)}) collective-permute-start(bf16[13,32,256]{2,1,0:T(8,128)(2,1)S(1)} %get-tuple-element.46), channel_id=1, source_target_pairs={{0,3},{1,2},{2,1},{3,0},{4,7},{5,6},{6,5},{7,4},{8,11},{9,10},{10,... | collective-permute-start | bytes 638984 | tf_op jit(solution)/shard_map/ppermute | solution.py:424
  35.6 8.9 %collective-permute-start.11 = (bf16[13,32,256]{2,1,0:T(8,128)(2,1)S(1)}, bf16[13,32,256]{2,1,0:T(8,128)(2,1)S(1)}, u32[]{:S(2)}, u32[]{:S(2)}) collective-permute-start(bf16[13,32,256]{2,1,0:T(8,128)(2,1)S(1)} %get-tuple-element.49), channel_id=1, source_target_pairs={{0,2},{1,3},{2,0},{3,1},{4,6},{5,7},{6,4},{7,5},{8,10},{9,11},{10,... | collective-permute-start | bytes 638984 | tf_op jit(solution)/shard_map/ppermute | solution.py:424
  36.4 11.7 %collective-permute-start.12 = (bf16[13,32,256]{2,1,0:T(8,128)(2,1)S(1)}, bf16[13,32,256]{2,1,0:T(8,128)(2,1)S(1)}, u32[]{:S(2)}, u32[]{:S(2)}) collective-permute-start(bf16[13,32,256]{2,1,0:T(8,128)(2,1)S(1)} %get-tuple-element.50), channel_id=1, source_target_pairs={{0,3},{1,2},{2,1},{3,0},{4,7},{5,6},{6,5},{7,4},{8,11},{9,10},{10,... | collective-permute-start | bytes 638984 | tf_op jit(solution)/shard_map/ppermute | solution.py:424
  41.9 6.1 %collective-permute-start.10 = (bf16[13,64,256]{2,1,0:T(8,128)(2,1)S(1)}, bf16[13,64,256]{2,1,0:T(8,128)(2,1)S(1)}, u32[]{:S(2)}, u32[]{:S(2)}) collective-permute-start(bf16[13,64,256]{2,1,0:T(8,128)(2,1)S(1)} %get-tuple-element.48), channel_id=1, source_target_pairs={{0,1},{1,0},{2,3},{3,2},{4,5},{5,4},{6,7},{7,6},{8,9},{9,8},{10,11... | collective-permute-start | bytes 1277960 | tf_op jit(solution)/shard_map/ppermute | solution.py:424

commit v8 on v7

--- a/solution.py
+++ b/solution.py
@@ -16,6 +16,8 @@
 
 MOMENTS = 13
 HALO = 8
+NEED = 6
+SKIP = HALO - NEED
 RHO, TEMP = 0, 4
 VMEM = pl.BlockSpec(memory_space=pltpu.VMEM)
 ANY = pl.BlockSpec(memory_space=pl.ANY)
@@ -130,18 +132,21 @@
         dst = given.at[first] if len(inputs[k].shape) == 2 else given.at[first:end]
         copies.append(pltpu.make_async_copy(inputs[k], dst, arrived.at[k]))
         copies[k].start()
-    strip[0:HALO, :] = jnp.zeros((HALO, rows), jnp.float32)
-    strip[HALO + cols :, :] = jnp.zeros((HALO, rows), jnp.float32)
+    wide = slab // 2 + 2 * HALO
+    lane = min(rows, 128)
     leaving = []
     done = 0
     for at, (first, end) in enumerate(GROUPS):
         copies[at].wait()
         for f in range(first, end):
-            strip[HALO : HALO + cols, :] = code(f, given[f]).T
+            strip[f, 0:HALO, :] = jnp.zeros((HALO, rows), jnp.float32)
+            strip[f, HALO + cols :, :] = jnp.zeros((HALO, rows), jnp.float32)
+            strip[f, HALO : HALO + cols, :] = code(f, given[f]).T
             for s in range(count):
-                here = pl.ds(message_start(me, s, slab), held[s].shape[1])
-                held[s][f] = strip[here, :].astype(jnp.bfloat16)
-            held[count][f] = strip[...].astype(jnp.bfloat16)
+                block = strip[f, pl.ds(message_start(me, s, slab), wide), :][SKIP : wide - SKIP]
+                halves = [block[:, p : p + lane] for p in range(0, rows, lane)]
+                held[s][f] = jnp.concatenate(halves, axis=0).astype(jnp.bfloat16)
+            held[count][f] = strip[f].astype(jnp.bfloat16)
         if at in (1, 3, 4, 5):
             span = pl.ds(done, end - done)
             for k, out in enumerate(outs):
@@ -163,29 +168,27 @@
     me = me_ref[0]
     slab = (tall.shape[1] - 2 * HALO) // n
     count = outs[0].shape[1]
+    wide = slab // 2 + 2 * HALO if two else count
+    line = lax.broadcasted_iota(jnp.int32, before.shape[1:], 0)
     for s in range(n):
         to = jnp.bitwise_xor(me, s)
+        even = to % 2 == 0
         start = to * slab
         if two:
-            start += jnp.where(to % 2 == 0, 0, slab // 2 + 2 * HALO)
+            start += jnp.where(even, 0, slab // 2)
         start = pl.multiple_of(start, 16)
         for f in range(MOMENTS):
-            outs[s][f] = tall[f, pl.ds(start, count), :]
-
-        def merge(tile, halo, at_start):
-            line = lax.broadcasted_iota(jnp.int32, halo.shape[1:], 0)
-            keep = (line < HALO) == at_start
-            for f in range(MOMENTS):
-                new, old = halo[f].astype(jnp.float32), outs[s][f, tile, :].astype(jnp.float32)
-                outs[s][f, tile, :] = jnp.where(keep, new, old).astype(jnp.bfloat16)
-
-        @pl.when(to == 0)
-        def _():
-            merge(slice(0, 2 * HALO), before, True)
-
-        @pl.when(to == n - 1)
-        def _():
-            merge(slice(count - 2 * HALO, count), after, False)
+            block = tall[f, pl.ds(start, wide), :].astype(jnp.float32)
+            first, last = block[: 2 * HALO], block[wide - 2 * HALO :]
+            first = jnp.where((line < HALO) & (to == 0), before[f].astype(jnp.float32), first)
+            last = jnp.where((line >= HALO) & (to == n - 1), after[f].astype(jnp.float32), last)
+            between = [block[2 * HALO : wide - 2 * HALO]] if wide > 4 * HALO else []
+            block = jnp.concatenate([first, *between, last], axis=0)
+            if two:
+                near_end = block[SKIP : SKIP + count]
+                far_end = block[wide - SKIP - count : wide - SKIP]
+                block = jnp.where(even, near_end, far_end)
+            outs[s][f] = block.astype(jnp.bfloat16)
 
 
 def grid_kernel(n, rows, slots, me_ref, *refs):
@@ -299,19 +302,27 @@
     lane = min(rows, 128)
     strips = rows // lane
 
+    part = wide - 2 * SKIP
+    lap = 2 * NEED
     for s in range(n):
-        here = pl.ds(s * rows, rows)
         for f in range(MOMENTS):
-            if not second:
-                u0[f, :, here] = decode(f, firsts[s][f].astype(jnp.float32))
-            else:
-                new = rests[s][f].astype(jnp.float32)
-                fresh = pl.ds(pl.multiple_of(jnp.where(right_first, 0, 2 * HALO), 16), core)
-                u0[f, fresh, here] = decode(f, new)
-                src = pl.ds(pl.multiple_of(jnp.where(right_first, 0, core), 16), 2 * HALO)
-                dst = pl.ds(pl.multiple_of(jnp.where(right_first, core, 0), 16), 2 * HALO)
-                old = firsts[s][f, src, :].astype(jnp.float32)
-                u0[f, dst, here] = decode(f, old)
+            if not two:
+                u0[f, :, pl.ds(s * rows, rows)] = decode(f, firsts[s][f].astype(jnp.float32))
+                continue
+            whole = decode(f, firsts[s][f].astype(jnp.float32))
+            for p in range(strips):
+                here = pl.ds(s * rows + p * lane, lane)
+                first = whole[p * part : (p + 1) * part]
+                u0[f, 0:8, here] = jnp.zeros((8, lane), jnp.float32)
+                u0[f, wide - 8 :, here] = jnp.zeros((8, lane), jnp.float32)
+                if not second:
+                    u0[f, SKIP : SKIP + part, here] = first
+                    continue
+                new = rests[s][f, :, p * lane : (p + 1) * lane].astype(jnp.float32)
+                new = decode(f, new)
+                left = jnp.concatenate([new, first[:lap]], axis=0)
+                right = jnp.concatenate([first[part - lap :], new], axis=0)
+                u0[f, SKIP : SKIP + part, here] = jnp.where(right_first, left, right)
 
     for s in range(n):
         for p in range(strips):
@@ -395,7 +406,7 @@
 def unpack_kernel(n, far, near, chunks, me_ref, *refs):
     staying, refs = refs[: len(near)], refs[len(near) :]
     out, tall, held, leaving = refs[-4:]
-    cols = tall.shape[0]
+    cols = tall.shape[1]
     slab = cols // n
     width = slab // chunks
     me = me_ref[0]
@@ -412,8 +423,8 @@
                     piece = staying[near.index(s)][f, c * width : (c + 1) * width, :]
                 else:
                     piece = refs[c * len(far) + far.index(s)][f]
-                tall[here, :] = piece.astype(jnp.float32)
-        held[f] = tall[...].T
+                tall[f, here, :] = piece.astype(jnp.float32)
+        held[f] = tall[f].T
         copies.append(pltpu.make_async_copy(held.at[f], out.at[f], leaving.at[f]))
         copies[f].start()
     for copy in copies:
@@ -437,6 +448,7 @@
     two = slab % 32 == 0
     core = slab // 2 if two else slab
     wide = core + 2 * HALO
+    lane = min(rows, 128)
     half = jnp.bfloat16
     me = lax.axis_index("gy").astype(jnp.int32).reshape(1)
     vel, stress, heat = (jnp.swapaxes(a, 0, 1) for a in (vel, stress, heat))
@@ -448,7 +460,8 @@
     inputs = (rho, vel, temp, stress, heat)
 
     def pack(arrays):
-        shapes = [message(wide)] * n if two else []
+        sent = (MOMENTS, (wide - 2 * SKIP) * (rows // lane), lane)
+        shapes = [jax.ShapeDtypeStruct(sent, half)] * n if two else []
         shapes += [message(cols + 2 * HALO)]
         return pl.pallas_call(
             functools.partial(pack_kernel, n, two),
@@ -456,7 +469,7 @@
             in_specs=[SMEM] + [HBM] * len(arrays),
             out_specs=[ANY] * len(shapes),
             scratch_shapes=[
-                pltpu.VMEM((cols + 2 * HALO, rows), jnp.float32),
+                pltpu.VMEM((MOMENTS, cols + 2 * HALO, rows), jnp.float32),
                 pltpu.VMEM((MOMENTS, rows, cols), jnp.float32),
                 pltpu.SemaphoreType.DMA((len(GROUPS),)),
             ]
@@ -473,8 +486,6 @@
         firsts = exchange(firsts, n, range(n))
     else:
         (tall,) = pack(inputs)
-
-    lane = min(rows, 128)
 
     def grid_of(slots, *ties):
         return pl.pallas_call(
@@ -589,7 +600,7 @@
         in_specs=[SMEM] + [VMEM] * (len(staying) + len(back)) + [ANY],
         out_specs=ANY,
         scratch_shapes=[
-            pltpu.VMEM((cols, rows), jnp.float32),
+            pltpu.VMEM((MOMENTS, cols, rows), jnp.float32),
             pltpu.VMEM((MOMENTS, rows, cols), jnp.float32),
             pltpu.SemaphoreType.DMA((MOMENTS,)),
         ],

time: 50.4 us -> 49.7 us (0.986)
  waiting for transfers between devices: 11.3 us -> 9.96 us
  Pallas kernels: 23.5 us -> 24.5 us
    ppermute x11, waiting for transfers between devices: 10.2 us -> 9.02 us  [to_partner(): lax.ppermute(array, 'gy', [(i, i ^ s) for i in range(n)])]
  transfers between devices with their start and end apart: 13 -> 13, of which waited for: 7 -> 6; matrix products, arithmetic and copies ran while one was open for 0% -> 0% of each run, Pallas kernels for 36% -> 38%
where the time goes in v8:
time: 49.7 us; the launch traced here: 49.6 us
  Pallas kernels  24.5 us (49%)
  starting transfers between devices  14.8 us (30%)
  waiting for transfers between devices  9.96 us (20%)
    pallas_call x2, Pallas kernels, sections(): pl.pallas_call(functools.partial(section_kernel, n, two, second, far, all...  10.6 us
    ppermute x11, starting transfers between devices, to_partner(): lax.ppermute(array, 'gy', [(i, i ^ s) for i in range(n)])  9.7 us
    ppermute x11, waiting for transfers between devices, to_partner(): lax.ppermute(array, 'gy', [(i, i ^ s) for i in range(n)])  9.02 us
    pallas_call x2, Pallas kernels, grid_of(): pl.pallas_call(functools.partial(grid_kernel, n, rows, slots), out_shape=...  4.03 us
    pallas_call x1, Pallas kernels, pack(): pl.pallas_call(functools.partial(pack_kernel, n, two), out_shape=shapes,...  3.81 us
    ppermute x1, starting transfers between devices, on_device(): after = lax.ppermute(left, 'gx', [(j, i) for i, j in up])  3.1 us
    pallas_call x1, Pallas kernels, finished(): pl.pallas_call(functools.partial(finish_kernel, n, near, parts, len(state...  2.7 us
    ppermute x1, starting transfers between devices, on_device(): before = lax.ppermute(right, 'gx', up)  2.03 us
  transfers between devices with their start and end apart: 13, of which 6 were waited for; matrix products, arithmetic and copies ran while one was open for 0% of the time, Pallas kernels for 38%

profile of v8, /device:TPU:0, one launch (start us, length us, event | category | flops | bytes accessed | tf_op | source)
XLA Modules:
  0.0 49.6 jit_solution(1613189251690202386)
XLA Ops:
  0.0 3.8 %pack.1 = (bf16[13,88,128]{2,1,0:T(8,128)(2,1)}, bf16[13,88,128]{2,1,0:T(8,128)(2,1)}, bf16[13,88,128]{2,1,0:T(8,128)(2,1)}, bf16[13,88,128]{2,1,0:T(8,128)(2,1)}, bf16[13,272,256]{2,1,0:T(8,128)(2,1)}) custom-call(s32[1]{0:T(128)} %bitcast.me_ref, f32[256,256]{1,0:T(8,128)} %refs_0_.1, f32[3,256,256]{2,1,0:T(8,128)} %bitcast.6, f32[256,256]{1,0:T(8,128)} %refs_2_.1, ...), custom_call_target="tpu_custom_call" | custom-call | flops 2000000000 | bytes 6000000 | tf_op jit(solution)/shard_map/pack/pallas_call | solution.py:466
  3.8 3.0 %collective-permute-start = (bf16[13,88,128]{2,1,0:T(8,128)(2,1)}, bf16[13,88,128]{2,1,0:T(8,128)(2,1)S(1)}, u32[]{:S(2)}, u32[]{:S(2)}) collective-permute-start(bf16[13,88,128]{2,1,0:T(8,128)(2,1)} %get-tuple-element.29), channel_id=1, source_target_pairs={{0,2},{1,3},{2,0},{3,1},{4,6},{5,7},{6,4},{7,5},{8,10},{9,11},{10,... | collective-permute-start | bytes 878600 | tf_op jit(solution)/shard_map/ppermute | solution.py:435
  6.8 0.0 collective-permute-start.1
  6.8 0.2 collective-permute-start.2
  7.0 1.9 %grid.2.refs_0_.tie = bf16[1024,256]{1,0:T(8,128)(2,1)S(1)} custom-call(s32[1]{0:T(128)} %bitcast.me_ref), custom_call_target="tpu_custom_call" | custom-call | flops 1000000000 | bytes 3000000 | tf_op jit(solution)/shard_map/grid/pallas_call | solution.py:491
  9.0 2.0 %collective-permute-start.3 = (bf16[13,16,256]{2,1,0:T(8,128)(2,1)S(1)}, bf16[13,16,256]{2,1,0:T(8,128)(2,1)S(1)}, u32[]{:S(2)}, u32[]{:S(2)}) collective-permute-start(bf16[13,16,256]{2,1,0:T(8,128)(2,1)S(1)} %get-tuple-element.36), channel_id=1, source_target_pairs={{0,4},{4,8},{8,12},{12,16},{16,20},{20,24},{24,28},{28,0},{1,5},{5... | collective-permute-start | bytes 319496 | tf_op jit(solution)/shard_map/ppermute | solution.py:515
  11.0 3.1 %collective-permute-start.4 = (bf16[13,16,256]{2,1,0:T(8,128)(2,1)S(1)}, bf16[13,16,256]{2,1,0:T(8,128)(2,1)S(1)}, u32[]{:S(2)}, u32[]{:S(2)}) collective-permute-start(bf16[13,16,256]{2,1,0:T(8,128)(2,1)S(1)} %get-tuple-element.37), channel_id=1, source_target_pairs={{4,0},{8,4},{12,8},{16,12},{20,16},{24,20},{28,24},{0,28},{5,1},{9... | collective-permute-start | bytes 319496 | tf_op jit(solution)/shard_map/ppermute | solution.py:516
  14.1 2.1 %grid.3.refs_1_ = bf16[1024,256]{1,0:T(8,128)(2,1)S(1)} custom-call(s32[1]{0:T(128)} %bitcast.me_ref), custom_call_target="tpu_custom_call" | custom-call | flops 1000000000 | bytes 3000000 | tf_op jit(solution)/shard_map/grid/pallas_call | solution.py:491
  16.2 0.8 %flip.1.refs_2_ = bf16[1024,512]{1,0:T(8,128)(2,1)S(1)} custom-call(bf16[1024,256]{1,0:T(8,128)(2,1)S(1)} %grid.2.refs_0_.tie, bf16[1024,256]{1,0:T(8,128)(2,1)S(1)} %grid.3.refs_1_), custom_call_target="tpu_custom_call" | custom-call | flops 300000000 | bytes 900000 | tf_op jit(solution)/shard_map/flip/pallas_call | solution.py:517
  17.1 0.2 collective-permute-done.3.before
  17.3 0.7 %collective-permute-done.4.after = bf16[13,16,256]{2,1,0:T(8,128)(2,1)S(1)} collective-permute-done((bf16[13,16,256]{2,1,0:T(8,128)(2,1)S(1)}, bf16[13,16,256]{2,1,0:T(8,128)(2,1)S(1)}, u32[]{:S(2)}, u32[]{:S(2)}) %collective-permute-start.4) | collective-permute-done | bytes 106528 | tf_op jit(solution)/shard_map/ppermute | solution.py:516
  18.0 0.5 %rest.1 = (bf16[13,32,256]{2,1,0:T(8,128)(2,1)S(1)}, bf16[13,32,256]{2,1,0:T(8,128)(2,1)S(1)}, bf16[13,32,256]{2,1,0:T(8,128)(2,1)S(1)}, bf16[13,32,256]{2,1,0:T(8,128)(2,1)S(1)}) custom-call(s32[1]{0:T(128)} %bitcast.me_ref, bf16[13,272,256]{2,1,0:T(8,128)(2,1)S(1)} %copy-done, bf16[13,16,256]{2,1,0:T(8,128)(2,1)S(1)} %collective-permute-done.3.before, ...), custom_call_target="tpu_custom_call" | custom-call | flops 200000000 | bytes 600000 | tf_op jit(solution)/shard_map/rest/pallas_call | solution.py:527
  18.5 1.6 %collective-permute-start.5 = (bf16[13,32,256]{2,1,0:T(8,128)(2,1)S(1)}, bf16[13,32,256]{2,1,0:T(8,128)(2,1)S(1)}, u32[]{:S(2)}, u32[]{:S(2)}) collective-permute-start(bf16[13,32,256]{2,1,0:T(8,128)(2,1)S(1)} %get-tuple-element.39), channel_id=1, source_target_pairs={{0,2},{1,3},{2,0},{3,1},{4,6},{5,7},{6,4},{7,5},{8,10},{9,11},{10,... | collective-permute-start | bytes 638984 | tf_op jit(solution)/shard_map/ppermute | solution.py:435
  20.1 0.0 collective-permute-start.6
  20.1 0.0 collective-permute-done.refs_4_
  20.1 0.6 %collective-permute-start.7 = (bf16[13,32,256]{2,1,0:T(8,128)(2,1)S(1)}, bf16[13,32,256]{2,1,0:T(8,128)(2,1)S(1)}, u32[]{:S(2)}, u32[]{:S(2)}) collective-permute-start(bf16[13,32,256]{2,1,0:T(8,128)(2,1)S(1)} %get-tuple-element.41), channel_id=1, source_target_pairs={{0,1},{1,0},{2,3},{3,2},{4,5},{5,4},{6,7},{7,6},{8,9},{9,8},{10,11... | collective-permute-start | bytes 638984 | tf_op jit(solution)/shard_map/ppermute | solution.py:435
  20.7 0.0 collective-permute-done.1.refs_5_
  20.7 5.1 %sections.2 = (bf16[13,32,256]{2,1,0:T(8,128)(2,1)S(1)}, bf16[13,32,256]{2,1,0:T(8,128)(2,1)S(1)}, f32[13,48,1024]{2,1,0:T(8,128)S(1)}, f32[13,32,1024]{2,1,0:T(8,128)S(1)}, bf16[416,1024]{1,0:T(8,128)(2,1)S(1)}) custom-call(s32[1]{0:T(128)} %bitcast.me_ref, bf16[1024,256]{1,0:T(8,128)(2,1)S(1)} %grid.2.refs_0_.tie, bf16[1024,256]{1,0:T(8,128)(2,1)S(1)} %grid.3.refs_1_, ...), custom_call_target="tpu_custom_call" | custom-call | flops 6000000000 | bytes 18000000 | tf_op jit(solution)/shard_map/sections/pallas_call | solution.py:544
  25.8 1.6 %collective-permute-start.8 = (bf16[13,32,256]{2,1,0:T(8,128)(2,1)S(1)}, bf16[13,32,256]{2,1,0:T(8,128)(2,1)S(1)}, u32[]{:S(2)}, u32[]{:S(2)}) collective-permute-start(bf16[13,32,256]{2,1,0:T(8,128)(2,1)S(1)} %get-tuple-element.42.refs_11_), channel_id=1, source_target_pairs={{0,2},{1,3},{2,0},{3,1},{4,6},{5,7},{6,4},{7,5},{8,10},{9,11},{10,... | collective-permute-start | bytes 638984 | tf_op jit(solution)/shard_map/ppermute | solution.py:435
  27.4 0.0 collective-permute-start.9
  27.4 0.0 collective-permute-done.5.refs_8_
  27.4 2.2 %collective-permute-done.6.refs_9_ = bf16[13,32,256]{2,1,0:T(8,128)(2,1)S(1)} collective-permute-done((bf16[13,32,256]{2,1,0:T(8,128)(2,1)S(1)}, bf16[13,32,256]{2,1,0:T(8,128)(2,1)S(1)}, u32[]{:S(2)}, u32[]{:S(2)}) %collective-permute-start.6) | collective-permute-done | bytes 213024 | tf_op jit(solution)/shard_map/ppermute | solution.py:435
  29.7 5.5 %sections.3 = (bf16[13,32,256]{2,1,0:T(8,128)(2,1)S(1)}, bf16[13,32,256]{2,1,0:T(8,128)(2,1)S(1)}, f32[13,48,1024]{2,1,0:T(8,128)S(1)}, f32[13,32,1024]{2,1,0:T(8,128)S(1)}, bf16[416,1024]{1,0:T(8,128)(2,1)S(1)}) custom-call(s32[1]{0:T(128)} %bitcast.me_ref, bf16[1024,256]{1,0:T(8,128)(2,1)S(1)} %grid.2.refs_0_.tie, bf16[1024,256]{1,0:T(8,128)(2,1)S(1)} %grid.3.refs_1_, ...), custom_call_target="tpu_custom_call" | custom-call | flops 6000000000 | bytes 18000000 | tf_op jit(solution)/shard_map/sections/pallas_call | solution.py:544
  35.2 0.2 collective-permute-start.11
  35.4 1.9 %collective-permute-start.12 = (bf16[13,32,256]{2,1,0:T(8,128)(2,1)S(1)}, bf16[13,32,256]{2,1,0:T(8,128)(2,1)S(1)}, u32[]{:S(2)}, u32[]{:S(2)}) collective-permute-start(bf16[13,32,256]{2,1,0:T(8,128)(2,1)S(1)} %get-tuple-element.50), channel_id=1, source_target_pairs={{0,3},{1,2},{2,1},{3,0},{4,7},{5,6},{6,5},{7,4},{8,11},{9,10},{10,... | collective-permute-start | bytes 638984 | tf_op jit(solution)/shard_map/ppermute | solution.py:435
  37.2 0.0 collective-permute-done.8.refs_8_.refs_0_.refs_2_
  37.2 0.6 %collective-permute-done.9.refs_9_.refs_1_.refs_3_ = bf16[13,32,256]{2,1,0:T(8,128)(2,1)S(1)} collective-permute-done((bf16[13,32,256]{2,1,0:T(8,128)(2,1)S(1)}, bf16[13,32,256]{2,1,0:T(8,128)(2,1)S(1)}, u32[]{:S(2)}, u32[]{:S(2)}) %collective-permute-start.9) | collective-permute-done | bytes 213024 | tf_op jit(solution)/shard_map/ppermute | solution.py:435
  37.8 2.7 %finish.1 = (f32[13,64,256]{2,1,0:T(8,128)S(1)}, bf16[13,64,256]{2,1,0:T(8,128)(2,1)S(1)}) custom-call(s32[1]{0:T(128)} %bitcast.me_ref, bf16[1024,256]{1,0:T(8,128)(2,1)S(1)} %grid.2.refs_0_.tie, bf16[1024,256]{1,0:T(8,128)(2,1)S(1)} %grid.3.refs_1_, f32[13,48,1024]{2,1,0:T(8,128)S(1)} %get-tuple-element.32.refs_2_, ...), custom_call_target="tpu_custom_call" | custom-call | flops 4000000000 | bytes 12000000 | tf_op jit(solution)/shard_map/finish/pallas_call | solution.py:562
  40.5 0.7 %collective-permute-start.10 = (bf16[13,64,256]{2,1,0:T(8,128)(2,1)S(1)}, bf16[13,64,256]{2,1,0:T(8,128)(2,1)S(1)}, u32[]{:S(2)}, u32[]{:S(2)}) collective-permute-start(bf16[13,64,256]{2,1,0:T(8,128)(2,1)S(1)} %get-tuple-element.48), channel_id=1, source_target_pairs={{0,1},{1,0},{2,3},{3,2},{4,5},{5,4},{6,7},{7,6},{8,9},{9,8},{10,11... | collective-permute-start | bytes 1277960 | tf_op jit(solution)/shard_map/ppermute | solution.py:435
  41.2 2.2 %collective-permute-done.11.refs_2_.refs_4_ = bf16[13,32,256]{2,1,0:T(8,128)(2,1)S(1)} collective-permute-done((bf16[13,32,256]{2,1,0:T(8,128)(2,1)S(1)}, bf16[13,32,256]{2,1,0:T(8,128)(2,1)S(1)}, u32[]{:S(2)}, u32[]{:S(2)}) %collective-permute-start.11) | collective-permute-done | bytes 213024 | tf_op jit(solution)/shard_map/ppermute | solution.py:435
  43.4 4.0 %collective-permute-done.12.refs_3_.refs_5_ = bf16[13,32,256]{2,1,0:T(8,128)(2,1)S(1)} collective-permute-done((bf16[13,32,256]{2,1,0:T(8,128)(2,1)S(1)}, bf16[13,32,256]{2,1,0:T(8,128)(2,1)S(1)}, u32[]{:S(2)}, u32[]{:S(2)}) %collective-permute-start.12) | collective-permute-done | bytes 213024 | tf_op jit(solution)/shard_map/ppermute | solution.py:435
  47.4 2.0 %unpack.1 = f32[13,256,256]{2,1,0:T(8,128)} custom-call(s32[1]{0:T(128)} %bitcast.me_ref, f32[13,64,256]{2,1,0:T(8,128)S(1)} %get-tuple-element.47.refs_0_, bf16[13,64,256]{2,1,0:T(8,128)(2,1)S(1)} %collective-permute-done.10.refs_1_, bf16[13,32,256]{2,1,0:T(8,128)(2,1)S(1)} %collective-permute-done.8.refs_8_.refs_0_.refs_2_, ...), custom_call_target="tpu_custom_call" | custom-call | flops 3000000000 | bytes 9000000 | tf_op jit(solution)/shard_map/unpack/pallas_call | solution.py:597
  (9 shorter events, 0.0 us)
Async XLA Ops:
  3.8 16.2 %collective-permute-start = (bf16[13,88,128]{2,1,0:T(8,128)(2,1)}, bf16[13,88,128]{2,1,0:T(8,128)(2,1)S(1)}, u32[]{:S(2)}, u32[]{:S(2)}) collective-permute-start(bf16[13,88,128]{2,1,0:T(8,128)(2,1)} %get-tuple-element.29), channel_id=1, source_target_pairs={{0,2},{1,3},{2,0},{3,1},{4,6},{5,7},{6,4},{7,5},{8,10},{9,11},{10,... | collective-permute-start | bytes 878600 | tf_op jit(solution)/shard_map/ppermute | solution.py:435
  6.8 13.9 %collective-permute-start.1 = (bf16[13,88,128]{2,1,0:T(8,128)(2,1)}, bf16[13,88,128]{2,1,0:T(8,128)(2,1)S(1)}, u32[]{:S(2)}, u32[]{:S(2)}) collective-permute-start(bf16[13,88,128]{2,1,0:T(8,128)(2,1)} %get-tuple-element.30), channel_id=1, source_target_pairs={{0,3},{1,2},{2,1},{3,0},{4,7},{5,6},{6,5},{7,4},{8,11},{9,10},{10,... | collective-permute-start | bytes 878600 | tf_op jit(solution)/shard_map/ppermute | solution.py:435
  6.8 2.1 %copy-start = (bf16[13,272,256]{2,1,0:T(8,128)(2,1)S(1)}, bf16[13,272,256]{2,1,0:T(8,128)(2,1)}, u32[]{:S(2)}) copy-start(bf16[13,272,256]{2,1,0:T(8,128)(2,1)} %get-tuple-element.35.tall) | copy-start | bytes 5431300
  6.8 13.9 %collective-permute-start.2 = (bf16[13,88,128]{2,1,0:T(8,128)(2,1)}, bf16[13,88,128]{2,1,0:T(8,128)(2,1)S(1)}, u32[]{:S(2)}, u32[]{:S(2)}) collective-permute-start(bf16[13,88,128]{2,1,0:T(8,128)(2,1)} %get-tuple-element.31), channel_id=1, source_target_pairs={{0,1},{1,0},{2,3},{3,2},{4,5},{5,4},{6,7},{7,6},{8,9},{9,8},{10,11... | collective-permute-start | bytes 878600 | tf_op jit(solution)/shard_map/ppermute | solution.py:435
  9.0 8.3 %collective-permute-start.3 = (bf16[13,16,256]{2,1,0:T(8,128)(2,1)S(1)}, bf16[13,16,256]{2,1,0:T(8,128)(2,1)S(1)}, u32[]{:S(2)}, u32[]{:S(2)}) collective-permute-start(bf16[13,16,256]{2,1,0:T(8,128)(2,1)S(1)} %get-tuple-element.36), channel_id=1, source_target_pairs={{0,4},{4,8},{8,12},{12,16},{16,20},{20,24},{24,28},{28,0},{1,5},{5... | collective-permute-start | bytes 319496 | tf_op jit(solution)/shard_map/ppermute | solution.py:515
  11.0 7.0 %collective-permute-start.4 = (bf16[13,16,256]{2,1,0:T(8,128)(2,1)S(1)}, bf16[13,16,256]{2,1,0:T(8,128)(2,1)S(1)}, u32[]{:S(2)}, u32[]{:S(2)}) collective-permute-start(bf16[13,16,256]{2,1,0:T(8,128)(2,1)S(1)} %get-tuple-element.37), channel_id=1, source_target_pairs={{4,0},{8,4},{12,8},{16,12},{20,16},{24,20},{28,24},{0,28},{5,1},{9... | collective-permute-start | bytes 319496 | tf_op jit(solution)/shard_map/ppermute | solution.py:516
  16.2 4.5 %copy-start.1 = (bf16[13,88,128]{2,1,0:T(8,128)(2,1)S(1)}, bf16[13,88,128]{2,1,0:T(8,128)(2,1)}, u32[]{:S(2)}) copy-start(bf16[13,88,128]{2,1,0:T(8,128)(2,1)} %get-tuple-element.28.refs_3_) | copy-start | bytes 878596
  18.5 8.9 %collective-permute-start.5 = (bf16[13,32,256]{2,1,0:T(8,128)(2,1)S(1)}, bf16[13,32,256]{2,1,0:T(8,128)(2,1)S(1)}, u32[]{:S(2)}, u32[]{:S(2)}) collective-permute-start(bf16[13,32,256]{2,1,0:T(8,128)(2,1)S(1)} %get-tuple-element.39), channel_id=1, source_target_pairs={{0,2},{1,3},{2,0},{3,1},{4,6},{5,7},{6,4},{7,5},{8,10},{9,11},{10,... | collective-permute-start | bytes 638984 | tf_op jit(solution)/shard_map/ppermute | solution.py:435
  20.1 9.6 %collective-permute-start.6 = (bf16[13,32,256]{2,1,0:T(8,128)(2,1)S(1)}, bf16[13,32,256]{2,1,0:T(8,128)(2,1)S(1)}, u32[]{:S(2)}, u32[]{:S(2)}) collective-permute-start(bf16[13,32,256]{2,1,0:T(8,128)(2,1)S(1)} %get-tuple-element.40), channel_id=1, source_target_pairs={{0,3},{1,2},{2,1},{3,0},{4,7},{5,6},{6,5},{7,4},{8,11},{9,10},{10,... | collective-permute-start | bytes 638984 | tf_op jit(solution)/shard_map/ppermute | solution.py:435
  20.1 9.6 %collective-permute-start.7 = (bf16[13,32,256]{2,1,0:T(8,128)(2,1)S(1)}, bf16[13,32,256]{2,1,0:T(8,128)(2,1)S(1)}, u32[]{:S(2)}, u32[]{:S(2)}) collective-permute-start(bf16[13,32,256]{2,1,0:T(8,128)(2,1)S(1)} %get-tuple-element.41), channel_id=1, source_target_pairs={{0,1},{1,0},{2,3},{3,2},{4,5},{5,4},{6,7},{7,6},{8,9},{9,8},{10,11... | collective-permute-start | bytes 638984 | tf_op jit(solution)/shard_map/ppermute | solution.py:435
  25.8 11.4 %collective-permute-start.8 = (bf16[13,32,256]{2,1,0:T(8,128)(2,1)S(1)}, bf16[13,32,256]{2,1,0:T(8,128)(2,1)S(1)}, u32[]{:S(2)}, u32[]{:S(2)}) collective-permute-start(bf16[13,32,256]{2,1,0:T(8,128)(2,1)S(1)} %get-tuple-element.42.refs_11_), channel_id=1, source_target_pairs={{0,2},{1,3},{2,0},{3,1},{4,6},{5,7},{6,4},{7,5},{8,10},{9,11},{10,... | collective-permute-start | bytes 638984 | tf_op jit(solution)/shard_map/ppermute | solution.py:435
  27.4 10.4 %collective-permute-start.9 = (bf16[13,32,256]{2,1,0:T(8,128)(2,1)S(1)}, bf16[13,32,256]{2,1,0:T(8,128)(2,1)S(1)}, u32[]{:S(2)}, u32[]{:S(2)}) collective-permute-start(bf16[13,32,256]{2,1,0:T(8,128)(2,1)S(1)} %get-tuple-element.46), channel_id=1, source_target_pairs={{0,3},{1,2},{2,1},{3,0},{4,7},{5,6},{6,5},{7,4},{8,11},{9,10},{10,... | collective-permute-start | bytes 638984 | tf_op jit(solution)/shard_map/ppermute | solution.py:435
  35.2 8.2 %collective-permute-start.11 = (bf16[13,32,256]{2,1,0:T(8,128)(2,1)S(1)}, bf16[13,32,256]{2,1,0:T(8,128)(2,1)S(1)}, u32[]{:S(2)}, u32[]{:S(2)}) collective-permute-start(bf16[13,32,256]{2,1,0:T(8,128)(2,1)S(1)} %get-tuple-element.49), channel_id=1, source_target_pairs={{0,2},{1,3},{2,0},{3,1},{4,6},{5,7},{6,4},{7,5},{8,10},{9,11},{10,... | collective-permute-start | bytes 638984 | tf_op jit(solution)/shard_map/ppermute | solution.py:435
  35.4 12.0 %collective-permute-start.12 = (bf16[13,32,256]{2,1,0:T(8,128)(2,1)S(1)}, bf16[13,32,256]{2,1,0:T(8,128)(2,1)S(1)}, u32[]{:S(2)}, u32[]{:S(2)}) collective-permute-start(bf16[13,32,256]{2,1,0:T(8,128)(2,1)S(1)} %get-tuple-element.50), channel_id=1, source_target_pairs={{0,3},{1,2},{2,1},{3,0},{4,7},{5,6},{6,5},{7,4},{8,11},{9,10},{10,... | collective-permute-start | bytes 638984 | tf_op jit(solution)/shard_map/ppermute | solution.py:435
  40.5 6.9 %collective-permute-start.10 = (bf16[13,64,256]{2,1,0:T(8,128)(2,1)S(1)}, bf16[13,64,256]{2,1,0:T(8,128)(2,1)S(1)}, u32[]{:S(2)}, u32[]{:S(2)}) collective-permute-start(bf16[13,64,256]{2,1,0:T(8,128)(2,1)S(1)} %get-tuple-element.48), channel_id=1, source_target_pairs={{0,1},{1,0},{2,3},{3,2},{4,5},{5,4},{6,7},{7,6},{8,9},{9,8},{10,11... | collective-permute-start | bytes 1277960 | tf_op jit(solution)/shard_map/ppermute | solution.py:435

commit v9 on v8

--- a/solution.py
+++ b/solution.py
@@ -353,15 +353,30 @@
             for f in range(MOMENTS):
                 fy1[f * core : (f + 1) * core, here] = flux(inner, 1, f).astype(jnp.bfloat16)
 
-    finish(n, far, me_ref, parts, grids, u1, r0, fy1, outs, product, turned)
+    def place(s, f):
+        return outs[far.index(s)].at[f]
+
+    finish(n, far, me_ref, parts, grids, u1, r0, fy1, place, product, turned)
+
+
+THIRDS = ((0, 5), (5, 9), (9, MOMENTS))
 
 
 def finish_kernel(n, near, parts, chunks, me_ref, *refs):
     grids, refs = refs[: len(parts)], refs[len(parts) :]
-    states, outs, product, turned = refs[: 3 * chunks], refs[-2 - len(near) : -2], *refs[-2:]
+    states, product, turned = refs[: 3 * chunks], *refs[-2:]
+    outs = refs[-2 - 1 - len(THIRDS) * (len(near) - 1) : -2]
     core = outs[0].shape[1] // chunks
+
+    def place(c, s, f):
+        span = slice(c * core, (c + 1) * core)
+        if s == 0:
+            return outs[0].at[f, span]
+        third = [first <= f < end for first, end in THIRDS].index(True)
+        return outs[1 + len(THIRDS) * (s - 1) + third].at[f - THIRDS[third][0], span]
+
     for c in range(chunks):
-        part = [out.at[:, c * core : (c + 1) * core, :] for out in outs]
+        part = functools.partial(place, c)
         finish(n, near, me_ref, parts, grids, *states[3 * c : 3 * c + 3], part, product, turned)
 
 
@@ -396,36 +411,38 @@
                 if src[f] is not None:
                     rate = rate + src[f]
                 rate = 0.5 * (r0[f, :, here] + rate)
-                outs[k][f, :, there] = rate.astype(outs[k].dtype)
+                target = outs(s, f)
+                target[:, there] = rate.astype(target.dtype)
 
 
 def arrived_kernel(*refs):
     refs[-1][...] = jnp.zeros_like(refs[-1])
 
 
-def unpack_kernel(n, far, near, chunks, me_ref, *refs):
-    staying, refs = refs[: len(near)], refs[len(near) :]
-    out, tall, held, leaving = refs[-4:]
-    cols = tall.shape[1]
-    slab = cols // n
+def unpack_kernel(n, slots, chunks, pieces, me_ref, *refs):
+    out, token, tall, held, leaving = refs[-5:]
+    token[...] = jnp.zeros_like(token)
+    rows, cols = held.shape[1:]
+    slab = cols // len(slots)
     width = slab // chunks
     me = me_ref[0]
     copies = []
     for f in range(MOMENTS):
-        for s in near + far:
+        for array, (s, c, first, end) in zip(refs, pieces):
+            if not first <= f < end:
+                continue
             of = jnp.bitwise_xor(me, s)
-            for c in range(chunks):
-                start = of * slab
+            for k in range(chunks) if c is None else (c,):
+                start = of % len(slots) * slab
                 if chunks == 2:
-                    start += jnp.where(of % 2 == 0, width * (1 - c), width * c)
+                    start += jnp.where(of % 2 == 0, width * (1 - k), width * k)
                 here = pl.ds(pl.multiple_of(start, 16), width)
-                if s in near:
-                    piece = staying[near.index(s)][f, c * width : (c + 1) * width, :]
-                else:
-                    piece = refs[c * len(far) + far.index(s)][f]
+                piece = array[f - first, k * width : (k + 1) * width] if c is None else array[f]
                 tall[f, here, :] = piece.astype(jnp.float32)
         held[f] = tall[f].T
-        copies.append(pltpu.make_async_copy(held.at[f], out.at[f], leaving.at[f]))
+        side = jnp.bitwise_xor(me, slots[0]) // len(slots) * cols
+        there = out.at[f, :, pl.ds(pl.multiple_of(side, 128), cols)]
+        copies.append(pltpu.make_async_copy(held.at[f], there, leaving.at[f]))
         copies[f].start()
     for copy in copies:
         copy.wait()
@@ -559,11 +576,13 @@
         return crossing, [u1, r0, fy1]
 
     def finished(states, *ties):
-        return pl.pallas_call(
+        thirds = [jax.ShapeDtypeStruct((end - first, slab, rows), half) for first, end in THIRDS]
+        shapes = [message(slab, jnp.float32)] + thirds * (len(near) - 1)
+        own, *others = pl.pallas_call(
             functools.partial(finish_kernel, n, near, parts, len(states) // 3),
-            out_shape=[message(slab, jnp.float32)] + [message(slab)] * (len(near) - 1),
+            out_shape=shapes,
             in_specs=[SMEM] + [VMEM] * (len(states) + 2) + [ANY] * len(ties),
-            out_specs=[VMEM] * len(near),
+            out_specs=[VMEM] * len(shapes),
             scratch_shapes=[
                 pltpu.VMEM((MOMENTS * core, rows), jnp.float32),
                 pltpu.VMEM((2 * MOMENTS, wide, lane), jnp.float32),
@@ -572,6 +591,8 @@
             cost_estimate=cost(4),
             name="finish",
         )(me, *grids, *states, *ties)
+        slots = [s for s in near[1:] for _ in THIRDS]
+        return [own, *exchange(others, n, slots)]
 
     if two:
         firsts, rests = far_first(firsts), far_first(rests)
@@ -584,30 +605,40 @@
         crossing, states = sections(False, *far_first(rests))
         staying = finished(states)
         back = exchange(crossing, n, far)
-    staying = exchange(staying, n, near)
+    chunks = 2 if two else 1
+    token = jax.ShapeDtypeStruct((8, 128), jnp.float32)
+
+    def unpack(slots, arrays, pieces, *before):
+        alias = {1 + len(arrays): 0} if before else {}
+        return pl.pallas_call(
+            functools.partial(unpack_kernel, n, slots, chunks, pieces),
+            out_shape=[jax.ShapeDtypeStruct((MOMENTS, rows, cols), jnp.float32), token],
+            in_specs=[SMEM] + [VMEM] * len(arrays) + [ANY] * len(before),
+            out_specs=[ANY, VMEM],
+            scratch_shapes=[
+                pltpu.VMEM((MOMENTS, cols // 2, rows), jnp.float32),
+                pltpu.VMEM((MOMENTS, rows, cols // 2), jnp.float32),
+                pltpu.SemaphoreType.DMA((MOMENTS,)),
+            ],
+            input_output_aliases=alias,
+            compiler_params=params(24),
+            cost_estimate=cost(0.01),
+            name="unpack",
+        )(me, *arrays, *before)
+
+    pieces = [(0, None, 0, MOMENTS)] + [(s, None, *span) for s in near[1:] for span in THIRDS]
+    out, turned_near = unpack(near, staying, tuple(pieces))
     arrived = pl.pallas_call(
         arrived_kernel,
-        out_shape=jax.ShapeDtypeStruct((8, 128), jnp.float32),
-        in_specs=[ANY] * len(back),
+        out_shape=token,
+        in_specs=[ANY] * (len(back) + 1),
         out_specs=VMEM,
         compiler_params=params(1),
         cost_estimate=cost(6),
         name="arrived",
-    )(*back)
-    out = pl.pallas_call(
-        functools.partial(unpack_kernel, n, far, near, 2 if two else 1),
-        out_shape=jax.ShapeDtypeStruct((MOMENTS, rows, cols), jnp.float32),
-        in_specs=[SMEM] + [VMEM] * (len(staying) + len(back)) + [ANY],
-        out_specs=ANY,
-        scratch_shapes=[
-            pltpu.VMEM((MOMENTS, cols, rows), jnp.float32),
-            pltpu.VMEM((MOMENTS, rows, cols), jnp.float32),
-            pltpu.SemaphoreType.DMA((MOMENTS,)),
-        ],
-        compiler_params=params(24),
-        cost_estimate=cost(3),
-        name="unpack",
-    )(me, *staying, *back, arrived)
+    )(*back, turned_near)
+    pieces = [(s, c, 0, MOMENTS) for c in range(chunks) for s in far]
+    out, _ = unpack(far, back, tuple(pieces), out, arrived)
     return jnp.swapaxes(out, 0, 1)
 
 

time: 49.7 us -> 49.7 us (level)
  waiting for transfers between devices: 9.96 us -> 8.04 us
  Pallas kernels: 24.5 us -> 25.9 us
  starting transfers between devices: 14.8 us -> 15.3 us
    ppermute x11 -> x13, waiting for transfers between devices: 9.02 us -> 7.09 us  [to_partner(): lax.ppermute(array, 'gy', [(i, i ^ s) for i in range(n)])]
    pallas_call x2 -> x3, Pallas kernels: 2.02 us -> 3.39 us  [the longest x2 3.39 us: unpack(): pl.pallas_call(functools.partial(unpack_kernel, n, slots, chunks, pieces)...]
    ppermute x11 -> x13, starting transfers between devices: 9.7 us -> 10.2 us  [to_partner(): lax.ppermute(array, 'gy', [(i, i ^ s) for i in range(n)])]
  transfers between devices with their start and end apart: 13 -> 15, of which waited for: 6 -> 7; matrix products, arithmetic and copies ran while one was open for 0% -> 0% of each run, Pallas kernels for 38% -> 40%
where the time goes in v9:
time: 49.7 us; the launch traced here: 49.6 us
  Pallas kernels  25.9 us (52%)
  starting transfers between devices  15.3 us (31%)
  waiting for transfers between devices  8.04 us (16%)
    pallas_call x2, Pallas kernels, sections(): pl.pallas_call(functools.partial(section_kernel, n, two, second, far, all...  10.6 us
    ppermute x13, starting transfers between devices, to_partner(): lax.ppermute(array, 'gy', [(i, i ^ s) for i in range(n)])  10.2 us
    ppermute x13, waiting for transfers between devices, to_partner(): lax.ppermute(array, 'gy', [(i, i ^ s) for i in range(n)])  7.09 us
    pallas_call x2, Pallas kernels, grid_of(): pl.pallas_call(functools.partial(grid_kernel, n, rows, slots), out_shape=...  4.03 us
    pallas_call x1, Pallas kernels, pack(): pl.pallas_call(functools.partial(pack_kernel, n, two), out_shape=shapes,...  3.81 us
    pallas_call x2, Pallas kernels, unpack(): pl.pallas_call(functools.partial(unpack_kernel, n, slots, chunks, pieces)...  3.39 us
    ppermute x1, starting transfers between devices, on_device(): after = lax.ppermute(left, 'gx', [(j, i) for i, j in up])  3.1 us
    pallas_call x1, Pallas kernels, finished(): pl.pallas_call(functools.partial(finish_kernel, n, near, parts, len(state...  2.71 us
  transfers between devices with their start and end apart: 15, of which 7 were waited for; matrix products, arithmetic and copies ran while one was open for 0% of the time, Pallas kernels for 40%

profile of v9, /device:TPU:0, one launch (start us, length us, event | category | flops | bytes accessed | tf_op | source)
XLA Modules:
  0.0 49.6 jit_solution(2828639185323217918)
XLA Ops:
  0.0 3.8 %pack.1 = (bf16[13,88,128]{2,1,0:T(8,128)(2,1)}, bf16[13,88,128]{2,1,0:T(8,128)(2,1)}, bf16[13,88,128]{2,1,0:T(8,128)(2,1)}, bf16[13,88,128]{2,1,0:T(8,128)(2,1)}, bf16[13,272,256]{2,1,0:T(8,128)(2,1)}) custom-call(s32[1]{0:T(128)} %bitcast.me_ref, f32[256,256]{1,0:T(8,128)} %refs_0_.1, f32[3,256,256]{2,1,0:T(8,128)} %bitcast.6, f32[256,256]{1,0:T(8,128)} %refs_2_.1, ...), custom_call_target="tpu_custom_call" | custom-call | flops 2000000000 | bytes 6000000 | tf_op jit(solution)/shard_map/pack/pallas_call | solution.py:483
  3.8 0.0 copy-start
  3.8 3.0 %collective-permute-start = (bf16[13,88,128]{2,1,0:T(8,128)(2,1)}, bf16[13,88,128]{2,1,0:T(8,128)(2,1)S(1)}, u32[]{:S(2)}, u32[]{:S(2)}) collective-permute-start(bf16[13,88,128]{2,1,0:T(8,128)(2,1)} %get-tuple-element.34), channel_id=1, source_target_pairs={{0,2},{1,3},{2,0},{3,1},{4,6},{5,7},{6,4},{7,5},{8,10},{9,11},{10,... | collective-permute-start | bytes 878600 | tf_op jit(solution)/shard_map/ppermute | solution.py:452
  6.8 0.0 collective-permute-start.1
  6.8 0.2 collective-permute-start.2
  7.0 1.9 %grid.2.refs_0_.tie = bf16[1024,256]{1,0:T(8,128)(2,1)S(1)} custom-call(s32[1]{0:T(128)} %bitcast.me_ref), custom_call_target="tpu_custom_call" | custom-call | flops 1000000000 | bytes 3000000 | tf_op jit(solution)/shard_map/grid/pallas_call | solution.py:508
  9.0 2.0 %collective-permute-start.5 = (bf16[13,16,256]{2,1,0:T(8,128)(2,1)S(1)}, bf16[13,16,256]{2,1,0:T(8,128)(2,1)S(1)}, u32[]{:S(2)}, u32[]{:S(2)}) collective-permute-start(bf16[13,16,256]{2,1,0:T(8,128)(2,1)S(1)} %get-tuple-element.40), channel_id=1, source_target_pairs={{0,4},{4,8},{8,12},{12,16},{16,20},{20,24},{24,28},{28,0},{1,5},{5... | collective-permute-start | bytes 319496 | tf_op jit(solution)/shard_map/ppermute | solution.py:532
  11.0 3.1 %collective-permute-start.6 = (bf16[13,16,256]{2,1,0:T(8,128)(2,1)S(1)}, bf16[13,16,256]{2,1,0:T(8,128)(2,1)S(1)}, u32[]{:S(2)}, u32[]{:S(2)}) collective-permute-start(bf16[13,16,256]{2,1,0:T(8,128)(2,1)S(1)} %get-tuple-element.41), channel_id=1, source_target_pairs={{4,0},{8,4},{12,8},{16,12},{20,16},{24,20},{28,24},{0,28},{5,1},{9... | collective-permute-start | bytes 319496 | tf_op jit(solution)/shard_map/ppermute | solution.py:533
  14.1 2.1 %grid.3.refs_1_ = bf16[1024,256]{1,0:T(8,128)(2,1)S(1)} custom-call(s32[1]{0:T(128)} %bitcast.me_ref), custom_call_target="tpu_custom_call" | custom-call | flops 1000000000 | bytes 3000000 | tf_op jit(solution)/shard_map/grid/pallas_call | solution.py:508
  16.2 0.8 %flip.1.refs_2_ = bf16[1024,512]{1,0:T(8,128)(2,1)S(1)} custom-call(bf16[1024,256]{1,0:T(8,128)(2,1)S(1)} %grid.2.refs_0_.tie, bf16[1024,256]{1,0:T(8,128)(2,1)S(1)} %grid.3.refs_1_), custom_call_target="tpu_custom_call" | custom-call | flops 300000000 | bytes 900000 | tf_op jit(solution)/shard_map/flip/pallas_call | solution.py:534
  17.1 0.2 collective-permute-done.5.before
  17.3 0.7 %collective-permute-done.6.after = bf16[13,16,256]{2,1,0:T(8,128)(2,1)S(1)} collective-permute-done((bf16[13,16,256]{2,1,0:T(8,128)(2,1)S(1)}, bf16[13,16,256]{2,1,0:T(8,128)(2,1)S(1)}, u32[]{:S(2)}, u32[]{:S(2)}) %collective-permute-start.6) | collective-permute-done | bytes 106528 | tf_op jit(solution)/shard_map/ppermute | solution.py:533
  18.0 0.5 %rest.1 = (bf16[13,32,256]{2,1,0:T(8,128)(2,1)S(1)}, bf16[13,32,256]{2,1,0:T(8,128)(2,1)S(1)}, bf16[13,32,256]{2,1,0:T(8,128)(2,1)S(1)}, bf16[13,32,256]{2,1,0:T(8,128)(2,1)S(1)}) custom-call(s32[1]{0:T(128)} %bitcast.me_ref, bf16[13,272,256]{2,1,0:T(8,128)(2,1)S(1)} %copy-done, bf16[13,16,256]{2,1,0:T(8,128)(2,1)S(1)} %collective-permute-done.5.before, ...), custom_call_target="tpu_custom_call" | custom-call | flops 200000000 | bytes 600000 | tf_op jit(solution)/shard_map/rest/pallas_call | solution.py:544
  18.5 1.6 %collective-permute-start.7 = (bf16[13,32,256]{2,1,0:T(8,128)(2,1)S(1)}, bf16[13,32,256]{2,1,0:T(8,128)(2,1)S(1)}, u32[]{:S(2)}, u32[]{:S(2)}) collective-permute-start(bf16[13,32,256]{2,1,0:T(8,128)(2,1)S(1)} %get-tuple-element.43), channel_id=1, source_target_pairs={{0,2},{1,3},{2,0},{3,1},{4,6},{5,7},{6,4},{7,5},{8,10},{9,11},{10,... | collective-permute-start | bytes 638984 | tf_op jit(solution)/shard_map/ppermute | solution.py:452
  20.1 0.0 collective-permute-done.refs_4_
  20.1 0.6 %collective-permute-start.9 = (bf16[13,32,256]{2,1,0:T(8,128)(2,1)S(1)}, bf16[13,32,256]{2,1,0:T(8,128)(2,1)S(1)}, u32[]{:S(2)}, u32[]{:S(2)}) collective-permute-start(bf16[13,32,256]{2,1,0:T(8,128)(2,1)S(1)} %get-tuple-element.45), channel_id=1, source_target_pairs={{0,1},{1,0},{2,3},{3,2},{4,5},{5,4},{6,7},{7,6},{8,9},{9,8},{10,11... | collective-permute-start | bytes 638984 | tf_op jit(solution)/shard_map/ppermute | solution.py:452
  20.7 5.1 %sections.2 = (bf16[13,32,256]{2,1,0:T(8,128)(2,1)S(1)}, bf16[13,32,256]{2,1,0:T(8,128)(2,1)S(1)}, f32[13,48,1024]{2,1,0:T(8,128)S(1)}, f32[13,32,1024]{2,1,0:T(8,128)S(1)}, bf16[416,1024]{1,0:T(8,128)(2,1)S(1)}) custom-call(s32[1]{0:T(128)} %bitcast.me_ref, bf16[1024,256]{1,0:T(8,128)(2,1)S(1)} %grid.2.refs_0_.tie, bf16[1024,256]{1,0:T(8,128)(2,1)S(1)} %grid.3.refs_1_, ...), custom_call_target="tpu_custom_call" | custom-call | flops 6000000000 | bytes 18000000 | tf_op jit(solution)/shard_map/sections/pallas_call | solution.py:561
  25.9 1.5 %collective-permute-start.3 = (bf16[13,32,256]{2,1,0:T(8,128)(2,1)S(1)}, bf16[13,32,256]{2,1,0:T(8,128)(2,1)S(1)}, u32[]{:S(2)}, u32[]{:S(2)}) collective-permute-start(bf16[13,32,256]{2,1,0:T(8,128)(2,1)S(1)} %get-tuple-element.37.refs_11_), channel_id=1, source_target_pairs={{0,2},{1,3},{2,0},{3,1},{4,6},{5,7},{6,4},{7,5},{8,10},{9,11},{10,... | collective-permute-start | bytes 638984 | tf_op jit(solution)/shard_map/ppermute | solution.py:452
  27.4 2.3 %collective-permute-done.8.refs_9_ = bf16[13,32,256]{2,1,0:T(8,128)(2,1)S(1)} collective-permute-done((bf16[13,32,256]{2,1,0:T(8,128)(2,1)S(1)}, bf16[13,32,256]{2,1,0:T(8,128)(2,1)S(1)}, u32[]{:S(2)}, u32[]{:S(2)}) %collective-permute-start.8) | collective-permute-done | bytes 213024 | tf_op jit(solution)/shard_map/ppermute | solution.py:452
  29.7 5.5 %sections.3 = (bf16[13,32,256]{2,1,0:T(8,128)(2,1)S(1)}, bf16[13,32,256]{2,1,0:T(8,128)(2,1)S(1)}, f32[13,48,1024]{2,1,0:T(8,128)S(1)}, f32[13,32,1024]{2,1,0:T(8,128)S(1)}, bf16[416,1024]{1,0:T(8,128)(2,1)S(1)}) custom-call(s32[1]{0:T(128)} %bitcast.me_ref, bf16[1024,256]{1,0:T(8,128)(2,1)S(1)} %grid.2.refs_0_.tie, bf16[1024,256]{1,0:T(8,128)(2,1)S(1)} %grid.3.refs_1_, ...), custom_call_target="tpu_custom_call" | custom-call | flops 6000000000 | bytes 18000000 | tf_op jit(solution)/shard_map/sections/pallas_call | solution.py:561
  35.2 0.2 collective-permute-start.10
  35.4 1.9 %collective-permute-start.11 = (bf16[13,32,256]{2,1,0:T(8,128)(2,1)S(1)}, bf16[13,32,256]{2,1,0:T(8,128)(2,1)S(1)}, u32[]{:S(2)}, u32[]{:S(2)}) collective-permute-start(bf16[13,32,256]{2,1,0:T(8,128)(2,1)S(1)} %get-tuple-element.47), channel_id=1, source_target_pairs={{0,3},{1,2},{2,1},{3,0},{4,7},{5,6},{6,5},{7,4},{8,11},{9,10},{10,... | collective-permute-start | bytes 638984 | tf_op jit(solution)/shard_map/ppermute | solution.py:452
  37.2 0.6 %collective-permute-done.4.refs_9_.refs_1_ = bf16[13,32,256]{2,1,0:T(8,128)(2,1)S(1)} collective-permute-done((bf16[13,32,256]{2,1,0:T(8,128)(2,1)S(1)}, bf16[13,32,256]{2,1,0:T(8,128)(2,1)S(1)}, u32[]{:S(2)}, u32[]{:S(2)}) %collective-permute-start.4) | collective-permute-done | bytes 213024 | tf_op jit(solution)/shard_map/ppermute | solution.py:452
  37.8 2.7 %finish.1 = (f32[13,64,256]{2,1,0:T(8,128)S(1)}, bf16[5,64,256]{2,1,0:T(8,128)(2,1)S(1)}, bf16[4,64,256]{2,1,0:T(8,128)(2,1)S(1)}, bf16[4,64,256]{2,1,0:T(8,128)(2,1)S(1)}) custom-call(s32[1]{0:T(128)} %bitcast.me_ref, bf16[1024,256]{1,0:T(8,128)(2,1)S(1)} %grid.2.refs_0_.tie, bf16[1024,256]{1,0:T(8,128)(2,1)S(1)} %grid.3.refs_1_, ...), custom_call_target="tpu_custom_call" | custom-call | flops 4000000000 | bytes 12000000 | tf_op jit(solution)/shard_map/finish/pallas_call | solution.py:581
  40.5 0.7 %collective-permute-start.12 = (bf16[5,64,256]{2,1,0:T(8,128)(2,1)S(1)}, bf16[5,64,256]{2,1,0:T(8,128)(2,1)S(1)}, u32[]{:S(2)}, u32[]{:S(2)}) collective-permute-start(bf16[5,64,256]{2,1,0:T(8,128)(2,1)S(1)} %get-tuple-element.55), channel_id=1, source_target_pairs={{0,1},{1,0},{2,3},{3,2},{4,5},{5,4},{6,7},{7,6},{8,9},{9,8},{10,11... | collective-permute-start | bytes 491528 | tf_op jit(solution)/shard_map/ppermute | solution.py:452
  41.2 0.1 collective-permute-start.13
  41.3 0.4 collective-permute-start.14
  41.7 0.8 %collective-permute-done.13.refs_2_ = bf16[4,64,256]{2,1,0:T(8,128)(2,1)S(1)} collective-permute-done((bf16[4,64,256]{2,1,0:T(8,128)(2,1)S(1)}, bf16[4,64,256]{2,1,0:T(8,128)(2,1)S(1)}, u32[]{:S(2)}, u32[]{:S(2)}) %collective-permute-start.13) | collective-permute-done | bytes 131104 | tf_op jit(solution)/shard_map/ppermute | solution.py:452
  42.6 0.2 collective-permute-done.14.refs_3_
  42.7 1.4 %unpack.2 = (f32[13,256,256]{2,1,0:T(8,128)}, f32[8,128]{1,0:T(8,128)S(1)}) custom-call(s32[1]{0:T(128)} %bitcast.me_ref, f32[13,64,256]{2,1,0:T(8,128)S(1)} %get-tuple-element.54.refs_0_, bf16[5,64,256]{2,1,0:T(8,128)(2,1)S(1)} %collective-permute-done.12.refs_1_, bf16[4,64,256]{2,1,0:T(8,128)(2,1)S(1)} %collective-permute-done.13.refs_2_, ...), custom_call_target="tpu_custom_call" | custom-call | flops 10000000 | bytes 30000 | tf_op jit(solution)/shard_map/unpack/pallas_call | solution.py:613
  44.2 3.2 %collective-permute-done.11.refs_3_ = bf16[13,32,256]{2,1,0:T(8,128)(2,1)S(1)} collective-permute-done((bf16[13,32,256]{2,1,0:T(8,128)(2,1)S(1)}, bf16[13,32,256]{2,1,0:T(8,128)(2,1)S(1)}, u32[]{:S(2)}, u32[]{:S(2)}) %collective-permute-start.11) | collective-permute-done | bytes 213024 | tf_op jit(solution)/shard_map/ppermute | solution.py:452
  47.4 2.0 %unpack.3 = (f32[13,256,256]{2,1,0:T(8,128)}, f32[8,128]{1,0:T(8,128)}) custom-call(s32[1]{0:T(128)} %bitcast.me_ref, bf16[13,32,256]{2,1,0:T(8,128)(2,1)S(1)} %collective-permute-done.3.refs_8_.refs_0_, bf16[13,32,256]{2,1,0:T(8,128)(2,1)S(1)} %collective-permute-done.4.refs_9_.refs_1_, ...), custom_call_target="tpu_custom_call", output_to_operand_aliasing={{0}: (5, {})} | custom-call | flops 10000000 | bytes 30000 | tf_op jit(solution)/shard_map/unpack/pallas_call | solution.py:613
  (14 shorter events, 0.0 us)
Async XLA Ops:
  3.8 5.1 %copy-start = (bf16[13,272,256]{2,1,0:T(8,128)(2,1)S(1)}, bf16[13,272,256]{2,1,0:T(8,128)(2,1)}, u32[]{:S(2)}) copy-start(bf16[13,272,256]{2,1,0:T(8,128)(2,1)} %get-tuple-element.39.tall) | copy-start | bytes 5431300
  3.8 16.2 %collective-permute-start = (bf16[13,88,128]{2,1,0:T(8,128)(2,1)}, bf16[13,88,128]{2,1,0:T(8,128)(2,1)S(1)}, u32[]{:S(2)}, u32[]{:S(2)}) collective-permute-start(bf16[13,88,128]{2,1,0:T(8,128)(2,1)} %get-tuple-element.34), channel_id=1, source_target_pairs={{0,2},{1,3},{2,0},{3,1},{4,6},{5,7},{6,4},{7,5},{8,10},{9,11},{10,... | collective-permute-start | bytes 878600 | tf_op jit(solution)/shard_map/ppermute | solution.py:452
  6.8 13.9 %collective-permute-start.1 = (bf16[13,88,128]{2,1,0:T(8,128)(2,1)}, bf16[13,88,128]{2,1,0:T(8,128)(2,1)S(1)}, u32[]{:S(2)}, u32[]{:S(2)}) collective-permute-start(bf16[13,88,128]{2,1,0:T(8,128)(2,1)} %get-tuple-element.35), channel_id=1, source_target_pairs={{0,3},{1,2},{2,1},{3,0},{4,7},{5,6},{6,5},{7,4},{8,11},{9,10},{10,... | collective-permute-start | bytes 878600 | tf_op jit(solution)/shard_map/ppermute | solution.py:452
  6.8 13.9 %collective-permute-start.2 = (bf16[13,88,128]{2,1,0:T(8,128)(2,1)}, bf16[13,88,128]{2,1,0:T(8,128)(2,1)S(1)}, u32[]{:S(2)}, u32[]{:S(2)}) collective-permute-start(bf16[13,88,128]{2,1,0:T(8,128)(2,1)} %get-tuple-element.36), channel_id=1, source_target_pairs={{0,1},{1,0},{2,3},{3,2},{4,5},{5,4},{6,7},{7,6},{8,9},{9,8},{10,11... | collective-permute-start | bytes 878600 | tf_op jit(solution)/shard_map/ppermute | solution.py:452
  9.0 8.3 %collective-permute-start.5 = (bf16[13,16,256]{2,1,0:T(8,128)(2,1)S(1)}, bf16[13,16,256]{2,1,0:T(8,128)(2,1)S(1)}, u32[]{:S(2)}, u32[]{:S(2)}) collective-permute-start(bf16[13,16,256]{2,1,0:T(8,128)(2,1)S(1)} %get-tuple-element.40), channel_id=1, source_target_pairs={{0,4},{4,8},{8,12},{12,16},{16,20},{20,24},{24,28},{28,0},{1,5},{5... | collective-permute-start | bytes 319496 | tf_op jit(solution)/shard_map/ppermute | solution.py:532
  11.0 7.0 %collective-permute-start.6 = (bf16[13,16,256]{2,1,0:T(8,128)(2,1)S(1)}, bf16[13,16,256]{2,1,0:T(8,128)(2,1)S(1)}, u32[]{:S(2)}, u32[]{:S(2)}) collective-permute-start(bf16[13,16,256]{2,1,0:T(8,128)(2,1)S(1)} %get-tuple-element.41), channel_id=1, source_target_pairs={{4,0},{8,4},{12,8},{16,12},{20,16},{24,20},{28,24},{0,28},{5,1},{9... | collective-permute-start | bytes 319496 | tf_op jit(solution)/shard_map/ppermute | solution.py:533
  16.2 4.5 %copy-start.1 = (bf16[13,88,128]{2,1,0:T(8,128)(2,1)S(1)}, bf16[13,88,128]{2,1,0:T(8,128)(2,1)}, u32[]{:S(2)}) copy-start(bf16[13,88,128]{2,1,0:T(8,128)(2,1)} %get-tuple-element.33.refs_3_) | copy-start | bytes 878596
  18.5 8.9 %collective-permute-start.7 = (bf16[13,32,256]{2,1,0:T(8,128)(2,1)S(1)}, bf16[13,32,256]{2,1,0:T(8,128)(2,1)S(1)}, u32[]{:S(2)}, u32[]{:S(2)}) collective-permute-start(bf16[13,32,256]{2,1,0:T(8,128)(2,1)S(1)} %get-tuple-element.43), channel_id=1, source_target_pairs={{0,2},{1,3},{2,0},{3,1},{4,6},{5,7},{6,4},{7,5},{8,10},{9,11},{10,... | collective-permute-start | bytes 638984 | tf_op jit(solution)/shard_map/ppermute | solution.py:452
  20.1 9.6 %collective-permute-start.8 = (bf16[13,32,256]{2,1,0:T(8,128)(2,1)S(1)}, bf16[13,32,256]{2,1,0:T(8,128)(2,1)S(1)}, u32[]{:S(2)}, u32[]{:S(2)}) collective-permute-start(bf16[13,32,256]{2,1,0:T(8,128)(2,1)S(1)} %get-tuple-element.44), channel_id=1, source_target_pairs={{0,3},{1,2},{2,1},{3,0},{4,7},{5,6},{6,5},{7,4},{8,11},{9,10},{10,... | collective-permute-start | bytes 638984 | tf_op jit(solution)/shard_map/ppermute | solution.py:452
  20.1 9.6 %collective-permute-start.9 = (bf16[13,32,256]{2,1,0:T(8,128)(2,1)S(1)}, bf16[13,32,256]{2,1,0:T(8,128)(2,1)S(1)}, u32[]{:S(2)}, u32[]{:S(2)}) collective-permute-start(bf16[13,32,256]{2,1,0:T(8,128)(2,1)S(1)} %get-tuple-element.45), channel_id=1, source_target_pairs={{0,1},{1,0},{2,3},{3,2},{4,5},{5,4},{6,7},{7,6},{8,9},{9,8},{10,11... | collective-permute-start | bytes 638984 | tf_op jit(solution)/shard_map/ppermute | solution.py:452
  25.9 11.4 %collective-permute-start.3 = (bf16[13,32,256]{2,1,0:T(8,128)(2,1)S(1)}, bf16[13,32,256]{2,1,0:T(8,128)(2,1)S(1)}, u32[]{:S(2)}, u32[]{:S(2)}) collective-permute-start(bf16[13,32,256]{2,1,0:T(8,128)(2,1)S(1)} %get-tuple-element.37.refs_11_), channel_id=1, source_target_pairs={{0,2},{1,3},{2,0},{3,1},{4,6},{5,7},{6,4},{7,5},{8,10},{9,11},{10,... | collective-permute-start | bytes 638984 | tf_op jit(solution)/shard_map/ppermute | solution.py:452
  27.4 10.4 %collective-permute-start.4 = (bf16[13,32,256]{2,1,0:T(8,128)(2,1)S(1)}, bf16[13,32,256]{2,1,0:T(8,128)(2,1)S(1)}, u32[]{:S(2)}, u32[]{:S(2)}) collective-permute-start(bf16[13,32,256]{2,1,0:T(8,128)(2,1)S(1)} %get-tuple-element.38), channel_id=1, source_target_pairs={{0,3},{1,2},{2,1},{3,0},{4,7},{5,6},{6,5},{7,4},{8,11},{9,10},{10,... | collective-permute-start | bytes 638984 | tf_op jit(solution)/shard_map/ppermute | solution.py:452
  35.2 9.0 %collective-permute-start.10 = (bf16[13,32,256]{2,1,0:T(8,128)(2,1)S(1)}, bf16[13,32,256]{2,1,0:T(8,128)(2,1)S(1)}, u32[]{:S(2)}, u32[]{:S(2)}) collective-permute-start(bf16[13,32,256]{2,1,0:T(8,128)(2,1)S(1)} %get-tuple-element.46), channel_id=1, source_target_pairs={{0,2},{1,3},{2,0},{3,1},{4,6},{5,7},{6,4},{7,5},{8,10},{9,11},{10,... | collective-permute-start | bytes 638984 | tf_op jit(solution)/shard_map/ppermute | solution.py:452
  35.4 12.0 %collective-permute-start.11 = (bf16[13,32,256]{2,1,0:T(8,128)(2,1)S(1)}, bf16[13,32,256]{2,1,0:T(8,128)(2,1)S(1)}, u32[]{:S(2)}, u32[]{:S(2)}) collective-permute-start(bf16[13,32,256]{2,1,0:T(8,128)(2,1)S(1)} %get-tuple-element.47), channel_id=1, source_target_pairs={{0,3},{1,2},{2,1},{3,0},{4,7},{5,6},{6,5},{7,4},{8,11},{9,10},{10,... | collective-permute-start | bytes 638984 | tf_op jit(solution)/shard_map/ppermute | solution.py:452
  40.5 2.2 %collective-permute-start.12 = (bf16[5,64,256]{2,1,0:T(8,128)(2,1)S(1)}, bf16[5,64,256]{2,1,0:T(8,128)(2,1)S(1)}, u32[]{:S(2)}, u32[]{:S(2)}) collective-permute-start(bf16[5,64,256]{2,1,0:T(8,128)(2,1)S(1)} %get-tuple-element.55), channel_id=1, source_target_pairs={{0,1},{1,0},{2,3},{3,2},{4,5},{5,4},{6,7},{7,6},{8,9},{9,8},{10,11... | collective-permute-start | bytes 491528 | tf_op jit(solution)/shard_map/ppermute | solution.py:452
  41.2 1.3 %collective-permute-start.13 = (bf16[4,64,256]{2,1,0:T(8,128)(2,1)S(1)}, bf16[4,64,256]{2,1,0:T(8,128)(2,1)S(1)}, u32[]{:S(2)}, u32[]{:S(2)}) collective-permute-start(bf16[4,64,256]{2,1,0:T(8,128)(2,1)S(1)} %get-tuple-element.56), channel_id=1, source_target_pairs={{0,1},{1,0},{2,3},{3,2},{4,5},{5,4},{6,7},{7,6},{8,9},{9,8},{10,11... | collective-permute-start | bytes 393224 | tf_op jit(solution)/shard_map/ppermute | solution.py:452
  41.3 1.5 %collective-permute-start.14 = (bf16[4,64,256]{2,1,0:T(8,128)(2,1)S(1)}, bf16[4,64,256]{2,1,0:T(8,128)(2,1)S(1)}, u32[]{:S(2)}, u32[]{:S(2)}) collective-permute-start(bf16[4,64,256]{2,1,0:T(8,128)(2,1)S(1)} %get-tuple-element.57), channel_id=1, source_target_pairs={{0,1},{1,0},{2,3},{3,2},{4,5},{5,4},{6,7},{7,6},{8,9},{9,8},{10,11... | collective-permute-start | bytes 393224 | tf_op jit(solution)/shard_map/ppermute | solution.py:452

commit v10 on v9

--- a/solution.py
+++ b/solution.py
@@ -419,9 +419,10 @@
     refs[-1][...] = jnp.zeros_like(refs[-1])
 
 
-def unpack_kernel(n, slots, chunks, pieces, me_ref, *refs):
-    out, token, tall, held, leaving = refs[-5:]
-    token[...] = jnp.zeros_like(token)
+def unpack_kernel(n, slots, chunks, pieces, token, me_ref, *refs):
+    out, tall, held, leaving = *refs[-4 - len(token) : -3 - len(token)], *refs[-3:]
+    for ref in refs[-3 - len(token) : -3]:
+        ref[...] = jnp.zeros_like(ref)
     rows, cols = held.shape[1:]
     slab = cols // len(slots)
     width = slab // chunks
@@ -610,11 +611,12 @@
 
     def unpack(slots, arrays, pieces, *before):
         alias = {1 + len(arrays): 0} if before else {}
+        tokens = [] if before else [token]
         return pl.pallas_call(
-            functools.partial(unpack_kernel, n, slots, chunks, pieces),
-            out_shape=[jax.ShapeDtypeStruct((MOMENTS, rows, cols), jnp.float32), token],
+            functools.partial(unpack_kernel, n, slots, chunks, pieces, tokens),
+            out_shape=[jax.ShapeDtypeStruct((MOMENTS, rows, cols), jnp.float32), *tokens],
             in_specs=[SMEM] + [VMEM] * len(arrays) + [ANY] * len(before),
-            out_specs=[ANY, VMEM],
+            out_specs=[ANY] + [VMEM] * len(tokens),
             scratch_shapes=[
                 pltpu.VMEM((MOMENTS, cols // 2, rows), jnp.float32),
                 pltpu.VMEM((MOMENTS, rows, cols // 2), jnp.float32),
@@ -638,7 +640,7 @@
         name="arrived",
     )(*back, turned_near)
     pieces = [(s, c, 0, MOMENTS) for c in range(chunks) for s in far]
-    out, _ = unpack(far, back, tuple(pieces), out, arrived)
+    (out,) = unpack(far, back, tuple(pieces), out, arrived)
     return jnp.swapaxes(out, 0, 1)
 
 

time: 49.7 us -> 49.1 us (0.988)
  Pallas kernels: 25.9 us -> 25.3 us
    pallas_call x2, Pallas kernels: 3.39 us -> 2.81 us  [unpack(): pl.pallas_call(functools.partial(unpack_kernel, n, slots, chunks, pieces,...]
  transfers between devices with their start and end apart: 15 -> 15, of which waited for: 7 -> 7; matrix products, arithmetic and copies ran while one was open for 0% -> 0% of each run, Pallas kernels for 40% -> 41%
where the time goes in v10:
time: 49.1 us; the launch traced here: 49 us
  Pallas kernels  25.3 us (52%)
  starting transfers between devices  15.3 us (31%)
  waiting for transfers between devices  8.04 us (16%)
    pallas_call x2, Pallas kernels, sections(): pl.pallas_call(functools.partial(section_kernel, n, two, second, far, all...  10.6 us
    ppermute x13, starting transfers between devices, to_partner(): lax.ppermute(array, 'gy', [(i, i ^ s) for i in range(n)])  10.2 us
    ppermute x13, waiting for transfers between devices, to_partner(): lax.ppermute(array, 'gy', [(i, i ^ s) for i in range(n)])  7.09 us
    pallas_call x2, Pallas kernels, grid_of(): pl.pallas_call(functools.partial(grid_kernel, n, rows, slots), out_shape=...  4.03 us
    pallas_call x1, Pallas kernels, pack(): pl.pallas_call(functools.partial(pack_kernel, n, two), out_shape=shapes,...  3.81 us
    ppermute x1, starting transfers between devices, on_device(): after = lax.ppermute(left, 'gx', [(j, i) for i, j in up])  3.1 us
    pallas_call x2, Pallas kernels, unpack(): pl.pallas_call(functools.partial(unpack_kernel, n, slots, chunks, pieces,...  2.81 us
    pallas_call x1, Pallas kernels, finished(): pl.pallas_call(functools.partial(finish_kernel, n, near, parts, len(state...  2.71 us
  transfers between devices with their start and end apart: 15, of which 7 were waited for; matrix products, arithmetic and copies ran while one was open for 0% of the time, Pallas kernels for 41%

profile of v10, /device:TPU:0, one launch (start us, length us, event | category | flops | bytes accessed | tf_op | source)
XLA Modules:
  0.0 49.0 jit_solution(10611704945778248721)
XLA Ops:
  0.0 3.8 %pack.1 = (bf16[13,88,128]{2,1,0:T(8,128)(2,1)}, bf16[13,88,128]{2,1,0:T(8,128)(2,1)}, bf16[13,88,128]{2,1,0:T(8,128)(2,1)}, bf16[13,88,128]{2,1,0:T(8,128)(2,1)}, bf16[13,272,256]{2,1,0:T(8,128)(2,1)}) custom-call(s32[1]{0:T(128)} %bitcast.me_ref, f32[256,256]{1,0:T(8,128)} %refs_0_.1, f32[3,256,256]{2,1,0:T(8,128)} %bitcast.6, f32[256,256]{1,0:T(8,128)} %refs_2_.1, ...), custom_call_target="tpu_custom_call" | custom-call | flops 2000000000 | bytes 6000000 | tf_op jit(solution)/shard_map/pack/pallas_call | solution.py:484
  3.8 0.0 copy-start
  3.8 3.0 %collective-permute-start = (bf16[13,88,128]{2,1,0:T(8,128)(2,1)}, bf16[13,88,128]{2,1,0:T(8,128)(2,1)S(1)}, u32[]{:S(2)}, u32[]{:S(2)}) collective-permute-start(bf16[13,88,128]{2,1,0:T(8,128)(2,1)} %get-tuple-element.33), channel_id=1, source_target_pairs={{0,2},{1,3},{2,0},{3,1},{4,6},{5,7},{6,4},{7,5},{8,10},{9,11},{10,... | collective-permute-start | bytes 878600 | tf_op jit(solution)/shard_map/ppermute | solution.py:453
  6.8 0.0 collective-permute-start.1
  6.8 0.2 collective-permute-start.2
  7.0 1.9 %grid.2.refs_0_.tie = bf16[1024,256]{1,0:T(8,128)(2,1)S(1)} custom-call(s32[1]{0:T(128)} %bitcast.me_ref), custom_call_target="tpu_custom_call" | custom-call | flops 1000000000 | bytes 3000000 | tf_op jit(solution)/shard_map/grid/pallas_call | solution.py:509
  9.0 2.0 %collective-permute-start.5 = (bf16[13,16,256]{2,1,0:T(8,128)(2,1)S(1)}, bf16[13,16,256]{2,1,0:T(8,128)(2,1)S(1)}, u32[]{:S(2)}, u32[]{:S(2)}) collective-permute-start(bf16[13,16,256]{2,1,0:T(8,128)(2,1)S(1)} %get-tuple-element.39), channel_id=1, source_target_pairs={{0,4},{4,8},{8,12},{12,16},{16,20},{20,24},{24,28},{28,0},{1,5},{5... | collective-permute-start | bytes 319496 | tf_op jit(solution)/shard_map/ppermute | solution.py:533
  11.0 3.1 %collective-permute-start.6 = (bf16[13,16,256]{2,1,0:T(8,128)(2,1)S(1)}, bf16[13,16,256]{2,1,0:T(8,128)(2,1)S(1)}, u32[]{:S(2)}, u32[]{:S(2)}) collective-permute-start(bf16[13,16,256]{2,1,0:T(8,128)(2,1)S(1)} %get-tuple-element.40), channel_id=1, source_target_pairs={{4,0},{8,4},{12,8},{16,12},{20,16},{24,20},{28,24},{0,28},{5,1},{9... | collective-permute-start | bytes 319496 | tf_op jit(solution)/shard_map/ppermute | solution.py:534
  14.1 2.1 %grid.3.refs_1_ = bf16[1024,256]{1,0:T(8,128)(2,1)S(1)} custom-call(s32[1]{0:T(128)} %bitcast.me_ref), custom_call_target="tpu_custom_call" | custom-call | flops 1000000000 | bytes 3000000 | tf_op jit(solution)/shard_map/grid/pallas_call | solution.py:509
  16.2 0.8 %flip.1.refs_2_ = bf16[1024,512]{1,0:T(8,128)(2,1)S(1)} custom-call(bf16[1024,256]{1,0:T(8,128)(2,1)S(1)} %grid.2.refs_0_.tie, bf16[1024,256]{1,0:T(8,128)(2,1)S(1)} %grid.3.refs_1_), custom_call_target="tpu_custom_call" | custom-call | flops 300000000 | bytes 900000 | tf_op jit(solution)/shard_map/flip/pallas_call | solution.py:535
  17.1 0.2 collective-permute-done.5.before
  17.3 0.7 %collective-permute-done.6.after = bf16[13,16,256]{2,1,0:T(8,128)(2,1)S(1)} collective-permute-done((bf16[13,16,256]{2,1,0:T(8,128)(2,1)S(1)}, bf16[13,16,256]{2,1,0:T(8,128)(2,1)S(1)}, u32[]{:S(2)}, u32[]{:S(2)}) %collective-permute-start.6) | collective-permute-done | bytes 106528 | tf_op jit(solution)/shard_map/ppermute | solution.py:534
  18.0 0.5 %rest.1 = (bf16[13,32,256]{2,1,0:T(8,128)(2,1)S(1)}, bf16[13,32,256]{2,1,0:T(8,128)(2,1)S(1)}, bf16[13,32,256]{2,1,0:T(8,128)(2,1)S(1)}, bf16[13,32,256]{2,1,0:T(8,128)(2,1)S(1)}) custom-call(s32[1]{0:T(128)} %bitcast.me_ref, bf16[13,272,256]{2,1,0:T(8,128)(2,1)S(1)} %copy-done, bf16[13,16,256]{2,1,0:T(8,128)(2,1)S(1)} %collective-permute-done.5.before, ...), custom_call_target="tpu_custom_call" | custom-call | flops 200000000 | bytes 600000 | tf_op jit(solution)/shard_map/rest/pallas_call | solution.py:545
  18.5 1.6 %collective-permute-start.7 = (bf16[13,32,256]{2,1,0:T(8,128)(2,1)S(1)}, bf16[13,32,256]{2,1,0:T(8,128)(2,1)S(1)}, u32[]{:S(2)}, u32[]{:S(2)}) collective-permute-start(bf16[13,32,256]{2,1,0:T(8,128)(2,1)S(1)} %get-tuple-element.42), channel_id=1, source_target_pairs={{0,2},{1,3},{2,0},{3,1},{4,6},{5,7},{6,4},{7,5},{8,10},{9,11},{10,... | collective-permute-start | bytes 638984 | tf_op jit(solution)/shard_map/ppermute | solution.py:453
  20.1 0.0 collective-permute-done.refs_4_
  20.1 0.6 %collective-permute-start.9 = (bf16[13,32,256]{2,1,0:T(8,128)(2,1)S(1)}, bf16[13,32,256]{2,1,0:T(8,128)(2,1)S(1)}, u32[]{:S(2)}, u32[]{:S(2)}) collective-permute-start(bf16[13,32,256]{2,1,0:T(8,128)(2,1)S(1)} %get-tuple-element.44), channel_id=1, source_target_pairs={{0,1},{1,0},{2,3},{3,2},{4,5},{5,4},{6,7},{7,6},{8,9},{9,8},{10,11... | collective-permute-start | bytes 638984 | tf_op jit(solution)/shard_map/ppermute | solution.py:453
  20.7 5.1 %sections.2 = (bf16[13,32,256]{2,1,0:T(8,128)(2,1)S(1)}, bf16[13,32,256]{2,1,0:T(8,128)(2,1)S(1)}, f32[13,48,1024]{2,1,0:T(8,128)S(1)}, f32[13,32,1024]{2,1,0:T(8,128)S(1)}, bf16[416,1024]{1,0:T(8,128)(2,1)S(1)}) custom-call(s32[1]{0:T(128)} %bitcast.me_ref, bf16[1024,256]{1,0:T(8,128)(2,1)S(1)} %grid.2.refs_0_.tie, bf16[1024,256]{1,0:T(8,128)(2,1)S(1)} %grid.3.refs_1_, ...), custom_call_target="tpu_custom_call" | custom-call | flops 6000000000 | bytes 18000000 | tf_op jit(solution)/shard_map/sections/pallas_call | solution.py:562
  25.9 1.5 %collective-permute-start.3 = (bf16[13,32,256]{2,1,0:T(8,128)(2,1)S(1)}, bf16[13,32,256]{2,1,0:T(8,128)(2,1)S(1)}, u32[]{:S(2)}, u32[]{:S(2)}) collective-permute-start(bf16[13,32,256]{2,1,0:T(8,128)(2,1)S(1)} %get-tuple-element.36.refs_11_), channel_id=1, source_target_pairs={{0,2},{1,3},{2,0},{3,1},{4,6},{5,7},{6,4},{7,5},{8,10},{9,11},{10,... | collective-permute-start | bytes 638984 | tf_op jit(solution)/shard_map/ppermute | solution.py:453
  27.4 2.3 %collective-permute-done.8.refs_9_ = bf16[13,32,256]{2,1,0:T(8,128)(2,1)S(1)} collective-permute-done((bf16[13,32,256]{2,1,0:T(8,128)(2,1)S(1)}, bf16[13,32,256]{2,1,0:T(8,128)(2,1)S(1)}, u32[]{:S(2)}, u32[]{:S(2)}) %collective-permute-start.8) | collective-permute-done | bytes 213024 | tf_op jit(solution)/shard_map/ppermute | solution.py:453
  29.7 5.5 %sections.3 = (bf16[13,32,256]{2,1,0:T(8,128)(2,1)S(1)}, bf16[13,32,256]{2,1,0:T(8,128)(2,1)S(1)}, f32[13,48,1024]{2,1,0:T(8,128)S(1)}, f32[13,32,1024]{2,1,0:T(8,128)S(1)}, bf16[416,1024]{1,0:T(8,128)(2,1)S(1)}) custom-call(s32[1]{0:T(128)} %bitcast.me_ref, bf16[1024,256]{1,0:T(8,128)(2,1)S(1)} %grid.2.refs_0_.tie, bf16[1024,256]{1,0:T(8,128)(2,1)S(1)} %grid.3.refs_1_, ...), custom_call_target="tpu_custom_call" | custom-call | flops 6000000000 | bytes 18000000 | tf_op jit(solution)/shard_map/sections/pallas_call | solution.py:562
  35.2 0.2 collective-permute-start.10
  35.4 1.9 %collective-permute-start.11 = (bf16[13,32,256]{2,1,0:T(8,128)(2,1)S(1)}, bf16[13,32,256]{2,1,0:T(8,128)(2,1)S(1)}, u32[]{:S(2)}, u32[]{:S(2)}) collective-permute-start(bf16[13,32,256]{2,1,0:T(8,128)(2,1)S(1)} %get-tuple-element.46), channel_id=1, source_target_pairs={{0,3},{1,2},{2,1},{3,0},{4,7},{5,6},{6,5},{7,4},{8,11},{9,10},{10,... | collective-permute-start | bytes 638984 | tf_op jit(solution)/shard_map/ppermute | solution.py:453
  37.2 0.6 %collective-permute-done.4.refs_9_.refs_1_ = bf16[13,32,256]{2,1,0:T(8,128)(2,1)S(1)} collective-permute-done((bf16[13,32,256]{2,1,0:T(8,128)(2,1)S(1)}, bf16[13,32,256]{2,1,0:T(8,128)(2,1)S(1)}, u32[]{:S(2)}, u32[]{:S(2)}) %collective-permute-start.4) | collective-permute-done | bytes 213024 | tf_op jit(solution)/shard_map/ppermute | solution.py:453
  37.8 2.7 %finish.1 = (f32[13,64,256]{2,1,0:T(8,128)S(1)}, bf16[5,64,256]{2,1,0:T(8,128)(2,1)S(1)}, bf16[4,64,256]{2,1,0:T(8,128)(2,1)S(1)}, bf16[4,64,256]{2,1,0:T(8,128)(2,1)S(1)}) custom-call(s32[1]{0:T(128)} %bitcast.me_ref, bf16[1024,256]{1,0:T(8,128)(2,1)S(1)} %grid.2.refs_0_.tie, bf16[1024,256]{1,0:T(8,128)(2,1)S(1)} %grid.3.refs_1_, ...), custom_call_target="tpu_custom_call" | custom-call | flops 4000000000 | bytes 12000000 | tf_op jit(solution)/shard_map/finish/pallas_call | solution.py:582
  40.5 0.7 %collective-permute-start.12 = (bf16[5,64,256]{2,1,0:T(8,128)(2,1)S(1)}, bf16[5,64,256]{2,1,0:T(8,128)(2,1)S(1)}, u32[]{:S(2)}, u32[]{:S(2)}) collective-permute-start(bf16[5,64,256]{2,1,0:T(8,128)(2,1)S(1)} %get-tuple-element.54), channel_id=1, source_target_pairs={{0,1},{1,0},{2,3},{3,2},{4,5},{5,4},{6,7},{7,6},{8,9},{9,8},{10,11... | collective-permute-start | bytes 491528 | tf_op jit(solution)/shard_map/ppermute | solution.py:453
  41.2 0.1 collective-permute-start.13
  41.3 0.4 collective-permute-start.14
  41.7 0.8 %collective-permute-done.13.refs_2_ = bf16[4,64,256]{2,1,0:T(8,128)(2,1)S(1)} collective-permute-done((bf16[4,64,256]{2,1,0:T(8,128)(2,1)S(1)}, bf16[4,64,256]{2,1,0:T(8,128)(2,1)S(1)}, u32[]{:S(2)}, u32[]{:S(2)}) %collective-permute-start.13) | collective-permute-done | bytes 131104 | tf_op jit(solution)/shard_map/ppermute | solution.py:453
  42.6 0.2 collective-permute-done.14.refs_3_
  42.7 1.4 %unpack.2 = (f32[13,256,256]{2,1,0:T(8,128)}, f32[8,128]{1,0:T(8,128)S(1)}) custom-call(s32[1]{0:T(128)} %bitcast.me_ref, f32[13,64,256]{2,1,0:T(8,128)S(1)} %get-tuple-element.53.refs_0_, bf16[5,64,256]{2,1,0:T(8,128)(2,1)S(1)} %collective-permute-done.12.refs_1_, bf16[4,64,256]{2,1,0:T(8,128)(2,1)S(1)} %collective-permute-done.13.refs_2_, ...), custom_call_target="tpu_custom_call" | custom-call | flops 10000000 | bytes 30000 | tf_op jit(solution)/shard_map/unpack/pallas_call | solution.py:615
  44.2 3.2 %collective-permute-done.11.refs_3_ = bf16[13,32,256]{2,1,0:T(8,128)(2,1)S(1)} collective-permute-done((bf16[13,32,256]{2,1,0:T(8,128)(2,1)S(1)}, bf16[13,32,256]{2,1,0:T(8,128)(2,1)S(1)}, u32[]{:S(2)}, u32[]{:S(2)}) %collective-permute-start.11) | collective-permute-done | bytes 213024 | tf_op jit(solution)/shard_map/ppermute | solution.py:453
  47.4 1.4 %unpack.3 = f32[13,256,256]{2,1,0:T(8,128)} custom-call(s32[1]{0:T(128)} %bitcast.me_ref, bf16[13,32,256]{2,1,0:T(8,128)(2,1)S(1)} %collective-permute-done.3.refs_8_.refs_0_, bf16[13,32,256]{2,1,0:T(8,128)(2,1)S(1)} %collective-permute-done.4.refs_9_.refs_1_, ...), custom_call_target="tpu_custom_call", output_to_operand_aliasing={{}: (5, {})} | custom-call | flops 10000000 | bytes 30000 | tf_op jit(solution)/shard_map/unpack/pallas_call | solution.py:615
  (14 shorter events, 0.0 us)
Async XLA Ops:
  3.8 5.1 %copy-start = (bf16[13,272,256]{2,1,0:T(8,128)(2,1)S(1)}, bf16[13,272,256]{2,1,0:T(8,128)(2,1)}, u32[]{:S(2)}) copy-start(bf16[13,272,256]{2,1,0:T(8,128)(2,1)} %get-tuple-element.38.tall) | copy-start | bytes 5431300
  3.8 16.2 %collective-permute-start = (bf16[13,88,128]{2,1,0:T(8,128)(2,1)}, bf16[13,88,128]{2,1,0:T(8,128)(2,1)S(1)}, u32[]{:S(2)}, u32[]{:S(2)}) collective-permute-start(bf16[13,88,128]{2,1,0:T(8,128)(2,1)} %get-tuple-element.33), channel_id=1, source_target_pairs={{0,2},{1,3},{2,0},{3,1},{4,6},{5,7},{6,4},{7,5},{8,10},{9,11},{10,... | collective-permute-start | bytes 878600 | tf_op jit(solution)/shard_map/ppermute | solution.py:453
  6.8 13.9 %collective-permute-start.1 = (bf16[13,88,128]{2,1,0:T(8,128)(2,1)}, bf16[13,88,128]{2,1,0:T(8,128)(2,1)S(1)}, u32[]{:S(2)}, u32[]{:S(2)}) collective-permute-start(bf16[13,88,128]{2,1,0:T(8,128)(2,1)} %get-tuple-element.34), channel_id=1, source_target_pairs={{0,3},{1,2},{2,1},{3,0},{4,7},{5,6},{6,5},{7,4},{8,11},{9,10},{10,... | collective-permute-start | bytes 878600 | tf_op jit(solution)/shard_map/ppermute | solution.py:453
  6.8 13.9 %collective-permute-start.2 = (bf16[13,88,128]{2,1,0:T(8,128)(2,1)}, bf16[13,88,128]{2,1,0:T(8,128)(2,1)S(1)}, u32[]{:S(2)}, u32[]{:S(2)}) collective-permute-start(bf16[13,88,128]{2,1,0:T(8,128)(2,1)} %get-tuple-element.35), channel_id=1, source_target_pairs={{0,1},{1,0},{2,3},{3,2},{4,5},{5,4},{6,7},{7,6},{8,9},{9,8},{10,11... | collective-permute-start | bytes 878600 | tf_op jit(solution)/shard_map/ppermute | solution.py:453
  9.0 8.3 %collective-permute-start.5 = (bf16[13,16,256]{2,1,0:T(8,128)(2,1)S(1)}, bf16[13,16,256]{2,1,0:T(8,128)(2,1)S(1)}, u32[]{:S(2)}, u32[]{:S(2)}) collective-permute-start(bf16[13,16,256]{2,1,0:T(8,128)(2,1)S(1)} %get-tuple-element.39), channel_id=1, source_target_pairs={{0,4},{4,8},{8,12},{12,16},{16,20},{20,24},{24,28},{28,0},{1,5},{5... | collective-permute-start | bytes 319496 | tf_op jit(solution)/shard_map/ppermute | solution.py:533
  11.0 7.0 %collective-permute-start.6 = (bf16[13,16,256]{2,1,0:T(8,128)(2,1)S(1)}, bf16[13,16,256]{2,1,0:T(8,128)(2,1)S(1)}, u32[]{:S(2)}, u32[]{:S(2)}) collective-permute-start(bf16[13,16,256]{2,1,0:T(8,128)(2,1)S(1)} %get-tuple-element.40), channel_id=1, source_target_pairs={{4,0},{8,4},{12,8},{16,12},{20,16},{24,20},{28,24},{0,28},{5,1},{9... | collective-permute-start | bytes 319496 | tf_op jit(solution)/shard_map/ppermute | solution.py:534
  16.2 4.5 %copy-start.1 = (bf16[13,88,128]{2,1,0:T(8,128)(2,1)S(1)}, bf16[13,88,128]{2,1,0:T(8,128)(2,1)}, u32[]{:S(2)}) copy-start(bf16[13,88,128]{2,1,0:T(8,128)(2,1)} %get-tuple-element.32.refs_3_) | copy-start | bytes 878596
  18.5 8.9 %collective-permute-start.7 = (bf16[13,32,256]{2,1,0:T(8,128)(2,1)S(1)}, bf16[13,32,256]{2,1,0:T(8,128)(2,1)S(1)}, u32[]{:S(2)}, u32[]{:S(2)}) collective-permute-start(bf16[13,32,256]{2,1,0:T(8,128)(2,1)S(1)} %get-tuple-element.42), channel_id=1, source_target_pairs={{0,2},{1,3},{2,0},{3,1},{4,6},{5,7},{6,4},{7,5},{8,10},{9,11},{10,... | collective-permute-start | bytes 638984 | tf_op jit(solution)/shard_map/ppermute | solution.py:453
  20.1 9.6 %collective-permute-start.8 = (bf16[13,32,256]{2,1,0:T(8,128)(2,1)S(1)}, bf16[13,32,256]{2,1,0:T(8,128)(2,1)S(1)}, u32[]{:S(2)}, u32[]{:S(2)}) collective-permute-start(bf16[13,32,256]{2,1,0:T(8,128)(2,1)S(1)} %get-tuple-element.43), channel_id=1, source_target_pairs={{0,3},{1,2},{2,1},{3,0},{4,7},{5,6},{6,5},{7,4},{8,11},{9,10},{10,... | collective-permute-start | bytes 638984 | tf_op jit(solution)/shard_map/ppermute | solution.py:453
  20.1 9.6 %collective-permute-start.9 = (bf16[13,32,256]{2,1,0:T(8,128)(2,1)S(1)}, bf16[13,32,256]{2,1,0:T(8,128)(2,1)S(1)}, u32[]{:S(2)}, u32[]{:S(2)}) collective-permute-start(bf16[13,32,256]{2,1,0:T(8,128)(2,1)S(1)} %get-tuple-element.44), channel_id=1, source_target_pairs={{0,1},{1,0},{2,3},{3,2},{4,5},{5,4},{6,7},{7,6},{8,9},{9,8},{10,11... | collective-permute-start | bytes 638984 | tf_op jit(solution)/shard_map/ppermute | solution.py:453
  25.9 11.4 %collective-permute-start.3 = (bf16[13,32,256]{2,1,0:T(8,128)(2,1)S(1)}, bf16[13,32,256]{2,1,0:T(8,128)(2,1)S(1)}, u32[]{:S(2)}, u32[]{:S(2)}) collective-permute-start(bf16[13,32,256]{2,1,0:T(8,128)(2,1)S(1)} %get-tuple-element.36.refs_11_), channel_id=1, source_target_pairs={{0,2},{1,3},{2,0},{3,1},{4,6},{5,7},{6,4},{7,5},{8,10},{9,11},{10,... | collective-permute-start | bytes 638984 | tf_op jit(solution)/shard_map/ppermute | solution.py:453
  27.4 10.4 %collective-permute-start.4 = (bf16[13,32,256]{2,1,0:T(8,128)(2,1)S(1)}, bf16[13,32,256]{2,1,0:T(8,128)(2,1)S(1)}, u32[]{:S(2)}, u32[]{:S(2)}) collective-permute-start(bf16[13,32,256]{2,1,0:T(8,128)(2,1)S(1)} %get-tuple-element.37), channel_id=1, source_target_pairs={{0,3},{1,2},{2,1},{3,0},{4,7},{5,6},{6,5},{7,4},{8,11},{9,10},{10,... | collective-permute-start | bytes 638984 | tf_op jit(solution)/shard_map/ppermute | solution.py:453
  35.2 9.0 %collective-permute-start.10 = (bf16[13,32,256]{2,1,0:T(8,128)(2,1)S(1)}, bf16[13,32,256]{2,1,0:T(8,128)(2,1)S(1)}, u32[]{:S(2)}, u32[]{:S(2)}) collective-permute-start(bf16[13,32,256]{2,1,0:T(8,128)(2,1)S(1)} %get-tuple-element.45), channel_id=1, source_target_pairs={{0,2},{1,3},{2,0},{3,1},{4,6},{5,7},{6,4},{7,5},{8,10},{9,11},{10,... | collective-permute-start | bytes 638984 | tf_op jit(solution)/shard_map/ppermute | solution.py:453
  35.4 12.0 %collective-permute-start.11 = (bf16[13,32,256]{2,1,0:T(8,128)(2,1)S(1)}, bf16[13,32,256]{2,1,0:T(8,128)(2,1)S(1)}, u32[]{:S(2)}, u32[]{:S(2)}) collective-permute-start(bf16[13,32,256]{2,1,0:T(8,128)(2,1)S(1)} %get-tuple-element.46), channel_id=1, source_target_pairs={{0,3},{1,2},{2,1},{3,0},{4,7},{5,6},{6,5},{7,4},{8,11},{9,10},{10,... | collective-permute-start | bytes 638984 | tf_op jit(solution)/shard_map/ppermute | solution.py:453
  40.5 2.2 %collective-permute-start.12 = (bf16[5,64,256]{2,1,0:T(8,128)(2,1)S(1)}, bf16[5,64,256]{2,1,0:T(8,128)(2,1)S(1)}, u32[]{:S(2)}, u32[]{:S(2)}) collective-permute-start(bf16[5,64,256]{2,1,0:T(8,128)(2,1)S(1)} %get-tuple-element.54), channel_id=1, source_target_pairs={{0,1},{1,0},{2,3},{3,2},{4,5},{5,4},{6,7},{7,6},{8,9},{9,8},{10,11... | collective-permute-start | bytes 491528 | tf_op jit(solution)/shard_map/ppermute | solution.py:453
  41.2 1.3 %collective-permute-start.13 = (bf16[4,64,256]{2,1,0:T(8,128)(2,1)S(1)}, bf16[4,64,256]{2,1,0:T(8,128)(2,1)S(1)}, u32[]{:S(2)}, u32[]{:S(2)}) collective-permute-start(bf16[4,64,256]{2,1,0:T(8,128)(2,1)S(1)} %get-tuple-element.55), channel_id=1, source_target_pairs={{0,1},{1,0},{2,3},{3,2},{4,5},{5,4},{6,7},{7,6},{8,9},{9,8},{10,11... | collective-permute-start | bytes 393224 | tf_op jit(solution)/shard_map/ppermute | solution.py:453
  41.3 1.5 %collective-permute-start.14 = (bf16[4,64,256]{2,1,0:T(8,128)(2,1)S(1)}, bf16[4,64,256]{2,1,0:T(8,128)(2,1)S(1)}, u32[]{:S(2)}, u32[]{:S(2)}) collective-permute-start(bf16[4,64,256]{2,1,0:T(8,128)(2,1)S(1)} %get-tuple-element.56), channel_id=1, source_target_pairs={{0,1},{1,0},{2,3},{3,2},{4,5},{5,4},{6,7},{7,6},{8,9},{9,8},{10,11... | collective-permute-start | bytes 393224 | tf_op jit(solution)/shard_map/ppermute | solution.py:453

commit v11 on v10

--- a/solution.py
+++ b/solution.py
@@ -115,12 +115,12 @@
     return pl.multiple_of(to * slab + jnp.where(to % 2 == 0, slab // 2, 0), 16)
 
 
-GROUPS = ((0, 1), (1, 4), (4, 5), (5, 8), (8, 10), (10, 13))
+GROUPS = ((0, 1), (1, 4), (4, 5), (5, 8), (8, 10), (10, 12), (12, 13))
 
 
 def pack_kernel(n, two, me_ref, *refs):
     (rho, vel, temp, stress, heat), refs = refs[:5], refs[5:]
-    inputs = (rho, vel, temp, stress.at[0:3], stress.at[3:5], heat)
+    inputs = (rho, vel, temp, stress.at[0:3], stress.at[3:5], heat.at[0:2], heat.at[2:3])
     count = n if two else 0
     outs, (strip, given, arrived), refs = refs[: count + 1], refs[count + 1 : count + 4], refs[count + 4 :]
     held, left_at = refs[:-1], refs[-1]
@@ -134,20 +134,20 @@
         copies[k].start()
     wide = slab // 2 + 2 * HALO
     lane = min(rows, 128)
+    strip[0:HALO, :] = jnp.zeros((HALO, rows), jnp.float32)
+    strip[HALO + cols :, :] = jnp.zeros((HALO, rows), jnp.float32)
     leaving = []
     done = 0
     for at, (first, end) in enumerate(GROUPS):
         copies[at].wait()
         for f in range(first, end):
-            strip[f, 0:HALO, :] = jnp.zeros((HALO, rows), jnp.float32)
-            strip[f, HALO + cols :, :] = jnp.zeros((HALO, rows), jnp.float32)
-            strip[f, HALO : HALO + cols, :] = code(f, given[f]).T
+            strip[HALO : HALO + cols, :] = code(f, given[f]).T
             for s in range(count):
-                block = strip[f, pl.ds(message_start(me, s, slab), wide), :][SKIP : wide - SKIP]
+                block = strip[pl.ds(message_start(me, s, slab), wide), :][SKIP : wide - SKIP]
                 halves = [block[:, p : p + lane] for p in range(0, rows, lane)]
                 held[s][f] = jnp.concatenate(halves, axis=0).astype(jnp.bfloat16)
-            held[count][f] = strip[f].astype(jnp.bfloat16)
-        if at in (1, 3, 4, 5):
+            held[count][f] = strip[...].astype(jnp.bfloat16)
+        if at > 0:
             span = pl.ds(done, end - done)
             for k, out in enumerate(outs):
                 copy = pltpu.make_async_copy(held[k].at[span], out.at[span], left_at.at[k, at - 1])
@@ -487,7 +487,7 @@
             in_specs=[SMEM] + [HBM] * len(arrays),
             out_specs=[ANY] * len(shapes),
             scratch_shapes=[
-                pltpu.VMEM((MOMENTS, cols + 2 * HALO, rows), jnp.float32),
+                pltpu.VMEM((cols + 2 * HALO, rows), jnp.float32),
                 pltpu.VMEM((MOMENTS, rows, cols), jnp.float32),
                 pltpu.SemaphoreType.DMA((len(GROUPS),)),
             ]

time: 49.1 us -> 48.9 us (level)
  no operation moved by 1% of the time
where the time goes in v11:
time: 48.9 us; the launch traced here: 48.8 us
  Pallas kernels  25.1 us (51%)
  starting transfers between devices  15.3 us (31%)
  waiting for transfers between devices  8.13 us (17%)
    pallas_call x2, Pallas kernels, sections(): pl.pallas_call(functools.partial(section_kernel, n, two, second, far, all...  10.6 us
    ppermute x13, starting transfers between devices, to_partner(): lax.ppermute(array, 'gy', [(i, i ^ s) for i in range(n)])  10.1 us
    ppermute x13, waiting for transfers between devices, to_partner(): lax.ppermute(array, 'gy', [(i, i ^ s) for i in range(n)])  7.18 us
    pallas_call x2, Pallas kernels, grid_of(): pl.pallas_call(functools.partial(grid_kernel, n, rows, slots), out_shape=...  4.03 us
    pallas_call x1, Pallas kernels, pack(): pl.pallas_call(functools.partial(pack_kernel, n, two), out_shape=shapes,...  3.61 us
    ppermute x1, starting transfers between devices, on_device(): after = lax.ppermute(left, 'gx', [(j, i) for i, j in up])  3.1 us
    pallas_call x2, Pallas kernels, unpack(): pl.pallas_call(functools.partial(unpack_kernel, n, slots, chunks, pieces,...  2.81 us
    pallas_call x1, Pallas kernels, finished(): pl.pallas_call(functools.partial(finish_kernel, n, near, parts, len(state...  2.71 us
  transfers between devices with their start and end apart: 15, of which 7 were waited for; matrix products, arithmetic and copies ran while one was open for 0% of the time, Pallas kernels for 41%

profile of v11, /device:TPU:0, one launch (start us, length us, event | category | flops | bytes accessed | tf_op | source)
XLA Modules:
  0.0 48.8 jit_solution(10992609640223738029)
XLA Ops:
  0.0 3.6 %pack.1 = (bf16[13,88,128]{2,1,0:T(8,128)(2,1)}, bf16[13,88,128]{2,1,0:T(8,128)(2,1)}, bf16[13,88,128]{2,1,0:T(8,128)(2,1)}, bf16[13,88,128]{2,1,0:T(8,128)(2,1)}, bf16[13,272,256]{2,1,0:T(8,128)(2,1)}) custom-call(s32[1]{0:T(128)} %bitcast.me_ref, f32[256,256]{1,0:T(8,128)} %refs_0_.1, f32[3,256,256]{2,1,0:T(8,128)} %bitcast.6, f32[256,256]{1,0:T(8,128)} %refs_2_.1, ...), custom_call_target="tpu_custom_call" | custom-call | flops 2000000000 | bytes 6000000 | tf_op jit(solution)/shard_map/pack/pallas_call | solution.py:484
  3.6 0.0 copy-start
  3.6 3.0 %collective-permute-start = (bf16[13,88,128]{2,1,0:T(8,128)(2,1)}, bf16[13,88,128]{2,1,0:T(8,128)(2,1)S(1)}, u32[]{:S(2)}, u32[]{:S(2)}) collective-permute-start(bf16[13,88,128]{2,1,0:T(8,128)(2,1)} %get-tuple-element.33), channel_id=1, source_target_pairs={{0,2},{1,3},{2,0},{3,1},{4,6},{5,7},{6,4},{7,5},{8,10},{9,11},{10,... | collective-permute-start | bytes 878600 | tf_op jit(solution)/shard_map/ppermute | solution.py:453
  6.6 0.0 collective-permute-start.1
  6.6 0.2 collective-permute-start.2
  6.8 1.9 %grid.2.refs_0_.tie = bf16[1024,256]{1,0:T(8,128)(2,1)S(1)} custom-call(s32[1]{0:T(128)} %bitcast.me_ref), custom_call_target="tpu_custom_call" | custom-call | flops 1000000000 | bytes 3000000 | tf_op jit(solution)/shard_map/grid/pallas_call | solution.py:509
  8.8 2.0 %collective-permute-start.5 = (bf16[13,16,256]{2,1,0:T(8,128)(2,1)S(1)}, bf16[13,16,256]{2,1,0:T(8,128)(2,1)S(1)}, u32[]{:S(2)}, u32[]{:S(2)}) collective-permute-start(bf16[13,16,256]{2,1,0:T(8,128)(2,1)S(1)} %get-tuple-element.39), channel_id=1, source_target_pairs={{0,4},{4,8},{8,12},{12,16},{16,20},{20,24},{24,28},{28,0},{1,5},{5... | collective-permute-start | bytes 319496 | tf_op jit(solution)/shard_map/ppermute | solution.py:533
  10.8 3.1 %collective-permute-start.6 = (bf16[13,16,256]{2,1,0:T(8,128)(2,1)S(1)}, bf16[13,16,256]{2,1,0:T(8,128)(2,1)S(1)}, u32[]{:S(2)}, u32[]{:S(2)}) collective-permute-start(bf16[13,16,256]{2,1,0:T(8,128)(2,1)S(1)} %get-tuple-element.40), channel_id=1, source_target_pairs={{4,0},{8,4},{12,8},{16,12},{20,16},{24,20},{28,24},{0,28},{5,1},{9... | collective-permute-start | bytes 319496 | tf_op jit(solution)/shard_map/ppermute | solution.py:534
  13.9 2.1 %grid.3.refs_1_ = bf16[1024,256]{1,0:T(8,128)(2,1)S(1)} custom-call(s32[1]{0:T(128)} %bitcast.me_ref), custom_call_target="tpu_custom_call" | custom-call | flops 1000000000 | bytes 3000000 | tf_op jit(solution)/shard_map/grid/pallas_call | solution.py:509
  16.0 0.8 %flip.1.refs_2_ = bf16[1024,512]{1,0:T(8,128)(2,1)S(1)} custom-call(bf16[1024,256]{1,0:T(8,128)(2,1)S(1)} %grid.2.refs_0_.tie, bf16[1024,256]{1,0:T(8,128)(2,1)S(1)} %grid.3.refs_1_), custom_call_target="tpu_custom_call" | custom-call | flops 300000000 | bytes 900000 | tf_op jit(solution)/shard_map/flip/pallas_call | solution.py:535
  16.9 0.2 collective-permute-done.5.before
  17.1 0.7 %collective-permute-done.6.after = bf16[13,16,256]{2,1,0:T(8,128)(2,1)S(1)} collective-permute-done((bf16[13,16,256]{2,1,0:T(8,128)(2,1)S(1)}, bf16[13,16,256]{2,1,0:T(8,128)(2,1)S(1)}, u32[]{:S(2)}, u32[]{:S(2)}) %collective-permute-start.6) | collective-permute-done | bytes 106528 | tf_op jit(solution)/shard_map/ppermute | solution.py:534
  17.8 0.5 %rest.1 = (bf16[13,32,256]{2,1,0:T(8,128)(2,1)S(1)}, bf16[13,32,256]{2,1,0:T(8,128)(2,1)S(1)}, bf16[13,32,256]{2,1,0:T(8,128)(2,1)S(1)}, bf16[13,32,256]{2,1,0:T(8,128)(2,1)S(1)}) custom-call(s32[1]{0:T(128)} %bitcast.me_ref, bf16[13,272,256]{2,1,0:T(8,128)(2,1)S(1)} %copy-done, bf16[13,16,256]{2,1,0:T(8,128)(2,1)S(1)} %collective-permute-done.5.before, ...), custom_call_target="tpu_custom_call" | custom-call | flops 200000000 | bytes 600000 | tf_op jit(solution)/shard_map/rest/pallas_call | solution.py:545
  18.3 1.6 %collective-permute-start.7 = (bf16[13,32,256]{2,1,0:T(8,128)(2,1)S(1)}, bf16[13,32,256]{2,1,0:T(8,128)(2,1)S(1)}, u32[]{:S(2)}, u32[]{:S(2)}) collective-permute-start(bf16[13,32,256]{2,1,0:T(8,128)(2,1)S(1)} %get-tuple-element.42), channel_id=1, source_target_pairs={{0,2},{1,3},{2,0},{3,1},{4,6},{5,7},{6,4},{7,5},{8,10},{9,11},{10,... | collective-permute-start | bytes 638984 | tf_op jit(solution)/shard_map/ppermute | solution.py:453
  19.9 0.0 collective-permute-start.8
  19.9 0.6 %collective-permute-start.9 = (bf16[13,32,256]{2,1,0:T(8,128)(2,1)S(1)}, bf16[13,32,256]{2,1,0:T(8,128)(2,1)S(1)}, u32[]{:S(2)}, u32[]{:S(2)}) collective-permute-start(bf16[13,32,256]{2,1,0:T(8,128)(2,1)S(1)} %get-tuple-element.44), channel_id=1, source_target_pairs={{0,1},{1,0},{2,3},{3,2},{4,5},{5,4},{6,7},{7,6},{8,9},{9,8},{10,11... | collective-permute-start | bytes 638984 | tf_op jit(solution)/shard_map/ppermute | solution.py:453
  20.5 5.1 %sections.2 = (bf16[13,32,256]{2,1,0:T(8,128)(2,1)S(1)}, bf16[13,32,256]{2,1,0:T(8,128)(2,1)S(1)}, f32[13,48,1024]{2,1,0:T(8,128)S(1)}, f32[13,32,1024]{2,1,0:T(8,128)S(1)}, bf16[416,1024]{1,0:T(8,128)(2,1)S(1)}) custom-call(s32[1]{0:T(128)} %bitcast.me_ref, bf16[1024,256]{1,0:T(8,128)(2,1)S(1)} %grid.2.refs_0_.tie, bf16[1024,256]{1,0:T(8,128)(2,1)S(1)} %grid.3.refs_1_, ...), custom_call_target="tpu_custom_call" | custom-call | flops 6000000000 | bytes 18000000 | tf_op jit(solution)/shard_map/sections/pallas_call | solution.py:562
  25.6 1.6 %collective-permute-start.3 = (bf16[13,32,256]{2,1,0:T(8,128)(2,1)S(1)}, bf16[13,32,256]{2,1,0:T(8,128)(2,1)S(1)}, u32[]{:S(2)}, u32[]{:S(2)}) collective-permute-start(bf16[13,32,256]{2,1,0:T(8,128)(2,1)S(1)} %get-tuple-element.36.refs_11_), channel_id=1, source_target_pairs={{0,2},{1,3},{2,0},{3,1},{4,6},{5,7},{6,4},{7,5},{8,10},{9,11},{10,... | collective-permute-start | bytes 638984 | tf_op jit(solution)/shard_map/ppermute | solution.py:453
  27.2 2.2 %collective-permute-done.8.refs_9_ = bf16[13,32,256]{2,1,0:T(8,128)(2,1)S(1)} collective-permute-done((bf16[13,32,256]{2,1,0:T(8,128)(2,1)S(1)}, bf16[13,32,256]{2,1,0:T(8,128)(2,1)S(1)}, u32[]{:S(2)}, u32[]{:S(2)}) %collective-permute-start.8) | collective-permute-done | bytes 213024 | tf_op jit(solution)/shard_map/ppermute | solution.py:453
  29.5 5.5 %sections.3 = (bf16[13,32,256]{2,1,0:T(8,128)(2,1)S(1)}, bf16[13,32,256]{2,1,0:T(8,128)(2,1)S(1)}, f32[13,48,1024]{2,1,0:T(8,128)S(1)}, f32[13,32,1024]{2,1,0:T(8,128)S(1)}, bf16[416,1024]{1,0:T(8,128)(2,1)S(1)}) custom-call(s32[1]{0:T(128)} %bitcast.me_ref, bf16[1024,256]{1,0:T(8,128)(2,1)S(1)} %grid.2.refs_0_.tie, bf16[1024,256]{1,0:T(8,128)(2,1)S(1)} %grid.3.refs_1_, ...), custom_call_target="tpu_custom_call" | custom-call | flops 6000000000 | bytes 18000000 | tf_op jit(solution)/shard_map/sections/pallas_call | solution.py:562
  35.0 0.2 collective-permute-start.10
  35.2 1.9 %collective-permute-start.11 = (bf16[13,32,256]{2,1,0:T(8,128)(2,1)S(1)}, bf16[13,32,256]{2,1,0:T(8,128)(2,1)S(1)}, u32[]{:S(2)}, u32[]{:S(2)}) collective-permute-start(bf16[13,32,256]{2,1,0:T(8,128)(2,1)S(1)} %get-tuple-element.46), channel_id=1, source_target_pairs={{0,3},{1,2},{2,1},{3,0},{4,7},{5,6},{6,5},{7,4},{8,11},{9,10},{10,... | collective-permute-start | bytes 638984 | tf_op jit(solution)/shard_map/ppermute | solution.py:453
  37.0 0.7 %collective-permute-done.4.refs_9_.refs_1_ = bf16[13,32,256]{2,1,0:T(8,128)(2,1)S(1)} collective-permute-done((bf16[13,32,256]{2,1,0:T(8,128)(2,1)S(1)}, bf16[13,32,256]{2,1,0:T(8,128)(2,1)S(1)}, u32[]{:S(2)}, u32[]{:S(2)}) %collective-permute-start.4) | collective-permute-done | bytes 213024 | tf_op jit(solution)/shard_map/ppermute | solution.py:453
  37.7 2.7 %finish.1 = (f32[13,64,256]{2,1,0:T(8,128)S(1)}, bf16[5,64,256]{2,1,0:T(8,128)(2,1)S(1)}, bf16[4,64,256]{2,1,0:T(8,128)(2,1)S(1)}, bf16[4,64,256]{2,1,0:T(8,128)(2,1)S(1)}) custom-call(s32[1]{0:T(128)} %bitcast.me_ref, bf16[1024,256]{1,0:T(8,128)(2,1)S(1)} %grid.2.refs_0_.tie, bf16[1024,256]{1,0:T(8,128)(2,1)S(1)} %grid.3.refs_1_, ...), custom_call_target="tpu_custom_call" | custom-call | flops 4000000000 | bytes 12000000 | tf_op jit(solution)/shard_map/finish/pallas_call | solution.py:582
  40.4 0.6 %collective-permute-start.12 = (bf16[5,64,256]{2,1,0:T(8,128)(2,1)S(1)}, bf16[5,64,256]{2,1,0:T(8,128)(2,1)S(1)}, u32[]{:S(2)}, u32[]{:S(2)}) collective-permute-start(bf16[5,64,256]{2,1,0:T(8,128)(2,1)S(1)} %get-tuple-element.54), channel_id=1, source_target_pairs={{0,1},{1,0},{2,3},{3,2},{4,5},{5,4},{6,7},{7,6},{8,9},{9,8},{10,11... | collective-permute-start | bytes 491528 | tf_op jit(solution)/shard_map/ppermute | solution.py:453
  41.0 0.1 collective-permute-start.13
  41.1 0.4 collective-permute-start.14
  41.5 0.8 %collective-permute-done.13.refs_2_ = bf16[4,64,256]{2,1,0:T(8,128)(2,1)S(1)} collective-permute-done((bf16[4,64,256]{2,1,0:T(8,128)(2,1)S(1)}, bf16[4,64,256]{2,1,0:T(8,128)(2,1)S(1)}, u32[]{:S(2)}, u32[]{:S(2)}) %collective-permute-start.13) | collective-permute-done | bytes 131104 | tf_op jit(solution)/shard_map/ppermute | solution.py:453
  42.4 0.2 collective-permute-done.14.refs_3_
  42.6 1.4 %unpack.2 = (f32[13,256,256]{2,1,0:T(8,128)}, f32[8,128]{1,0:T(8,128)S(1)}) custom-call(s32[1]{0:T(128)} %bitcast.me_ref, f32[13,64,256]{2,1,0:T(8,128)S(1)} %get-tuple-element.53.refs_0_, bf16[5,64,256]{2,1,0:T(8,128)(2,1)S(1)} %collective-permute-done.12.refs_1_, bf16[4,64,256]{2,1,0:T(8,128)(2,1)S(1)} %collective-permute-done.13.refs_2_, ...), custom_call_target="tpu_custom_call" | custom-call | flops 10000000 | bytes 30000 | tf_op jit(solution)/shard_map/unpack/pallas_call | solution.py:615
  44.0 3.2 %collective-permute-done.11.refs_3_ = bf16[13,32,256]{2,1,0:T(8,128)(2,1)S(1)} collective-permute-done((bf16[13,32,256]{2,1,0:T(8,128)(2,1)S(1)}, bf16[13,32,256]{2,1,0:T(8,128)(2,1)S(1)}, u32[]{:S(2)}, u32[]{:S(2)}) %collective-permute-start.11) | collective-permute-done | bytes 213024 | tf_op jit(solution)/shard_map/ppermute | solution.py:453
  47.2 1.4 %unpack.3 = f32[13,256,256]{2,1,0:T(8,128)} custom-call(s32[1]{0:T(128)} %bitcast.me_ref, bf16[13,32,256]{2,1,0:T(8,128)(2,1)S(1)} %collective-permute-done.3.refs_8_.refs_0_, bf16[13,32,256]{2,1,0:T(8,128)(2,1)S(1)} %collective-permute-done.4.refs_9_.refs_1_, ...), custom_call_target="tpu_custom_call", output_to_operand_aliasing={{}: (5, {})} | custom-call | flops 10000000 | bytes 30000 | tf_op jit(solution)/shard_map/unpack/pallas_call | solution.py:615
  (14 shorter events, 0.0 us)
Async XLA Ops:
  3.6 5.1 %copy-start = (bf16[13,272,256]{2,1,0:T(8,128)(2,1)S(1)}, bf16[13,272,256]{2,1,0:T(8,128)(2,1)}, u32[]{:S(2)}) copy-start(bf16[13,272,256]{2,1,0:T(8,128)(2,1)} %get-tuple-element.38.tall) | copy-start | bytes 5431300
  3.6 16.2 %collective-permute-start = (bf16[13,88,128]{2,1,0:T(8,128)(2,1)}, bf16[13,88,128]{2,1,0:T(8,128)(2,1)S(1)}, u32[]{:S(2)}, u32[]{:S(2)}) collective-permute-start(bf16[13,88,128]{2,1,0:T(8,128)(2,1)} %get-tuple-element.33), channel_id=1, source_target_pairs={{0,2},{1,3},{2,0},{3,1},{4,6},{5,7},{6,4},{7,5},{8,10},{9,11},{10,... | collective-permute-start | bytes 878600 | tf_op jit(solution)/shard_map/ppermute | solution.py:453
  6.6 13.9 %collective-permute-start.1 = (bf16[13,88,128]{2,1,0:T(8,128)(2,1)}, bf16[13,88,128]{2,1,0:T(8,128)(2,1)S(1)}, u32[]{:S(2)}, u32[]{:S(2)}) collective-permute-start(bf16[13,88,128]{2,1,0:T(8,128)(2,1)} %get-tuple-element.34), channel_id=1, source_target_pairs={{0,3},{1,2},{2,1},{3,0},{4,7},{5,6},{6,5},{7,4},{8,11},{9,10},{10,... | collective-permute-start | bytes 878600 | tf_op jit(solution)/shard_map/ppermute | solution.py:453
  6.6 13.9 %collective-permute-start.2 = (bf16[13,88,128]{2,1,0:T(8,128)(2,1)}, bf16[13,88,128]{2,1,0:T(8,128)(2,1)S(1)}, u32[]{:S(2)}, u32[]{:S(2)}) collective-permute-start(bf16[13,88,128]{2,1,0:T(8,128)(2,1)} %get-tuple-element.35), channel_id=1, source_target_pairs={{0,1},{1,0},{2,3},{3,2},{4,5},{5,4},{6,7},{7,6},{8,9},{9,8},{10,11... | collective-permute-start | bytes 878600 | tf_op jit(solution)/shard_map/ppermute | solution.py:453
  8.8 8.3 %collective-permute-start.5 = (bf16[13,16,256]{2,1,0:T(8,128)(2,1)S(1)}, bf16[13,16,256]{2,1,0:T(8,128)(2,1)S(1)}, u32[]{:S(2)}, u32[]{:S(2)}) collective-permute-start(bf16[13,16,256]{2,1,0:T(8,128)(2,1)S(1)} %get-tuple-element.39), channel_id=1, source_target_pairs={{0,4},{4,8},{8,12},{12,16},{16,20},{20,24},{24,28},{28,0},{1,5},{5... | collective-permute-start | bytes 319496 | tf_op jit(solution)/shard_map/ppermute | solution.py:533
  10.8 7.0 %collective-permute-start.6 = (bf16[13,16,256]{2,1,0:T(8,128)(2,1)S(1)}, bf16[13,16,256]{2,1,0:T(8,128)(2,1)S(1)}, u32[]{:S(2)}, u32[]{:S(2)}) collective-permute-start(bf16[13,16,256]{2,1,0:T(8,128)(2,1)S(1)} %get-tuple-element.40), channel_id=1, source_target_pairs={{4,0},{8,4},{12,8},{16,12},{20,16},{24,20},{28,24},{0,28},{5,1},{9... | collective-permute-start | bytes 319496 | tf_op jit(solution)/shard_map/ppermute | solution.py:534
  16.0 4.5 %copy-start.1 = (bf16[13,88,128]{2,1,0:T(8,128)(2,1)S(1)}, bf16[13,88,128]{2,1,0:T(8,128)(2,1)}, u32[]{:S(2)}) copy-start(bf16[13,88,128]{2,1,0:T(8,128)(2,1)} %get-tuple-element.32.refs_3_) | copy-start | bytes 878596
  18.3 8.9 %collective-permute-start.7 = (bf16[13,32,256]{2,1,0:T(8,128)(2,1)S(1)}, bf16[13,32,256]{2,1,0:T(8,128)(2,1)S(1)}, u32[]{:S(2)}, u32[]{:S(2)}) collective-permute-start(bf16[13,32,256]{2,1,0:T(8,128)(2,1)S(1)} %get-tuple-element.42), channel_id=1, source_target_pairs={{0,2},{1,3},{2,0},{3,1},{4,6},{5,7},{6,4},{7,5},{8,10},{9,11},{10,... | collective-permute-start | bytes 638984 | tf_op jit(solution)/shard_map/ppermute | solution.py:453
  19.9 9.6 %collective-permute-start.8 = (bf16[13,32,256]{2,1,0:T(8,128)(2,1)S(1)}, bf16[13,32,256]{2,1,0:T(8,128)(2,1)S(1)}, u32[]{:S(2)}, u32[]{:S(2)}) collective-permute-start(bf16[13,32,256]{2,1,0:T(8,128)(2,1)S(1)} %get-tuple-element.43), channel_id=1, source_target_pairs={{0,3},{1,2},{2,1},{3,0},{4,7},{5,6},{6,5},{7,4},{8,11},{9,10},{10,... | collective-permute-start | bytes 638984 | tf_op jit(solution)/shard_map/ppermute | solution.py:453
  19.9 9.6 %collective-permute-start.9 = (bf16[13,32,256]{2,1,0:T(8,128)(2,1)S(1)}, bf16[13,32,256]{2,1,0:T(8,128)(2,1)S(1)}, u32[]{:S(2)}, u32[]{:S(2)}) collective-permute-start(bf16[13,32,256]{2,1,0:T(8,128)(2,1)S(1)} %get-tuple-element.44), channel_id=1, source_target_pairs={{0,1},{1,0},{2,3},{3,2},{4,5},{5,4},{6,7},{7,6},{8,9},{9,8},{10,11... | collective-permute-start | bytes 638984 | tf_op jit(solution)/shard_map/ppermute | solution.py:453
  25.6 11.4 %collective-permute-start.3 = (bf16[13,32,256]{2,1,0:T(8,128)(2,1)S(1)}, bf16[13,32,256]{2,1,0:T(8,128)(2,1)S(1)}, u32[]{:S(2)}, u32[]{:S(2)}) collective-permute-start(bf16[13,32,256]{2,1,0:T(8,128)(2,1)S(1)} %get-tuple-element.36.refs_11_), channel_id=1, source_target_pairs={{0,2},{1,3},{2,0},{3,1},{4,6},{5,7},{6,4},{7,5},{8,10},{9,11},{10,... | collective-permute-start | bytes 638984 | tf_op jit(solution)/shard_map/ppermute | solution.py:453
  27.2 10.5 %collective-permute-start.4 = (bf16[13,32,256]{2,1,0:T(8,128)(2,1)S(1)}, bf16[13,32,256]{2,1,0:T(8,128)(2,1)S(1)}, u32[]{:S(2)}, u32[]{:S(2)}) collective-permute-start(bf16[13,32,256]{2,1,0:T(8,128)(2,1)S(1)} %get-tuple-element.37), channel_id=1, source_target_pairs={{0,3},{1,2},{2,1},{3,0},{4,7},{5,6},{6,5},{7,4},{8,11},{9,10},{10,... | collective-permute-start | bytes 638984 | tf_op jit(solution)/shard_map/ppermute | solution.py:453
  35.0 9.0 %collective-permute-start.10 = (bf16[13,32,256]{2,1,0:T(8,128)(2,1)S(1)}, bf16[13,32,256]{2,1,0:T(8,128)(2,1)S(1)}, u32[]{:S(2)}, u32[]{:S(2)}) collective-permute-start(bf16[13,32,256]{2,1,0:T(8,128)(2,1)S(1)} %get-tuple-element.45), channel_id=1, source_target_pairs={{0,2},{1,3},{2,0},{3,1},{4,6},{5,7},{6,4},{7,5},{8,10},{9,11},{10,... | collective-permute-start | bytes 638984 | tf_op jit(solution)/shard_map/ppermute | solution.py:453
  35.2 12.0 %collective-permute-start.11 = (bf16[13,32,256]{2,1,0:T(8,128)(2,1)S(1)}, bf16[13,32,256]{2,1,0:T(8,128)(2,1)S(1)}, u32[]{:S(2)}, u32[]{:S(2)}) collective-permute-start(bf16[13,32,256]{2,1,0:T(8,128)(2,1)S(1)} %get-tuple-element.46), channel_id=1, source_target_pairs={{0,3},{1,2},{2,1},{3,0},{4,7},{5,6},{6,5},{7,4},{8,11},{9,10},{10,... | collective-permute-start | bytes 638984 | tf_op jit(solution)/shard_map/ppermute | solution.py:453
  40.4 2.2 %collective-permute-start.12 = (bf16[5,64,256]{2,1,0:T(8,128)(2,1)S(1)}, bf16[5,64,256]{2,1,0:T(8,128)(2,1)S(1)}, u32[]{:S(2)}, u32[]{:S(2)}) collective-permute-start(bf16[5,64,256]{2,1,0:T(8,128)(2,1)S(1)} %get-tuple-element.54), channel_id=1, source_target_pairs={{0,1},{1,0},{2,3},{3,2},{4,5},{5,4},{6,7},{7,6},{8,9},{9,8},{10,11... | collective-permute-start | bytes 491528 | tf_op jit(solution)/shard_map/ppermute | solution.py:453
  41.0 1.3 %collective-permute-start.13 = (bf16[4,64,256]{2,1,0:T(8,128)(2,1)S(1)}, bf16[4,64,256]{2,1,0:T(8,128)(2,1)S(1)}, u32[]{:S(2)}, u32[]{:S(2)}) collective-permute-start(bf16[4,64,256]{2,1,0:T(8,128)(2,1)S(1)} %get-tuple-element.55), channel_id=1, source_target_pairs={{0,1},{1,0},{2,3},{3,2},{4,5},{5,4},{6,7},{7,6},{8,9},{9,8},{10,11... | collective-permute-start | bytes 393224 | tf_op jit(solution)/shard_map/ppermute | solution.py:453
  41.1 1.5 %collective-permute-start.14 = (bf16[4,64,256]{2,1,0:T(8,128)(2,1)S(1)}, bf16[4,64,256]{2,1,0:T(8,128)(2,1)S(1)}, u32[]{:S(2)}, u32[]{:S(2)}) collective-permute-start(bf16[4,64,256]{2,1,0:T(8,128)(2,1)S(1)} %get-tuple-element.56), channel_id=1, source_target_pairs={{0,1},{1,0},{2,3},{3,2},{4,5},{5,4},{6,7},{7,6},{8,9},{9,8},{10,11... | collective-permute-start | bytes 393224 | tf_op jit(solution)/shard_map/ppermute | solution.py:453

commit v12 on v11

--- a/solution.py
+++ b/solution.py
@@ -146,11 +146,16 @@
                 block = strip[pl.ds(message_start(me, s, slab), wide), :][SKIP : wide - SKIP]
                 halves = [block[:, p : p + lane] for p in range(0, rows, lane)]
                 held[s][f] = jnp.concatenate(halves, axis=0).astype(jnp.bfloat16)
-            held[count][f] = strip[...].astype(jnp.bfloat16)
+            for d in range(n):
+                start = d * slab + (slab // 2 if two and d % 2 else 0)
+                block = strip[start : start + held[count].shape[2], :]
+                held[count][d, f] = block.astype(jnp.bfloat16)
         if at > 0:
             span = pl.ds(done, end - done)
             for k, out in enumerate(outs):
-                copy = pltpu.make_async_copy(held[k].at[span], out.at[span], left_at.at[k, at - 1])
+                at_span = (slice(None), span) if k == count else span
+                mine, there = held[k].at[at_span], out.at[at_span]
+                copy = pltpu.make_async_copy(mine, there, left_at.at[k, at - 1])
                 copy.start()
                 leaving.append(copy)
             done = end
@@ -159,26 +164,20 @@
 
 
 def edge_kernel(tall, tie, left, right):
-    cols = tall.shape[1] - 2 * HALO
-    left[...] = tall[:, 0 : 2 * HALO, :]
-    right[...] = tall[:, cols : cols + 2 * HALO, :]
+    n, _, wide, _ = tall.shape
+    left[...] = tall[0, :, 0 : 2 * HALO, :]
+    right[...] = tall[n - 1, :, wide - 2 * HALO : wide, :]
 
 
 def rest_kernel(n, two, me_ref, tall, before, after, *outs):
     me = me_ref[0]
-    slab = (tall.shape[1] - 2 * HALO) // n
-    count = outs[0].shape[1]
-    wide = slab // 2 + 2 * HALO if two else count
+    count, wide = outs[0].shape[1], tall.shape[2]
     line = lax.broadcasted_iota(jnp.int32, before.shape[1:], 0)
     for s in range(n):
         to = jnp.bitwise_xor(me, s)
         even = to % 2 == 0
-        start = to * slab
-        if two:
-            start += jnp.where(even, 0, slab // 2)
-        start = pl.multiple_of(start, 16)
         for f in range(MOMENTS):
-            block = tall[f, pl.ds(start, wide), :].astype(jnp.float32)
+            block = tall[to, f].astype(jnp.float32)
             first, last = block[: 2 * HALO], block[wide - 2 * HALO :]
             first = jnp.where((line < HALO) & (to == 0), before[f].astype(jnp.float32), first)
             last = jnp.where((line >= HALO) & (to == n - 1), after[f].astype(jnp.float32), last)
@@ -480,7 +479,7 @@
     def pack(arrays):
         sent = (MOMENTS, (wide - 2 * SKIP) * (rows // lane), lane)
         shapes = [jax.ShapeDtypeStruct(sent, half)] * n if two else []
-        shapes += [message(cols + 2 * HALO)]
+        shapes += [jax.ShapeDtypeStruct((n, MOMENTS, wide, rows), half)]
         return pl.pallas_call(
             functools.partial(pack_kernel, n, two),
             out_shape=shapes,

time: 48.9 us -> 48.9 us (level)
  no operation moved by 1% of the time
where the time goes in v12:
time: 48.9 us; the launch traced here: 48.8 us
  Pallas kernels  25.1 us (51%)
  starting transfers between devices  15.4 us (31%)
  waiting for transfers between devices  8.05 us (16%)
    pallas_call x2, Pallas kernels, sections(): pl.pallas_call(functools.partial(section_kernel, n, two, second, far, all...  10.6 us
    ppermute x13, starting transfers between devices, to_partner(): lax.ppermute(array, 'gy', [(i, i ^ s) for i in range(n)])  10.2 us
    ppermute x13, waiting for transfers between devices, to_partner(): lax.ppermute(array, 'gy', [(i, i ^ s) for i in range(n)])  7.1 us
    pallas_call x2, Pallas kernels, grid_of(): pl.pallas_call(functools.partial(grid_kernel, n, rows, slots), out_shape=...  4.03 us
    pallas_call x1, Pallas kernels, pack(): pl.pallas_call(functools.partial(pack_kernel, n, two), out_shape=shapes,...  3.63 us
    ppermute x1, starting transfers between devices, on_device(): after = lax.ppermute(left, 'gx', [(j, i) for i, j in up])  3.1 us
    pallas_call x2, Pallas kernels, unpack(): pl.pallas_call(functools.partial(unpack_kernel, n, slots, chunks, pieces,...  2.81 us
    pallas_call x1, Pallas kernels, finished(): pl.pallas_call(functools.partial(finish_kernel, n, near, parts, len(state...  2.7 us
  transfers between devices with their start and end apart: 15, of which 7 were waited for; matrix products, arithmetic and copies ran while one was open for 0% of the time, Pallas kernels for 41%

profile of v12, /device:TPU:0, one launch (start us, length us, event | category | flops | bytes accessed | tf_op | source)
XLA Modules:
  0.0 48.8 jit_solution(16967955663407181868)
XLA Ops:
  0.0 3.6 %pack.1 = (bf16[13,88,128]{2,1,0:T(8,128)(2,1)}, bf16[13,88,128]{2,1,0:T(8,128)(2,1)}, bf16[13,88,128]{2,1,0:T(8,128)(2,1)}, bf16[13,88,128]{2,1,0:T(8,128)(2,1)}, bf16[4,13,48,256]{3,2,1,0:T(8,128)(2,1)}) custom-call(s32[1]{0:T(128)} %bitcast.me_ref, f32[256,256]{1,0:T(8,128)} %refs_0_.1, f32[3,256,256]{2,1,0:T(8,128)} %bitcast.6, f32[256,256]{1,0:T(8,128)} %refs_2_.1, ...), custom_call_target="tpu_custom_call" | custom-call | flops 2000000000 | bytes 6000000 | tf_op jit(solution)/shard_map/pack/pallas_call | solution.py:483
  3.6 0.0 copy-start
  3.6 3.0 %collective-permute-start = (bf16[13,88,128]{2,1,0:T(8,128)(2,1)}, bf16[13,88,128]{2,1,0:T(8,128)(2,1)S(1)}, u32[]{:S(2)}, u32[]{:S(2)}) collective-permute-start(bf16[13,88,128]{2,1,0:T(8,128)(2,1)} %get-tuple-element.33), channel_id=1, source_target_pairs={{0,2},{1,3},{2,0},{3,1},{4,6},{5,7},{6,4},{7,5},{8,10},{9,11},{10,... | collective-permute-start | bytes 878600 | tf_op jit(solution)/shard_map/ppermute | solution.py:452
  6.7 0.0 collective-permute-start.1
  6.7 0.2 collective-permute-start.2
  6.8 1.9 %grid.2.refs_0_.tie = bf16[1024,256]{1,0:T(8,128)(2,1)S(1)} custom-call(s32[1]{0:T(128)} %bitcast.me_ref), custom_call_target="tpu_custom_call" | custom-call | flops 1000000000 | bytes 3000000 | tf_op jit(solution)/shard_map/grid/pallas_call | solution.py:508
  8.8 2.0 %collective-permute-start.5 = (bf16[13,16,256]{2,1,0:T(8,128)(2,1)S(1)}, bf16[13,16,256]{2,1,0:T(8,128)(2,1)S(1)}, u32[]{:S(2)}, u32[]{:S(2)}) collective-permute-start(bf16[13,16,256]{2,1,0:T(8,128)(2,1)S(1)} %get-tuple-element.39), channel_id=1, source_target_pairs={{0,4},{4,8},{8,12},{12,16},{16,20},{20,24},{24,28},{28,0},{1,5},{5... | collective-permute-start | bytes 319496 | tf_op jit(solution)/shard_map/ppermute | solution.py:532
  10.8 3.1 %collective-permute-start.6 = (bf16[13,16,256]{2,1,0:T(8,128)(2,1)S(1)}, bf16[13,16,256]{2,1,0:T(8,128)(2,1)S(1)}, u32[]{:S(2)}, u32[]{:S(2)}) collective-permute-start(bf16[13,16,256]{2,1,0:T(8,128)(2,1)S(1)} %get-tuple-element.40), channel_id=1, source_target_pairs={{4,0},{8,4},{12,8},{16,12},{20,16},{24,20},{28,24},{0,28},{5,1},{9... | collective-permute-start | bytes 319496 | tf_op jit(solution)/shard_map/ppermute | solution.py:533
  13.9 2.1 %grid.3.refs_1_ = bf16[1024,256]{1,0:T(8,128)(2,1)S(1)} custom-call(s32[1]{0:T(128)} %bitcast.me_ref), custom_call_target="tpu_custom_call" | custom-call | flops 1000000000 | bytes 3000000 | tf_op jit(solution)/shard_map/grid/pallas_call | solution.py:508
  16.1 0.8 %flip.1.refs_2_ = bf16[1024,512]{1,0:T(8,128)(2,1)S(1)} custom-call(bf16[1024,256]{1,0:T(8,128)(2,1)S(1)} %grid.2.refs_0_.tie, bf16[1024,256]{1,0:T(8,128)(2,1)S(1)} %grid.3.refs_1_), custom_call_target="tpu_custom_call" | custom-call | flops 300000000 | bytes 900000 | tf_op jit(solution)/shard_map/flip/pallas_call | solution.py:534
  16.9 0.2 collective-permute-done.5.before
  17.1 0.7 %collective-permute-done.6.after = bf16[13,16,256]{2,1,0:T(8,128)(2,1)S(1)} collective-permute-done((bf16[13,16,256]{2,1,0:T(8,128)(2,1)S(1)}, bf16[13,16,256]{2,1,0:T(8,128)(2,1)S(1)}, u32[]{:S(2)}, u32[]{:S(2)}) %collective-permute-start.6) | collective-permute-done | bytes 106528 | tf_op jit(solution)/shard_map/ppermute | solution.py:533
  17.8 0.5 %rest.1 = (bf16[13,32,256]{2,1,0:T(8,128)(2,1)S(1)}, bf16[13,32,256]{2,1,0:T(8,128)(2,1)S(1)}, bf16[13,32,256]{2,1,0:T(8,128)(2,1)S(1)}, bf16[13,32,256]{2,1,0:T(8,128)(2,1)S(1)}) custom-call(s32[1]{0:T(128)} %bitcast.me_ref, bf16[4,13,48,256]{3,2,1,0:T(8,128)(2,1)S(1)} %copy-done, bf16[13,16,256]{2,1,0:T(8,128)(2,1)S(1)} %collective-permute-done.5.before, ...), custom_call_target="tpu_custom_call" | custom-call | flops 200000000 | bytes 600000 | tf_op jit(solution)/shard_map/rest/pallas_call | solution.py:544
  18.3 1.6 %collective-permute-start.7 = (bf16[13,32,256]{2,1,0:T(8,128)(2,1)S(1)}, bf16[13,32,256]{2,1,0:T(8,128)(2,1)S(1)}, u32[]{:S(2)}, u32[]{:S(2)}) collective-permute-start(bf16[13,32,256]{2,1,0:T(8,128)(2,1)S(1)} %get-tuple-element.42), channel_id=1, source_target_pairs={{0,2},{1,3},{2,0},{3,1},{4,6},{5,7},{6,4},{7,5},{8,10},{9,11},{10,... | collective-permute-start | bytes 638984 | tf_op jit(solution)/shard_map/ppermute | solution.py:452
  19.9 0.0 collective-permute-start.8
  19.9 0.6 %collective-permute-start.9 = (bf16[13,32,256]{2,1,0:T(8,128)(2,1)S(1)}, bf16[13,32,256]{2,1,0:T(8,128)(2,1)S(1)}, u32[]{:S(2)}, u32[]{:S(2)}) collective-permute-start(bf16[13,32,256]{2,1,0:T(8,128)(2,1)S(1)} %get-tuple-element.44), channel_id=1, source_target_pairs={{0,1},{1,0},{2,3},{3,2},{4,5},{5,4},{6,7},{7,6},{8,9},{9,8},{10,11... | collective-permute-start | bytes 638984 | tf_op jit(solution)/shard_map/ppermute | solution.py:452
  20.5 5.1 %sections.2 = (bf16[13,32,256]{2,1,0:T(8,128)(2,1)S(1)}, bf16[13,32,256]{2,1,0:T(8,128)(2,1)S(1)}, f32[13,48,1024]{2,1,0:T(8,128)S(1)}, f32[13,32,1024]{2,1,0:T(8,128)S(1)}, bf16[416,1024]{1,0:T(8,128)(2,1)S(1)}) custom-call(s32[1]{0:T(128)} %bitcast.me_ref, bf16[1024,256]{1,0:T(8,128)(2,1)S(1)} %grid.2.refs_0_.tie, bf16[1024,256]{1,0:T(8,128)(2,1)S(1)} %grid.3.refs_1_, ...), custom_call_target="tpu_custom_call" | custom-call | flops 6000000000 | bytes 18000000 | tf_op jit(solution)/shard_map/sections/pallas_call | solution.py:561
  25.6 1.6 %collective-permute-start.3 = (bf16[13,32,256]{2,1,0:T(8,128)(2,1)S(1)}, bf16[13,32,256]{2,1,0:T(8,128)(2,1)S(1)}, u32[]{:S(2)}, u32[]{:S(2)}) collective-permute-start(bf16[13,32,256]{2,1,0:T(8,128)(2,1)S(1)} %get-tuple-element.36.refs_11_), channel_id=1, source_target_pairs={{0,2},{1,3},{2,0},{3,1},{4,6},{5,7},{6,4},{7,5},{8,10},{9,11},{10,... | collective-permute-start | bytes 638984 | tf_op jit(solution)/shard_map/ppermute | solution.py:452
  27.2 2.3 %collective-permute-done.8.refs_9_ = bf16[13,32,256]{2,1,0:T(8,128)(2,1)S(1)} collective-permute-done((bf16[13,32,256]{2,1,0:T(8,128)(2,1)S(1)}, bf16[13,32,256]{2,1,0:T(8,128)(2,1)S(1)}, u32[]{:S(2)}, u32[]{:S(2)}) %collective-permute-start.8) | collective-permute-done | bytes 213024 | tf_op jit(solution)/shard_map/ppermute | solution.py:452
  29.5 5.5 %sections.3 = (bf16[13,32,256]{2,1,0:T(8,128)(2,1)S(1)}, bf16[13,32,256]{2,1,0:T(8,128)(2,1)S(1)}, f32[13,48,1024]{2,1,0:T(8,128)S(1)}, f32[13,32,1024]{2,1,0:T(8,128)S(1)}, bf16[416,1024]{1,0:T(8,128)(2,1)S(1)}) custom-call(s32[1]{0:T(128)} %bitcast.me_ref, bf16[1024,256]{1,0:T(8,128)(2,1)S(1)} %grid.2.refs_0_.tie, bf16[1024,256]{1,0:T(8,128)(2,1)S(1)} %grid.3.refs_1_, ...), custom_call_target="tpu_custom_call" | custom-call | flops 6000000000 | bytes 18000000 | tf_op jit(solution)/shard_map/sections/pallas_call | solution.py:561
  35.0 0.2 collective-permute-start.10
  35.2 1.9 %collective-permute-start.11 = (bf16[13,32,256]{2,1,0:T(8,128)(2,1)S(1)}, bf16[13,32,256]{2,1,0:T(8,128)(2,1)S(1)}, u32[]{:S(2)}, u32[]{:S(2)}) collective-permute-start(bf16[13,32,256]{2,1,0:T(8,128)(2,1)S(1)} %get-tuple-element.46), channel_id=1, source_target_pairs={{0,3},{1,2},{2,1},{3,0},{4,7},{5,6},{6,5},{7,4},{8,11},{9,10},{10,... | collective-permute-start | bytes 638984 | tf_op jit(solution)/shard_map/ppermute | solution.py:452
  37.0 0.6 %collective-permute-done.4.refs_9_.refs_1_ = bf16[13,32,256]{2,1,0:T(8,128)(2,1)S(1)} collective-permute-done((bf16[13,32,256]{2,1,0:T(8,128)(2,1)S(1)}, bf16[13,32,256]{2,1,0:T(8,128)(2,1)S(1)}, u32[]{:S(2)}, u32[]{:S(2)}) %collective-permute-start.4) | collective-permute-done | bytes 213024 | tf_op jit(solution)/shard_map/ppermute | solution.py:452
  37.6 2.7 %finish.1 = (f32[13,64,256]{2,1,0:T(8,128)S(1)}, bf16[5,64,256]{2,1,0:T(8,128)(2,1)S(1)}, bf16[4,64,256]{2,1,0:T(8,128)(2,1)S(1)}, bf16[4,64,256]{2,1,0:T(8,128)(2,1)S(1)}) custom-call(s32[1]{0:T(128)} %bitcast.me_ref, bf16[1024,256]{1,0:T(8,128)(2,1)S(1)} %grid.2.refs_0_.tie, bf16[1024,256]{1,0:T(8,128)(2,1)S(1)} %grid.3.refs_1_, ...), custom_call_target="tpu_custom_call" | custom-call | flops 4000000000 | bytes 12000000 | tf_op jit(solution)/shard_map/finish/pallas_call | solution.py:581
  40.3 0.7 %collective-permute-start.12 = (bf16[5,64,256]{2,1,0:T(8,128)(2,1)S(1)}, bf16[5,64,256]{2,1,0:T(8,128)(2,1)S(1)}, u32[]{:S(2)}, u32[]{:S(2)}) collective-permute-start(bf16[5,64,256]{2,1,0:T(8,128)(2,1)S(1)} %get-tuple-element.54), channel_id=1, source_target_pairs={{0,1},{1,0},{2,3},{3,2},{4,5},{5,4},{6,7},{7,6},{8,9},{9,8},{10,11... | collective-permute-start | bytes 491528 | tf_op jit(solution)/shard_map/ppermute | solution.py:452
  41.0 0.1 collective-permute-start.13
  41.1 0.4 collective-permute-start.14
  41.5 0.8 %collective-permute-done.13.refs_2_ = bf16[4,64,256]{2,1,0:T(8,128)(2,1)S(1)} collective-permute-done((bf16[4,64,256]{2,1,0:T(8,128)(2,1)S(1)}, bf16[4,64,256]{2,1,0:T(8,128)(2,1)S(1)}, u32[]{:S(2)}, u32[]{:S(2)}) %collective-permute-start.13) | collective-permute-done | bytes 131104 | tf_op jit(solution)/shard_map/ppermute | solution.py:452
  42.4 0.2 collective-permute-done.14.refs_3_
  42.6 1.4 %unpack.2 = (f32[13,256,256]{2,1,0:T(8,128)}, f32[8,128]{1,0:T(8,128)S(1)}) custom-call(s32[1]{0:T(128)} %bitcast.me_ref, f32[13,64,256]{2,1,0:T(8,128)S(1)} %get-tuple-element.53.refs_0_, bf16[5,64,256]{2,1,0:T(8,128)(2,1)S(1)} %collective-permute-done.12.refs_1_, bf16[4,64,256]{2,1,0:T(8,128)(2,1)S(1)} %collective-permute-done.13.refs_2_, ...), custom_call_target="tpu_custom_call" | custom-call | flops 10000000 | bytes 30000 | tf_op jit(solution)/shard_map/unpack/pallas_call | solution.py:614
  44.0 3.2 %collective-permute-done.11.refs_3_ = bf16[13,32,256]{2,1,0:T(8,128)(2,1)S(1)} collective-permute-done((bf16[13,32,256]{2,1,0:T(8,128)(2,1)S(1)}, bf16[13,32,256]{2,1,0:T(8,128)(2,1)S(1)}, u32[]{:S(2)}, u32[]{:S(2)}) %collective-permute-start.11) | collective-permute-done | bytes 213024 | tf_op jit(solution)/shard_map/ppermute | solution.py:452
  47.2 1.4 %unpack.3 = f32[13,256,256]{2,1,0:T(8,128)} custom-call(s32[1]{0:T(128)} %bitcast.me_ref, bf16[13,32,256]{2,1,0:T(8,128)(2,1)S(1)} %collective-permute-done.3.refs_8_.refs_0_, bf16[13,32,256]{2,1,0:T(8,128)(2,1)S(1)} %collective-permute-done.4.refs_9_.refs_1_, ...), custom_call_target="tpu_custom_call", output_to_operand_aliasing={{}: (5, {})} | custom-call | flops 10000000 | bytes 30000 | tf_op jit(solution)/shard_map/unpack/pallas_call | solution.py:614
  (14 shorter events, 0.0 us)
Async XLA Ops:
  3.6 5.1 %copy-start = (bf16[4,13,48,256]{3,2,1,0:T(8,128)(2,1)S(1)}, bf16[4,13,48,256]{3,2,1,0:T(8,128)(2,1)}, u32[]{:S(2)}) copy-start(bf16[4,13,48,256]{3,2,1,0:T(8,128)(2,1)} %get-tuple-element.38.tall) | copy-start | bytes 3833860
  3.6 16.2 %collective-permute-start = (bf16[13,88,128]{2,1,0:T(8,128)(2,1)}, bf16[13,88,128]{2,1,0:T(8,128)(2,1)S(1)}, u32[]{:S(2)}, u32[]{:S(2)}) collective-permute-start(bf16[13,88,128]{2,1,0:T(8,128)(2,1)} %get-tuple-element.33), channel_id=1, source_target_pairs={{0,2},{1,3},{2,0},{3,1},{4,6},{5,7},{6,4},{7,5},{8,10},{9,11},{10,... | collective-permute-start | bytes 878600 | tf_op jit(solution)/shard_map/ppermute | solution.py:452
  6.7 13.9 %collective-permute-start.1 = (bf16[13,88,128]{2,1,0:T(8,128)(2,1)}, bf16[13,88,128]{2,1,0:T(8,128)(2,1)S(1)}, u32[]{:S(2)}, u32[]{:S(2)}) collective-permute-start(bf16[13,88,128]{2,1,0:T(8,128)(2,1)} %get-tuple-element.34), channel_id=1, source_target_pairs={{0,3},{1,2},{2,1},{3,0},{4,7},{5,6},{6,5},{7,4},{8,11},{9,10},{10,... | collective-permute-start | bytes 878600 | tf_op jit(solution)/shard_map/ppermute | solution.py:452
  6.7 13.9 %collective-permute-start.2 = (bf16[13,88,128]{2,1,0:T(8,128)(2,1)}, bf16[13,88,128]{2,1,0:T(8,128)(2,1)S(1)}, u32[]{:S(2)}, u32[]{:S(2)}) collective-permute-start(bf16[13,88,128]{2,1,0:T(8,128)(2,1)} %get-tuple-element.35), channel_id=1, source_target_pairs={{0,1},{1,0},{2,3},{3,2},{4,5},{5,4},{6,7},{7,6},{8,9},{9,8},{10,11... | collective-permute-start | bytes 878600 | tf_op jit(solution)/shard_map/ppermute | solution.py:452
  8.8 8.3 %collective-permute-start.5 = (bf16[13,16,256]{2,1,0:T(8,128)(2,1)S(1)}, bf16[13,16,256]{2,1,0:T(8,128)(2,1)S(1)}, u32[]{:S(2)}, u32[]{:S(2)}) collective-permute-start(bf16[13,16,256]{2,1,0:T(8,128)(2,1)S(1)} %get-tuple-element.39), channel_id=1, source_target_pairs={{0,4},{4,8},{8,12},{12,16},{16,20},{20,24},{24,28},{28,0},{1,5},{5... | collective-permute-start | bytes 319496 | tf_op jit(solution)/shard_map/ppermute | solution.py:532
  10.8 7.0 %collective-permute-start.6 = (bf16[13,16,256]{2,1,0:T(8,128)(2,1)S(1)}, bf16[13,16,256]{2,1,0:T(8,128)(2,1)S(1)}, u32[]{:S(2)}, u32[]{:S(2)}) collective-permute-start(bf16[13,16,256]{2,1,0:T(8,128)(2,1)S(1)} %get-tuple-element.40), channel_id=1, source_target_pairs={{4,0},{8,4},{12,8},{16,12},{20,16},{24,20},{28,24},{0,28},{5,1},{9... | collective-permute-start | bytes 319496 | tf_op jit(solution)/shard_map/ppermute | solution.py:533
  16.0 4.5 %copy-start.1 = (bf16[13,88,128]{2,1,0:T(8,128)(2,1)S(1)}, bf16[13,88,128]{2,1,0:T(8,128)(2,1)}, u32[]{:S(2)}) copy-start(bf16[13,88,128]{2,1,0:T(8,128)(2,1)} %get-tuple-element.32.refs_3_) | copy-start | bytes 878596
  18.3 8.9 %collective-permute-start.7 = (bf16[13,32,256]{2,1,0:T(8,128)(2,1)S(1)}, bf16[13,32,256]{2,1,0:T(8,128)(2,1)S(1)}, u32[]{:S(2)}, u32[]{:S(2)}) collective-permute-start(bf16[13,32,256]{2,1,0:T(8,128)(2,1)S(1)} %get-tuple-element.42), channel_id=1, source_target_pairs={{0,2},{1,3},{2,0},{3,1},{4,6},{5,7},{6,4},{7,5},{8,10},{9,11},{10,... | collective-permute-start | bytes 638984 | tf_op jit(solution)/shard_map/ppermute | solution.py:452
  19.9 9.6 %collective-permute-start.8 = (bf16[13,32,256]{2,1,0:T(8,128)(2,1)S(1)}, bf16[13,32,256]{2,1,0:T(8,128)(2,1)S(1)}, u32[]{:S(2)}, u32[]{:S(2)}) collective-permute-start(bf16[13,32,256]{2,1,0:T(8,128)(2,1)S(1)} %get-tuple-element.43), channel_id=1, source_target_pairs={{0,3},{1,2},{2,1},{3,0},{4,7},{5,6},{6,5},{7,4},{8,11},{9,10},{10,... | collective-permute-start | bytes 638984 | tf_op jit(solution)/shard_map/ppermute | solution.py:452
  19.9 9.6 %collective-permute-start.9 = (bf16[13,32,256]{2,1,0:T(8,128)(2,1)S(1)}, bf16[13,32,256]{2,1,0:T(8,128)(2,1)S(1)}, u32[]{:S(2)}, u32[]{:S(2)}) collective-permute-start(bf16[13,32,256]{2,1,0:T(8,128)(2,1)S(1)} %get-tuple-element.44), channel_id=1, source_target_pairs={{0,1},{1,0},{2,3},{3,2},{4,5},{5,4},{6,7},{7,6},{8,9},{9,8},{10,11... | collective-permute-start | bytes 638984 | tf_op jit(solution)/shard_map/ppermute | solution.py:452
  25.6 11.4 %collective-permute-start.3 = (bf16[13,32,256]{2,1,0:T(8,128)(2,1)S(1)}, bf16[13,32,256]{2,1,0:T(8,128)(2,1)S(1)}, u32[]{:S(2)}, u32[]{:S(2)}) collective-permute-start(bf16[13,32,256]{2,1,0:T(8,128)(2,1)S(1)} %get-tuple-element.36.refs_11_), channel_id=1, source_target_pairs={{0,2},{1,3},{2,0},{3,1},{4,6},{5,7},{6,4},{7,5},{8,10},{9,11},{10,... | collective-permute-start | bytes 638984 | tf_op jit(solution)/shard_map/ppermute | solution.py:452
  27.2 10.4 %collective-permute-start.4 = (bf16[13,32,256]{2,1,0:T(8,128)(2,1)S(1)}, bf16[13,32,256]{2,1,0:T(8,128)(2,1)S(1)}, u32[]{:S(2)}, u32[]{:S(2)}) collective-permute-start(bf16[13,32,256]{2,1,0:T(8,128)(2,1)S(1)} %get-tuple-element.37), channel_id=1, source_target_pairs={{0,3},{1,2},{2,1},{3,0},{4,7},{5,6},{6,5},{7,4},{8,11},{9,10},{10,... | collective-permute-start | bytes 638984 | tf_op jit(solution)/shard_map/ppermute | solution.py:452
  35.0 9.0 %collective-permute-start.10 = (bf16[13,32,256]{2,1,0:T(8,128)(2,1)S(1)}, bf16[13,32,256]{2,1,0:T(8,128)(2,1)S(1)}, u32[]{:S(2)}, u32[]{:S(2)}) collective-permute-start(bf16[13,32,256]{2,1,0:T(8,128)(2,1)S(1)} %get-tuple-element.45), channel_id=1, source_target_pairs={{0,2},{1,3},{2,0},{3,1},{4,6},{5,7},{6,4},{7,5},{8,10},{9,11},{10,... | collective-permute-start | bytes 638984 | tf_op jit(solution)/shard_map/ppermute | solution.py:452
  35.2 12.0 %collective-permute-start.11 = (bf16[13,32,256]{2,1,0:T(8,128)(2,1)S(1)}, bf16[13,32,256]{2,1,0:T(8,128)(2,1)S(1)}, u32[]{:S(2)}, u32[]{:S(2)}) collective-permute-start(bf16[13,32,256]{2,1,0:T(8,128)(2,1)S(1)} %get-tuple-element.46), channel_id=1, source_target_pairs={{0,3},{1,2},{2,1},{3,0},{4,7},{5,6},{6,5},{7,4},{8,11},{9,10},{10,... | collective-permute-start | bytes 638984 | tf_op jit(solution)/shard_map/ppermute | solution.py:452
  40.3 2.2 %collective-permute-start.12 = (bf16[5,64,256]{2,1,0:T(8,128)(2,1)S(1)}, bf16[5,64,256]{2,1,0:T(8,128)(2,1)S(1)}, u32[]{:S(2)}, u32[]{:S(2)}) collective-permute-start(bf16[5,64,256]{2,1,0:T(8,128)(2,1)S(1)} %get-tuple-element.54), channel_id=1, source_target_pairs={{0,1},{1,0},{2,3},{3,2},{4,5},{5,4},{6,7},{7,6},{8,9},{9,8},{10,11... | collective-permute-start | bytes 491528 | tf_op jit(solution)/shard_map/ppermute | solution.py:452
  41.0 1.3 %collective-permute-start.13 = (bf16[4,64,256]{2,1,0:T(8,128)(2,1)S(1)}, bf16[4,64,256]{2,1,0:T(8,128)(2,1)S(1)}, u32[]{:S(2)}, u32[]{:S(2)}) collective-permute-start(bf16[4,64,256]{2,1,0:T(8,128)(2,1)S(1)} %get-tuple-element.55), channel_id=1, source_target_pairs={{0,1},{1,0},{2,3},{3,2},{4,5},{5,4},{6,7},{7,6},{8,9},{9,8},{10,11... | collective-permute-start | bytes 393224 | tf_op jit(solution)/shard_map/ppermute | solution.py:452
  41.1 1.5 %collective-permute-start.14 = (bf16[4,64,256]{2,1,0:T(8,128)(2,1)S(1)}, bf16[4,64,256]{2,1,0:T(8,128)(2,1)S(1)}, u32[]{:S(2)}, u32[]{:S(2)}) collective-permute-start(bf16[4,64,256]{2,1,0:T(8,128)(2,1)S(1)} %get-tuple-element.56), channel_id=1, source_target_pairs={{0,1},{1,0},{2,3},{3,2},{4,5},{5,4},{6,7},{7,6},{8,9},{9,8},{10,11... | collective-permute-start | bytes 393224 | tf_op jit(solution)/shard_map/ppermute | solution.py:452

commit v13 on v11

--- a/solution.py
+++ b/solution.py
@@ -291,7 +291,7 @@
     grids, refs = refs[: len(parts)], refs[len(parts) :]
     firsts, refs = in_slots(refs[:n]), refs[n:]
     if second:
-        rests, refs = in_slots(refs[:n]), refs[n + 1 :]
+        rests, refs = refs[:n], refs[n + 1 :]
     outs, refs = refs[: len(far)], refs[len(far) :]
     u1, r0, fy1, u0, fy0, product, turned = refs
     wide, size = u0.shape[1:]
@@ -596,7 +596,7 @@
         return [own, *exchange(others, n, slots)]
 
     if two:
-        firsts, rests = far_first(firsts), far_first(rests)
+        firsts = far_first(firsts)
         crossing, states = sections(False, *firsts)
         back = exchange(crossing, n, far)
         crossing, more = sections(True, *firsts, *rests, crossing[0])

time: 48.9 us -> 50.1 us (1.025)
  waiting for transfers between devices: 8.13 us -> 9.15 us
    ppermute x13, waiting for transfers between devices: 7.18 us -> 8.2 us  [to_partner(): lax.ppermute(array, 'gy', [(i, i ^ s) for i in range(n)])]
  transfers between devices with their start and end apart: 15 -> 15, of which waited for: 7 -> 7; matrix products, arithmetic and copies ran while one was open for 0% -> 0% of each run, Pallas kernels for 41% -> 40%
where the time goes in v13:
time: 50.1 us; the launch traced here: 50 us
  Pallas kernels  25.1 us (50%)
  starting transfers between devices  15.5 us (31%)
  waiting for transfers between devices  9.15 us (18%)
    pallas_call x2, Pallas kernels, sections(): pl.pallas_call(functools.partial(section_kernel, n, two, second, far, all...  10.6 us
    ppermute x13, starting transfers between devices, to_partner(): lax.ppermute(array, 'gy', [(i, i ^ s) for i in range(n)])  10.3 us
    ppermute x13, waiting for transfers between devices, to_partner(): lax.ppermute(array, 'gy', [(i, i ^ s) for i in range(n)])  8.2 us
    pallas_call x2, Pallas kernels, grid_of(): pl.pallas_call(functools.partial(grid_kernel, n, rows, slots), out_shape=...  4.03 us
    pallas_call x1, Pallas kernels, pack(): pl.pallas_call(functools.partial(pack_kernel, n, two), out_shape=shapes,...  3.61 us
    ppermute x1, starting transfers between devices, on_device(): after = lax.ppermute(left, 'gx', [(j, i) for i, j in up])  3.1 us
    pallas_call x2, Pallas kernels, unpack(): pl.pallas_call(functools.partial(unpack_kernel, n, slots, chunks, pieces,...  2.81 us
    pallas_call x1, Pallas kernels, finished(): pl.pallas_call(functools.partial(finish_kernel, n, near, parts, len(state...  2.71 us
  transfers between devices with their start and end apart: 15, of which 7 were waited for; matrix products, arithmetic and copies ran while one was open for 0% of the time, Pallas kernels for 40%

profile of v13, /device:TPU:0, one launch (start us, length us, event | category | flops | bytes accessed | tf_op | source)
XLA Modules:
  0.0 50.0 jit_solution(6959272540276271539)
XLA Ops:
  0.0 3.6 %pack.1 = (bf16[13,88,128]{2,1,0:T(8,128)(2,1)}, bf16[13,88,128]{2,1,0:T(8,128)(2,1)}, bf16[13,88,128]{2,1,0:T(8,128)(2,1)}, bf16[13,88,128]{2,1,0:T(8,128)(2,1)}, bf16[13,272,256]{2,1,0:T(8,128)(2,1)}) custom-call(s32[1]{0:T(128)} %bitcast.me_ref, f32[256,256]{1,0:T(8,128)} %refs_0_.1, f32[3,256,256]{2,1,0:T(8,128)} %bitcast.6, f32[256,256]{1,0:T(8,128)} %refs_2_.1, ...), custom_call_target="tpu_custom_call" | custom-call | flops 2000000000 | bytes 6000000 | tf_op jit(solution)/shard_map/pack/pallas_call | solution.py:484
  3.6 0.0 copy-start
  3.6 3.0 %collective-permute-start = (bf16[13,88,128]{2,1,0:T(8,128)(2,1)}, bf16[13,88,128]{2,1,0:T(8,128)(2,1)S(1)}, u32[]{:S(2)}, u32[]{:S(2)}) collective-permute-start(bf16[13,88,128]{2,1,0:T(8,128)(2,1)} %get-tuple-element.33), channel_id=1, source_target_pairs={{0,2},{1,3},{2,0},{3,1},{4,6},{5,7},{6,4},{7,5},{8,10},{9,11},{10,... | collective-permute-start | bytes 878600 | tf_op jit(solution)/shard_map/ppermute | solution.py:453
  6.6 0.2 collective-permute-start.2
  6.8 1.9 %grid.2.refs_0_.tie = bf16[1024,256]{1,0:T(8,128)(2,1)S(1)} custom-call(s32[1]{0:T(128)} %bitcast.me_ref), custom_call_target="tpu_custom_call" | custom-call | flops 1000000000 | bytes 3000000 | tf_op jit(solution)/shard_map/grid/pallas_call | solution.py:509
  8.8 2.0 %collective-permute-start.5 = (bf16[13,16,256]{2,1,0:T(8,128)(2,1)S(1)}, bf16[13,16,256]{2,1,0:T(8,128)(2,1)S(1)}, u32[]{:S(2)}, u32[]{:S(2)}) collective-permute-start(bf16[13,16,256]{2,1,0:T(8,128)(2,1)S(1)} %get-tuple-element.39), channel_id=1, source_target_pairs={{0,4},{4,8},{8,12},{12,16},{16,20},{20,24},{24,28},{28,0},{1,5},{5... | collective-permute-start | bytes 319496 | tf_op jit(solution)/shard_map/ppermute | solution.py:533
  10.8 3.1 %collective-permute-start.6 = (bf16[13,16,256]{2,1,0:T(8,128)(2,1)S(1)}, bf16[13,16,256]{2,1,0:T(8,128)(2,1)S(1)}, u32[]{:S(2)}, u32[]{:S(2)}) collective-permute-start(bf16[13,16,256]{2,1,0:T(8,128)(2,1)S(1)} %get-tuple-element.40), channel_id=1, source_target_pairs={{4,0},{8,4},{12,8},{16,12},{20,16},{24,20},{28,24},{0,28},{5,1},{9... | collective-permute-start | bytes 319496 | tf_op jit(solution)/shard_map/ppermute | solution.py:534
  13.9 2.1 %grid.3.refs_1_ = bf16[1024,256]{1,0:T(8,128)(2,1)S(1)} custom-call(s32[1]{0:T(128)} %bitcast.me_ref), custom_call_target="tpu_custom_call" | custom-call | flops 1000000000 | bytes 3000000 | tf_op jit(solution)/shard_map/grid/pallas_call | solution.py:509
  16.0 0.8 %flip.1.refs_2_ = bf16[1024,512]{1,0:T(8,128)(2,1)S(1)} custom-call(bf16[1024,256]{1,0:T(8,128)(2,1)S(1)} %grid.2.refs_0_.tie, bf16[1024,256]{1,0:T(8,128)(2,1)S(1)} %grid.3.refs_1_), custom_call_target="tpu_custom_call" | custom-call | flops 300000000 | bytes 900000 | tf_op jit(solution)/shard_map/flip/pallas_call | solution.py:535
  16.9 0.2 collective-permute-done.5.before
  17.1 0.7 %collective-permute-done.6.after = bf16[13,16,256]{2,1,0:T(8,128)(2,1)S(1)} collective-permute-done((bf16[13,16,256]{2,1,0:T(8,128)(2,1)S(1)}, bf16[13,16,256]{2,1,0:T(8,128)(2,1)S(1)}, u32[]{:S(2)}, u32[]{:S(2)}) %collective-permute-start.6) | collective-permute-done | bytes 106528 | tf_op jit(solution)/shard_map/ppermute | solution.py:534
  17.8 0.5 rest.1
  18.3 0.1 collective-permute-start.7
  18.4 1.6 %collective-permute-start.8 = (bf16[13,32,256]{2,1,0:T(8,128)(2,1)S(1)}, bf16[13,32,256]{2,1,0:T(8,128)(2,1)S(1)}, u32[]{:S(2)}, u32[]{:S(2)}) collective-permute-start(bf16[13,32,256]{2,1,0:T(8,128)(2,1)S(1)} %get-tuple-element.43), channel_id=1, source_target_pairs={{0,2},{1,3},{2,0},{3,1},{4,6},{5,7},{6,4},{7,5},{8,10},{9,11},{10,... | collective-permute-start | bytes 638984 | tf_op jit(solution)/shard_map/ppermute | solution.py:453
  20.0 0.3 collective-permute-start.9
  20.3 5.1 %sections.2 = (bf16[13,32,256]{2,1,0:T(8,128)(2,1)S(1)}, bf16[13,32,256]{2,1,0:T(8,128)(2,1)S(1)}, f32[13,48,1024]{2,1,0:T(8,128)S(1)}, f32[13,32,1024]{2,1,0:T(8,128)S(1)}, bf16[416,1024]{1,0:T(8,128)(2,1)S(1)}) custom-call(s32[1]{0:T(128)} %bitcast.me_ref, bf16[1024,256]{1,0:T(8,128)(2,1)S(1)} %grid.2.refs_0_.tie, bf16[1024,256]{1,0:T(8,128)(2,1)S(1)} %grid.3.refs_1_, ...), custom_call_target="tpu_custom_call" | custom-call | flops 6000000000 | bytes 18000000 | tf_op jit(solution)/shard_map/sections/pallas_call | solution.py:562
  25.4 1.6 %collective-permute-start.3 = (bf16[13,32,256]{2,1,0:T(8,128)(2,1)S(1)}, bf16[13,32,256]{2,1,0:T(8,128)(2,1)S(1)}, u32[]{:S(2)}, u32[]{:S(2)}) collective-permute-start(bf16[13,32,256]{2,1,0:T(8,128)(2,1)S(1)} %get-tuple-element.36.refs_11_), channel_id=1, source_target_pairs={{0,2},{1,3},{2,0},{3,1},{4,6},{5,7},{6,4},{7,5},{8,10},{9,11},{10,... | collective-permute-start | bytes 638984 | tf_op jit(solution)/shard_map/ppermute | solution.py:453
  26.9 0.2 collective-permute-start.4
  27.1 3.0 %collective-permute-done.9.refs_10_ = bf16[13,32,256]{2,1,0:T(8,128)(2,1)S(1)} collective-permute-done((bf16[13,32,256]{2,1,0:T(8,128)(2,1)S(1)}, bf16[13,32,256]{2,1,0:T(8,128)(2,1)S(1)}, u32[]{:S(2)}, u32[]{:S(2)}) %collective-permute-start.9) | collective-permute-done | bytes 213024 | tf_op jit(solution)/shard_map/ppermute | solution.py:453
  30.2 5.5 %sections.3 = (bf16[13,32,256]{2,1,0:T(8,128)(2,1)S(1)}, bf16[13,32,256]{2,1,0:T(8,128)(2,1)S(1)}, f32[13,48,1024]{2,1,0:T(8,128)S(1)}, f32[13,32,1024]{2,1,0:T(8,128)S(1)}, bf16[416,1024]{1,0:T(8,128)(2,1)S(1)}) custom-call(s32[1]{0:T(128)} %bitcast.me_ref, bf16[1024,256]{1,0:T(8,128)(2,1)S(1)} %grid.2.refs_0_.tie, bf16[1024,256]{1,0:T(8,128)(2,1)S(1)} %grid.3.refs_1_, ...), custom_call_target="tpu_custom_call" | custom-call | flops 6000000000 | bytes 18000000 | tf_op jit(solution)/shard_map/sections/pallas_call | solution.py:562
  35.7 1.6 %collective-permute-start.10 = (bf16[13,32,256]{2,1,0:T(8,128)(2,1)S(1)}, bf16[13,32,256]{2,1,0:T(8,128)(2,1)S(1)}, u32[]{:S(2)}, u32[]{:S(2)}) collective-permute-start(bf16[13,32,256]{2,1,0:T(8,128)(2,1)S(1)} %get-tuple-element.45), channel_id=1, source_target_pairs={{0,2},{1,3},{2,0},{3,1},{4,6},{5,7},{6,4},{7,5},{8,10},{9,11},{10,... | collective-permute-start | bytes 638984 | tf_op jit(solution)/shard_map/ppermute | solution.py:453
  37.3 0.6 %collective-permute-start.11 = (bf16[13,32,256]{2,1,0:T(8,128)(2,1)S(1)}, bf16[13,32,256]{2,1,0:T(8,128)(2,1)S(1)}, u32[]{:S(2)}, u32[]{:S(2)}) collective-permute-start(bf16[13,32,256]{2,1,0:T(8,128)(2,1)S(1)} %get-tuple-element.46), channel_id=1, source_target_pairs={{0,3},{1,2},{2,1},{3,0},{4,7},{5,6},{6,5},{7,4},{8,11},{9,10},{10,... | collective-permute-start | bytes 638984 | tf_op jit(solution)/shard_map/ppermute | solution.py:453
  37.8 1.5 %collective-permute-done.4.refs_9_.refs_1_ = bf16[13,32,256]{2,1,0:T(8,128)(2,1)S(1)} collective-permute-done((bf16[13,32,256]{2,1,0:T(8,128)(2,1)S(1)}, bf16[13,32,256]{2,1,0:T(8,128)(2,1)S(1)}, u32[]{:S(2)}, u32[]{:S(2)}) %collective-permute-start.4) | collective-permute-done | bytes 213024 | tf_op jit(solution)/shard_map/ppermute | solution.py:453
  39.3 2.7 %finish.1 = (f32[13,64,256]{2,1,0:T(8,128)S(1)}, bf16[5,64,256]{2,1,0:T(8,128)(2,1)S(1)}, bf16[4,64,256]{2,1,0:T(8,128)(2,1)S(1)}, bf16[4,64,256]{2,1,0:T(8,128)(2,1)S(1)}) custom-call(s32[1]{0:T(128)} %bitcast.me_ref, bf16[1024,256]{1,0:T(8,128)(2,1)S(1)} %grid.2.refs_0_.tie, bf16[1024,256]{1,0:T(8,128)(2,1)S(1)} %grid.3.refs_1_, ...), custom_call_target="tpu_custom_call" | custom-call | flops 4000000000 | bytes 12000000 | tf_op jit(solution)/shard_map/finish/pallas_call | solution.py:582
  42.0 0.8 %collective-permute-start.12 = (bf16[5,64,256]{2,1,0:T(8,128)(2,1)S(1)}, bf16[5,64,256]{2,1,0:T(8,128)(2,1)S(1)}, u32[]{:S(2)}, u32[]{:S(2)}) collective-permute-start(bf16[5,64,256]{2,1,0:T(8,128)(2,1)S(1)} %get-tuple-element.54), channel_id=1, source_target_pairs={{0,1},{1,0},{2,3},{3,2},{4,5},{5,4},{6,7},{7,6},{8,9},{9,8},{10,11... | collective-permute-start | bytes 491528 | tf_op jit(solution)/shard_map/ppermute | solution.py:453
  42.8 0.1 collective-permute-start.13
  42.9 0.4 collective-permute-start.14
  43.3 0.8 %collective-permute-done.13.refs_2_ = bf16[4,64,256]{2,1,0:T(8,128)(2,1)S(1)} collective-permute-done((bf16[4,64,256]{2,1,0:T(8,128)(2,1)S(1)}, bf16[4,64,256]{2,1,0:T(8,128)(2,1)S(1)}, u32[]{:S(2)}, u32[]{:S(2)}) %collective-permute-start.13) | collective-permute-done | bytes 131104 | tf_op jit(solution)/shard_map/ppermute | solution.py:453
  44.2 0.2 collective-permute-done.14.refs_3_
  44.3 1.4 %unpack.2 = (f32[13,256,256]{2,1,0:T(8,128)}, f32[8,128]{1,0:T(8,128)S(1)}) custom-call(s32[1]{0:T(128)} %bitcast.me_ref, f32[13,64,256]{2,1,0:T(8,128)S(1)} %get-tuple-element.53.refs_0_, bf16[5,64,256]{2,1,0:T(8,128)(2,1)S(1)} %collective-permute-done.12.refs_1_, bf16[4,64,256]{2,1,0:T(8,128)(2,1)S(1)} %collective-permute-done.13.refs_2_, ...), custom_call_target="tpu_custom_call" | custom-call | flops 10000000 | bytes 30000 | tf_op jit(solution)/shard_map/unpack/pallas_call | solution.py:615
  45.8 2.7 %collective-permute-done.11.refs_3_ = bf16[13,32,256]{2,1,0:T(8,128)(2,1)S(1)} collective-permute-done((bf16[13,32,256]{2,1,0:T(8,128)(2,1)S(1)}, bf16[13,32,256]{2,1,0:T(8,128)(2,1)S(1)}, u32[]{:S(2)}, u32[]{:S(2)}) %collective-permute-start.11) | collective-permute-done | bytes 213024 | tf_op jit(solution)/shard_map/ppermute | solution.py:453
  48.4 1.4 %unpack.3 = f32[13,256,256]{2,1,0:T(8,128)} custom-call(s32[1]{0:T(128)} %bitcast.me_ref, bf16[13,32,256]{2,1,0:T(8,128)(2,1)S(1)} %collective-permute-done.3.refs_8_.refs_0_, bf16[13,32,256]{2,1,0:T(8,128)(2,1)S(1)} %collective-permute-done.4.refs_9_.refs_1_, ...), custom_call_target="tpu_custom_call", output_to_operand_aliasing={{}: (5, {})} | custom-call | flops 10000000 | bytes 30000 | tf_op jit(solution)/shard_map/unpack/pallas_call | solution.py:615
  (14 shorter events, 0.0 us)
Async XLA Ops:
  3.6 5.1 %copy-start = (bf16[13,272,256]{2,1,0:T(8,128)(2,1)S(1)}, bf16[13,272,256]{2,1,0:T(8,128)(2,1)}, u32[]{:S(2)}) copy-start(bf16[13,272,256]{2,1,0:T(8,128)(2,1)} %get-tuple-element.38.tall) | copy-start | bytes 5431300
  3.6 16.3 %collective-permute-start = (bf16[13,88,128]{2,1,0:T(8,128)(2,1)}, bf16[13,88,128]{2,1,0:T(8,128)(2,1)S(1)}, u32[]{:S(2)}, u32[]{:S(2)}) collective-permute-start(bf16[13,88,128]{2,1,0:T(8,128)(2,1)} %get-tuple-element.33), channel_id=1, source_target_pairs={{0,2},{1,3},{2,0},{3,1},{4,6},{5,7},{6,4},{7,5},{8,10},{9,11},{10,... | collective-permute-start | bytes 878600 | tf_op jit(solution)/shard_map/ppermute | solution.py:453
  6.6 13.6 %collective-permute-start.1 = (bf16[13,88,128]{2,1,0:T(8,128)(2,1)}, bf16[13,88,128]{2,1,0:T(8,128)(2,1)S(1)}, u32[]{:S(2)}, u32[]{:S(2)}) collective-permute-start(bf16[13,88,128]{2,1,0:T(8,128)(2,1)} %get-tuple-element.34), channel_id=1, source_target_pairs={{0,3},{1,2},{2,1},{3,0},{4,7},{5,6},{6,5},{7,4},{8,11},{9,10},{10,... | collective-permute-start | bytes 878600 | tf_op jit(solution)/shard_map/ppermute | solution.py:453
  6.6 13.6 %collective-permute-start.2 = (bf16[13,88,128]{2,1,0:T(8,128)(2,1)}, bf16[13,88,128]{2,1,0:T(8,128)(2,1)S(1)}, u32[]{:S(2)}, u32[]{:S(2)}) collective-permute-start(bf16[13,88,128]{2,1,0:T(8,128)(2,1)} %get-tuple-element.35), channel_id=1, source_target_pairs={{0,1},{1,0},{2,3},{3,2},{4,5},{5,4},{6,7},{7,6},{8,9},{9,8},{10,11... | collective-permute-start | bytes 878600 | tf_op jit(solution)/shard_map/ppermute | solution.py:453
  8.8 8.3 %collective-permute-start.5 = (bf16[13,16,256]{2,1,0:T(8,128)(2,1)S(1)}, bf16[13,16,256]{2,1,0:T(8,128)(2,1)S(1)}, u32[]{:S(2)}, u32[]{:S(2)}) collective-permute-start(bf16[13,16,256]{2,1,0:T(8,128)(2,1)S(1)} %get-tuple-element.39), channel_id=1, source_target_pairs={{0,4},{4,8},{8,12},{12,16},{16,20},{20,24},{24,28},{28,0},{1,5},{5... | collective-permute-start | bytes 319496 | tf_op jit(solution)/shard_map/ppermute | solution.py:533
  10.8 7.0 %collective-permute-start.6 = (bf16[13,16,256]{2,1,0:T(8,128)(2,1)S(1)}, bf16[13,16,256]{2,1,0:T(8,128)(2,1)S(1)}, u32[]{:S(2)}, u32[]{:S(2)}) collective-permute-start(bf16[13,16,256]{2,1,0:T(8,128)(2,1)S(1)} %get-tuple-element.40), channel_id=1, source_target_pairs={{4,0},{8,4},{12,8},{16,12},{20,16},{24,20},{28,24},{0,28},{5,1},{9... | collective-permute-start | bytes 319496 | tf_op jit(solution)/shard_map/ppermute | solution.py:534
  16.0 4.2 %copy-start.1 = (bf16[13,88,128]{2,1,0:T(8,128)(2,1)S(1)}, bf16[13,88,128]{2,1,0:T(8,128)(2,1)}, u32[]{:S(2)}) copy-start(bf16[13,88,128]{2,1,0:T(8,128)(2,1)} %get-tuple-element.32.refs_3_) | copy-start | bytes 878596
  18.3 8.8 %collective-permute-start.7 = (bf16[13,32,256]{2,1,0:T(8,128)(2,1)S(1)}, bf16[13,32,256]{2,1,0:T(8,128)(2,1)S(1)}, u32[]{:S(2)}, u32[]{:S(2)}) collective-permute-start(bf16[13,32,256]{2,1,0:T(8,128)(2,1)S(1)} %get-tuple-element.42), channel_id=1, source_target_pairs={{0,1},{1,0},{2,3},{3,2},{4,5},{5,4},{6,7},{7,6},{8,9},{9,8},{10,11... | collective-permute-start | bytes 638984 | tf_op jit(solution)/shard_map/ppermute | solution.py:453
  18.4 8.7 %collective-permute-start.8 = (bf16[13,32,256]{2,1,0:T(8,128)(2,1)S(1)}, bf16[13,32,256]{2,1,0:T(8,128)(2,1)S(1)}, u32[]{:S(2)}, u32[]{:S(2)}) collective-permute-start(bf16[13,32,256]{2,1,0:T(8,128)(2,1)S(1)} %get-tuple-element.43), channel_id=1, source_target_pairs={{0,2},{1,3},{2,0},{3,1},{4,6},{5,7},{6,4},{7,5},{8,10},{9,11},{10,... | collective-permute-start | bytes 638984 | tf_op jit(solution)/shard_map/ppermute | solution.py:453
  20.0 10.2 %collective-permute-start.9 = (bf16[13,32,256]{2,1,0:T(8,128)(2,1)S(1)}, bf16[13,32,256]{2,1,0:T(8,128)(2,1)S(1)}, u32[]{:S(2)}, u32[]{:S(2)}) collective-permute-start(bf16[13,32,256]{2,1,0:T(8,128)(2,1)S(1)} %get-tuple-element.44), channel_id=1, source_target_pairs={{0,3},{1,2},{2,1},{3,0},{4,7},{5,6},{6,5},{7,4},{8,11},{9,10},{10,... | collective-permute-start | bytes 638984 | tf_op jit(solution)/shard_map/ppermute | solution.py:453
  25.4 12.5 %collective-permute-start.3 = (bf16[13,32,256]{2,1,0:T(8,128)(2,1)S(1)}, bf16[13,32,256]{2,1,0:T(8,128)(2,1)S(1)}, u32[]{:S(2)}, u32[]{:S(2)}) collective-permute-start(bf16[13,32,256]{2,1,0:T(8,128)(2,1)S(1)} %get-tuple-element.36.refs_11_), channel_id=1, source_target_pairs={{0,2},{1,3},{2,0},{3,1},{4,6},{5,7},{6,4},{7,5},{8,10},{9,11},{10,... | collective-permute-start | bytes 638984 | tf_op jit(solution)/shard_map/ppermute | solution.py:453
  26.9 12.4 %collective-permute-start.4 = (bf16[13,32,256]{2,1,0:T(8,128)(2,1)S(1)}, bf16[13,32,256]{2,1,0:T(8,128)(2,1)S(1)}, u32[]{:S(2)}, u32[]{:S(2)}) collective-permute-start(bf16[13,32,256]{2,1,0:T(8,128)(2,1)S(1)} %get-tuple-element.37), channel_id=1, source_target_pairs={{0,3},{1,2},{2,1},{3,0},{4,7},{5,6},{6,5},{7,4},{8,11},{9,10},{10,... | collective-permute-start | bytes 638984 | tf_op jit(solution)/shard_map/ppermute | solution.py:453
  35.7 10.1 %collective-permute-start.10 = (bf16[13,32,256]{2,1,0:T(8,128)(2,1)S(1)}, bf16[13,32,256]{2,1,0:T(8,128)(2,1)S(1)}, u32[]{:S(2)}, u32[]{:S(2)}) collective-permute-start(bf16[13,32,256]{2,1,0:T(8,128)(2,1)S(1)} %get-tuple-element.45), channel_id=1, source_target_pairs={{0,2},{1,3},{2,0},{3,1},{4,6},{5,7},{6,4},{7,5},{8,10},{9,11},{10,... | collective-permute-start | bytes 638984 | tf_op jit(solution)/shard_map/ppermute | solution.py:453
  37.3 11.2 %collective-permute-start.11 = (bf16[13,32,256]{2,1,0:T(8,128)(2,1)S(1)}, bf16[13,32,256]{2,1,0:T(8,128)(2,1)S(1)}, u32[]{:S(2)}, u32[]{:S(2)}) collective-permute-start(bf16[13,32,256]{2,1,0:T(8,128)(2,1)S(1)} %get-tuple-element.46), channel_id=1, source_target_pairs={{0,3},{1,2},{2,1},{3,0},{4,7},{5,6},{6,5},{7,4},{8,11},{9,10},{10,... | collective-permute-start | bytes 638984 | tf_op jit(solution)/shard_map/ppermute | solution.py:453
  42.0 2.3 %collective-permute-start.12 = (bf16[5,64,256]{2,1,0:T(8,128)(2,1)S(1)}, bf16[5,64,256]{2,1,0:T(8,128)(2,1)S(1)}, u32[]{:S(2)}, u32[]{:S(2)}) collective-permute-start(bf16[5,64,256]{2,1,0:T(8,128)(2,1)S(1)} %get-tuple-element.54), channel_id=1, source_target_pairs={{0,1},{1,0},{2,3},{3,2},{4,5},{5,4},{6,7},{7,6},{8,9},{9,8},{10,11... | collective-permute-start | bytes 491528 | tf_op jit(solution)/shard_map/ppermute | solution.py:453
  42.8 1.3 %collective-permute-start.13 = (bf16[4,64,256]{2,1,0:T(8,128)(2,1)S(1)}, bf16[4,64,256]{2,1,0:T(8,128)(2,1)S(1)}, u32[]{:S(2)}, u32[]{:S(2)}) collective-permute-start(bf16[4,64,256]{2,1,0:T(8,128)(2,1)S(1)} %get-tuple-element.55), channel_id=1, source_target_pairs={{0,1},{1,0},{2,3},{3,2},{4,5},{5,4},{6,7},{7,6},{8,9},{9,8},{10,11... | collective-permute-start | bytes 393224 | tf_op jit(solution)/shard_map/ppermute | solution.py:453
  42.9 1.5 %collective-permute-start.14 = (bf16[4,64,256]{2,1,0:T(8,128)(2,1)S(1)}, bf16[4,64,256]{2,1,0:T(8,128)(2,1)S(1)}, u32[]{:S(2)}, u32[]{:S(2)}) collective-permute-start(bf16[4,64,256]{2,1,0:T(8,128)(2,1)S(1)} %get-tuple-element.56), channel_id=1, source_target_pairs={{0,1},{1,0},{2,3},{3,2},{4,5},{5,4},{6,7},{7,6},{8,9},{9,8},{10,11... | collective-permute-start | bytes 393224 | tf_op jit(solution)/shard_map/ppermute | solution.py:453

commit v14 on v11

--- a/solution.py
+++ b/solution.py
@@ -279,12 +279,12 @@
 
 def far_first(arrays):
     half = len(arrays) // 2
-    return [arrays[0], *arrays[half:], *arrays[1:half]]
+    return [arrays[0], *arrays[half:][::-1], *arrays[1:half]]
 
 
 def in_slots(arrays):
     half = len(arrays) // 2
-    return [arrays[0], *arrays[half + 1 :], *arrays[1 : half + 1]]
+    return [arrays[0], *arrays[half + 1 :], *arrays[1 : half + 1][::-1]]
 
 
 def section_kernel(n, two, second, far, parts, me_ref, *refs):

time: 48.9 us -> 50.2 us (1.027)
  waiting for transfers between devices: 8.13 us -> 10 us
  starting transfers between devices: 15.3 us -> 14.6 us
    ppermute x13, waiting for transfers between devices: 7.18 us -> 8.99 us  [to_partner(): lax.ppermute(array, 'gy', [(i, i ^ s) for i in range(n)])]
  transfers between devices with their start and end apart: 15 -> 15, of which waited for: 7 -> 7; matrix products, arithmetic and copies ran while one was open for 0% -> 0% of each run, Pallas kernels for 41% -> 40%
where the time goes in v14:
time: 50.2 us; the launch traced here: 50.1 us
  Pallas kernels  25.1 us (50%)
  starting transfers between devices  14.6 us (29%)
  waiting for transfers between devices  10 us (20%)
    pallas_call x2, Pallas kernels, sections(): pl.pallas_call(functools.partial(section_kernel, n, two, second, far, all...  10.6 us
    ppermute x13, starting transfers between devices, to_partner(): lax.ppermute(array, 'gy', [(i, i ^ s) for i in range(n)])  9.71 us
    ppermute x13, waiting for transfers between devices, to_partner(): lax.ppermute(array, 'gy', [(i, i ^ s) for i in range(n)])  8.99 us
    pallas_call x2, Pallas kernels, grid_of(): pl.pallas_call(functools.partial(grid_kernel, n, rows, slots), out_shape=...  4.03 us
    pallas_call x1, Pallas kernels, pack(): pl.pallas_call(functools.partial(pack_kernel, n, two), out_shape=shapes,...  3.61 us
    ppermute x1, starting transfers between devices, on_device(): after = lax.ppermute(left, 'gx', [(j, i) for i, j in up])  3.1 us
    pallas_call x2, Pallas kernels, unpack(): pl.pallas_call(functools.partial(unpack_kernel, n, slots, chunks, pieces,...  2.81 us
    pallas_call x1, Pallas kernels, finished(): pl.pallas_call(functools.partial(finish_kernel, n, near, parts, len(state...  2.7 us
  transfers between devices with their start and end apart: 15, of which 7 were waited for; matrix products, arithmetic and copies ran while one was open for 0% of the time, Pallas kernels for 40%

profile of v14, /device:TPU:0, one launch (start us, length us, event | category | flops | bytes accessed | tf_op | source)
XLA Modules:
  0.0 50.1 jit_solution(6995028010795388395)
XLA Ops:
  0.0 3.6 %pack.1 = (bf16[13,88,128]{2,1,0:T(8,128)(2,1)}, bf16[13,88,128]{2,1,0:T(8,128)(2,1)}, bf16[13,88,128]{2,1,0:T(8,128)(2,1)}, bf16[13,88,128]{2,1,0:T(8,128)(2,1)}, bf16[13,272,256]{2,1,0:T(8,128)(2,1)}) custom-call(s32[1]{0:T(128)} %bitcast.me_ref, f32[256,256]{1,0:T(8,128)} %refs_0_.1, f32[3,256,256]{2,1,0:T(8,128)} %bitcast.6, f32[256,256]{1,0:T(8,128)} %refs_2_.1, ...), custom_call_target="tpu_custom_call" | custom-call | flops 2000000000 | bytes 6000000 | tf_op jit(solution)/shard_map/pack/pallas_call | solution.py:484
  3.6 2.4 %collective-permute-start = (bf16[13,88,128]{2,1,0:T(8,128)(2,1)}, bf16[13,88,128]{2,1,0:T(8,128)(2,1)S(1)}, u32[]{:S(2)}, u32[]{:S(2)}) collective-permute-start(bf16[13,88,128]{2,1,0:T(8,128)(2,1)} %get-tuple-element.33), channel_id=1, source_target_pairs={{0,3},{1,2},{2,1},{3,0},{4,7},{5,6},{6,5},{7,4},{8,11},{9,10},{10,... | collective-permute-start | bytes 878600 | tf_op jit(solution)/shard_map/ppermute | solution.py:453
  6.1 0.6 %collective-permute-start.1 = (bf16[13,88,128]{2,1,0:T(8,128)(2,1)}, bf16[13,88,128]{2,1,0:T(8,128)(2,1)S(1)}, u32[]{:S(2)}, u32[]{:S(2)}) collective-permute-start(bf16[13,88,128]{2,1,0:T(8,128)(2,1)} %get-tuple-element.34), channel_id=1, source_target_pairs={{0,2},{1,3},{2,0},{3,1},{4,6},{5,7},{6,4},{7,5},{8,10},{9,11},{10,... | collective-permute-start | bytes 878600 | tf_op jit(solution)/shard_map/ppermute | solution.py:453
  6.7 0.0 collective-permute-start.2
  6.8 1.9 %grid.2.refs_0_.tie = bf16[1024,256]{1,0:T(8,128)(2,1)S(1)} custom-call(s32[1]{0:T(128)} %bitcast.me_ref), custom_call_target="tpu_custom_call" | custom-call | flops 1000000000 | bytes 3000000 | tf_op jit(solution)/shard_map/grid/pallas_call | solution.py:509
  8.7 1.8 %collective-permute-start.5 = (bf16[13,16,256]{2,1,0:T(8,128)(2,1)S(1)}, bf16[13,16,256]{2,1,0:T(8,128)(2,1)S(1)}, u32[]{:S(2)}, u32[]{:S(2)}) collective-permute-start(bf16[13,16,256]{2,1,0:T(8,128)(2,1)S(1)} %get-tuple-element.39), channel_id=1, source_target_pairs={{0,4},{4,8},{8,12},{12,16},{16,20},{20,24},{24,28},{28,0},{1,5},{5... | collective-permute-start | bytes 319496 | tf_op jit(solution)/shard_map/ppermute | solution.py:533
  10.5 3.1 %collective-permute-start.6 = (bf16[13,16,256]{2,1,0:T(8,128)(2,1)S(1)}, bf16[13,16,256]{2,1,0:T(8,128)(2,1)S(1)}, u32[]{:S(2)}, u32[]{:S(2)}) collective-permute-start(bf16[13,16,256]{2,1,0:T(8,128)(2,1)S(1)} %get-tuple-element.40), channel_id=1, source_target_pairs={{4,0},{8,4},{12,8},{16,12},{20,16},{24,20},{28,24},{0,28},{5,1},{9... | collective-permute-start | bytes 319496 | tf_op jit(solution)/shard_map/ppermute | solution.py:534
  13.7 2.1 %grid.3.refs_1_ = bf16[1024,256]{1,0:T(8,128)(2,1)S(1)} custom-call(s32[1]{0:T(128)} %bitcast.me_ref), custom_call_target="tpu_custom_call" | custom-call | flops 1000000000 | bytes 3000000 | tf_op jit(solution)/shard_map/grid/pallas_call | solution.py:509
  15.8 0.8 %flip.1.refs_2_ = bf16[1024,512]{1,0:T(8,128)(2,1)S(1)} custom-call(bf16[1024,256]{1,0:T(8,128)(2,1)S(1)} %grid.2.refs_0_.tie, bf16[1024,256]{1,0:T(8,128)(2,1)S(1)} %grid.3.refs_1_), custom_call_target="tpu_custom_call" | custom-call | flops 300000000 | bytes 900000 | tf_op jit(solution)/shard_map/flip/pallas_call | solution.py:535
  16.6 0.5 collective-permute-done.5.before
  17.0 0.6 %collective-permute-done.6.after = bf16[13,16,256]{2,1,0:T(8,128)(2,1)S(1)} collective-permute-done((bf16[13,16,256]{2,1,0:T(8,128)(2,1)S(1)}, bf16[13,16,256]{2,1,0:T(8,128)(2,1)S(1)}, u32[]{:S(2)}, u32[]{:S(2)}) %collective-permute-start.6) | collective-permute-done | bytes 106528 | tf_op jit(solution)/shard_map/ppermute | solution.py:534
  17.6 0.5 rest.1
  18.1 0.1 collective-permute-start.7
  18.2 1.5 %collective-permute-start.8 = (bf16[13,32,256]{2,1,0:T(8,128)(2,1)S(1)}, bf16[13,32,256]{2,1,0:T(8,128)(2,1)S(1)}, u32[]{:S(2)}, u32[]{:S(2)}) collective-permute-start(bf16[13,32,256]{2,1,0:T(8,128)(2,1)S(1)} %get-tuple-element.43), channel_id=1, source_target_pairs={{0,2},{1,3},{2,0},{3,1},{4,6},{5,7},{6,4},{7,5},{8,10},{9,11},{10,... | collective-permute-start | bytes 638984 | tf_op jit(solution)/shard_map/ppermute | solution.py:453
  19.7 0.4 collective-permute-start.9
  20.1 0.0 collective-permute-done.1.refs_5_
  20.1 5.1 %sections.2 = (bf16[13,32,256]{2,1,0:T(8,128)(2,1)S(1)}, bf16[13,32,256]{2,1,0:T(8,128)(2,1)S(1)}, f32[13,48,1024]{2,1,0:T(8,128)S(1)}, f32[13,32,1024]{2,1,0:T(8,128)S(1)}, bf16[416,1024]{1,0:T(8,128)(2,1)S(1)}) custom-call(s32[1]{0:T(128)} %bitcast.me_ref, bf16[1024,256]{1,0:T(8,128)(2,1)S(1)} %grid.2.refs_0_.tie, bf16[1024,256]{1,0:T(8,128)(2,1)S(1)} %grid.3.refs_1_, ...), custom_call_target="tpu_custom_call" | custom-call | flops 6000000000 | bytes 18000000 | tf_op jit(solution)/shard_map/sections/pallas_call | solution.py:562
  25.2 2.4 %collective-permute-start.3 = (bf16[13,32,256]{2,1,0:T(8,128)(2,1)S(1)}, bf16[13,32,256]{2,1,0:T(8,128)(2,1)S(1)}, u32[]{:S(2)}, u32[]{:S(2)}) collective-permute-start(bf16[13,32,256]{2,1,0:T(8,128)(2,1)S(1)} %get-tuple-element.36.refs_11_), channel_id=1, source_target_pairs={{0,2},{1,3},{2,0},{3,1},{4,6},{5,7},{6,4},{7,5},{8,10},{9,11},{10,... | collective-permute-start | bytes 638984 | tf_op jit(solution)/shard_map/ppermute | solution.py:453
  27.6 2.6 %collective-permute-done.8.refs_9_ = bf16[13,32,256]{2,1,0:T(8,128)(2,1)S(1)} collective-permute-done((bf16[13,32,256]{2,1,0:T(8,128)(2,1)S(1)}, bf16[13,32,256]{2,1,0:T(8,128)(2,1)S(1)}, u32[]{:S(2)}, u32[]{:S(2)}) %collective-permute-start.8) | collective-permute-done | bytes 213024 | tf_op jit(solution)/shard_map/ppermute | solution.py:453
  30.2 5.5 %sections.3 = (bf16[13,32,256]{2,1,0:T(8,128)(2,1)S(1)}, bf16[13,32,256]{2,1,0:T(8,128)(2,1)S(1)}, f32[13,48,1024]{2,1,0:T(8,128)S(1)}, f32[13,32,1024]{2,1,0:T(8,128)S(1)}, bf16[416,1024]{1,0:T(8,128)(2,1)S(1)}) custom-call(s32[1]{0:T(128)} %bitcast.me_ref, bf16[1024,256]{1,0:T(8,128)(2,1)S(1)} %grid.2.refs_0_.tie, bf16[1024,256]{1,0:T(8,128)(2,1)S(1)} %grid.3.refs_1_, ...), custom_call_target="tpu_custom_call" | custom-call | flops 6000000000 | bytes 18000000 | tf_op jit(solution)/shard_map/sections/pallas_call | solution.py:562
  35.7 1.1 %collective-permute-start.10 = (bf16[13,32,256]{2,1,0:T(8,128)(2,1)S(1)}, bf16[13,32,256]{2,1,0:T(8,128)(2,1)S(1)}, u32[]{:S(2)}, u32[]{:S(2)}) collective-permute-start(bf16[13,32,256]{2,1,0:T(8,128)(2,1)S(1)} %get-tuple-element.45), channel_id=1, source_target_pairs={{0,2},{1,3},{2,0},{3,1},{4,6},{5,7},{6,4},{7,5},{8,10},{9,11},{10,... | collective-permute-start | bytes 638984 | tf_op jit(solution)/shard_map/ppermute | solution.py:453
  36.9 0.5 %collective-permute-start.11 = (bf16[13,32,256]{2,1,0:T(8,128)(2,1)S(1)}, bf16[13,32,256]{2,1,0:T(8,128)(2,1)S(1)}, u32[]{:S(2)}, u32[]{:S(2)}) collective-permute-start(bf16[13,32,256]{2,1,0:T(8,128)(2,1)S(1)} %get-tuple-element.46), channel_id=1, source_target_pairs={{0,3},{1,2},{2,1},{3,0},{4,7},{5,6},{6,5},{7,4},{8,11},{9,10},{10,... | collective-permute-start | bytes 638984 | tf_op jit(solution)/shard_map/ppermute | solution.py:453
  37.4 2.0 %collective-permute-done.4.refs_9_.refs_1_ = bf16[13,32,256]{2,1,0:T(8,128)(2,1)S(1)} collective-permute-done((bf16[13,32,256]{2,1,0:T(8,128)(2,1)S(1)}, bf16[13,32,256]{2,1,0:T(8,128)(2,1)S(1)}, u32[]{:S(2)}, u32[]{:S(2)}) %collective-permute-start.4) | collective-permute-done | bytes 213024 | tf_op jit(solution)/shard_map/ppermute | solution.py:453
  39.4 2.7 %finish.1 = (f32[13,64,256]{2,1,0:T(8,128)S(1)}, bf16[5,64,256]{2,1,0:T(8,128)(2,1)S(1)}, bf16[4,64,256]{2,1,0:T(8,128)(2,1)S(1)}, bf16[4,64,256]{2,1,0:T(8,128)(2,1)S(1)}) custom-call(s32[1]{0:T(128)} %bitcast.me_ref, bf16[1024,256]{1,0:T(8,128)(2,1)S(1)} %grid.2.refs_0_.tie, bf16[1024,256]{1,0:T(8,128)(2,1)S(1)} %grid.3.refs_1_, ...), custom_call_target="tpu_custom_call" | custom-call | flops 4000000000 | bytes 12000000 | tf_op jit(solution)/shard_map/finish/pallas_call | solution.py:582
  42.1 0.1 collective-permute-start.12
  42.2 0.5 collective-permute-start.13
  42.7 0.1 collective-permute-start.14
  42.8 1.0 %collective-permute-done.13.refs_2_ = bf16[4,64,256]{2,1,0:T(8,128)(2,1)S(1)} collective-permute-done((bf16[4,64,256]{2,1,0:T(8,128)(2,1)S(1)}, bf16[4,64,256]{2,1,0:T(8,128)(2,1)S(1)}, u32[]{:S(2)}, u32[]{:S(2)}) %collective-permute-start.13) | collective-permute-done | bytes 131104 | tf_op jit(solution)/shard_map/ppermute | solution.py:453
  43.8 0.3 collective-permute-done.14.refs_3_
  44.0 1.4 %unpack.2 = (f32[13,256,256]{2,1,0:T(8,128)}, f32[8,128]{1,0:T(8,128)S(1)}) custom-call(s32[1]{0:T(128)} %bitcast.me_ref, f32[13,64,256]{2,1,0:T(8,128)S(1)} %get-tuple-element.53.refs_0_, bf16[5,64,256]{2,1,0:T(8,128)(2,1)S(1)} %collective-permute-done.12.refs_1_, bf16[4,64,256]{2,1,0:T(8,128)(2,1)S(1)} %collective-permute-done.13.refs_2_, ...), custom_call_target="tpu_custom_call" | custom-call | flops 10000000 | bytes 30000 | tf_op jit(solution)/shard_map/unpack/pallas_call | solution.py:615
  45.5 3.0 %collective-permute-done.11.refs_3_ = bf16[13,32,256]{2,1,0:T(8,128)(2,1)S(1)} collective-permute-done((bf16[13,32,256]{2,1,0:T(8,128)(2,1)S(1)}, bf16[13,32,256]{2,1,0:T(8,128)(2,1)S(1)}, u32[]{:S(2)}, u32[]{:S(2)}) %collective-permute-start.11) | collective-permute-done | bytes 213024 | tf_op jit(solution)/shard_map/ppermute | solution.py:453
  48.5 1.4 %unpack.3 = f32[13,256,256]{2,1,0:T(8,128)} custom-call(s32[1]{0:T(128)} %bitcast.me_ref, bf16[13,32,256]{2,1,0:T(8,128)(2,1)S(1)} %collective-permute-done.3.refs_8_.refs_0_, bf16[13,32,256]{2,1,0:T(8,128)(2,1)S(1)} %collective-permute-done.4.refs_9_.refs_1_, ...), custom_call_target="tpu_custom_call", output_to_operand_aliasing={{}: (5, {})} | custom-call | flops 10000000 | bytes 30000 | tf_op jit(solution)/shard_map/unpack/pallas_call | solution.py:615
  (14 shorter events, 0.0 us)
Async XLA Ops:
  3.6 5.1 %copy-start = (bf16[13,272,256]{2,1,0:T(8,128)(2,1)S(1)}, bf16[13,272,256]{2,1,0:T(8,128)(2,1)}, u32[]{:S(2)}) copy-start(bf16[13,272,256]{2,1,0:T(8,128)(2,1)} %get-tuple-element.38.tall) | copy-start | bytes 5431300
  3.6 16.0 %collective-permute-start = (bf16[13,88,128]{2,1,0:T(8,128)(2,1)}, bf16[13,88,128]{2,1,0:T(8,128)(2,1)S(1)}, u32[]{:S(2)}, u32[]{:S(2)}) collective-permute-start(bf16[13,88,128]{2,1,0:T(8,128)(2,1)} %get-tuple-element.33), channel_id=1, source_target_pairs={{0,3},{1,2},{2,1},{3,0},{4,7},{5,6},{6,5},{7,4},{8,11},{9,10},{10,... | collective-permute-start | bytes 878600 | tf_op jit(solution)/shard_map/ppermute | solution.py:453
  6.1 14.0 %collective-permute-start.1 = (bf16[13,88,128]{2,1,0:T(8,128)(2,1)}, bf16[13,88,128]{2,1,0:T(8,128)(2,1)S(1)}, u32[]{:S(2)}, u32[]{:S(2)}) collective-permute-start(bf16[13,88,128]{2,1,0:T(8,128)(2,1)} %get-tuple-element.34), channel_id=1, source_target_pairs={{0,2},{1,3},{2,0},{3,1},{4,6},{5,7},{6,4},{7,5},{8,10},{9,11},{10,... | collective-permute-start | bytes 878600 | tf_op jit(solution)/shard_map/ppermute | solution.py:453
  6.7 13.4 %collective-permute-start.2 = (bf16[13,88,128]{2,1,0:T(8,128)(2,1)}, bf16[13,88,128]{2,1,0:T(8,128)(2,1)S(1)}, u32[]{:S(2)}, u32[]{:S(2)}) collective-permute-start(bf16[13,88,128]{2,1,0:T(8,128)(2,1)} %get-tuple-element.35), channel_id=1, source_target_pairs={{0,1},{1,0},{2,3},{3,2},{4,5},{5,4},{6,7},{7,6},{8,9},{9,8},{10,11... | collective-permute-start | bytes 878600 | tf_op jit(solution)/shard_map/ppermute | solution.py:453
  8.7 8.3 %collective-permute-start.5 = (bf16[13,16,256]{2,1,0:T(8,128)(2,1)S(1)}, bf16[13,16,256]{2,1,0:T(8,128)(2,1)S(1)}, u32[]{:S(2)}, u32[]{:S(2)}) collective-permute-start(bf16[13,16,256]{2,1,0:T(8,128)(2,1)S(1)} %get-tuple-element.39), channel_id=1, source_target_pairs={{0,4},{4,8},{8,12},{12,16},{16,20},{20,24},{24,28},{28,0},{1,5},{5... | collective-permute-start | bytes 319496 | tf_op jit(solution)/shard_map/ppermute | solution.py:533
  10.5 7.1 %collective-permute-start.6 = (bf16[13,16,256]{2,1,0:T(8,128)(2,1)S(1)}, bf16[13,16,256]{2,1,0:T(8,128)(2,1)S(1)}, u32[]{:S(2)}, u32[]{:S(2)}) collective-permute-start(bf16[13,16,256]{2,1,0:T(8,128)(2,1)S(1)} %get-tuple-element.40), channel_id=1, source_target_pairs={{4,0},{8,4},{12,8},{16,12},{20,16},{24,20},{28,24},{0,28},{5,1},{9... | collective-permute-start | bytes 319496 | tf_op jit(solution)/shard_map/ppermute | solution.py:534
  15.8 4.3 %copy-start.1 = (bf16[13,88,128]{2,1,0:T(8,128)(2,1)S(1)}, bf16[13,88,128]{2,1,0:T(8,128)(2,1)}, u32[]{:S(2)}) copy-start(bf16[13,88,128]{2,1,0:T(8,128)(2,1)} %get-tuple-element.32.refs_3_) | copy-start | bytes 878596
  18.1 9.4 %collective-permute-start.7 = (bf16[13,32,256]{2,1,0:T(8,128)(2,1)S(1)}, bf16[13,32,256]{2,1,0:T(8,128)(2,1)S(1)}, u32[]{:S(2)}, u32[]{:S(2)}) collective-permute-start(bf16[13,32,256]{2,1,0:T(8,128)(2,1)S(1)} %get-tuple-element.42), channel_id=1, source_target_pairs={{0,3},{1,2},{2,1},{3,0},{4,7},{5,6},{6,5},{7,4},{8,11},{9,10},{10,... | collective-permute-start | bytes 638984 | tf_op jit(solution)/shard_map/ppermute | solution.py:453
  18.2 12.0 %collective-permute-start.8 = (bf16[13,32,256]{2,1,0:T(8,128)(2,1)S(1)}, bf16[13,32,256]{2,1,0:T(8,128)(2,1)S(1)}, u32[]{:S(2)}, u32[]{:S(2)}) collective-permute-start(bf16[13,32,256]{2,1,0:T(8,128)(2,1)S(1)} %get-tuple-element.43), channel_id=1, source_target_pairs={{0,2},{1,3},{2,0},{3,1},{4,6},{5,7},{6,4},{7,5},{8,10},{9,11},{10,... | collective-permute-start | bytes 638984 | tf_op jit(solution)/shard_map/ppermute | solution.py:453
  19.7 10.5 %collective-permute-start.9 = (bf16[13,32,256]{2,1,0:T(8,128)(2,1)S(1)}, bf16[13,32,256]{2,1,0:T(8,128)(2,1)S(1)}, u32[]{:S(2)}, u32[]{:S(2)}) collective-permute-start(bf16[13,32,256]{2,1,0:T(8,128)(2,1)S(1)} %get-tuple-element.44), channel_id=1, source_target_pairs={{0,1},{1,0},{2,3},{3,2},{4,5},{5,4},{6,7},{7,6},{8,9},{9,8},{10,11... | collective-permute-start | bytes 638984 | tf_op jit(solution)/shard_map/ppermute | solution.py:453
  25.2 12.2 %collective-permute-start.3 = (bf16[13,32,256]{2,1,0:T(8,128)(2,1)S(1)}, bf16[13,32,256]{2,1,0:T(8,128)(2,1)S(1)}, u32[]{:S(2)}, u32[]{:S(2)}) collective-permute-start(bf16[13,32,256]{2,1,0:T(8,128)(2,1)S(1)} %get-tuple-element.36.refs_11_), channel_id=1, source_target_pairs={{0,2},{1,3},{2,0},{3,1},{4,6},{5,7},{6,4},{7,5},{8,10},{9,11},{10,... | collective-permute-start | bytes 638984 | tf_op jit(solution)/shard_map/ppermute | solution.py:453
  27.6 11.8 %collective-permute-start.4 = (bf16[13,32,256]{2,1,0:T(8,128)(2,1)S(1)}, bf16[13,32,256]{2,1,0:T(8,128)(2,1)S(1)}, u32[]{:S(2)}, u32[]{:S(2)}) collective-permute-start(bf16[13,32,256]{2,1,0:T(8,128)(2,1)S(1)} %get-tuple-element.37), channel_id=1, source_target_pairs={{0,3},{1,2},{2,1},{3,0},{4,7},{5,6},{6,5},{7,4},{8,11},{9,10},{10,... | collective-permute-start | bytes 638984 | tf_op jit(solution)/shard_map/ppermute | solution.py:453
  35.7 9.7 %collective-permute-start.10 = (bf16[13,32,256]{2,1,0:T(8,128)(2,1)S(1)}, bf16[13,32,256]{2,1,0:T(8,128)(2,1)S(1)}, u32[]{:S(2)}, u32[]{:S(2)}) collective-permute-start(bf16[13,32,256]{2,1,0:T(8,128)(2,1)S(1)} %get-tuple-element.45), channel_id=1, source_target_pairs={{0,2},{1,3},{2,0},{3,1},{4,6},{5,7},{6,4},{7,5},{8,10},{9,11},{10,... | collective-permute-start | bytes 638984 | tf_op jit(solution)/shard_map/ppermute | solution.py:453
  36.9 11.6 %collective-permute-start.11 = (bf16[13,32,256]{2,1,0:T(8,128)(2,1)S(1)}, bf16[13,32,256]{2,1,0:T(8,128)(2,1)S(1)}, u32[]{:S(2)}, u32[]{:S(2)}) collective-permute-start(bf16[13,32,256]{2,1,0:T(8,128)(2,1)S(1)} %get-tuple-element.46), channel_id=1, source_target_pairs={{0,3},{1,2},{2,1},{3,0},{4,7},{5,6},{6,5},{7,4},{8,11},{9,10},{10,... | collective-permute-start | bytes 638984 | tf_op jit(solution)/shard_map/ppermute | solution.py:453
  42.1 1.9 %collective-permute-start.12 = (bf16[5,64,256]{2,1,0:T(8,128)(2,1)S(1)}, bf16[5,64,256]{2,1,0:T(8,128)(2,1)S(1)}, u32[]{:S(2)}, u32[]{:S(2)}) collective-permute-start(bf16[5,64,256]{2,1,0:T(8,128)(2,1)S(1)} %get-tuple-element.54), channel_id=1, source_target_pairs={{0,1},{1,0},{2,3},{3,2},{4,5},{5,4},{6,7},{7,6},{8,9},{9,8},{10,11... | collective-permute-start | bytes 491528 | tf_op jit(solution)/shard_map/ppermute | solution.py:453
  42.2 1.5 %collective-permute-start.13 = (bf16[4,64,256]{2,1,0:T(8,128)(2,1)S(1)}, bf16[4,64,256]{2,1,0:T(8,128)(2,1)S(1)}, u32[]{:S(2)}, u32[]{:S(2)}) collective-permute-start(bf16[4,64,256]{2,1,0:T(8,128)(2,1)S(1)} %get-tuple-element.55), channel_id=1, source_target_pairs={{0,1},{1,0},{2,3},{3,2},{4,5},{5,4},{6,7},{7,6},{8,9},{9,8},{10,11... | collective-permute-start | bytes 393224 | tf_op jit(solution)/shard_map/ppermute | solution.py:453
  42.7 1.3 %collective-permute-start.14 = (bf16[4,64,256]{2,1,0:T(8,128)(2,1)S(1)}, bf16[4,64,256]{2,1,0:T(8,128)(2,1)S(1)}, u32[]{:S(2)}, u32[]{:S(2)}) collective-permute-start(bf16[4,64,256]{2,1,0:T(8,128)(2,1)S(1)} %get-tuple-element.56), channel_id=1, source_target_pairs={{0,1},{1,0},{2,3},{3,2},{4,5},{5,4},{6,7},{7,6},{8,9},{9,8},{10,11... | collective-permute-start | bytes 393224 | tf_op jit(solution)/shard_map/ppermute | solution.py:453
